TPU v7x, 256 devices: a whole 4x4x8 slice. The times are simulated.
256 devices in a mesh: row: 8 (over x, z_lo), col: 32 (over z_hi, y, core).
Axes of the slice: x: 4, y: 4, z: 8 (z_hi: 4, z_lo: 2; z = z_hi * 2 + z_lo), core: 2. Of those that a mesh axis runs over, the one named last changes fastest.
Arguments:
- features: bfloat16 [65536, 256], P(('row', 'col')), may hold values from -6 to 6
- cotangent: bfloat16 [65536, 256], P(('row', 'col')), may hold values from -6 to 6
- weight: bfloat16 [256, 256], replicated, may hold values from -0.375 to 0.375
- bias: float32 [256], replicated, may hold values from -3 to 3
- adjacency: bfloat16 [8, 6144, 128, 128], P('row', 'col'), may hold values from -0.078125 to 0.078125
- tile_rows: int32 [8, 6144], P('row', 'col'), may hold values from 0 to 63
- tile_cols: int32 [8, 6144], P('row', 'col'), may hold values from 0 to 15
- live_tiles: int32 [8, 32], P('row', 'col'), may hold values from 24 to 192, as said below
Outputs:
- layer_out: bfloat16 [65536, 256], P(('row', 'col'))
- features_grad: bfloat16 [65536, 256], P(('row', 'col'))
- weight_grad: float32 [256, 256], replicated
- bias_grad: float32 [256], replicated
Inputs may be any that keep to these rules, and one draw needn't show every extreme that they name: `live_tiles`: each value is 192, 96, 48 or 24, and some block has 192.
All inputs are finite; a program needn't handle non-finite values.
Results may differ from a plain program's by a relative error of at most 0.025.
Values may be sent and summed in bfloat16 or wider, within the bound.
No kernel may reach another device: no remote copies, remote signals or barrier semaphores. Data moves between devices by JAX's collectives and lax.ppermute only.
A program may use at most 128 MiB of HBM per device.

v0:
```python
import functools
import math

import jax
import jax.numpy as jnp
from jax import lax
from jax.experimental import pallas as pl
from jax.experimental.pallas import tpu as pltpu
from jax.sharding import PartitionSpec as P

GELU_ROOT = 0.7978845608028654
GELU_CUBIC = 0.044715

N_X, N_ZL, N_ZH, N_Y, N_CORE = 4, 2, 4, 4, 2
N_ROW = N_X * N_ZL
N_COL = N_ZH * N_Y * N_CORE
GROUP = 24
VMEM_LIMIT = 60 * 1024 * 1024
LANES = 128


def row_shift(value, dx, dzl):
    pairs = []
    for i in range(N_ROW):
        x, zl = divmod(i, N_ZL)
        pairs.append((i, (x + dx) % N_X * N_ZL + (zl ^ dzl)))
    return lax.ppermute(value, "row", pairs)


def col_shift(value, dzh=0, dy=0, dcore=0):
    pairs = []
    for i in range(N_COL):
        zh, y, core = i // (N_Y * N_CORE), i // N_CORE % N_Y, i % N_CORE
        pairs.append(
            (i, ((zh + dzh) % N_ZH * N_Y + (y + dy) % N_Y) * N_CORE + (core ^ dcore))
        )
    return lax.ppermute(value, "col", pairs)


def tile_kernel(transposed, src_sizes, out_sizes, live, take, put, tiles, *refs):
    n_src, n_out = len(src_sizes), len(out_sizes)
    sources = refs[:n_src]
    outs = refs[n_src : n_src + n_out]
    src, acc, staged, in_sems, out_sems = refs[n_src + n_out :]
    step = pl.program_id(0)

    @pl.when(step == 0)
    def _():
        copies, first = [], 0
        for k, size in enumerate(src_sizes):
            copies.append(
                pltpu.make_async_copy(
                    sources[k], src.at[pl.ds(first, size)], in_sems.at[k]
                )
            )
            first += size
        for copy in copies:
            copy.start()

        @pl.loop(0, acc.shape[0])
        def _(i):
            acc[i] = jnp.zeros(acc.shape[1:], jnp.float32)

        for copy in copies:
            copy.wait()

    @pl.when(step * GROUP < live[0])
    def _():
        @pl.loop(0, GROUP // 8)
        def _(i):
            for j in range(8):
                k = i * 8 + j
                slot = step * GROUP + k
                product = lax.dot_general(
                    tiles[0, k],
                    src[take[slot]],
                    (((0 if transposed else 1,), (0,)), ((), ())),
                    preferred_element_type=jnp.float32,
                )
                acc[put[slot]] += product

    @pl.when(step == pl.num_programs(0) - 1)
    def _():
        copies, first = [], 0
        for k, size in enumerate(out_sizes):
            start = first

            @pl.loop(0, size)
            def _(i):
                staged[start + i] = acc[start + i].astype(jnp.bfloat16)

            copies.append(
                pltpu.make_async_copy(
                    staged.at[pl.ds(start, size)], outs[k], out_sems.at[k]
                )
            )
            copies[-1].start()
            first += size
        for copy in copies:
            copy.wait()


def tile_sum(adjacency, live, take, put, sources, out_sizes, transposed):
    slots, tile = adjacency.shape[1], adjacency.shape[2]
    width = sources[0].shape[-1]
    sources = [s.reshape(-1, tile, width) for s in sources]
    src_sizes = [s.shape[0] for s in sources]

    def tile_block(i, live, take, put):
        return (0, jnp.minimum(i, live[0] // GROUP - 1), 0, 0)

    anywhere = pl.BlockSpec(memory_space=pl.ANY)
    return pl.pallas_call(
        functools.partial(tile_kernel, transposed, src_sizes, out_sizes),
        grid_spec=pltpu.PrefetchScalarGridSpec(
            num_scalar_prefetch=3,
            grid=(slots // GROUP,),
            in_specs=[pl.BlockSpec((1, GROUP, tile, tile), tile_block)]
            + [anywhere] * len(sources),
            out_specs=[anywhere] * len(out_sizes),
            scratch_shapes=[
                pltpu.VMEM((sum(src_sizes), tile, width), jnp.bfloat16),
                pltpu.VMEM((sum(out_sizes), tile, width), jnp.float32),
                pltpu.VMEM((sum(out_sizes), tile, width), jnp.bfloat16),
                pltpu.SemaphoreType.DMA((len(sources),)),
                pltpu.SemaphoreType.DMA((len(out_sizes),)),
            ],
        ),
        out_shape=[
            jax.ShapeDtypeStruct((size, tile, width), jnp.bfloat16)
            for size in out_sizes
        ],
        compiler_params=pltpu.CompilerParams(vmem_limit_bytes=VMEM_LIMIT),
        cost_estimate=pl.CostEstimate(
            flops=2 * slots * tile * tile * width,
            bytes_accessed=slots * tile * tile * 2,
            transcendentals=0,
        ),
    )(live, take, put, adjacency, *sources)


def split_dot(exact, other, dims):
    high = exact.astype(jnp.bfloat16)
    low = (exact - high.astype(jnp.float32)).astype(jnp.bfloat16)
    dot = functools.partial(
        lax.dot_general, dimension_numbers=dims, preferred_element_type=jnp.float32
    )
    return dot(high, other) + dot(low, other)


def middle_kernel(h0, h1, h2, h3, weight, bias, cotangent, out, grad, load):
    total = (
        h0[...].astype(jnp.float32)
        + h1[...].astype(jnp.float32)
        + h2[...].astype(jnp.float32)
        + h3[...].astype(jnp.float32)
    )
    shifted = split_dot(total, weight[...], (((1,), (0,)), ((), ()))) + bias[...]
    tanh_term = jnp.tanh(GELU_ROOT * (shifted + GELU_CUBIC * shifted * shifted * shifted))
    out[...] = (0.5 * shifted * (1.0 + tanh_term)).astype(jnp.bfloat16)
    slope = 0.5 * (1.0 + tanh_term) + 0.5 * shifted * (
        1.0 - tanh_term * tanh_term
    ) * GELU_ROOT * (1.0 + 3.0 * GELU_CUBIC * shifted * shifted)
    pre_grad = cotangent[...].astype(jnp.float32) * slope
    rounded = pre_grad.astype(jnp.bfloat16)
    grad[...] = rounded
    rows = (((0,), (0,)), ((), ()))
    load[:, : total.shape[1]] = split_dot(total, rounded, rows)
    ones = jnp.ones((total.shape[0], LANES), jnp.bfloat16)
    load[:, total.shape[1] :] = split_dot(pre_grad, ones, rows)


def middle(pieces, weight, bias, cotangent):
    rows, width = cotangent.shape
    vmem = pl.BlockSpec(memory_space=pltpu.VMEM)
    return pl.pallas_call(
        middle_kernel,
        in_specs=[vmem] * 7,
        out_specs=[vmem] * 3,
        out_shape=[
            jax.ShapeDtypeStruct((rows, width), jnp.bfloat16),
            jax.ShapeDtypeStruct((rows, width), jnp.bfloat16),
            jax.ShapeDtypeStruct((width, width + LANES), jnp.float32),
        ],
        compiler_params=pltpu.CompilerParams(vmem_limit_bytes=VMEM_LIMIT),
    )(*pieces, weight, bias.reshape(1, width), cotangent)


def last_kernel(pieces, weight, out):
    total = pieces[0].astype(jnp.float32)
    for k in range(1, pieces.shape[0]):
        total += pieces[k].astype(jnp.float32)
    out[...] = lax.dot_general(
        total.astype(jnp.bfloat16),
        weight[...],
        (((1,), (1,)), ((), ())),
        preferred_element_type=jnp.float32,
    ).astype(jnp.bfloat16)


def last(pieces, weight):
    _, rows, width = pieces.shape
    vmem = pl.BlockSpec(memory_space=pltpu.VMEM)
    return pl.pallas_call(
        last_kernel,
        in_specs=[vmem] * 2,
        out_specs=vmem,
        out_shape=jax.ShapeDtypeStruct((rows, width), jnp.bfloat16),
    )(pieces, weight)


def merge(pieces):
    return sum((p.astype(jnp.float32) for p in pieces[1:]), pieces[0].astype(jnp.float32)).astype(
        jnp.bfloat16
    )


def shards(features, cotangent, weight, bias, adjacency, tile_rows, tile_cols, live_tiles):
    vertices, width = features.shape
    tile = adjacency.shape[2]
    scale = 1.0 / math.sqrt(vertices * N_ROW * N_COL)
    live = live_tiles.reshape(1)
    row_id, col_id = lax.axis_index("row"), lax.axis_index("col")
    my_x, my_zl = row_id // N_ZL, row_id % N_ZL
    my_zh, my_y, my_core = col_id // 8, col_id // 2 % 4, col_id % 2

    per = vertices // tile
    r, c = tile_rows[0], tile_cols[0]
    rc, cc = r // per, c // per
    r_zh, r_y, r_core = rc // 8, rc // 2 % 4, rc % 2
    c_x, c_zl = cc // 2, cc % 2
    half = (r_core ^ my_core) * 16
    ahead = (r_zh - my_zh) & 3
    part = ((ahead == 3) | (ahead == 0)).astype(jnp.int32)
    place = ((ahead == 1) | (ahead == 0)).astype(jnp.int32)
    put_rows = (half + part * 8 + ((r_y - my_y) & 3) * 2 + place) * per + r % per
    take_rows = (half + ((my_y - r_y) & 3) * 4 + ((my_zh - r_zh) & 3)) * per + r % per
    take_cols = (((my_x - c_x) & 3) * 2 + (c_zl ^ my_zl)) * per + c % per

    moves = [(dx, dzl) for dx in range(N_X) for dzl in range(N_ZL)]
    with jax.named_scope("gather_features"):
        sources = [features] + [row_shift(features, *m) for m in moves[1:]]
    with jax.named_scope("tiles_forward"):
        parts = tile_sum(
            adjacency, live, take_cols, put_rows, sources, [8 * per] * 4, False
        )
    with jax.named_scope("sum_over_col"):
        sums = []
        for keep, send in zip(parts[:2], parts[2:]):
            other = col_shift(send, dcore=1)
            cut = [slice(2 * per * k, 2 * per * (k + 1)) for k in range(N_Y)]
            added = [merge([keep[s], other[s]]) for s in cut]
            arrived = [added[0]] + [col_shift(added[k], dy=k) for k in (2, 1, 3)]
            sums.append(merge([p[:per] for p in arrived]))
            sums.append(merge([p[per:] for p in arrived]))
        pieces = [sums[3]] + [col_shift(sums[i], dzh=k) for i, k in enumerate((2, 1, 3))]
        pieces = [p.reshape(vertices, width) for p in pieces]
    with jax.named_scope("pointwise"):
        layer_out, grad, load = middle(pieces, weight, bias, cotangent)
    with jax.named_scope("gather_gradients"):
        stack = jnp.concatenate([col_shift(grad, dzh=k) for k in range(1, N_ZH)])
        ours = [col_shift(grad, dy=k) for k in range(1, N_Y)]
    with jax.named_scope("sum_weight_grad"):
        load = lax.all_to_all(load[:, None], ("row", "col"), 0, 0, tiled=True)
        load, stack, *ours = lax.optimization_barrier((load, stack, *ours))
        total = jnp.sum(load, axis=0, keepdims=True) * scale
        spread = jnp.broadcast_to(total, load.shape)
        load = lax.all_to_all(spread, ("row", "col"), 0, 0, tiled=True)
    with jax.named_scope("gather_gradients"):
        theirs = [col_shift(stack, dy=k) for k in range(1, N_Y)]
        *theirs, load = lax.optimization_barrier((*theirs, load))
        here = [grad, stack]
        for pair in zip(ours, theirs):
            here += pair
        there = [col_shift(p, dcore=1) for p in here]
    weight_grad, bias_grad = load[:, 0, :width], load[:, 0, width]
    with jax.named_scope("tiles_backward"):
        (back,) = tile_sum(adjacency, live, take_rows, c, here + there, [N_ROW * per], True)
    with jax.named_scope("sum_over_row"):
        back = lax.all_to_all(
            back.reshape(N_ROW, vertices, width), "row", 0, 0, tiled=True
        )
        features_grad = last(back, weight)
    return layer_out, features_grad, weight_grad, bias_grad


def solution(mesh):
    placed = (
        P(("row", "col"), None),
        P(("row", "col"), None),
        P(),
        P(),
        P("row", "col", None, None),
        P("row", "col"),
        P("row", "col"),
        P("row", "col"),
    )
    return jax.shard_map(
        shards,
        mesh=mesh,
        in_specs=placed,
        out_specs=(P(("row", "col"), None), P(("row", "col"), None), P(), P()),
        check_vma=False,
    )
```

profile of v0, /device:TPU:1, one launch (start us, length us, event | category | flops | bytes accessed | tf_op | source)
XLA Modules:
  0.0 209.6 jit_solution(2289069416412966518)
XLA Ops:
  0.6 5.0 %collective-permute-start.4 = (bf16[256,256]{1,0:T(8,128)(2,1)}, bf16[256,256]{1,0:T(8,128)(2,1)S(1)}, u32[]{:S(2)}, u32[]{:S(2)}) collective-permute-start(bf16[256,256]{1,0:T(8,128)(2,1)} %param.8), channel_id=1, source_target_pairs={{0,160},{32,128},{64,224},{96,192},{128,32},{160,0},{192,96},{224,... | collective-permute-start | bytes 393224 | tf_op jit(solution)/shard_map/gather_features/ppermute | solution.py:27
  6.6 1.2 collective-permute-start.1
  7.8 1.6 collective-permute-start
  10.1 1.3 multiply_add_fusion
  11.4 1.2 collective-permute-start.6
  12.6 3.8 %collective-permute-done.3 = bf16[256,256]{1,0:T(8,128)(2,1)S(1)} collective-permute-done((bf16[256,256]{1,0:T(8,128)(2,1)}, bf16[256,256]{1,0:T(8,128)(2,1)S(1)}, u32[]{:S(2)}, u32[]{:S(2)}) %collective-permute-start.3) | collective-permute-done | bytes 131104 | tf_op jit(solution)/shard_map/gather_features/ppermute | solution.py:27
  16.4 1.3 fusion.2
  17.8 1.7 collective-permute-done.1
  19.5 1.8 collective-permute-done.5
  21.9 6.6 %tiles_forward.1 = (bf16[16,128,256]{2,1,0:T(8,128)(2,1)}, bf16[16,128,256]{2,1,0:T(8,128)(2,1)}, bf16[16,128,256]{2,1,0:T(8,128)(2,1)}, bf16[16,128,256]{2,1,0:T(8,128)(2,1)}) custom-call(s32[1]{0:T(128)} %bitcast.37.live, s32[192]{0:T(256)} %get-tuple-element.51.take, s32[192]{0:T(256)} %get-tuple-element.52.put, bf16[1,192,128,128]{3,2,1,0:T(8,128)(2,1)} %tiles.3, ...), custom_call_target="tpu_custom_call" | custom-call | flops 1610612736 | bytes 6291456 | tf_op jit(solution)/shard_map/tiles_forward/pallas_call | solution.py:113
  28.5 4.4 %collective-permute-start.7 = (bf16[16,128,256]{2,1,0:T(8,128)(2,1)}, bf16[16,128,256]{2,1,0:T(8,128)(2,1)S(1)}, u32[]{:S(2)}, u32[]{:S(2)}) collective-permute-start(bf16[16,128,256]{2,1,0:T(8,128)(2,1)} %get-tuple-element.21), channel_id=1, source_target_pairs={{0,1},{1,0},{2,3},{3,2},{4,5},{5,4},{6,7},{7,6},{8,9},{9,8},{10,11... | collective-permute-start | bytes 3145736 | tf_op jit(solution)/shard_map/sum_over_col/ppermute | solution.py:37
  33.0 2.4 %collective-permute-done.7 = bf16[16,128,256]{2,1,0:T(8,128)(2,1)S(1)} collective-permute-done((bf16[16,128,256]{2,1,0:T(8,128)(2,1)}, bf16[16,128,256]{2,1,0:T(8,128)(2,1)S(1)}, u32[]{:S(2)}, u32[]{:S(2)}) %collective-permute-start.7) | collective-permute-done | bytes 1048608 | tf_op jit(solution)/shard_map/sum_over_col/ppermute | solution.py:37
  35.4 1.5 add_convert_fusion.7
  36.9 2.8 %collective-permute-start.10 = (bf16[4,128,256]{2,1,0:T(8,128)(2,1)S(1)}, bf16[4,128,256]{2,1,0:T(8,128)(2,1)S(1)}, u32[]{:S(2)}, u32[]{:S(2)}) collective-permute-start(bf16[4,128,256]{2,1,0:T(8,128)(2,1)S(1)} %get-tuple-element.44), channel_id=1, source_target_pairs={{0,6},{1,7},{2,0},{3,1},{4,2},{5,3},{6,4},{7,5},{8,14},{9,15},{10,... | collective-permute-start | bytes 786440 | tf_op jit(solution)/shard_map/sum_over_col/ppermute | solution.py:37
  39.7 5.7 %collective-permute-start.8 = (bf16[4,128,256]{2,1,0:T(8,128)(2,1)S(1)}, bf16[4,128,256]{2,1,0:T(8,128)(2,1)S(1)}, u32[]{:S(2)}, u32[]{:S(2)}) collective-permute-start(bf16[4,128,256]{2,1,0:T(8,128)(2,1)S(1)} %get-tuple-element.46), channel_id=1, source_target_pairs={{0,4},{1,5},{2,6},{3,7},{4,0},{5,1},{6,2},{7,3},{8,12},{9,13},{10,... | collective-permute-start | bytes 786440 | tf_op jit(solution)/shard_map/sum_over_col/ppermute | solution.py:37
  45.3 1.5 add_convert_fusion.3
  48.4 3.0 %collective-permute-start.12 = (bf16[4,128,256]{2,1,0:T(8,128)(2,1)S(1)}, bf16[4,128,256]{2,1,0:T(8,128)(2,1)S(1)}, u32[]{:S(2)}, u32[]{:S(2)}) collective-permute-start(bf16[4,128,256]{2,1,0:T(8,128)(2,1)S(1)} %get-tuple-element.42), channel_id=1, source_target_pairs={{0,4},{1,5},{2,6},{3,7},{4,0},{5,1},{6,2},{7,3},{8,12},{9,13},{10,... | collective-permute-start | bytes 786440 | tf_op jit(solution)/shard_map/sum_over_col/ppermute | solution.py:37
  51.4 5.3 %collective-permute-done.8 = bf16[4,128,256]{2,1,0:T(8,128)(2,1)S(1)} collective-permute-done((bf16[4,128,256]{2,1,0:T(8,128)(2,1)S(1)}, bf16[4,128,256]{2,1,0:T(8,128)(2,1)S(1)}, u32[]{:S(2)}, u32[]{:S(2)}) %collective-permute-start.8) | collective-permute-done | bytes 262176 | tf_op jit(solution)/shard_map/sum_over_col/ppermute | solution.py:37
  57.5 3.9 %collective-permute-start.17 = (bf16[2,128,256]{2,1,0:T(8,128)(2,1)S(1)}, bf16[2,128,256]{2,1,0:T(8,128)(2,1)S(1)}, u32[]{:S(2)}, u32[]{:S(2)}) collective-permute-start(bf16[2,128,256]{2,1,0:T(8,128)(2,1)S(1)} %get-tuple-element.47), channel_id=1, source_target_pairs={{0,24},{1,25},{2,26},{3,27},{4,28},{5,29},{6,30},{7,31},{8,0},{9,1... | collective-permute-start | bytes 393224 | tf_op jit(solution)/shard_map/sum_over_col/ppermute | solution.py:37
  61.6 6.3 %collective-permute-done.12 = bf16[4,128,256]{2,1,0:T(8,128)(2,1)S(1)} collective-permute-done((bf16[4,128,256]{2,1,0:T(8,128)(2,1)S(1)}, bf16[4,128,256]{2,1,0:T(8,128)(2,1)S(1)}, u32[]{:S(2)}, u32[]{:S(2)}) %collective-permute-start.12) | collective-permute-done | bytes 262176 | tf_op jit(solution)/shard_map/sum_over_col/ppermute | solution.py:37
  68.1 1.3 collective-permute-start.16
  69.4 4.9 %collective-permute-start.15 = (bf16[2,128,256]{2,1,0:T(8,128)(2,1)S(1)}, bf16[2,128,256]{2,1,0:T(8,128)(2,1)S(1)}, u32[]{:S(2)}, u32[]{:S(2)}) collective-permute-start(bf16[2,128,256]{2,1,0:T(8,128)(2,1)S(1)} %get-tuple-element.50), channel_id=1, source_target_pairs={{0,16},{1,17},{2,18},{3,19},{4,20},{5,21},{6,22},{7,23},{8,24},{9,... | collective-permute-start | bytes 393224 | tf_op jit(solution)/shard_map/sum_over_col/ppermute | solution.py:37
  74.5 5.3 %collective-permute-done.15 = bf16[2,128,256]{2,1,0:T(8,128)(2,1)S(1)} collective-permute-done((bf16[2,128,256]{2,1,0:T(8,128)(2,1)S(1)}, bf16[2,128,256]{2,1,0:T(8,128)(2,1)S(1)}, u32[]{:S(2)}, u32[]{:S(2)}) %collective-permute-start.15) | collective-permute-done | bytes 131104 | tf_op jit(solution)/shard_map/sum_over_col/ppermute | solution.py:37
  80.5 2.7 %pointwise.1 = (bf16[256,256]{1,0:T(8,128)(2,1)}, bf16[256,256]{1,0:T(8,128)(2,1)}, f32[256,384]{1,0:T(8,128)}) custom-call(bf16[256,256]{1,0:T(8,128)(2,1)} %bitcast.41, bf16[256,256]{1,0:T(8,128)(2,1)} %bitcast.67, bf16[256,256]{1,0:T(8,128)(2,1)} %bitcast.66, bf16[256,256]{1,0:T(8,128)(2,1)} %bitcast.65, bf16[256,256]{1,0:T(8,128)(2,1)} %weight.3, ...), custom_call_target="tpu_custom_call" | custom-call | tf_op jit(solution)/shard_map/pointwise/pallas_call | solution.py:176
  83.2 2.1 %copy.12 = f32[256,1,384]{2,1,0:T(1,128)} copy(f32[256,1,384]{2,0,1:T(8,128)} %bitcast.49) | data formatting | bytes 786432 | tf_op jit(solution)/shard_map/sum_weight_grad/broadcast_in_dim | solution.py:264
  85.3 14.5 %all-to-all-start = ((f32[256,1,384]{2,1,0:T(1,128)}), f32[256,1,384]{2,1,0:T(1,128)S(1)}, u32[]{:S(2)}, u32[]{:S(2)}) async-start(f32[256,1,384]{2,1,0:T(1,128)} %copy.12), calls=%async_computation | async-start | bytes 786432 | tf_op jit(solution)/shard_map/sum_weight_grad/all_to_all | solution.py:264
  99.9 5.0 %collective-permute-start.20 = (bf16[256,256]{1,0:T(8,128)(2,1)}, bf16[256,256]{1,0:T(8,128)(2,1)S(1)}, u32[]{:S(2)}, u32[]{:S(2)}) collective-permute-start(bf16[256,256]{1,0:T(8,128)(2,1)} %get-tuple-element.25), channel_id=1, source_target_pairs={{0,24},{1,25},{2,26},{3,27},{4,28},{5,29},{6,30},{7,31},{8,0},{9,1... | collective-permute-start | bytes 393224 | tf_op jit(solution)/shard_map/gather_gradients/ppermute | solution.py:37
  104.9 1.4 collective-permute-start.19
  106.3 2.3 %collective-permute-start.18 = (bf16[256,256]{1,0:T(8,128)(2,1)}, bf16[256,256]{1,0:T(8,128)(2,1)S(1)}, u32[]{:S(2)}, u32[]{:S(2)}) collective-permute-start(bf16[256,256]{1,0:T(8,128)(2,1)} %get-tuple-element.25), channel_id=1, source_target_pairs={{0,8},{1,9},{2,10},{3,11},{4,12},{5,13},{6,14},{7,15},{8,16},{9,17... | collective-permute-start | bytes 393224 | tf_op jit(solution)/shard_map/gather_gradients/ppermute | solution.py:37
  108.5 2.6 %collective-permute-start.23 = (bf16[256,256]{1,0:T(8,128)(2,1)}, bf16[256,256]{1,0:T(8,128)(2,1)S(1)}, u32[]{:S(2)}, u32[]{:S(2)}) collective-permute-start(bf16[256,256]{1,0:T(8,128)(2,1)} %get-tuple-element.25), channel_id=1, source_target_pairs={{0,6},{1,7},{2,0},{3,1},{4,2},{5,3},{6,4},{7,5},{8,14},{9,15},{10,... | collective-permute-start | bytes 393224 | tf_op jit(solution)/shard_map/gather_gradients/ppermute | solution.py:37
  111.6 3.9 %collective-permute-done.20 = bf16[256,256]{1,0:T(8,128)(2,1)S(1)} collective-permute-done((bf16[256,256]{1,0:T(8,128)(2,1)}, bf16[256,256]{1,0:T(8,128)(2,1)S(1)}, u32[]{:S(2)}, u32[]{:S(2)}) %collective-permute-start.20) | collective-permute-done | bytes 131104 | tf_op jit(solution)/shard_map/gather_gradients/ppermute | solution.py:37
  115.5 1.2 collective-permute-start.21
  116.7 3.7 %collective-permute-done.19 = bf16[256,256]{1,0:T(8,128)(2,1)S(1)} collective-permute-done((bf16[256,256]{1,0:T(8,128)(2,1)}, bf16[256,256]{1,0:T(8,128)(2,1)S(1)}, u32[]{:S(2)}, u32[]{:S(2)}) %collective-permute-start.19) | collective-permute-done | bytes 131104 | tf_op jit(solution)/shard_map/gather_gradients/ppermute | solution.py:37
  120.4 3.2 %collective-permute-done.18 = bf16[256,256]{1,0:T(8,128)(2,1)S(1)} collective-permute-done((bf16[256,256]{1,0:T(8,128)(2,1)}, bf16[256,256]{1,0:T(8,128)(2,1)S(1)}, u32[]{:S(2)}, u32[]{:S(2)}) %collective-permute-start.18) | collective-permute-done | bytes 131104 | tf_op jit(solution)/shard_map/gather_gradients/ppermute | solution.py:37
  125.0 14.6 %all-to-all-start.1 = ((f32[256,1,384]{2,1,0:T(1,128)}), f32[256,1,384]{2,1,0:T(1,128)S(1)}, u32[]{:S(2)}, u32[]{:S(2)}) async-start(f32[256,1,384]{2,1,0:T(1,128)} %broadcast_in_dim.10), calls=%async_computation.1 | async-start | bytes 786432 | tf_op jit(solution)/shard_map/sum_weight_grad/all_to_all | solution.py:268
  139.6 2.7 %collective-permute-start.26 = (bf16[768,256]{1,0:T(8,128)(2,1)S(1)}, bf16[768,256]{1,0:T(8,128)(2,1)S(1)}, u32[]{:S(2)}, u32[]{:S(2)}) collective-permute-start(bf16[768,256]{1,0:T(8,128)(2,1)S(1)} %pad_maximum_fusion), channel_id=1, source_target_pairs={{0,6},{1,7},{2,0},{3,1},{4,2},{5,3},{6,4},{7,5},{8,14},{9,15},{10,... | collective-permute-start | bytes 1179656 | tf_op jit(solution)/shard_map/gather_gradients/ppermute | solution.py:37
  143.4 1.2 collective-permute-start.27
  144.6 11.7 %collective-permute-done.26 = bf16[768,256]{1,0:T(8,128)(2,1)S(1)} collective-permute-done((bf16[768,256]{1,0:T(8,128)(2,1)S(1)}, bf16[768,256]{1,0:T(8,128)(2,1)S(1)}, u32[]{:S(2)}, u32[]{:S(2)}) %collective-permute-start.26) | collective-permute-done | bytes 393248 | tf_op jit(solution)/shard_map/gather_gradients/ppermute | solution.py:37
  156.3 7.3 %collective-permute-start.29 = (bf16[256,256]{1,0:T(8,128)(2,1)S(1)}, bf16[256,256]{1,0:T(8,128)(2,1)}, u32[]{:S(2)}, u32[]{:S(2)}) collective-permute-start(bf16[256,256]{1,0:T(8,128)(2,1)S(1)} %collective-permute-done.21), channel_id=1, source_target_pairs={{0,1},{1,0},{2,3},{3,2},{4,5},{5,4},{6,7},{7,6},{8,9},{9,8},{10,11... | collective-permute-start | bytes 393224 | tf_op jit(solution)/shard_map/gather_gradients/ppermute | solution.py:37
  163.6 3.0 %collective-permute-done.24 = bf16[768,256]{1,0:T(8,128)(2,1)S(1)} collective-permute-done((bf16[768,256]{1,0:T(8,128)(2,1)S(1)}, bf16[768,256]{1,0:T(8,128)(2,1)S(1)}, u32[]{:S(2)}, u32[]{:S(2)}) %collective-permute-start.24) | collective-permute-done | bytes 393248 | tf_op jit(solution)/shard_map/gather_gradients/ppermute | solution.py:37
  167.7 2.1 collective-permute-done.31
  170.2 1.0 collective-permute-done.33
  172.6 6.6 %tiles_backward.1 = bf16[16,128,256]{2,1,0:T(8,128)(2,1)} custom-call(s32[1]{0:T(128)} %bitcast.38.live, s32[192]{0:T(256)} %get-tuple-element.36.take, s32[192]{0:T(256)} %bitcast.69, bf16[1,192,128,128]{3,2,1,0:T(8,128)(2,1)} %tiles.3, bf16[2,128,256]{2,1,0:T(8,128)(2,1)} %bitcast.57, bf16[6,128,256]{2,1,0:T(8,128)(2,1)} %bitcast.40, ...), custom_call_target="tpu_custom_call" | custom-call | flops 1610612736 | bytes 6291456 | tf_op jit(solution)/shard_map/tiles_backward/pallas_call | solution.py:113
  179.2 11.5 %all-to-all-start.2 = ((bf16[8,256,256]{2,1,0:T(8,128)(2,1)}), bf16[8,256,256]{2,1,0:T(8,128)(2,1)S(1)}, u32[]{:S(2)}, u32[]{:S(2)}) async-start(bf16[8,256,256]{2,1,0:T(8,128)(2,1)} %bitcast.39), calls=%async_computation.2 | async-start | bytes 2097152 | tf_op jit(solution)/shard_map/sum_over_row/all_to_all | solution.py:280
  191.6 1.6 slice_reduce_fusion
  193.2 13.2 %all-to-all-done.2.pieces = bf16[8,256,256]{2,1,0:T(8,128)(2,1)S(1)} async-done(((bf16[8,256,256]{2,1,0:T(8,128)(2,1)}), bf16[8,256,256]{2,1,0:T(8,128)(2,1)S(1)}, u32[]{:S(2)}, u32[]{:S(2)}) %all-to-all-start.2) | async-done | bytes 1048608 | tf_op jit(solution)/shard_map/sum_over_row/all_to_all | solution.py:280
  206.4 1.0 copy-done
  207.5 2.2 %sum_over_row.1 = bf16[256,256]{1,0:T(8,128)(2,1)} custom-call(bf16[8,256,256]{2,1,0:T(8,128)(2,1)} %copy-done, bf16[256,256]{1,0:T(8,128)(2,1)} %weight.3), custom_call_target="tpu_custom_call" | custom-call | tf_op jit(solution)/shard_map/sum_over_row/pallas_call | solution.py:204
  (94 shorter events, 11.9 us)
Async XLA Ops:
  0.6 10.8 %collective-permute-start.4 = (bf16[256,256]{1,0:T(8,128)(2,1)}, bf16[256,256]{1,0:T(8,128)(2,1)S(1)}, u32[]{:S(2)}, u32[]{:S(2)}) collective-permute-start(bf16[256,256]{1,0:T(8,128)(2,1)} %param.8), channel_id=1, source_target_pairs={{0,160},{32,128},{64,224},{96,192},{128,32},{160,0},{192,96},{224,... | collective-permute-start | bytes 393224 | tf_op jit(solution)/shard_map/gather_features/ppermute | solution.py:27
  5.6 10.8 %collective-permute-start.3 = (bf16[256,256]{1,0:T(8,128)(2,1)}, bf16[256,256]{1,0:T(8,128)(2,1)S(1)}, u32[]{:S(2)}, u32[]{:S(2)}) collective-permute-start(bf16[256,256]{1,0:T(8,128)(2,1)} %param.8), channel_id=1, source_target_pairs={{0,128},{32,160},{64,192},{96,224},{128,0},{160,32},{192,64},{224,... | collective-permute-start | bytes 393224 | tf_op jit(solution)/shard_map/gather_features/ppermute | solution.py:27
  5.9 11.9 %collective-permute-start.2 = (bf16[256,256]{1,0:T(8,128)(2,1)}, bf16[256,256]{1,0:T(8,128)(2,1)S(1)}, u32[]{:S(2)}, u32[]{:S(2)}) collective-permute-start(bf16[256,256]{1,0:T(8,128)(2,1)} %param.8), channel_id=1, source_target_pairs={{0,96},{32,64},{64,160},{96,128},{128,224},{160,192},{192,32},{224... | collective-permute-start | bytes 393224 | tf_op jit(solution)/shard_map/gather_features/ppermute | solution.py:27
  6.6 12.8 %collective-permute-start.1 = (bf16[256,256]{1,0:T(8,128)(2,1)}, bf16[256,256]{1,0:T(8,128)(2,1)S(1)}, u32[]{:S(2)}, u32[]{:S(2)}) collective-permute-start(bf16[256,256]{1,0:T(8,128)(2,1)} %param.8), channel_id=1, source_target_pairs={{0,64},{32,96},{64,128},{96,160},{128,192},{160,224},{192,0},{224,... | collective-permute-start | bytes 393224 | tf_op jit(solution)/shard_map/gather_features/ppermute | solution.py:27
  7.8 11.6 %collective-permute-start = (bf16[256,256]{1,0:T(8,128)(2,1)}, bf16[256,256]{1,0:T(8,128)(2,1)S(1)}, u32[]{:S(2)}, u32[]{:S(2)}) collective-permute-start(bf16[256,256]{1,0:T(8,128)(2,1)} %param.8), channel_id=1, source_target_pairs={{0,32},{32,0},{64,96},{96,64},{128,160},{160,128},{192,224},{224,1... | collective-permute-start | bytes 393224 | tf_op jit(solution)/shard_map/gather_features/ppermute | solution.py:27
  11.4 9.8 %copy-start.9 = (bf16[256,256]{1,0:T(8,128)(2,1)}, bf16[256,256]{1,0:T(8,128)(2,1)S(1)}, u32[]{:S(2)}) copy-start(bf16[256,256]{1,0:T(8,128)(2,1)S(1)} %collective-permute-done.4) | copy-start | bytes 393220
  11.4 8.1 %collective-permute-start.6 = (bf16[256,256]{1,0:T(8,128)(2,1)}, bf16[256,256]{1,0:T(8,128)(2,1)S(1)}, u32[]{:S(2)}, u32[]{:S(2)}) collective-permute-start(bf16[256,256]{1,0:T(8,128)(2,1)} %param.8), channel_id=1, source_target_pairs={{0,224},{32,192},{64,32},{96,0},{128,96},{160,64},{192,160},{224,1... | collective-permute-start | bytes 393224 | tf_op jit(solution)/shard_map/gather_features/ppermute | solution.py:27
  16.4 4.8 %collective-permute-start.5 = (bf16[256,256]{1,0:T(8,128)(2,1)}, bf16[256,256]{1,0:T(8,128)(2,1)S(1)}, u32[]{:S(2)}, u32[]{:S(2)}) collective-permute-start(bf16[256,256]{1,0:T(8,128)(2,1)} %param.8), channel_id=1, source_target_pairs={{0,192},{32,224},{64,0},{96,32},{128,64},{160,96},{192,128},{224,1... | collective-permute-start | bytes 393224 | tf_op jit(solution)/shard_map/gather_features/ppermute | solution.py:27
  28.5 6.9 %collective-permute-start.7 = (bf16[16,128,256]{2,1,0:T(8,128)(2,1)}, bf16[16,128,256]{2,1,0:T(8,128)(2,1)S(1)}, u32[]{:S(2)}, u32[]{:S(2)}) collective-permute-start(bf16[16,128,256]{2,1,0:T(8,128)(2,1)} %get-tuple-element.21), channel_id=1, source_target_pairs={{0,1},{1,0},{2,3},{3,2},{4,5},{5,4},{6,7},{7,6},{8,9},{9,8},{10,11... | collective-permute-start | bytes 3145736 | tf_op jit(solution)/shard_map/sum_over_col/ppermute | solution.py:37
  32.9 12.5 %collective-permute-start.11 = (bf16[16,128,256]{2,1,0:T(8,128)(2,1)}, bf16[16,128,256]{2,1,0:T(8,128)(2,1)S(1)}, u32[]{:S(2)}, u32[]{:S(2)}) collective-permute-start(bf16[16,128,256]{2,1,0:T(8,128)(2,1)} %get-tuple-element.23), channel_id=1, source_target_pairs={{0,1},{1,0},{2,3},{3,2},{4,5},{5,4},{6,7},{7,6},{8,9},{9,8},{10,11... | collective-permute-start | bytes 3145736 | tf_op jit(solution)/shard_map/sum_over_col/ppermute | solution.py:37
  36.9 11.5 %collective-permute-start.10 = (bf16[4,128,256]{2,1,0:T(8,128)(2,1)S(1)}, bf16[4,128,256]{2,1,0:T(8,128)(2,1)S(1)}, u32[]{:S(2)}, u32[]{:S(2)}) collective-permute-start(bf16[4,128,256]{2,1,0:T(8,128)(2,1)S(1)} %get-tuple-element.44), channel_id=1, source_target_pairs={{0,6},{1,7},{2,0},{3,1},{4,2},{5,3},{6,4},{7,5},{8,14},{9,15},{10,... | collective-permute-start | bytes 786440 | tf_op jit(solution)/shard_map/sum_over_col/ppermute | solution.py:37
  39.7 11.7 %collective-permute-start.9 = (bf16[4,128,256]{2,1,0:T(8,128)(2,1)S(1)}, bf16[4,128,256]{2,1,0:T(8,128)(2,1)S(1)}, u32[]{:S(2)}, u32[]{:S(2)}) collective-permute-start(bf16[4,128,256]{2,1,0:T(8,128)(2,1)S(1)} %get-tuple-element.45), channel_id=1, source_target_pairs={{0,2},{1,3},{2,4},{3,5},{4,6},{5,7},{6,0},{7,1},{8,10},{9,11},{10,... | collective-permute-start | bytes 786440 | tf_op jit(solution)/shard_map/sum_over_col/ppermute | solution.py:37
  39.7 17.0 %collective-permute-start.8 = (bf16[4,128,256]{2,1,0:T(8,128)(2,1)S(1)}, bf16[4,128,256]{2,1,0:T(8,128)(2,1)S(1)}, u32[]{:S(2)}, u32[]{:S(2)}) collective-permute-start(bf16[4,128,256]{2,1,0:T(8,128)(2,1)S(1)} %get-tuple-element.46), channel_id=1, source_target_pairs={{0,4},{1,5},{2,6},{3,7},{4,0},{5,1},{6,2},{7,3},{8,12},{9,13},{10,... | collective-permute-start | bytes 786440 | tf_op jit(solution)/shard_map/sum_over_col/ppermute | solution.py:37
  46.8 14.5 %collective-permute-start.14 = (bf16[4,128,256]{2,1,0:T(8,128)(2,1)S(1)}, bf16[4,128,256]{2,1,0:T(8,128)(2,1)S(1)}, u32[]{:S(2)}, u32[]{:S(2)}) collective-permute-start(bf16[4,128,256]{2,1,0:T(8,128)(2,1)S(1)} %get-tuple-element.40), channel_id=1, source_target_pairs={{0,6},{1,7},{2,0},{3,1},{4,2},{5,3},{6,4},{7,5},{8,14},{9,15},{10,... | collective-permute-start | bytes 786440 | tf_op jit(solution)/shard_map/sum_over_col/ppermute | solution.py:37
  47.6 14.0 %collective-permute-start.13 = (bf16[4,128,256]{2,1,0:T(8,128)(2,1)S(1)}, bf16[4,128,256]{2,1,0:T(8,128)(2,1)S(1)}, u32[]{:S(2)}, u32[]{:S(2)}) collective-permute-start(bf16[4,128,256]{2,1,0:T(8,128)(2,1)S(1)} %get-tuple-element.41), channel_id=1, source_target_pairs={{0,2},{1,3},{2,4},{3,5},{4,6},{5,7},{6,0},{7,1},{8,10},{9,11},{10,... | collective-permute-start | bytes 786440 | tf_op jit(solution)/shard_map/sum_over_col/ppermute | solution.py:37
  48.4 19.6 %collective-permute-start.12 = (bf16[4,128,256]{2,1,0:T(8,128)(2,1)S(1)}, bf16[4,128,256]{2,1,0:T(8,128)(2,1)S(1)}, u32[]{:S(2)}, u32[]{:S(2)}) collective-permute-start(bf16[4,128,256]{2,1,0:T(8,128)(2,1)S(1)} %get-tuple-element.42), channel_id=1, source_target_pairs={{0,4},{1,5},{2,6},{3,7},{4,0},{5,1},{6,2},{7,3},{8,12},{9,13},{10,... | collective-permute-start | bytes 786440 | tf_op jit(solution)/shard_map/sum_over_col/ppermute | solution.py:37
  57.5 16.8 %collective-permute-start.17 = (bf16[2,128,256]{2,1,0:T(8,128)(2,1)S(1)}, bf16[2,128,256]{2,1,0:T(8,128)(2,1)S(1)}, u32[]{:S(2)}, u32[]{:S(2)}) collective-permute-start(bf16[2,128,256]{2,1,0:T(8,128)(2,1)S(1)} %get-tuple-element.47), channel_id=1, source_target_pairs={{0,24},{1,25},{2,26},{3,27},{4,28},{5,29},{6,30},{7,31},{8,0},{9,1... | collective-permute-start | bytes 393224 | tf_op jit(solution)/shard_map/sum_over_col/ppermute | solution.py:37
  68.1 6.4 %collective-permute-start.16 = (bf16[2,128,256]{2,1,0:T(8,128)(2,1)S(1)}, bf16[2,128,256]{2,1,0:T(8,128)(2,1)S(1)}, u32[]{:S(2)}, u32[]{:S(2)}) collective-permute-start(bf16[2,128,256]{2,1,0:T(8,128)(2,1)S(1)} %get-tuple-element.49), channel_id=1, source_target_pairs={{0,8},{1,9},{2,10},{3,11},{4,12},{5,13},{6,14},{7,15},{8,16},{9,17... | collective-permute-start | bytes 393224 | tf_op jit(solution)/shard_map/sum_over_col/ppermute | solution.py:37
  69.4 10.4 %collective-permute-start.15 = (bf16[2,128,256]{2,1,0:T(8,128)(2,1)S(1)}, bf16[2,128,256]{2,1,0:T(8,128)(2,1)S(1)}, u32[]{:S(2)}, u32[]{:S(2)}) collective-permute-start(bf16[2,128,256]{2,1,0:T(8,128)(2,1)S(1)} %get-tuple-element.50), channel_id=1, source_target_pairs={{0,16},{1,17},{2,18},{3,19},{4,20},{5,21},{6,22},{7,23},{8,24},{9,... | collective-permute-start | bytes 393224 | tf_op jit(solution)/shard_map/sum_over_col/ppermute | solution.py:37
  74.4 5.5 %copy-start.21 = (bf16[2,128,256]{2,1,0:T(8,128)(2,1)}, bf16[2,128,256]{2,1,0:T(8,128)(2,1)S(1)}, u32[]{:S(2)}) copy-start(bf16[2,128,256]{2,1,0:T(8,128)(2,1)S(1)} %collective-permute-done.17) | copy-start | bytes 393220
  74.5 5.3 %copy-start.22 = (bf16[2,128,256]{2,1,0:T(8,128)(2,1)}, bf16[2,128,256]{2,1,0:T(8,128)(2,1)S(1)}, u32[]{:S(2)}) copy-start(bf16[2,128,256]{2,1,0:T(8,128)(2,1)S(1)} %collective-permute-done.16) | copy-start | bytes 393220
  85.3 38.4 %all-to-all-start = ((f32[256,1,384]{2,1,0:T(1,128)}), f32[256,1,384]{2,1,0:T(1,128)S(1)}, u32[]{:S(2)}, u32[]{:S(2)}) async-start(f32[256,1,384]{2,1,0:T(1,128)} %copy.12), calls=%async_computation | async-start | bytes 786432 | tf_op jit(solution)/shard_map/sum_weight_grad/all_to_all | solution.py:264
  99.9 15.6 %collective-permute-start.20 = (bf16[256,256]{1,0:T(8,128)(2,1)}, bf16[256,256]{1,0:T(8,128)(2,1)S(1)}, u32[]{:S(2)}, u32[]{:S(2)}) collective-permute-start(bf16[256,256]{1,0:T(8,128)(2,1)} %get-tuple-element.25), channel_id=1, source_target_pairs={{0,24},{1,25},{2,26},{3,27},{4,28},{5,29},{6,30},{7,31},{8,0},{9,1... | collective-permute-start | bytes 393224 | tf_op jit(solution)/shard_map/gather_gradients/ppermute | solution.py:37
  104.9 15.5 %collective-permute-start.19 = (bf16[256,256]{1,0:T(8,128)(2,1)}, bf16[256,256]{1,0:T(8,128)(2,1)S(1)}, u32[]{:S(2)}, u32[]{:S(2)}) collective-permute-start(bf16[256,256]{1,0:T(8,128)(2,1)} %get-tuple-element.25), channel_id=1, source_target_pairs={{0,16},{1,17},{2,18},{3,19},{4,20},{5,21},{6,22},{7,23},{8,24},{9,... | collective-permute-start | bytes 393224 | tf_op jit(solution)/shard_map/gather_gradients/ppermute | solution.py:37
  106.3 17.3 %collective-permute-start.18 = (bf16[256,256]{1,0:T(8,128)(2,1)}, bf16[256,256]{1,0:T(8,128)(2,1)S(1)}, u32[]{:S(2)}, u32[]{:S(2)}) collective-permute-start(bf16[256,256]{1,0:T(8,128)(2,1)} %get-tuple-element.25), channel_id=1, source_target_pairs={{0,8},{1,9},{2,10},{3,11},{4,12},{5,13},{6,14},{7,15},{8,16},{9,17... | collective-permute-start | bytes 393224 | tf_op jit(solution)/shard_map/gather_gradients/ppermute | solution.py:37
  108.5 15.1 %collective-permute-start.23 = (bf16[256,256]{1,0:T(8,128)(2,1)}, bf16[256,256]{1,0:T(8,128)(2,1)S(1)}, u32[]{:S(2)}, u32[]{:S(2)}) collective-permute-start(bf16[256,256]{1,0:T(8,128)(2,1)} %get-tuple-element.25), channel_id=1, source_target_pairs={{0,6},{1,7},{2,0},{3,1},{4,2},{5,3},{6,4},{7,5},{8,14},{9,15},{10,... | collective-permute-start | bytes 393224 | tf_op jit(solution)/shard_map/gather_gradients/ppermute | solution.py:37
  111.1 12.5 %collective-permute-start.22 = (bf16[256,256]{1,0:T(8,128)(2,1)}, bf16[256,256]{1,0:T(8,128)(2,1)S(1)}, u32[]{:S(2)}, u32[]{:S(2)}) collective-permute-start(bf16[256,256]{1,0:T(8,128)(2,1)} %get-tuple-element.25), channel_id=1, source_target_pairs={{0,4},{1,5},{2,6},{3,7},{4,0},{5,1},{6,2},{7,3},{8,12},{9,13},{10,... | collective-permute-start | bytes 393224 | tf_op jit(solution)/shard_map/gather_gradients/ppermute | solution.py:37
  115.5 8.2 %collective-permute-start.21 = (bf16[256,256]{1,0:T(8,128)(2,1)}, bf16[256,256]{1,0:T(8,128)(2,1)S(1)}, u32[]{:S(2)}, u32[]{:S(2)}) collective-permute-start(bf16[256,256]{1,0:T(8,128)(2,1)} %get-tuple-element.25), channel_id=1, source_target_pairs={{0,2},{1,3},{2,4},{3,5},{4,6},{5,7},{6,0},{7,1},{8,10},{9,11},{10,... | collective-permute-start | bytes 393224 | tf_op jit(solution)/shard_map/gather_gradients/ppermute | solution.py:37
  123.6 48.2 %copy-start.1 = (bf16[768,256]{1,0:T(8,128)(2,1)}, bf16[768,256]{1,0:T(8,128)(2,1)S(1)}, u32[]{:S(2)}) copy-start(bf16[768,256]{1,0:T(8,128)(2,1)S(1)} %pad_maximum_fusion) | copy-start | bytes 1179652
  123.6 48.2 %copy-start.14 = (bf16[256,256]{1,0:T(8,128)(2,1)}, bf16[256,256]{1,0:T(8,128)(2,1)S(1)}, u32[]{:S(2)}) copy-start(bf16[256,256]{1,0:T(8,128)(2,1)S(1)} %collective-permute-done.23) | copy-start | bytes 393220
  123.7 48.1 %copy-start.15 = (bf16[256,256]{1,0:T(8,128)(2,1)}, bf16[256,256]{1,0:T(8,128)(2,1)S(1)}, u32[]{:S(2)}) copy-start(bf16[256,256]{1,0:T(8,128)(2,1)S(1)} %collective-permute-done.22) | copy-start | bytes 393220
  123.7 48.1 %copy-start.16 = (bf16[256,256]{1,0:T(8,128)(2,1)}, bf16[256,256]{1,0:T(8,128)(2,1)S(1)}, u32[]{:S(2)}) copy-start(bf16[256,256]{1,0:T(8,128)(2,1)S(1)} %collective-permute-done.21) | copy-start | bytes 393220
  125.0 41.6 %all-to-all-start.1 = ((f32[256,1,384]{2,1,0:T(1,128)}), f32[256,1,384]{2,1,0:T(1,128)S(1)}, u32[]{:S(2)}, u32[]{:S(2)}) async-start(f32[256,1,384]{2,1,0:T(1,128)} %broadcast_in_dim.10), calls=%async_computation.1 | async-start | bytes 786432 | tf_op jit(solution)/shard_map/sum_weight_grad/all_to_all | solution.py:268
  139.6 16.7 %collective-permute-start.26 = (bf16[768,256]{1,0:T(8,128)(2,1)S(1)}, bf16[768,256]{1,0:T(8,128)(2,1)S(1)}, u32[]{:S(2)}, u32[]{:S(2)}) collective-permute-start(bf16[768,256]{1,0:T(8,128)(2,1)S(1)} %pad_maximum_fusion), channel_id=1, source_target_pairs={{0,6},{1,7},{2,0},{3,1},{4,2},{5,3},{6,4},{7,5},{8,14},{9,15},{10,... | collective-permute-start | bytes 1179656 | tf_op jit(solution)/shard_map/gather_gradients/ppermute | solution.py:37
  142.3 21.3 %collective-permute-start.25 = (bf16[768,256]{1,0:T(8,128)(2,1)S(1)}, bf16[768,256]{1,0:T(8,128)(2,1)S(1)}, u32[]{:S(2)}, u32[]{:S(2)}) collective-permute-start(bf16[768,256]{1,0:T(8,128)(2,1)S(1)} %pad_maximum_fusion), channel_id=1, source_target_pairs={{0,4},{1,5},{2,6},{3,7},{4,0},{5,1},{6,2},{7,3},{8,12},{9,13},{10,... | collective-permute-start | bytes 1179656 | tf_op jit(solution)/shard_map/gather_gradients/ppermute | solution.py:37
  142.8 23.8 %collective-permute-start.24 = (bf16[768,256]{1,0:T(8,128)(2,1)S(1)}, bf16[768,256]{1,0:T(8,128)(2,1)S(1)}, u32[]{:S(2)}, u32[]{:S(2)}) collective-permute-start(bf16[768,256]{1,0:T(8,128)(2,1)S(1)} %pad_maximum_fusion), channel_id=1, source_target_pairs={{0,2},{1,3},{2,4},{3,5},{4,6},{5,7},{6,0},{7,1},{8,10},{9,11},{10,... | collective-permute-start | bytes 1179656 | tf_op jit(solution)/shard_map/gather_gradients/ppermute | solution.py:37
  143.4 23.8 %collective-permute-start.27 = (bf16[256,256]{1,0:T(8,128)(2,1)}, bf16[256,256]{1,0:T(8,128)(2,1)}, u32[]{:S(2)}, u32[]{:S(2)}) collective-permute-start(bf16[256,256]{1,0:T(8,128)(2,1)} %get-tuple-element.25), channel_id=1, source_target_pairs={{0,1},{1,0},{2,3},{3,2},{4,5},{5,4},{6,7},{7,6},{8,9},{9,8},{10,11... | collective-permute-start | bytes 393224 | tf_op jit(solution)/shard_map/gather_gradients/ppermute | solution.py:37
  144.6 26.5 %collective-permute-start.28 = (bf16[768,256]{1,0:T(8,128)(2,1)S(1)}, bf16[768,256]{1,0:T(8,128)(2,1)S(1)}, u32[]{:S(2)}, u32[]{:S(2)}) collective-permute-start(bf16[768,256]{1,0:T(8,128)(2,1)S(1)} %pad_maximum_fusion), channel_id=1, source_target_pairs={{0,1},{1,0},{2,3},{3,2},{4,5},{5,4},{6,7},{7,6},{8,9},{9,8},{10,11... | collective-permute-start | bytes 1179656 | tf_op jit(solution)/shard_map/gather_gradients/ppermute | solution.py:37
  156.3 15.5 %copy-start.2 = (bf16[768,256]{1,0:T(8,128)(2,1)}, bf16[768,256]{1,0:T(8,128)(2,1)S(1)}, u32[]{:S(2)}) copy-start(bf16[768,256]{1,0:T(8,128)(2,1)S(1)} %collective-permute-done.26) | copy-start | bytes 1179652
  156.3 11.3 %collective-permute-start.29 = (bf16[256,256]{1,0:T(8,128)(2,1)S(1)}, bf16[256,256]{1,0:T(8,128)(2,1)}, u32[]{:S(2)}, u32[]{:S(2)}) collective-permute-start(bf16[256,256]{1,0:T(8,128)(2,1)S(1)} %collective-permute-done.21), channel_id=1, source_target_pairs={{0,1},{1,0},{2,3},{3,2},{4,5},{5,4},{6,7},{7,6},{8,9},{9,8},{10,11... | collective-permute-start | bytes 393224 | tf_op jit(solution)/shard_map/gather_gradients/ppermute | solution.py:37
  163.6 8.2 %copy-start.3 = (bf16[768,256]{1,0:T(8,128)(2,1)}, bf16[768,256]{1,0:T(8,128)(2,1)S(1)}, u32[]{:S(2)}) copy-start(bf16[768,256]{1,0:T(8,128)(2,1)S(1)} %collective-permute-done.25) | copy-start | bytes 1179652
  166.6 5.2 %copy-start.4 = (bf16[768,256]{1,0:T(8,128)(2,1)}, bf16[768,256]{1,0:T(8,128)(2,1)S(1)}, u32[]{:S(2)}) copy-start(bf16[768,256]{1,0:T(8,128)(2,1)S(1)} %collective-permute-done.24) | copy-start | bytes 1179652
  166.6 4.5 %collective-permute-start.30 = (bf16[768,256]{1,0:T(8,128)(2,1)S(1)}, bf16[768,256]{1,0:T(8,128)(2,1)S(1)}, u32[]{:S(2)}, u32[]{:S(2)}) collective-permute-start(bf16[768,256]{1,0:T(8,128)(2,1)S(1)} %collective-permute-done.24), channel_id=1, source_target_pairs={{0,1},{1,0},{2,3},{3,2},{4,5},{5,4},{6,7},{7,6},{8,9},{9,8},{10,11... | collective-permute-start | bytes 1179656 | tf_op jit(solution)/shard_map/gather_gradients/ppermute | solution.py:37
  167.1 4.1 %collective-permute-start.32 = (bf16[768,256]{1,0:T(8,128)(2,1)S(1)}, bf16[768,256]{1,0:T(8,128)(2,1)S(1)}, u32[]{:S(2)}, u32[]{:S(2)}) collective-permute-start(bf16[768,256]{1,0:T(8,128)(2,1)S(1)} %collective-permute-done.25), channel_id=1, source_target_pairs={{0,1},{1,0},{2,3},{3,2},{4,5},{5,4},{6,7},{7,6},{8,9},{9,8},{10,11... | collective-permute-start | bytes 1179656 | tf_op jit(solution)/shard_map/gather_gradients/ppermute | solution.py:37
  167.2 4.0 %collective-permute-start.34 = (bf16[768,256]{1,0:T(8,128)(2,1)S(1)}, bf16[768,256]{1,0:T(8,128)(2,1)S(1)}, u32[]{:S(2)}, u32[]{:S(2)}) collective-permute-start(bf16[768,256]{1,0:T(8,128)(2,1)S(1)} %collective-permute-done.26), channel_id=1, source_target_pairs={{0,1},{1,0},{2,3},{3,2},{4,5},{5,4},{6,7},{7,6},{8,9},{9,8},{10,11... | collective-permute-start | bytes 1179656 | tf_op jit(solution)/shard_map/gather_gradients/ppermute | solution.py:37
  167.6 2.1 %collective-permute-start.31 = (bf16[256,256]{1,0:T(8,128)(2,1)S(1)}, bf16[256,256]{1,0:T(8,128)(2,1)S(1)}, u32[]{:S(2)}, u32[]{:S(2)}) collective-permute-start(bf16[256,256]{1,0:T(8,128)(2,1)S(1)} %collective-permute-done.22), channel_id=1, source_target_pairs={{0,1},{1,0},{2,3},{3,2},{4,5},{5,4},{6,7},{7,6},{8,9},{9,8},{10,11... | collective-permute-start | bytes 393224 | tf_op jit(solution)/shard_map/gather_gradients/ppermute | solution.py:37
  169.8 1.4 collective-permute-start.33
  179.2 27.2 %all-to-all-start.2 = ((bf16[8,256,256]{2,1,0:T(8,128)(2,1)}), bf16[8,256,256]{2,1,0:T(8,128)(2,1)S(1)}, u32[]{:S(2)}, u32[]{:S(2)}) async-start(bf16[8,256,256]{2,1,0:T(8,128)(2,1)} %bitcast.39), calls=%async_computation.2 | async-start | bytes 2097152 | tf_op jit(solution)/shard_map/sum_over_row/all_to_all | solution.py:280
  (14 other events, 22.3 us)
where the time goes:
time: 210 us
  starting transfers between devices  105 us (50%)
  waiting for transfers between devices  68.8 us (33%)
  Pallas kernels  18.1 us (9%)
  local copies, waits for them, and re-layouts  9.24 us (4%)
  other arithmetic  6.89 us (3%)
    ppermute x28, starting transfers between devices, col_shift(): return lax.ppermute(value, 'col', pairs)  54.3 us
    ppermute x28, waiting for transfers between devices, col_shift(): return lax.ppermute(value, 'col', pairs)  48.3 us
    all_to_all x1, starting transfers between devices, shards(): load = lax.all_to_all(spread, ('row', 'col'), 0, 0, tiled=True)  14.6 us
    all_to_all x1, starting transfers between devices, shards(): load = lax.all_to_all(load[:, None], ('row', 'col'), 0, 0, tiled=True)  14.5 us
    all_to_all x1, waiting for transfers between devices, shards(): lax.all_to_all(back.reshape(N_ROW, vertices, width), 'row', 0, 0, tiled=T...  13.2 us
    pallas_call x2, Pallas kernels, tile_sum(): pl.pallas_call(functools.partial(tile_kernel, transposed, src_sizes, out_...  13.2 us
    all_to_all x1, starting transfers between devices, shards(): lax.all_to_all(back.reshape(N_ROW, vertices, width), 'row', 0, 0, tiled=T...  11.5 us
    ppermute x7, starting transfers between devices, row_shift(): return lax.ppermute(value, 'row', pairs)  10 us
  transfers between devices with their start and end apart: 38, of which 17 were waited for; matrix products, arithmetic and copies ran while one was open for 4% of the time, Pallas kernels for 0%

commit v1 on v0

--- a/solution.py
+++ b/solution.py
@@ -41,63 +41,64 @@
     n_src, n_out = len(src_sizes), len(out_sizes)
     sources = refs[:n_src]
     outs = refs[n_src : n_src + n_out]
-    src, acc, staged, in_sems, out_sems = refs[n_src + n_out :]
-    step = pl.program_id(0)
-
-    @pl.when(step == 0)
-    def _():
-        copies, first = [], 0
-        for k, size in enumerate(src_sizes):
-            copies.append(
-                pltpu.make_async_copy(
-                    sources[k], src.at[pl.ds(first, size)], in_sems.at[k]
-                )
-            )
-            first += size
-        for copy in copies:
-            copy.start()
-
-        @pl.loop(0, acc.shape[0])
-        def _(i):
-            acc[i] = jnp.zeros(acc.shape[1:], jnp.float32)
-
-        for copy in copies:
-            copy.wait()
-
-    @pl.when(step * GROUP < live[0])
-    def _():
+    held, src, acc, staged, tile_sems, in_sems, out_sems = refs[n_src + n_out :]
+    groups = live[0] // GROUP
+
+    def tile_copy(g):
+        rows = pl.ds(g * GROUP, GROUP)
+        return pltpu.make_async_copy(tiles.at[0, rows], held.at[rows], tile_sems.at[g])
+
+    copies, first = [], 0
+    for k, size in enumerate(src_sizes):
+        copies.append(
+            pltpu.make_async_copy(sources[k], src.at[pl.ds(first, size)], in_sems.at[k])
+        )
+        first += size
+    for copy in copies:
+        copy.start()
+
+    @pl.loop(0, groups)
+    def _(g):
+        tile_copy(g).start()
+
+    @pl.loop(0, acc.shape[0])
+    def _(i):
+        acc[i] = jnp.zeros(acc.shape[1:], jnp.float32)
+
+    for copy in copies:
+        copy.wait()
+
+    @pl.loop(0, groups)
+    def _(g):
+        tile_copy(g).wait()
+
         @pl.loop(0, GROUP // 8)
         def _(i):
             for j in range(8):
-                k = i * 8 + j
-                slot = step * GROUP + k
+                slot = g * GROUP + i * 8 + j
                 product = lax.dot_general(
-                    tiles[0, k],
+                    held[slot],
                     src[take[slot]],
                     (((0 if transposed else 1,), (0,)), ((), ())),
                     preferred_element_type=jnp.float32,
                 )
                 acc[put[slot]] += product
 
-    @pl.when(step == pl.num_programs(0) - 1)
-    def _():
-        copies, first = [], 0
-        for k, size in enumerate(out_sizes):
-            start = first
-
-            @pl.loop(0, size)
-            def _(i):
-                staged[start + i] = acc[start + i].astype(jnp.bfloat16)
-
-            copies.append(
-                pltpu.make_async_copy(
-                    staged.at[pl.ds(start, size)], outs[k], out_sems.at[k]
-                )
-            )
-            copies[-1].start()
-            first += size
-        for copy in copies:
-            copy.wait()
+    copies, first = [], 0
+    for k, size in enumerate(out_sizes):
+        start = first
+
+        @pl.loop(0, size)
+        def _(i):
+            staged[start + i] = acc[start + i].astype(jnp.bfloat16)
+
+        copies.append(
+            pltpu.make_async_copy(staged.at[pl.ds(start, size)], outs[k], out_sems.at[k])
+        )
+        copies[-1].start()
+        first += size
+    for copy in copies:
+        copy.wait()
 
 
 def tile_sum(adjacency, live, take, put, sources, out_sizes, transposed):
@@ -105,27 +106,21 @@
     width = sources[0].shape[-1]
     sources = [s.reshape(-1, tile, width) for s in sources]
     src_sizes = [s.shape[0] for s in sources]
-
-    def tile_block(i, live, take, put):
-        return (0, jnp.minimum(i, live[0] // GROUP - 1), 0, 0)
-
     anywhere = pl.BlockSpec(memory_space=pl.ANY)
+    scalars = pl.BlockSpec(memory_space=pltpu.SMEM)
     return pl.pallas_call(
         functools.partial(tile_kernel, transposed, src_sizes, out_sizes),
-        grid_spec=pltpu.PrefetchScalarGridSpec(
-            num_scalar_prefetch=3,
-            grid=(slots // GROUP,),
-            in_specs=[pl.BlockSpec((1, GROUP, tile, tile), tile_block)]
-            + [anywhere] * len(sources),
-            out_specs=[anywhere] * len(out_sizes),
-            scratch_shapes=[
-                pltpu.VMEM((sum(src_sizes), tile, width), jnp.bfloat16),
-                pltpu.VMEM((sum(out_sizes), tile, width), jnp.float32),
-                pltpu.VMEM((sum(out_sizes), tile, width), jnp.bfloat16),
-                pltpu.SemaphoreType.DMA((len(sources),)),
-                pltpu.SemaphoreType.DMA((len(out_sizes),)),
-            ],
-        ),
+        in_specs=[scalars] * 3 + [anywhere] * (1 + len(sources)),
+        out_specs=[anywhere] * len(out_sizes),
+        scratch_shapes=[
+            pltpu.VMEM((slots, tile, tile), jnp.bfloat16),
+            pltpu.VMEM((sum(src_sizes), tile, width), jnp.bfloat16),
+            pltpu.VMEM((sum(out_sizes), tile, width), jnp.float32),
+            pltpu.VMEM((sum(out_sizes), tile, width), jnp.bfloat16),
+            pltpu.SemaphoreType.DMA((slots // GROUP,)),
+            pltpu.SemaphoreType.DMA((len(sources),)),
+            pltpu.SemaphoreType.DMA((len(out_sizes),)),
+        ],
         out_shape=[
             jax.ShapeDtypeStruct((size, tile, width), jnp.bfloat16)
             for size in out_sizes
@@ -148,7 +143,7 @@
     return dot(high, other) + dot(low, other)
 
 
-def middle_kernel(h0, h1, h2, h3, weight, bias, cotangent, out, grad, load):
+def middle_kernel(h0, h1, h2, h3, weight, bias, cotangent, out, grad, total_out, pre_out):
     total = (
         h0[...].astype(jnp.float32)
         + h1[...].astype(jnp.float32)
@@ -162,12 +157,9 @@
         1.0 - tanh_term * tanh_term
     ) * GELU_ROOT * (1.0 + 3.0 * GELU_CUBIC * shifted * shifted)
     pre_grad = cotangent[...].astype(jnp.float32) * slope
-    rounded = pre_grad.astype(jnp.bfloat16)
-    grad[...] = rounded
-    rows = (((0,), (0,)), ((), ()))
-    load[:, : total.shape[1]] = split_dot(total, rounded, rows)
-    ones = jnp.ones((total.shape[0], LANES), jnp.bfloat16)
-    load[:, total.shape[1] :] = split_dot(pre_grad, ones, rows)
+    grad[...] = pre_grad.astype(jnp.bfloat16)
+    total_out[...] = total
+    pre_out[...] = pre_grad
 
 
 def middle(pieces, weight, bias, cotangent):
@@ -176,14 +168,32 @@
     return pl.pallas_call(
         middle_kernel,
         in_specs=[vmem] * 7,
-        out_specs=[vmem] * 3,
-        out_shape=[
-            jax.ShapeDtypeStruct((rows, width), jnp.bfloat16),
-            jax.ShapeDtypeStruct((rows, width), jnp.bfloat16),
-            jax.ShapeDtypeStruct((width, width + LANES), jnp.float32),
-        ],
+        out_specs=[vmem] * 4,
+        out_shape=[jax.ShapeDtypeStruct((rows, width), jnp.bfloat16)] * 2
+        + [jax.ShapeDtypeStruct((rows, width), jnp.float32)] * 2,
         compiler_params=pltpu.CompilerParams(vmem_limit_bytes=VMEM_LIMIT),
     )(*pieces, weight, bias.reshape(1, width), cotangent)
+
+
+def load_kernel(total, pre_grad, load):
+    width = total.shape[1]
+    rows = (((0,), (0,)), ((), ()))
+    rounded = pre_grad[...].astype(jnp.bfloat16)
+    load[:, :width] = split_dot(total[...], rounded, rows)
+    ones = jnp.ones((total.shape[0], LANES), jnp.bfloat16)
+    load[:, width:] = split_dot(pre_grad[...], ones, rows)
+
+
+def loads(total, pre_grad):
+    width = total.shape[1]
+    vmem = pl.BlockSpec(memory_space=pltpu.VMEM)
+    return pl.pallas_call(
+        load_kernel,
+        in_specs=[vmem] * 2,
+        out_specs=vmem,
+        out_shape=jax.ShapeDtypeStruct((width, width + LANES), jnp.float32),
+        compiler_params=pltpu.CompilerParams(vmem_limit_bytes=VMEM_LIMIT),
+    )(total, pre_grad)
 
 
 def last_kernel(pieces, weight, out):
@@ -234,7 +244,10 @@
     part = ((ahead == 3) | (ahead == 0)).astype(jnp.int32)
     place = ((ahead == 1) | (ahead == 0)).astype(jnp.int32)
     put_rows = (half + part * 8 + ((r_y - my_y) & 3) * 2 + place) * per + r % per
-    take_rows = (half + ((my_y - r_y) & 3) * 4 + ((my_zh - r_zh) & 3)) * per + r % per
+    back_y, back_zh = (my_y - r_y) & 3, (my_zh - r_zh) & 3
+    take_rows = jnp.where(back_zh == 0, 3 + back_y, 3 * back_y + 3 + back_zh)
+    take_rows = jnp.where(back_y == 0, back_zh, take_rows)
+    take_rows = (half + take_rows) * per + r % per
     take_cols = (((my_x - c_x) & 3) * 2 + (c_zl ^ my_zl)) * per + c % per
 
     moves = [(dx, dzl) for dx in range(N_X) for dzl in range(N_ZL)]
@@ -245,35 +258,38 @@
             adjacency, live, take_cols, put_rows, sources, [8 * per] * 4, False
         )
     with jax.named_scope("sum_over_col"):
-        sums = []
+        sums, pieces = [], []
         for keep, send in zip(parts[:2], parts[2:]):
             other = col_shift(send, dcore=1)
             cut = [slice(2 * per * k, 2 * per * (k + 1)) for k in range(N_Y)]
             added = [merge([keep[s], other[s]]) for s in cut]
             arrived = [added[0]] + [col_shift(added[k], dy=k) for k in (2, 1, 3)]
-            sums.append(merge([p[:per] for p in arrived]))
-            sums.append(merge([p[per:] for p in arrived]))
-        pieces = [sums[3]] + [col_shift(sums[i], dzh=k) for i, k in enumerate((2, 1, 3))]
+            if pieces:
+                *arrived, pieces[1] = lax.optimization_barrier((*arrived, pieces[1]))
+            sums = [merge([p[:per] for p in arrived]), merge([p[per:] for p in arrived])]
+            if not pieces:
+                pieces = [col_shift(sums[0], dzh=2), col_shift(sums[1], dzh=1)]
+            else:
+                pieces += [col_shift(sums[0], dzh=3), sums[1]]
         pieces = [p.reshape(vertices, width) for p in pieces]
     with jax.named_scope("pointwise"):
-        layer_out, grad, load = middle(pieces, weight, bias, cotangent)
+        layer_out, grad, total, pre_grad = middle(pieces, weight, bias, cotangent)
     with jax.named_scope("gather_gradients"):
-        stack = jnp.concatenate([col_shift(grad, dzh=k) for k in range(1, N_ZH)])
-        ours = [col_shift(grad, dy=k) for k in range(1, N_Y)]
+        near = [col_shift(grad, dzh=k) for k in range(1, N_ZH)]
+        ours = jnp.concatenate([col_shift(grad, dy=k) for k in range(1, N_Y)])
+        stack = jnp.concatenate(near)
     with jax.named_scope("sum_weight_grad"):
-        load = lax.all_to_all(load[:, None], ("row", "col"), 0, 0, tiled=True)
-        load, stack, *ours = lax.optimization_barrier((load, stack, *ours))
-        total = jnp.sum(load, axis=0, keepdims=True) * scale
-        spread = jnp.broadcast_to(total, load.shape)
-        load = lax.all_to_all(spread, ("row", "col"), 0, 0, tiled=True)
+        load = loads(total, pre_grad).reshape(N_COL, -1, width + LANES)
+        load = jnp.sum(lax.all_to_all(load, "col", 0, 0, tiled=True), axis=0)
+        load = jnp.broadcast_to(load, (N_ROW,) + load.shape)
+        load = jnp.sum(lax.all_to_all(load, "row", 0, 0, tiled=True), axis=0) * scale
+        load = jnp.broadcast_to(load, (N_COL,) + load.shape)
+        load = lax.all_to_all(load, "col", 0, 0, tiled=True).reshape(width, -1)
+        weight_grad, bias_grad = load[:, :width], load[:, width]
     with jax.named_scope("gather_gradients"):
         theirs = [col_shift(stack, dy=k) for k in range(1, N_Y)]
-        *theirs, load = lax.optimization_barrier((*theirs, load))
-        here = [grad, stack]
-        for pair in zip(ours, theirs):
-            here += pair
+        here = [grad, stack, ours] + theirs
         there = [col_shift(p, dcore=1) for p in here]
-    weight_grad, bias_grad = load[:, 0, :width], load[:, 0, width]
     with jax.named_scope("tiles_backward"):
         (back,) = tile_sum(adjacency, live, take_rows, c, here + there, [N_ROW * per], True)
     with jax.named_scope("sum_over_row"):

time: 210 us -> 187 us (0.89)
  starting transfers between devices: 105 us -> 85.2 us
  waiting for transfers between devices: 68.8 us -> 55.4 us
  Pallas kernels: 18.1 us -> 31.1 us
  local copies, waits for them, and re-layouts: 9.24 us -> 6.04 us
    ppermute x28 -> x26, starting transfers between devices: 54.3 us -> 39.6 us  [col_shift(): return lax.ppermute(value, 'col', pairs)]
    ppermute x28 -> x26, waiting for transfers between devices: 48.3 us -> 34.5 us  [col_shift(): return lax.ppermute(value, 'col', pairs)]
    pallas_call x2, Pallas kernels: 13.2 us -> 24.4 us  [tile_sum(): pl.pallas_call(functools.partial(tile_kernel, transposed, src_sizes, out_...]
    all_to_all x1, starting transfers between devices: 11.5 us -> 4.98 us  [shards(): lax.all_to_all(back.reshape(N_ROW, vertices, width), 'row', 0, 0, tiled=T...]
    pallas_call x1 -> x2, Pallas kernels: 2.73 us -> 4.59 us  [the longest x1 2.47 us: middle(): pl.pallas_call(middle_kernel, in_specs=[vmem] * 7, out_specs=[vmem] * 4,...]
    all_to_all x2 -> x3, starting transfers between devices: 29.1 us -> 30.5 us  [the longest x1 12.2 us: shards(): load = jnp.sum(lax.all_to_all(load, 'col', 0, 0, tiled=True), axis=0)]
    unnamed x49 -> x48, local copies, waits for them, and re-layouts: 4.37 us -> 3.17 us
  transfers between devices with their start and end apart: 38 -> 37, of which waited for: 17 -> 16; matrix products, arithmetic and copies ran while one was open for 4% -> 5% of each run, Pallas kernels for 0% -> 7%
where the time goes in v1:
time: 187 us; the launch traced here: 186 us
  starting transfers between devices  85.2 us (46%)
  waiting for transfers between devices  55.4 us (30%)
  Pallas kernels  31.1 us (17%)
  other arithmetic  6.61 us (4%)
  local copies, waits for them, and re-layouts  6.04 us (3%)
    ppermute x26, starting transfers between devices, col_shift(): return lax.ppermute(value, 'col', pairs)  39.6 us
    ppermute x26, waiting for transfers between devices, col_shift(): return lax.ppermute(value, 'col', pairs)  34.5 us
    pallas_call x2, Pallas kernels, tile_sum(): pl.pallas_call(functools.partial(tile_kernel, transposed, src_sizes, out_...  24.4 us
    all_to_all x1, starting transfers between devices, shards(): load = jnp.sum(lax.all_to_all(load, 'col', 0, 0, tiled=True), axis=0)  12.2 us
    all_to_all x1, waiting for transfers between devices, shards(): lax.all_to_all(back.reshape(N_ROW, vertices, width), 'row', 0, 0, tiled=T...  12 us
    all_to_all x1, starting transfers between devices, shards(): lax.all_to_all(load, 'row', 0, 0, tiled=True)  11.6 us
    ppermute x7, starting transfers between devices, row_shift(): return lax.ppermute(value, 'row', pairs)  10 us
    ppermute x7, waiting for transfers between devices, row_shift(): return lax.ppermute(value, 'row', pairs)  7.27 us
  transfers between devices with their start and end apart: 37, of which 16 were waited for; matrix products, arithmetic and copies ran while one was open for 5% of the time, Pallas kernels for 7%

profile of v1, /device:TPU:1, one launch (start us, length us, event | category | flops | bytes accessed | tf_op | source)
XLA Modules:
  0.0 186.0 jit_solution(2262956861077205779)
XLA Ops:
  0.6 5.0 %collective-permute-start.4 = (bf16[256,256]{1,0:T(8,128)(2,1)}, bf16[256,256]{1,0:T(8,128)(2,1)S(1)}, u32[]{:S(2)}, u32[]{:S(2)}) collective-permute-start(bf16[256,256]{1,0:T(8,128)(2,1)} %param.8), channel_id=1, source_target_pairs={{0,160},{32,128},{64,224},{96,192},{128,32},{160,0},{192,96},{224,... | collective-permute-start | bytes 393224 | tf_op jit(solution)/shard_map/gather_features/ppermute | solution.py:27
  5.9 0.8 collective-permute-start.2
  6.6 1.2 collective-permute-start.1
  7.8 1.6 collective-permute-start
  10.1 1.3 multiply_add_fusion
  11.4 1.2 collective-permute-start.6
  12.6 3.8 %collective-permute-done.3 = bf16[256,256]{1,0:T(8,128)(2,1)S(1)} collective-permute-done((bf16[256,256]{1,0:T(8,128)(2,1)}, bf16[256,256]{1,0:T(8,128)(2,1)S(1)}, u32[]{:S(2)}, u32[]{:S(2)}) %collective-permute-start.3) | collective-permute-done | bytes 131104 | tf_op jit(solution)/shard_map/gather_features/ppermute | solution.py:27
  16.4 1.4 fusion.2
  17.8 1.7 collective-permute-done.1
  19.5 1.8 collective-permute-done.5
  21.9 11.8 %tiles_forward.1 = (bf16[16,128,256]{2,1,0:T(8,128)(2,1)}, bf16[16,128,256]{2,1,0:T(8,128)(2,1)}, bf16[16,128,256]{2,1,0:T(8,128)(2,1)}, bf16[16,128,256]{2,1,0:T(8,128)(2,1)}) custom-call(s32[1]{0:T(128)} %bitcast.31.live, s32[192]{0:T(256)} %get-tuple-element.45.take, s32[192]{0:T(256)} %get-tuple-element.46.put, bf16[1,192,128,128]{3,2,1,0:T(8,128)(2,1)} %tiles.3, ...), custom_call_target="tpu_custom_call" | custom-call | flops 1610612736 | bytes 6291456 | tf_op jit(solution)/shard_map/tiles_forward/pallas_call | solution.py:111
  34.3 2.4 %collective-permute-done.7 = bf16[16,128,256]{2,1,0:T(8,128)(2,1)S(1)} collective-permute-done((bf16[16,128,256]{2,1,0:T(8,128)(2,1)}, bf16[16,128,256]{2,1,0:T(8,128)(2,1)S(1)}, u32[]{:S(2)}, u32[]{:S(2)}) %collective-permute-start.7) | collective-permute-done | bytes 1048608 | tf_op jit(solution)/shard_map/sum_over_col/ppermute | solution.py:37
  36.7 1.5 add_convert_fusion.7
  38.2 3.8 %collective-permute-start.10 = (bf16[4,128,256]{2,1,0:T(8,128)(2,1)S(1)}, bf16[4,128,256]{2,1,0:T(8,128)(2,1)S(1)}, u32[]{:S(2)}, u32[]{:S(2)}) collective-permute-start(bf16[4,128,256]{2,1,0:T(8,128)(2,1)S(1)} %get-tuple-element.38), channel_id=1, source_target_pairs={{0,6},{1,7},{2,0},{3,1},{4,2},{5,3},{6,4},{7,5},{8,14},{9,15},{10,... | collective-permute-start | bytes 786440 | tf_op jit(solution)/shard_map/sum_over_col/ppermute | solution.py:37
  42.0 1.3 collective-permute-start.8
  43.3 1.5 add_convert_fusion
  44.8 1.5 collective-permute-start.15
  47.0 5.9 %collective-permute-done.10 = bf16[4,128,256]{2,1,0:T(8,128)(2,1)S(1)} collective-permute-done((bf16[4,128,256]{2,1,0:T(8,128)(2,1)S(1)}, bf16[4,128,256]{2,1,0:T(8,128)(2,1)S(1)}, u32[]{:S(2)}, u32[]{:S(2)}) %collective-permute-start.10) | collective-permute-done | bytes 262176 | tf_op jit(solution)/shard_map/sum_over_col/ppermute | solution.py:37
  52.8 2.6 %collective-permute-done.9 = bf16[4,128,256]{2,1,0:T(8,128)(2,1)S(1)} collective-permute-done((bf16[4,128,256]{2,1,0:T(8,128)(2,1)S(1)}, bf16[4,128,256]{2,1,0:T(8,128)(2,1)S(1)}, u32[]{:S(2)}, u32[]{:S(2)}) %collective-permute-start.9) | collective-permute-done | bytes 262176 | tf_op jit(solution)/shard_map/sum_over_col/ppermute | solution.py:37
  55.7 5.0 %collective-permute-start.11 = (bf16[2,128,256]{2,1,0:T(8,128)(2,1)S(1)}, bf16[2,128,256]{2,1,0:T(8,128)(2,1)S(1)}, u32[]{:S(2)}, u32[]{:S(2)}) collective-permute-start(bf16[2,128,256]{2,1,0:T(8,128)(2,1)S(1)} %get-tuple-element.44), channel_id=1, source_target_pairs={{0,16},{1,17},{2,18},{3,19},{4,20},{5,21},{6,22},{7,23},{8,24},{9,... | collective-permute-start | bytes 393224 | tf_op jit(solution)/shard_map/sum_over_col/ppermute | solution.py:37
  60.7 3.4 %collective-permute-done.15 = bf16[4,128,256]{2,1,0:T(8,128)(2,1)S(1)} collective-permute-done((bf16[4,128,256]{2,1,0:T(8,128)(2,1)S(1)}, bf16[4,128,256]{2,1,0:T(8,128)(2,1)S(1)}, u32[]{:S(2)}, u32[]{:S(2)}) %collective-permute-start.15) | collective-permute-done | bytes 262176 | tf_op jit(solution)/shard_map/sum_over_col/ppermute | solution.py:37
  64.1 3.2 %collective-permute-done.14 = bf16[4,128,256]{2,1,0:T(8,128)(2,1)S(1)} collective-permute-done((bf16[4,128,256]{2,1,0:T(8,128)(2,1)S(1)}, bf16[4,128,256]{2,1,0:T(8,128)(2,1)S(1)}, u32[]{:S(2)}, u32[]{:S(2)}) %collective-permute-start.14) | collective-permute-done | bytes 262176 | tf_op jit(solution)/shard_map/sum_over_col/ppermute | solution.py:37
  67.3 0.8 add_convert_fusion.8
  68.8 5.0 %collective-permute-done.17 = bf16[2,128,256]{2,1,0:T(8,128)(2,1)S(1)} collective-permute-done((bf16[2,128,256]{2,1,0:T(8,128)(2,1)S(1)}, bf16[2,128,256]{2,1,0:T(8,128)(2,1)S(1)}, u32[]{:S(2)}, u32[]{:S(2)}) %collective-permute-start.17) | collective-permute-done | bytes 131104 | tf_op jit(solution)/shard_map/sum_over_col/ppermute | solution.py:37
  74.4 2.5 %pointwise.1 = (bf16[256,256]{1,0:T(8,128)(2,1)}, bf16[256,256]{1,0:T(8,128)(2,1)}, f32[256,256]{1,0:T(8,128)}, f32[256,256]{1,0:T(8,128)}) custom-call(bf16[256,256]{1,0:T(8,128)(2,1)} %bitcast.59, bf16[256,256]{1,0:T(8,128)(2,1)} %bitcast.58, bf16[256,256]{1,0:T(8,128)(2,1)} %bitcast.60, bf16[256,256]{1,0:T(8,128)(2,1)} %bitcast.39, ...), custom_call_target="tpu_custom_call" | custom-call | tf_op jit(solution)/shard_map/pointwise/pallas_call | solution.py:168
  76.9 2.1 %sum_weight_grad.1 = f32[256,384]{1,0:T(8,128)} custom-call(f32[256,256]{1,0:T(8,128)} %get-tuple-element.28.total, f32[256,256]{1,0:T(8,128)} %get-tuple-element.29.pre_grad), custom_call_target="tpu_custom_call" | custom-call | tf_op jit(solution)/shard_map/sum_weight_grad/pallas_call | solution.py:190
  79.0 12.2 %all-to-all-start.1 = ((f32[32,8,384]{2,1,0:T(8,128)}), f32[32,8,384]{2,1,0:T(8,128)S(1)}, u32[]{:S(2)}, u32[]{:S(2)}) async-start(f32[32,8,384]{2,1,0:T(8,128)} %bitcast.36), calls=%async_computation.1 | async-start | bytes 786432 | tf_op jit(solution)/shard_map/sum_weight_grad/all_to_all | solution.py:283
  91.2 2.4 %collective-permute-start.18 = (bf16[256,256]{1,0:T(8,128)(2,1)}, bf16[256,256]{1,0:T(8,128)(2,1)S(1)}, u32[]{:S(2)}, u32[]{:S(2)}) collective-permute-start(bf16[256,256]{1,0:T(8,128)(2,1)} %get-tuple-element.27), channel_id=1, source_target_pairs={{0,8},{1,9},{2,10},{3,11},{4,12},{5,13},{6,14},{7,15},{8,16},{9,17... | collective-permute-start | bytes 393224 | tf_op jit(solution)/shard_map/gather_gradients/ppermute | solution.py:37
  93.6 3.3 %collective-permute-start.19 = (bf16[256,256]{1,0:T(8,128)(2,1)}, bf16[256,256]{1,0:T(8,128)(2,1)S(1)}, u32[]{:S(2)}, u32[]{:S(2)}) collective-permute-start(bf16[256,256]{1,0:T(8,128)(2,1)} %get-tuple-element.27), channel_id=1, source_target_pairs={{0,16},{1,17},{2,18},{3,19},{4,20},{5,21},{6,22},{7,23},{8,24},{9,... | collective-permute-start | bytes 393224 | tf_op jit(solution)/shard_map/gather_gradients/ppermute | solution.py:37
  96.9 2.4 %collective-permute-start.23 = (bf16[256,256]{1,0:T(8,128)(2,1)}, bf16[256,256]{1,0:T(8,128)(2,1)S(1)}, u32[]{:S(2)}, u32[]{:S(2)}) collective-permute-start(bf16[256,256]{1,0:T(8,128)(2,1)} %get-tuple-element.27), channel_id=1, source_target_pairs={{0,6},{1,7},{2,0},{3,1},{4,2},{5,3},{6,4},{7,5},{8,14},{9,15},{10,... | collective-permute-start | bytes 393224 | tf_op jit(solution)/shard_map/gather_gradients/ppermute | solution.py:37
  100.5 4.5 %collective-permute-done.18 = bf16[256,256]{1,0:T(8,128)(2,1)S(1)} collective-permute-done((bf16[256,256]{1,0:T(8,128)(2,1)}, bf16[256,256]{1,0:T(8,128)(2,1)S(1)}, u32[]{:S(2)}, u32[]{:S(2)}) %collective-permute-start.18) | collective-permute-done | bytes 131104 | tf_op jit(solution)/shard_map/gather_gradients/ppermute | solution.py:37
  105.0 2.2 %collective-permute-start.20 = (bf16[256,256]{1,0:T(8,128)(2,1)}, bf16[256,256]{1,0:T(8,128)(2,1)S(1)}, u32[]{:S(2)}, u32[]{:S(2)}) collective-permute-start(bf16[256,256]{1,0:T(8,128)(2,1)} %get-tuple-element.27), channel_id=1, source_target_pairs={{0,24},{1,25},{2,26},{3,27},{4,28},{5,29},{6,30},{7,31},{8,0},{9,1... | collective-permute-start | bytes 393224 | tf_op jit(solution)/shard_map/gather_gradients/ppermute | solution.py:37
  107.1 2.7 %collective-permute-done.19 = bf16[256,256]{1,0:T(8,128)(2,1)S(1)} collective-permute-done((bf16[256,256]{1,0:T(8,128)(2,1)}, bf16[256,256]{1,0:T(8,128)(2,1)S(1)}, u32[]{:S(2)}, u32[]{:S(2)}) %collective-permute-start.19) | collective-permute-done | bytes 131104 | tf_op jit(solution)/shard_map/gather_gradients/ppermute | solution.py:37
  110.5 11.6 %all-to-all-start.2 = ((f32[8,8,384]{2,1,0:T(8,128)}), f32[8,8,384]{2,1,0:T(8,128)S(1)}, u32[]{:S(2)}, u32[]{:S(2)}) async-start(f32[8,8,384]{2,1,0:T(8,128)} %broadcast_in_dim.6), calls=%async_computation.2 | async-start | bytes 196608 | tf_op jit(solution)/shard_map/sum_weight_grad/all_to_all | solution.py:285
  122.2 2.6 %collective-permute-start.26 = (bf16[768,256]{1,0:T(8,128)(2,1)S(1)}, bf16[768,256]{1,0:T(8,128)(2,1)S(1)}, u32[]{:S(2)}, u32[]{:S(2)}) collective-permute-start(bf16[768,256]{1,0:T(8,128)(2,1)S(1)} %constant_dynamic-update-slice_fusion), channel_id=1, source_target_pairs={{0,6},{1,7},{2,0},{3,1},{4,2},{5,3},{6,4},{7,5},{8,14},{9,15},{10,... | collective-permute-start | bytes 1179656 | tf_op jit(solution)/shard_map/gather_gradients/ppermute | solution.py:37
  125.9 1.6 all-to-all-done.2
  127.6 0.8 broadcast_in_dim.7
  128.4 6.7 %all-to-all-start.3 = ((f32[32,8,384]{2,1,0:T(8,128)}), f32[32,8,384]{2,1,0:T(8,128)S(1)}, u32[]{:S(2)}, u32[]{:S(2)}) async-start(f32[32,8,384]{2,1,0:T(8,128)} %broadcast_in_dim.7), calls=%async_computation.3 | async-start | bytes 786432 | tf_op jit(solution)/shard_map/sum_weight_grad/all_to_all | solution.py:287
  135.8 0.9 collective-permute-done.27
  137.0 9.3 %collective-permute-start.32 = (bf16[768,256]{1,0:T(8,128)(2,1)S(1)}, bf16[768,256]{1,0:T(8,128)(2,1)S(1)}, u32[]{:S(2)}, u32[]{:S(2)}) collective-permute-start(bf16[768,256]{1,0:T(8,128)(2,1)S(1)} %collective-permute-done.26), channel_id=1, source_target_pairs={{0,1},{1,0},{2,3},{3,2},{4,5},{5,4},{6,7},{7,6},{8,9},{9,8},{10,11... | collective-permute-start | bytes 1179656 | tf_op jit(solution)/shard_map/gather_gradients/ppermute | solution.py:37
  146.3 2.6 %collective-permute-done.24 = bf16[768,256]{1,0:T(8,128)(2,1)S(1)} collective-permute-done((bf16[768,256]{1,0:T(8,128)(2,1)S(1)}, bf16[768,256]{1,0:T(8,128)(2,1)S(1)}, u32[]{:S(2)}, u32[]{:S(2)}) %collective-permute-start.24) | collective-permute-done | bytes 393248 | tf_op jit(solution)/shard_map/gather_gradients/ppermute | solution.py:37
  149.7 1.3 collective-permute-done.30
  151.0 0.7 copy-done.10
  151.8 12.6 %tiles_backward.1 = bf16[16,128,256]{2,1,0:T(8,128)(2,1)} custom-call(s32[1]{0:T(128)} %bitcast.32.live, s32[192]{0:T(256)} %get-tuple-element.30.take, s32[192]{0:T(256)} %bitcast.62, bf16[1,192,128,128]{3,2,1,0:T(8,128)(2,1)} %tiles.3, bf16[2,128,256]{2,1,0:T(8,128)(2,1)} %bitcast.54, bf16[6,128,256]{2,1,0:T(8,128)(2,1)} %bitcast.38, ...), custom_call_target="tpu_custom_call" | custom-call | flops 1610612736 | bytes 6291456 | tf_op jit(solution)/shard_map/tiles_backward/pallas_call | solution.py:111
  164.4 5.0 %all-to-all-start = ((bf16[8,256,256]{2,1,0:T(8,128)(2,1)}), bf16[8,256,256]{2,1,0:T(8,128)(2,1)S(1)}, u32[]{:S(2)}, u32[]{:S(2)}) async-start(bf16[8,256,256]{2,1,0:T(8,128)(2,1)} %bitcast.33), calls=%async_computation | async-start | bytes 2097152 | tf_op jit(solution)/shard_map/sum_over_row/all_to_all | solution.py:296
  170.8 12.0 %all-to-all-done.pieces = bf16[8,256,256]{2,1,0:T(8,128)(2,1)S(1)} async-done(((bf16[8,256,256]{2,1,0:T(8,128)(2,1)}), bf16[8,256,256]{2,1,0:T(8,128)(2,1)S(1)}, u32[]{:S(2)}, u32[]{:S(2)}) %all-to-all-start) | async-done | bytes 1048608 | tf_op jit(solution)/shard_map/sum_over_row/all_to_all | solution.py:296
  182.8 1.0 copy-done
  183.8 2.2 %sum_over_row.1 = bf16[256,256]{1,0:T(8,128)(2,1)} custom-call(bf16[8,256,256]{2,1,0:T(8,128)(2,1)} %copy-done, bf16[256,256]{1,0:T(8,128)(2,1)} %weight.3), custom_call_target="tpu_custom_call" | custom-call | tf_op jit(solution)/shard_map/sum_over_row/pallas_call | solution.py:214
  (94 shorter events, 9.8 us)
Async XLA Ops:
  0.6 10.8 %collective-permute-start.4 = (bf16[256,256]{1,0:T(8,128)(2,1)}, bf16[256,256]{1,0:T(8,128)(2,1)S(1)}, u32[]{:S(2)}, u32[]{:S(2)}) collective-permute-start(bf16[256,256]{1,0:T(8,128)(2,1)} %param.8), channel_id=1, source_target_pairs={{0,160},{32,128},{64,224},{96,192},{128,32},{160,0},{192,96},{224,... | collective-permute-start | bytes 393224 | tf_op jit(solution)/shard_map/gather_features/ppermute | solution.py:27
  5.6 10.8 %collective-permute-start.3 = (bf16[256,256]{1,0:T(8,128)(2,1)}, bf16[256,256]{1,0:T(8,128)(2,1)S(1)}, u32[]{:S(2)}, u32[]{:S(2)}) collective-permute-start(bf16[256,256]{1,0:T(8,128)(2,1)} %param.8), channel_id=1, source_target_pairs={{0,128},{32,160},{64,192},{96,224},{128,0},{160,32},{192,64},{224,... | collective-permute-start | bytes 393224 | tf_op jit(solution)/shard_map/gather_features/ppermute | solution.py:27
  5.9 11.9 %collective-permute-start.2 = (bf16[256,256]{1,0:T(8,128)(2,1)}, bf16[256,256]{1,0:T(8,128)(2,1)S(1)}, u32[]{:S(2)}, u32[]{:S(2)}) collective-permute-start(bf16[256,256]{1,0:T(8,128)(2,1)} %param.8), channel_id=1, source_target_pairs={{0,96},{32,64},{64,160},{96,128},{128,224},{160,192},{192,32},{224... | collective-permute-start | bytes 393224 | tf_op jit(solution)/shard_map/gather_features/ppermute | solution.py:27
  6.6 12.8 %collective-permute-start.1 = (bf16[256,256]{1,0:T(8,128)(2,1)}, bf16[256,256]{1,0:T(8,128)(2,1)S(1)}, u32[]{:S(2)}, u32[]{:S(2)}) collective-permute-start(bf16[256,256]{1,0:T(8,128)(2,1)} %param.8), channel_id=1, source_target_pairs={{0,64},{32,96},{64,128},{96,160},{128,192},{160,224},{192,0},{224,... | collective-permute-start | bytes 393224 | tf_op jit(solution)/shard_map/gather_features/ppermute | solution.py:27
  7.8 11.6 %collective-permute-start = (bf16[256,256]{1,0:T(8,128)(2,1)}, bf16[256,256]{1,0:T(8,128)(2,1)S(1)}, u32[]{:S(2)}, u32[]{:S(2)}) collective-permute-start(bf16[256,256]{1,0:T(8,128)(2,1)} %param.8), channel_id=1, source_target_pairs={{0,32},{32,0},{64,96},{96,64},{128,160},{160,128},{192,224},{224,1... | collective-permute-start | bytes 393224 | tf_op jit(solution)/shard_map/gather_features/ppermute | solution.py:27
  11.4 9.8 %copy-start.11 = (bf16[256,256]{1,0:T(8,128)(2,1)}, bf16[256,256]{1,0:T(8,128)(2,1)S(1)}, u32[]{:S(2)}) copy-start(bf16[256,256]{1,0:T(8,128)(2,1)S(1)} %collective-permute-done.4) | copy-start | bytes 393220
  11.4 8.1 %collective-permute-start.6 = (bf16[256,256]{1,0:T(8,128)(2,1)}, bf16[256,256]{1,0:T(8,128)(2,1)S(1)}, u32[]{:S(2)}, u32[]{:S(2)}) collective-permute-start(bf16[256,256]{1,0:T(8,128)(2,1)} %param.8), channel_id=1, source_target_pairs={{0,224},{32,192},{64,32},{96,0},{128,96},{160,64},{192,160},{224,1... | collective-permute-start | bytes 393224 | tf_op jit(solution)/shard_map/gather_features/ppermute | solution.py:27
  16.4 4.8 %copy-start.12 = (bf16[256,256]{1,0:T(8,128)(2,1)}, bf16[256,256]{1,0:T(8,128)(2,1)S(1)}, u32[]{:S(2)}) copy-start(bf16[256,256]{1,0:T(8,128)(2,1)S(1)} %collective-permute-done.3) | copy-start | bytes 393220
  16.4 4.8 %collective-permute-start.5 = (bf16[256,256]{1,0:T(8,128)(2,1)}, bf16[256,256]{1,0:T(8,128)(2,1)S(1)}, u32[]{:S(2)}, u32[]{:S(2)}) collective-permute-start(bf16[256,256]{1,0:T(8,128)(2,1)} %param.8), channel_id=1, source_target_pairs={{0,192},{32,224},{64,0},{96,32},{128,64},{160,96},{192,128},{224,1... | collective-permute-start | bytes 393224 | tf_op jit(solution)/shard_map/gather_features/ppermute | solution.py:27
  17.8 3.5 %copy-start.13 = (bf16[256,256]{1,0:T(8,128)(2,1)}, bf16[256,256]{1,0:T(8,128)(2,1)S(1)}, u32[]{:S(2)}) copy-start(bf16[256,256]{1,0:T(8,128)(2,1)S(1)} %collective-permute-done.2) | copy-start | bytes 393220
  33.7 3.0 %collective-permute-start.7 = (bf16[16,128,256]{2,1,0:T(8,128)(2,1)}, bf16[16,128,256]{2,1,0:T(8,128)(2,1)S(1)}, u32[]{:S(2)}, u32[]{:S(2)}) collective-permute-start(bf16[16,128,256]{2,1,0:T(8,128)(2,1)} %get-tuple-element.18), channel_id=1, source_target_pairs={{0,1},{1,0},{2,3},{3,2},{4,5},{5,4},{6,7},{7,6},{8,9},{9,8},{10,11... | collective-permute-start | bytes 3145736 | tf_op jit(solution)/shard_map/sum_over_col/ppermute | solution.py:37
  33.8 9.5 %collective-permute-start.12 = (bf16[16,128,256]{2,1,0:T(8,128)(2,1)}, bf16[16,128,256]{2,1,0:T(8,128)(2,1)S(1)}, u32[]{:S(2)}, u32[]{:S(2)}) collective-permute-start(bf16[16,128,256]{2,1,0:T(8,128)(2,1)} %get-tuple-element.20), channel_id=1, source_target_pairs={{0,1},{1,0},{2,3},{3,2},{4,5},{5,4},{6,7},{7,6},{8,9},{9,8},{10,11... | collective-permute-start | bytes 3145736 | tf_op jit(solution)/shard_map/sum_over_col/ppermute | solution.py:37
  38.2 14.6 %collective-permute-start.10 = (bf16[4,128,256]{2,1,0:T(8,128)(2,1)S(1)}, bf16[4,128,256]{2,1,0:T(8,128)(2,1)S(1)}, u32[]{:S(2)}, u32[]{:S(2)}) collective-permute-start(bf16[4,128,256]{2,1,0:T(8,128)(2,1)S(1)} %get-tuple-element.38), channel_id=1, source_target_pairs={{0,6},{1,7},{2,0},{3,1},{4,2},{5,3},{6,4},{7,5},{8,14},{9,15},{10,... | collective-permute-start | bytes 786440 | tf_op jit(solution)/shard_map/sum_over_col/ppermute | solution.py:37
  42.0 13.4 %collective-permute-start.9 = (bf16[4,128,256]{2,1,0:T(8,128)(2,1)S(1)}, bf16[4,128,256]{2,1,0:T(8,128)(2,1)S(1)}, u32[]{:S(2)}, u32[]{:S(2)}) collective-permute-start(bf16[4,128,256]{2,1,0:T(8,128)(2,1)S(1)} %get-tuple-element.39), channel_id=1, source_target_pairs={{0,2},{1,3},{2,4},{3,5},{4,6},{5,7},{6,0},{7,1},{8,10},{9,11},{10,... | collective-permute-start | bytes 786440 | tf_op jit(solution)/shard_map/sum_over_col/ppermute | solution.py:37
  42.0 13.4 %collective-permute-start.8 = (bf16[4,128,256]{2,1,0:T(8,128)(2,1)S(1)}, bf16[4,128,256]{2,1,0:T(8,128)(2,1)S(1)}, u32[]{:S(2)}, u32[]{:S(2)}) collective-permute-start(bf16[4,128,256]{2,1,0:T(8,128)(2,1)S(1)} %get-tuple-element.40), channel_id=1, source_target_pairs={{0,4},{1,5},{2,6},{3,7},{4,0},{5,1},{6,2},{7,3},{8,12},{9,13},{10,... | collective-permute-start | bytes 786440 | tf_op jit(solution)/shard_map/sum_over_col/ppermute | solution.py:37
  44.8 19.2 %collective-permute-start.15 = (bf16[4,128,256]{2,1,0:T(8,128)(2,1)S(1)}, bf16[4,128,256]{2,1,0:T(8,128)(2,1)S(1)}, u32[]{:S(2)}, u32[]{:S(2)}) collective-permute-start(bf16[4,128,256]{2,1,0:T(8,128)(2,1)S(1)} %get-tuple-element.33), channel_id=1, source_target_pairs={{0,6},{1,7},{2,0},{3,1},{4,2},{5,3},{6,4},{7,5},{8,14},{9,15},{10,... | collective-permute-start | bytes 786440 | tf_op jit(solution)/shard_map/sum_over_col/ppermute | solution.py:37
  46.3 21.0 %collective-permute-start.14 = (bf16[4,128,256]{2,1,0:T(8,128)(2,1)S(1)}, bf16[4,128,256]{2,1,0:T(8,128)(2,1)S(1)}, u32[]{:S(2)}, u32[]{:S(2)}) collective-permute-start(bf16[4,128,256]{2,1,0:T(8,128)(2,1)S(1)} %get-tuple-element.34), channel_id=1, source_target_pairs={{0,2},{1,3},{2,4},{3,5},{4,6},{5,7},{6,0},{7,1},{8,10},{9,11},{10,... | collective-permute-start | bytes 786440 | tf_op jit(solution)/shard_map/sum_over_col/ppermute | solution.py:37
  52.8 14.5 %collective-permute-start.13 = (bf16[4,128,256]{2,1,0:T(8,128)(2,1)S(1)}, bf16[4,128,256]{2,1,0:T(8,128)(2,1)S(1)}, u32[]{:S(2)}, u32[]{:S(2)}) collective-permute-start(bf16[4,128,256]{2,1,0:T(8,128)(2,1)S(1)} %get-tuple-element.35), channel_id=1, source_target_pairs={{0,4},{1,5},{2,6},{3,7},{4,0},{5,1},{6,2},{7,3},{8,12},{9,13},{10,... | collective-permute-start | bytes 786440 | tf_op jit(solution)/shard_map/sum_over_col/ppermute | solution.py:37
  55.6 11.7 %collective-permute-start.16 = (bf16[2,128,256]{2,1,0:T(8,128)(2,1)S(1)}, bf16[2,128,256]{2,1,0:T(8,128)(2,1)S(1)}, u32[]{:S(2)}, u32[]{:S(2)}) collective-permute-start(bf16[2,128,256]{2,1,0:T(8,128)(2,1)S(1)} %get-tuple-element.43), channel_id=1, source_target_pairs={{0,8},{1,9},{2,10},{3,11},{4,12},{5,13},{6,14},{7,15},{8,16},{9,17... | collective-permute-start | bytes 393224 | tf_op jit(solution)/shard_map/sum_over_col/ppermute | solution.py:37
  55.7 13.0 %collective-permute-start.11 = (bf16[2,128,256]{2,1,0:T(8,128)(2,1)S(1)}, bf16[2,128,256]{2,1,0:T(8,128)(2,1)S(1)}, u32[]{:S(2)}, u32[]{:S(2)}) collective-permute-start(bf16[2,128,256]{2,1,0:T(8,128)(2,1)S(1)} %get-tuple-element.44), channel_id=1, source_target_pairs={{0,16},{1,17},{2,18},{3,19},{4,20},{5,21},{6,22},{7,23},{8,24},{9,... | collective-permute-start | bytes 393224 | tf_op jit(solution)/shard_map/sum_over_col/ppermute | solution.py:37
  67.3 6.4 %copy-start.19 = (bf16[2,128,256]{2,1,0:T(8,128)(2,1)}, bf16[2,128,256]{2,1,0:T(8,128)(2,1)S(1)}, u32[]{:S(2)}) copy-start(bf16[2,128,256]{2,1,0:T(8,128)(2,1)S(1)} %collective-permute-done.16) | copy-start | bytes 393220
  68.1 5.6 %collective-permute-start.17 = (bf16[2,128,256]{2,1,0:T(8,128)(2,1)S(1)}, bf16[2,128,256]{2,1,0:T(8,128)(2,1)S(1)}, u32[]{:S(2)}, u32[]{:S(2)}) collective-permute-start(bf16[2,128,256]{2,1,0:T(8,128)(2,1)S(1)} %get-tuple-element.42), channel_id=1, source_target_pairs={{0,24},{1,25},{2,26},{3,27},{4,28},{5,29},{6,30},{7,31},{8,0},{9,1... | collective-permute-start | bytes 393224 | tf_op jit(solution)/shard_map/sum_over_col/ppermute | solution.py:37
  68.7 5.0 %copy-start.20 = (bf16[2,128,256]{2,1,0:T(8,128)(2,1)}, bf16[2,128,256]{2,1,0:T(8,128)(2,1)S(1)}, u32[]{:S(2)}) copy-start(bf16[2,128,256]{2,1,0:T(8,128)(2,1)S(1)} %collective-permute-done.11) | copy-start | bytes 393220
  79.0 30.9 %all-to-all-start.1 = ((f32[32,8,384]{2,1,0:T(8,128)}), f32[32,8,384]{2,1,0:T(8,128)S(1)}, u32[]{:S(2)}, u32[]{:S(2)}) async-start(f32[32,8,384]{2,1,0:T(8,128)} %bitcast.36), calls=%async_computation.1 | async-start | bytes 786432 | tf_op jit(solution)/shard_map/sum_weight_grad/all_to_all | solution.py:283
  91.2 13.7 %collective-permute-start.18 = (bf16[256,256]{1,0:T(8,128)(2,1)}, bf16[256,256]{1,0:T(8,128)(2,1)S(1)}, u32[]{:S(2)}, u32[]{:S(2)}) collective-permute-start(bf16[256,256]{1,0:T(8,128)(2,1)} %get-tuple-element.27), channel_id=1, source_target_pairs={{0,8},{1,9},{2,10},{3,11},{4,12},{5,13},{6,14},{7,15},{8,16},{9,17... | collective-permute-start | bytes 393224 | tf_op jit(solution)/shard_map/gather_gradients/ppermute | solution.py:37
  93.6 16.2 %collective-permute-start.19 = (bf16[256,256]{1,0:T(8,128)(2,1)}, bf16[256,256]{1,0:T(8,128)(2,1)S(1)}, u32[]{:S(2)}, u32[]{:S(2)}) collective-permute-start(bf16[256,256]{1,0:T(8,128)(2,1)} %get-tuple-element.27), channel_id=1, source_target_pairs={{0,16},{1,17},{2,18},{3,19},{4,20},{5,21},{6,22},{7,23},{8,24},{9,... | collective-permute-start | bytes 393224 | tf_op jit(solution)/shard_map/gather_gradients/ppermute | solution.py:37
  96.9 38.5 %collective-permute-start.23 = (bf16[256,256]{1,0:T(8,128)(2,1)}, bf16[256,256]{1,0:T(8,128)(2,1)S(1)}, u32[]{:S(2)}, u32[]{:S(2)}) collective-permute-start(bf16[256,256]{1,0:T(8,128)(2,1)} %get-tuple-element.27), channel_id=1, source_target_pairs={{0,6},{1,7},{2,0},{3,1},{4,2},{5,3},{6,4},{7,5},{8,14},{9,15},{10,... | collective-permute-start | bytes 393224 | tf_op jit(solution)/shard_map/gather_gradients/ppermute | solution.py:37
  99.3 35.7 %collective-permute-start.22 = (bf16[256,256]{1,0:T(8,128)(2,1)}, bf16[256,256]{1,0:T(8,128)(2,1)S(1)}, u32[]{:S(2)}, u32[]{:S(2)}) collective-permute-start(bf16[256,256]{1,0:T(8,128)(2,1)} %get-tuple-element.27), channel_id=1, source_target_pairs={{0,4},{1,5},{2,6},{3,7},{4,0},{5,1},{6,2},{7,3},{8,12},{9,13},{10,... | collective-permute-start | bytes 393224 | tf_op jit(solution)/shard_map/gather_gradients/ppermute | solution.py:37
  99.9 25.4 %collective-permute-start.21 = (bf16[256,256]{1,0:T(8,128)(2,1)}, bf16[256,256]{1,0:T(8,128)(2,1)S(1)}, u32[]{:S(2)}, u32[]{:S(2)}) collective-permute-start(bf16[256,256]{1,0:T(8,128)(2,1)} %get-tuple-element.27), channel_id=1, source_target_pairs={{0,2},{1,3},{2,4},{3,5},{4,6},{5,7},{6,0},{7,1},{8,10},{9,11},{10,... | collective-permute-start | bytes 393224 | tf_op jit(solution)/shard_map/gather_gradients/ppermute | solution.py:37
  105.0 17.2 %collective-permute-start.20 = (bf16[256,256]{1,0:T(8,128)(2,1)}, bf16[256,256]{1,0:T(8,128)(2,1)S(1)}, u32[]{:S(2)}, u32[]{:S(2)}) collective-permute-start(bf16[256,256]{1,0:T(8,128)(2,1)} %get-tuple-element.27), channel_id=1, source_target_pairs={{0,24},{1,25},{2,26},{3,27},{4,28},{5,29},{6,30},{7,31},{8,0},{9,1... | collective-permute-start | bytes 393224 | tf_op jit(solution)/shard_map/gather_gradients/ppermute | solution.py:37
  110.5 17.0 %all-to-all-start.2 = ((f32[8,8,384]{2,1,0:T(8,128)}), f32[8,8,384]{2,1,0:T(8,128)S(1)}, u32[]{:S(2)}, u32[]{:S(2)}) async-start(f32[8,8,384]{2,1,0:T(8,128)} %broadcast_in_dim.6), calls=%async_computation.2 | async-start | bytes 196608 | tf_op jit(solution)/shard_map/sum_weight_grad/all_to_all | solution.py:285
  122.2 29.5 %copy-start.2 = (bf16[768,256]{1,0:T(8,128)(2,1)}, bf16[768,256]{1,0:T(8,128)(2,1)S(1)}, u32[]{:S(2)}) copy-start(bf16[768,256]{1,0:T(8,128)(2,1)S(1)} %constant_dynamic-update-slice_fusion) | copy-start | bytes 1179652
  122.2 14.8 %collective-permute-start.26 = (bf16[768,256]{1,0:T(8,128)(2,1)S(1)}, bf16[768,256]{1,0:T(8,128)(2,1)S(1)}, u32[]{:S(2)}, u32[]{:S(2)}) collective-permute-start(bf16[768,256]{1,0:T(8,128)(2,1)S(1)} %constant_dynamic-update-slice_fusion), channel_id=1, source_target_pairs={{0,6},{1,7},{2,0},{3,1},{4,2},{5,3},{6,4},{7,5},{8,14},{9,15},{10,... | collective-permute-start | bytes 1179656 | tf_op jit(solution)/shard_map/gather_gradients/ppermute | solution.py:37
  124.8 21.5 %collective-permute-start.25 = (bf16[768,256]{1,0:T(8,128)(2,1)S(1)}, bf16[768,256]{1,0:T(8,128)(2,1)S(1)}, u32[]{:S(2)}, u32[]{:S(2)}) collective-permute-start(bf16[768,256]{1,0:T(8,128)(2,1)S(1)} %constant_dynamic-update-slice_fusion), channel_id=1, source_target_pairs={{0,4},{1,5},{2,6},{3,7},{4,0},{5,1},{6,2},{7,3},{8,12},{9,13},{10,... | collective-permute-start | bytes 1179656 | tf_op jit(solution)/shard_map/gather_gradients/ppermute | solution.py:37
  125.3 23.6 %collective-permute-start.24 = (bf16[768,256]{1,0:T(8,128)(2,1)S(1)}, bf16[768,256]{1,0:T(8,128)(2,1)S(1)}, u32[]{:S(2)}, u32[]{:S(2)}) collective-permute-start(bf16[768,256]{1,0:T(8,128)(2,1)S(1)} %constant_dynamic-update-slice_fusion), channel_id=1, source_target_pairs={{0,2},{1,3},{2,4},{3,5},{4,6},{5,7},{6,0},{7,1},{8,10},{9,11},{10,... | collective-permute-start | bytes 1179656 | tf_op jit(solution)/shard_map/gather_gradients/ppermute | solution.py:37
  128.4 36.0 %all-to-all-start.3 = ((f32[32,8,384]{2,1,0:T(8,128)}), f32[32,8,384]{2,1,0:T(8,128)S(1)}, u32[]{:S(2)}, u32[]{:S(2)}) async-start(f32[32,8,384]{2,1,0:T(8,128)} %broadcast_in_dim.7), calls=%async_computation.3 | async-start | bytes 786432 | tf_op jit(solution)/shard_map/sum_weight_grad/all_to_all | solution.py:287
  135.1 1.6 collective-permute-start.27
  135.4 14.2 %collective-permute-start.28 = (bf16[768,256]{1,0:T(8,128)(2,1)S(1)}, bf16[768,256]{1,0:T(8,128)(2,1)S(1)}, u32[]{:S(2)}, u32[]{:S(2)}) collective-permute-start(bf16[768,256]{1,0:T(8,128)(2,1)S(1)} %constant_dynamic-update-slice_fusion), channel_id=1, source_target_pairs={{0,1},{1,0},{2,3},{3,2},{4,5},{5,4},{6,7},{7,6},{8,9},{9,8},{10,11... | collective-permute-start | bytes 1179656 | tf_op jit(solution)/shard_map/gather_gradients/ppermute | solution.py:37
  135.8 15.9 %copy-start.1 = (bf16[768,256]{1,0:T(8,128)(2,1)}, bf16[768,256]{1,0:T(8,128)(2,1)S(1)}, u32[]{:S(2)}) copy-start(bf16[768,256]{1,0:T(8,128)(2,1)S(1)} %constant_dynamic-update-slice_fusion.3) | copy-start | bytes 1179652
  136.7 15.0 %copy-start.16 = (bf16[256,256]{1,0:T(8,128)(2,1)}, bf16[256,256]{1,0:T(8,128)(2,1)S(1)}, u32[]{:S(2)}) copy-start(bf16[256,256]{1,0:T(8,128)(2,1)S(1)} %collective-permute-done.27) | copy-start | bytes 393220
  136.7 12.9 %collective-permute-start.29 = (bf16[768,256]{1,0:T(8,128)(2,1)S(1)}, bf16[768,256]{1,0:T(8,128)(2,1)S(1)}, u32[]{:S(2)}, u32[]{:S(2)}) collective-permute-start(bf16[768,256]{1,0:T(8,128)(2,1)S(1)} %constant_dynamic-update-slice_fusion.3), channel_id=1, source_target_pairs={{0,1},{1,0},{2,3},{3,2},{4,5},{5,4},{6,7},{7,6},{8,9},{9,8},{10,11... | collective-permute-start | bytes 1179656 | tf_op jit(solution)/shard_map/gather_gradients/ppermute | solution.py:37
  137.0 14.7 %copy-start.3 = (bf16[768,256]{1,0:T(8,128)(2,1)}, bf16[768,256]{1,0:T(8,128)(2,1)S(1)}, u32[]{:S(2)}) copy-start(bf16[768,256]{1,0:T(8,128)(2,1)S(1)} %collective-permute-done.26) | copy-start | bytes 1179652
  137.0 12.7 %collective-permute-start.32 = (bf16[768,256]{1,0:T(8,128)(2,1)S(1)}, bf16[768,256]{1,0:T(8,128)(2,1)S(1)}, u32[]{:S(2)}, u32[]{:S(2)}) collective-permute-start(bf16[768,256]{1,0:T(8,128)(2,1)S(1)} %collective-permute-done.26), channel_id=1, source_target_pairs={{0,1},{1,0},{2,3},{3,2},{4,5},{5,4},{6,7},{7,6},{8,9},{9,8},{10,11... | collective-permute-start | bytes 1179656 | tf_op jit(solution)/shard_map/gather_gradients/ppermute | solution.py:37
  146.2 5.5 %copy-start.4 = (bf16[768,256]{1,0:T(8,128)(2,1)}, bf16[768,256]{1,0:T(8,128)(2,1)S(1)}, u32[]{:S(2)}) copy-start(bf16[768,256]{1,0:T(8,128)(2,1)S(1)} %collective-permute-done.25) | copy-start | bytes 1179652
  146.2 3.4 %collective-permute-start.31 = (bf16[768,256]{1,0:T(8,128)(2,1)S(1)}, bf16[768,256]{1,0:T(8,128)(2,1)S(1)}, u32[]{:S(2)}, u32[]{:S(2)}) collective-permute-start(bf16[768,256]{1,0:T(8,128)(2,1)S(1)} %collective-permute-done.25), channel_id=1, source_target_pairs={{0,1},{1,0},{2,3},{3,2},{4,5},{5,4},{6,7},{7,6},{8,9},{9,8},{10,11... | collective-permute-start | bytes 1179656 | tf_op jit(solution)/shard_map/gather_gradients/ppermute | solution.py:37
  149.0 2.8 %copy-start.5 = (bf16[768,256]{1,0:T(8,128)(2,1)}, bf16[768,256]{1,0:T(8,128)(2,1)S(1)}, u32[]{:S(2)}) copy-start(bf16[768,256]{1,0:T(8,128)(2,1)S(1)} %collective-permute-done.24) | copy-start | bytes 1179652
  149.0 2.0 %collective-permute-start.30 = (bf16[768,256]{1,0:T(8,128)(2,1)S(1)}, bf16[768,256]{1,0:T(8,128)(2,1)S(1)}, u32[]{:S(2)}, u32[]{:S(2)}) collective-permute-start(bf16[768,256]{1,0:T(8,128)(2,1)S(1)} %collective-permute-done.24), channel_id=1, source_target_pairs={{0,1},{1,0},{2,3},{3,2},{4,5},{5,4},{6,7},{7,6},{8,9},{9,8},{10,11... | collective-permute-start | bytes 1179656 | tf_op jit(solution)/shard_map/gather_gradients/ppermute | solution.py:37
  164.4 18.4 %all-to-all-start = ((bf16[8,256,256]{2,1,0:T(8,128)(2,1)}), bf16[8,256,256]{2,1,0:T(8,128)(2,1)S(1)}, u32[]{:S(2)}, u32[]{:S(2)}) async-start(bf16[8,256,256]{2,1,0:T(8,128)(2,1)} %bitcast.33), calls=%async_computation | async-start | bytes 2097152 | tf_op jit(solution)/shard_map/sum_over_row/all_to_all | solution.py:296
  (11 other events, 17.0 us)

commit v2 on v1

--- a/solution.py
+++ b/solution.py
@@ -19,14 +19,6 @@
 LANES = 128
 
 
-def row_shift(value, dx, dzl):
-    pairs = []
-    for i in range(N_ROW):
-        x, zl = divmod(i, N_ZL)
-        pairs.append((i, (x + dx) % N_X * N_ZL + (zl ^ dzl)))
-    return lax.ppermute(value, "row", pairs)
-
-
 def col_shift(value, dzh=0, dy=0, dcore=0):
     pairs = []
     for i in range(N_COL):
@@ -72,17 +64,15 @@
     def _(g):
         tile_copy(g).wait()
 
-        @pl.loop(0, GROUP // 8)
-        def _(i):
-            for j in range(8):
-                slot = g * GROUP + i * 8 + j
-                product = lax.dot_general(
-                    held[slot],
-                    src[take[slot]],
-                    (((0 if transposed else 1,), (0,)), ((), ())),
-                    preferred_element_type=jnp.float32,
-                )
-                acc[put[slot]] += product
+        for j in range(GROUP):
+            slot = g * GROUP + j
+            product = lax.dot_general(
+                held[slot],
+                src[take[slot]],
+                (((0 if transposed else 1,), (0,)), ((), ())),
+                preferred_element_type=jnp.float32,
+            )
+            acc[put[slot]] += product
 
     copies, first = [], 0
     for k, size in enumerate(out_sizes):
@@ -216,6 +206,7 @@
         in_specs=[vmem] * 2,
         out_specs=vmem,
         out_shape=jax.ShapeDtypeStruct((rows, width), jnp.bfloat16),
+        compiler_params=pltpu.CompilerParams(vmem_limit_bytes=VMEM_LIMIT),
     )(pieces, weight)
 
 
@@ -230,32 +221,26 @@
     tile = adjacency.shape[2]
     scale = 1.0 / math.sqrt(vertices * N_ROW * N_COL)
     live = live_tiles.reshape(1)
-    row_id, col_id = lax.axis_index("row"), lax.axis_index("col")
-    my_x, my_zl = row_id // N_ZL, row_id % N_ZL
+    col_id = lax.axis_index("col")
     my_zh, my_y, my_core = col_id // 8, col_id // 2 % 4, col_id % 2
 
     per = vertices // tile
     r, c = tile_rows[0], tile_cols[0]
-    rc, cc = r // per, c // per
+    rc = r // per
     r_zh, r_y, r_core = rc // 8, rc // 2 % 4, rc % 2
-    c_x, c_zl = cc // 2, cc % 2
     half = (r_core ^ my_core) * 16
     ahead = (r_zh - my_zh) & 3
     part = ((ahead == 3) | (ahead == 0)).astype(jnp.int32)
     place = ((ahead == 1) | (ahead == 0)).astype(jnp.int32)
     put_rows = (half + part * 8 + ((r_y - my_y) & 3) * 2 + place) * per + r % per
-    back_y, back_zh = (my_y - r_y) & 3, (my_zh - r_zh) & 3
-    take_rows = jnp.where(back_zh == 0, 3 + back_y, 3 * back_y + 3 + back_zh)
-    take_rows = jnp.where(back_y == 0, back_zh, take_rows)
-    take_rows = (half + take_rows) * per + r % per
-    take_cols = (((my_x - c_x) & 3) * 2 + (c_zl ^ my_zl)) * per + c % per
-
-    moves = [(dx, dzl) for dx in range(N_X) for dzl in range(N_ZL)]
+    take_rows = (half + ((my_y - r_y) & 3) * 4 + ((my_zh - r_zh) & 3)) * per + r % per
+
     with jax.named_scope("gather_features"):
-        sources = [features] + [row_shift(features, *m) for m in moves[1:]]
+        copies = jnp.broadcast_to(features, (N_ROW,) + features.shape)
+        source = lax.all_to_all(copies, "row", 0, 0, tiled=True)
     with jax.named_scope("tiles_forward"):
         parts = tile_sum(
-            adjacency, live, take_cols, put_rows, sources, [8 * per] * 4, False
+            adjacency, live, c, put_rows, [source], [8 * per] * 4, False
         )
     with jax.named_scope("sum_over_col"):
         sums, pieces = [], []
@@ -276,10 +261,10 @@
         layer_out, grad, total, pre_grad = middle(pieces, weight, bias, cotangent)
     with jax.named_scope("gather_gradients"):
         near = [col_shift(grad, dzh=k) for k in range(1, N_ZH)]
-        ours = jnp.concatenate([col_shift(grad, dy=k) for k in range(1, N_Y)])
-        stack = jnp.concatenate(near)
+        load = loads(total, pre_grad).reshape(N_COL, -1, width + LANES)
+        *near, load = lax.optimization_barrier((*near, load))
+        here = [jnp.concatenate([grad] + near)]
     with jax.named_scope("sum_weight_grad"):
-        load = loads(total, pre_grad).reshape(N_COL, -1, width + LANES)
         load = jnp.sum(lax.all_to_all(load, "col", 0, 0, tiled=True), axis=0)
         load = jnp.broadcast_to(load, (N_ROW,) + load.shape)
         load = jnp.sum(lax.all_to_all(load, "row", 0, 0, tiled=True), axis=0) * scale
@@ -287,8 +272,7 @@
         load = lax.all_to_all(load, "col", 0, 0, tiled=True).reshape(width, -1)
         weight_grad, bias_grad = load[:, :width], load[:, width]
     with jax.named_scope("gather_gradients"):
-        theirs = [col_shift(stack, dy=k) for k in range(1, N_Y)]
-        here = [grad, stack, ours] + theirs
+        here += [col_shift(here[0], dy=k) for k in range(1, N_Y)]
         there = [col_shift(p, dcore=1) for p in here]
     with jax.named_scope("tiles_backward"):
         (back,) = tile_sum(adjacency, live, take_rows, c, here + there, [N_ROW * per], True)

time: 187 us -> 174 us (0.930)
  starting transfers between devices: 85.2 us -> 63.3 us
  Pallas kernels: 31.1 us -> 16.8 us
  waiting for transfers between devices: 55.4 us -> 69 us
  blocking collectives: 0 us -> 8.12 us
  local copies, waits for them, and re-layouts: 6.04 us -> 8.54 us
    pallas_call x2, Pallas kernels: 24.4 us -> 10 us  [tile_sum(): pl.pallas_call(functools.partial(tile_kernel, transposed, src_sizes, out_...]
    all_to_all x1, waiting for transfers between devices: 0.01 us -> 11.2 us  [shards(): load = jnp.sum(lax.all_to_all(load, 'col', 0, 0, tiled=True), axis=0)]
    ppermute x7 -> x0, starting transfers between devices: 10 us -> none  [row_shift(): return lax.ppermute(value, 'row', pairs)]
    all_to_all x1, waiting for transfers between devices: 1.64 us -> 11.3 us  [shards(): source = lax.all_to_all(copies, 'row', 0, 0, tiled=True)]
    all_to_all x0 -> x1, blocking collectives: none -> 8.12 us  [shards(): lax.all_to_all(load, 'row', 0, 0, tiled=True)]
    ppermute x26 -> x21, waiting for transfers between devices: 34.5 us -> 26.7 us  [col_shift(): return lax.ppermute(value, 'col', pairs)]
    ppermute x7 -> x0, waiting for transfers between devices: 7.27 us -> none  [row_shift(): return lax.ppermute(value, 'row', pairs)]
    all_to_all x1, starting transfers between devices: 11.6 us -> 6.2 us  [shards(): source = lax.all_to_all(copies, 'row', 0, 0, tiled=True)]
  transfers between devices with their start and end apart: 37 -> 25, of which waited for: 16 -> 14; matrix products, arithmetic and copies ran while one was open for 5% -> 6% of each run, Pallas kernels for 7% -> 4%
where the time goes in v2:
time: 174 us
  waiting for transfers between devices  69 us (40%)
  starting transfers between devices  63.3 us (36%)
  Pallas kernels  16.8 us (10%)
  local copies, waits for them, and re-layouts  8.54 us (5%)
  blocking collectives  8.12 us (5%)
  other arithmetic  6.52 us (4%)
    ppermute x21, starting transfers between devices, col_shift(): return lax.ppermute(value, 'col', pairs)  38.8 us
    ppermute x21, waiting for transfers between devices, col_shift(): return lax.ppermute(value, 'col', pairs)  26.7 us
    all_to_all x1, waiting for transfers between devices, shards(): lax.all_to_all(back.reshape(N_ROW, vertices, width), 'row', 0, 0, tiled=T...  14.7 us
    all_to_all x1, waiting for transfers between devices, shards(): source = lax.all_to_all(copies, 'row', 0, 0, tiled=True)  11.3 us
    all_to_all x1, waiting for transfers between devices, shards(): load = jnp.sum(lax.all_to_all(load, 'col', 0, 0, tiled=True), axis=0)  11.2 us
    pallas_call x2, Pallas kernels, tile_sum(): pl.pallas_call(functools.partial(tile_kernel, transposed, src_sizes, out_...  10 us
    all_to_all x1, starting transfers between devices, shards(): load = jnp.sum(lax.all_to_all(load, 'col', 0, 0, tiled=True), axis=0)  9.45 us
    all_to_all x1, blocking collectives, shards(): lax.all_to_all(load, 'row', 0, 0, tiled=True)  8.12 us
  transfers between devices with their start and end apart: 25, of which 14 were waited for; matrix products, arithmetic and copies ran while one was open for 6% of the time, Pallas kernels for 4%

profile of v2, /device:TPU:1, one launch (start us, length us, event | category | flops | bytes accessed | tf_op | source)
XLA Modules:
  0.0 173.8 jit_solution(9088003951709215742)
XLA Ops:
  0.6 1.9 %broadcast_in_dim.9 = bf16[8,256,256]{2,1,0:T(8,128)(2,1)} broadcast(bf16[256,256]{1,0:T(8,128)(2,1)} %param.8), dimensions={1,2} | broadcast | bytes 1179648 | tf_op jit(solution)/shard_map/gather_features/broadcast_in_dim | solution.py:239
  2.6 6.2 %all-to-all-start = ((bf16[8,256,256]{2,1,0:T(8,128)(2,1)}), bf16[8,256,256]{2,1,0:T(8,128)(2,1)S(1)}, u32[]{:S(2)}, u32[]{:S(2)}) async-start(bf16[8,256,256]{2,1,0:T(8,128)(2,1)} %broadcast_in_dim.9), calls=%async_computation | async-start | bytes 2097152 | tf_op jit(solution)/shard_map/gather_features/all_to_all | solution.py:240
  9.4 1.3 multiply_add_fusion
  10.7 1.3 multiply_add_fusion.1.put
  12.0 11.3 %all-to-all-done = bf16[8,256,256]{2,1,0:T(8,128)(2,1)S(1)} async-done(((bf16[8,256,256]{2,1,0:T(8,128)(2,1)}), bf16[8,256,256]{2,1,0:T(8,128)(2,1)S(1)}, u32[]{:S(2)}, u32[]{:S(2)}) %all-to-all-start) | async-done | bytes 1048608 | tf_op jit(solution)/shard_map/gather_features/all_to_all | solution.py:240
  23.3 1.0 copy-done.1
  24.3 5.0 %tiles_forward.1 = (bf16[16,128,256]{2,1,0:T(8,128)(2,1)}, bf16[16,128,256]{2,1,0:T(8,128)(2,1)}, bf16[16,128,256]{2,1,0:T(8,128)(2,1)}, bf16[16,128,256]{2,1,0:T(8,128)(2,1)}) custom-call(s32[1]{0:T(128)} %bitcast.20.live, s32[192]{0:T(256)} %bitcast.39, s32[192]{0:T(256)} %multiply_add_fusion.1.put, bf16[1,192,128,128]{3,2,1,0:T(8,128)(2,1)} %tiles.3, ...), custom_call_target="tpu_custom_call" | custom-call | flops 1610612736 | bytes 6291456 | tf_op jit(solution)/shard_map/tiles_forward/pallas_call | solution.py:101
  29.3 2.2 %collective-permute-start = (bf16[16,128,256]{2,1,0:T(8,128)(2,1)}, bf16[16,128,256]{2,1,0:T(8,128)(2,1)S(1)}, u32[]{:S(2)}, u32[]{:S(2)}) collective-permute-start(bf16[16,128,256]{2,1,0:T(8,128)(2,1)} %get-tuple-element.22), channel_id=1, source_target_pairs={{0,1},{1,0},{2,3},{3,2},{4,5},{5,4},{6,7},{7,6},{8,9},{9,8},{10,11... | collective-permute-start | bytes 3145736 | tf_op jit(solution)/shard_map/sum_over_col/ppermute | solution.py:29
  31.6 2.4 %collective-permute-done = bf16[16,128,256]{2,1,0:T(8,128)(2,1)S(1)} collective-permute-done((bf16[16,128,256]{2,1,0:T(8,128)(2,1)}, bf16[16,128,256]{2,1,0:T(8,128)(2,1)S(1)}, u32[]{:S(2)}, u32[]{:S(2)}) %collective-permute-start) | collective-permute-done | bytes 1048608 | tf_op jit(solution)/shard_map/sum_over_col/ppermute | solution.py:29
  34.0 1.5 add_convert_fusion.7
  35.5 3.4 %collective-permute-start.3 = (bf16[4,128,256]{2,1,0:T(8,128)(2,1)S(1)}, bf16[4,128,256]{2,1,0:T(8,128)(2,1)S(1)}, u32[]{:S(2)}, u32[]{:S(2)}) collective-permute-start(bf16[4,128,256]{2,1,0:T(8,128)(2,1)S(1)} %get-tuple-element.46), channel_id=1, source_target_pairs={{0,6},{1,7},{2,0},{3,1},{4,2},{5,3},{6,4},{7,5},{8,14},{9,15},{10,... | collective-permute-start | bytes 786440 | tf_op jit(solution)/shard_map/sum_over_col/ppermute | solution.py:29
  39.2 4.8 %collective-permute-start.1 = (bf16[4,128,256]{2,1,0:T(8,128)(2,1)S(1)}, bf16[4,128,256]{2,1,0:T(8,128)(2,1)S(1)}, u32[]{:S(2)}, u32[]{:S(2)}) collective-permute-start(bf16[4,128,256]{2,1,0:T(8,128)(2,1)S(1)} %get-tuple-element.48), channel_id=1, source_target_pairs={{0,4},{1,5},{2,6},{3,7},{4,0},{5,1},{6,2},{7,3},{8,12},{9,13},{10,... | collective-permute-start | bytes 786440 | tf_op jit(solution)/shard_map/sum_over_col/ppermute | solution.py:29
  44.0 1.5 add_convert_fusion
  45.5 0.8 collective-permute-start.8
  46.3 0.8 collective-permute-start.7
  47.1 3.0 %collective-permute-start.6 = (bf16[4,128,256]{2,1,0:T(8,128)(2,1)S(1)}, bf16[4,128,256]{2,1,0:T(8,128)(2,1)S(1)}, u32[]{:S(2)}, u32[]{:S(2)}) collective-permute-start(bf16[4,128,256]{2,1,0:T(8,128)(2,1)S(1)} %get-tuple-element.43), channel_id=1, source_target_pairs={{0,4},{1,5},{2,6},{3,7},{4,0},{5,1},{6,2},{7,3},{8,12},{9,13},{10,... | collective-permute-start | bytes 786440 | tf_op jit(solution)/shard_map/sum_over_col/ppermute | solution.py:29
  50.1 5.3 %collective-permute-done.1 = bf16[4,128,256]{2,1,0:T(8,128)(2,1)S(1)} collective-permute-done((bf16[4,128,256]{2,1,0:T(8,128)(2,1)S(1)}, bf16[4,128,256]{2,1,0:T(8,128)(2,1)S(1)}, u32[]{:S(2)}, u32[]{:S(2)}) %collective-permute-start.1) | collective-permute-done | bytes 262176 | tf_op jit(solution)/shard_map/sum_over_col/ppermute | solution.py:29
  55.5 3.5 %collective-permute-start.9 = (bf16[2,128,256]{2,1,0:T(8,128)(2,1)S(1)}, bf16[2,128,256]{2,1,0:T(8,128)(2,1)S(1)}, u32[]{:S(2)}, u32[]{:S(2)}) collective-permute-start(bf16[2,128,256]{2,1,0:T(8,128)(2,1)S(1)} %get-tuple-element.51), channel_id=1, source_target_pairs={{0,8},{1,9},{2,10},{3,11},{4,12},{5,13},{6,14},{7,15},{8,16},{9,17... | collective-permute-start | bytes 393224 | tf_op jit(solution)/shard_map/sum_over_col/ppermute | solution.py:29
  59.0 3.8 %collective-permute-start.4 = (bf16[2,128,256]{2,1,0:T(8,128)(2,1)S(1)}, bf16[2,128,256]{2,1,0:T(8,128)(2,1)S(1)}, u32[]{:S(2)}, u32[]{:S(2)}) collective-permute-start(bf16[2,128,256]{2,1,0:T(8,128)(2,1)S(1)} %get-tuple-element.52), channel_id=1, source_target_pairs={{0,16},{1,17},{2,18},{3,19},{4,20},{5,21},{6,22},{7,23},{8,24},{9,... | collective-permute-start | bytes 393224 | tf_op jit(solution)/shard_map/sum_over_col/ppermute | solution.py:29
  62.8 3.8 %collective-permute-done.6 = bf16[4,128,256]{2,1,0:T(8,128)(2,1)S(1)} collective-permute-done((bf16[4,128,256]{2,1,0:T(8,128)(2,1)S(1)}, bf16[4,128,256]{2,1,0:T(8,128)(2,1)S(1)}, u32[]{:S(2)}, u32[]{:S(2)}) %collective-permute-start.6) | collective-permute-done | bytes 262176 | tf_op jit(solution)/shard_map/sum_over_col/ppermute | solution.py:29
  66.6 0.8 add_convert_fusion.8
  67.4 5.1 %collective-permute-start.10 = (bf16[2,128,256]{2,1,0:T(8,128)(2,1)S(1)}, bf16[2,128,256]{2,1,0:T(8,128)(2,1)S(1)}, u32[]{:S(2)}, u32[]{:S(2)}) collective-permute-start(bf16[2,128,256]{2,1,0:T(8,128)(2,1)S(1)} %get-tuple-element.50), channel_id=1, source_target_pairs={{0,24},{1,25},{2,26},{3,27},{4,28},{5,29},{6,30},{7,31},{8,0},{9,1... | collective-permute-start | bytes 393224 | tf_op jit(solution)/shard_map/sum_over_col/ppermute | solution.py:29
  72.6 5.1 %collective-permute-done.10 = bf16[2,128,256]{2,1,0:T(8,128)(2,1)S(1)} collective-permute-done((bf16[2,128,256]{2,1,0:T(8,128)(2,1)S(1)}, bf16[2,128,256]{2,1,0:T(8,128)(2,1)S(1)}, u32[]{:S(2)}, u32[]{:S(2)}) %collective-permute-start.10) | collective-permute-done | bytes 131104 | tf_op jit(solution)/shard_map/sum_over_col/ppermute | solution.py:29
  77.6 0.7 copy-done.12
  78.3 2.5 %pointwise.1 = (bf16[256,256]{1,0:T(8,128)(2,1)}, bf16[256,256]{1,0:T(8,128)(2,1)}, f32[256,256]{1,0:T(8,128)}, f32[256,256]{1,0:T(8,128)}) custom-call(bf16[256,256]{1,0:T(8,128)(2,1)} %bitcast.37, bf16[256,256]{1,0:T(8,128)(2,1)} %bitcast.36, bf16[256,256]{1,0:T(8,128)(2,1)} %bitcast.38, bf16[256,256]{1,0:T(8,128)(2,1)} %bitcast.35, ...), custom_call_target="tpu_custom_call" | custom-call | tf_op jit(solution)/shard_map/pointwise/pallas_call | solution.py:158
  80.8 2.2 %collective-permute-start.13 = (bf16[256,256]{1,0:T(8,128)(2,1)}, bf16[256,256]{1,0:T(8,128)(2,1)S(1)}, u32[]{:S(2)}, u32[]{:S(2)}) collective-permute-start(bf16[256,256]{1,0:T(8,128)(2,1)} %get-tuple-element.31), channel_id=1, source_target_pairs={{0,24},{1,25},{2,26},{3,27},{4,28},{5,29},{6,30},{7,31},{8,0},{9,1... | collective-permute-start | bytes 393224 | tf_op jit(solution)/shard_map/gather_gradients/ppermute | solution.py:29
  83.0 3.4 %collective-permute-start.12 = (bf16[256,256]{1,0:T(8,128)(2,1)}, bf16[256,256]{1,0:T(8,128)(2,1)S(1)}, u32[]{:S(2)}, u32[]{:S(2)}) collective-permute-start(bf16[256,256]{1,0:T(8,128)(2,1)} %get-tuple-element.31), channel_id=1, source_target_pairs={{0,16},{1,17},{2,18},{3,19},{4,20},{5,21},{6,22},{7,23},{8,24},{9,... | collective-permute-start | bytes 393224 | tf_op jit(solution)/shard_map/gather_gradients/ppermute | solution.py:29
  86.5 2.1 %gather_gradients.1 = f32[256,384]{1,0:T(8,128)} custom-call(f32[256,256]{1,0:T(8,128)} %get-tuple-element.32.total, f32[256,256]{1,0:T(8,128)} %get-tuple-element.33.pre_grad), custom_call_target="tpu_custom_call" | custom-call | tf_op jit(solution)/shard_map/gather_gradients/pallas_call | solution.py:180
  88.7 1.8 %collective-permute-done.13 = bf16[256,256]{1,0:T(8,128)(2,1)S(1)} collective-permute-done((bf16[256,256]{1,0:T(8,128)(2,1)}, bf16[256,256]{1,0:T(8,128)(2,1)S(1)}, u32[]{:S(2)}, u32[]{:S(2)}) %collective-permute-start.13) | collective-permute-done | bytes 131104 | tf_op jit(solution)/shard_map/gather_gradients/ppermute | solution.py:29
  90.4 4.7 %collective-permute-done.12 = bf16[256,256]{1,0:T(8,128)(2,1)S(1)} collective-permute-done((bf16[256,256]{1,0:T(8,128)(2,1)}, bf16[256,256]{1,0:T(8,128)(2,1)S(1)}, u32[]{:S(2)}, u32[]{:S(2)}) %collective-permute-start.12) | collective-permute-done | bytes 131104 | tf_op jit(solution)/shard_map/gather_gradients/ppermute | solution.py:29
  95.4 9.4 %all-to-all-start.2 = ((f32[32,8,384]{2,1,0:T(8,128)}), f32[32,8,384]{2,1,0:T(8,128)S(1)}, u32[]{:S(2)}, u32[]{:S(2)}) async-start(f32[32,8,384]{2,1,0:T(8,128)} %bitcast.26), calls=%async_computation.2 | async-start | bytes 786432 | tf_op jit(solution)/shard_map/sum_weight_grad/all_to_all | solution.py:268
  104.9 0.9 constant_dynamic-update-slice_fusion.3
  105.9 2.7 %collective-permute-start.16 = (bf16[1024,256]{1,0:T(8,128)(2,1)S(1)}, bf16[1024,256]{1,0:T(8,128)(2,1)S(1)}, u32[]{:S(2)}, u32[]{:S(2)}) collective-permute-start(bf16[1024,256]{1,0:T(8,128)(2,1)S(1)} %constant_dynamic-update-slice_fusion), channel_id=1, source_target_pairs={{0,6},{1,7},{2,0},{3,1},{4,2},{5,3},{6,4},{7,5},{8,14},{9,15},{10,... | collective-permute-start | bytes 1572872 | tf_op jit(solution)/shard_map/gather_gradients/ppermute | solution.py:29
  109.7 11.2 %all-to-all-done.2 = f32[32,8,384]{2,1,0:T(8,128)S(1)} async-done(((f32[32,8,384]{2,1,0:T(8,128)}), f32[32,8,384]{2,1,0:T(8,128)S(1)}, u32[]{:S(2)}, u32[]{:S(2)}) %all-to-all-start.2) | async-done | bytes 393248 | tf_op jit(solution)/shard_map/sum_weight_grad/all_to_all | solution.py:268
  121.0 8.1 %all_to_all.25 = f32[8,8,384]{2,1,0:T(8,128)S(1)} all-to-all(f32[8,8,384]{2,1,0:T(8,128)S(1)} %broadcast_in_dim.10), channel_id=1, replica_groups=mesh['row'=8,'col'=32] {'row'}, dimensions={0} | all-to-all | bytes 196608 | tf_op jit(solution)/shard_map/sum_weight_grad/all_to_all | solution.py:270
  129.1 0.8 broadcast_in_dim.11
  129.9 5.3 %all-to-all-start.4 = ((f32[32,8,384]{2,1,0:T(8,128)}), f32[32,8,384]{2,1,0:T(8,128)S(1)}, u32[]{:S(2)}, u32[]{:S(2)}) async-start(f32[32,8,384]{2,1,0:T(8,128)} %broadcast_in_dim.11), calls=%async_computation.4 | async-start | bytes 786432 | tf_op jit(solution)/shard_map/sum_weight_grad/all_to_all | solution.py:272
  136.2 1.9 %collective-permute-done.14 = bf16[1024,256]{1,0:T(8,128)(2,1)S(1)} collective-permute-done((bf16[1024,256]{1,0:T(8,128)(2,1)S(1)}, bf16[1024,256]{1,0:T(8,128)(2,1)S(1)}, u32[]{:S(2)}, u32[]{:S(2)}) %collective-permute-start.14) | collective-permute-done | bytes 524320 | tf_op jit(solution)/shard_map/gather_gradients/ppermute | solution.py:29
  138.7 1.4 collective-permute-done.18
  140.1 0.8 copy-done.9
  140.9 5.0 %tiles_backward.1 = bf16[16,128,256]{2,1,0:T(8,128)(2,1)} custom-call(s32[1]{0:T(128)} %bitcast.21.live, s32[192]{0:T(256)} %get-tuple-element.38.take, s32[192]{0:T(256)} %bitcast.40, bf16[1,192,128,128]{3,2,1,0:T(8,128)(2,1)} %tiles.3, bf16[8,128,256]{2,1,0:T(8,128)(2,1)} %bitcast.27, bf16[8,128,256]{2,1,0:T(8,128)(2,1)} %bitcast.30, ...), custom_call_target="tpu_custom_call" | custom-call | flops 1610612736 | bytes 6291456 | tf_op jit(solution)/shard_map/tiles_backward/pallas_call | solution.py:101
  146.0 5.1 %all-to-all-done.4 = f32[32,8,384]{2,1,0:T(8,128)S(1)} async-done(((f32[32,8,384]{2,1,0:T(8,128)}), f32[32,8,384]{2,1,0:T(8,128)S(1)}, u32[]{:S(2)}, u32[]{:S(2)}) %all-to-all-start.4) | async-done | bytes 393248 | tf_op jit(solution)/shard_map/sum_weight_grad/all_to_all | solution.py:272
  151.0 3.6 %all-to-all-start.1 = ((bf16[8,256,256]{2,1,0:T(8,128)(2,1)}), bf16[8,256,256]{2,1,0:T(8,128)(2,1)S(1)}, u32[]{:S(2)}, u32[]{:S(2)}) async-start(bf16[8,256,256]{2,1,0:T(8,128)(2,1)} %bitcast.22), calls=%async_computation.1 | async-start | bytes 2097152 | tf_op jit(solution)/shard_map/sum_over_row/all_to_all | solution.py:280
  154.6 0.7 slice.152
  155.3 0.7 slice_reduce_fusion
  156.0 14.7 %all-to-all-done.1.pieces = bf16[8,256,256]{2,1,0:T(8,128)(2,1)S(1)} async-done(((bf16[8,256,256]{2,1,0:T(8,128)(2,1)}), bf16[8,256,256]{2,1,0:T(8,128)(2,1)S(1)}, u32[]{:S(2)}, u32[]{:S(2)}) %all-to-all-start.1) | async-done | bytes 1048608 | tf_op jit(solution)/shard_map/sum_over_row/all_to_all | solution.py:280
  170.7 1.0 copy-done
  171.7 2.2 %sum_over_row.1 = bf16[256,256]{1,0:T(8,128)(2,1)} custom-call(bf16[8,256,256]{2,1,0:T(8,128)(2,1)} %copy-done, bf16[256,256]{1,0:T(8,128)(2,1)} %weight.3), custom_call_target="tpu_custom_call" | custom-call | tf_op jit(solution)/shard_map/sum_over_row/pallas_call | solution.py:204
  (52 shorter events, 4.0 us)
Async XLA Ops:
  2.6 20.7 %all-to-all-start = ((bf16[8,256,256]{2,1,0:T(8,128)(2,1)}), bf16[8,256,256]{2,1,0:T(8,128)(2,1)S(1)}, u32[]{:S(2)}, u32[]{:S(2)}) async-start(bf16[8,256,256]{2,1,0:T(8,128)(2,1)} %broadcast_in_dim.9), calls=%async_computation | async-start | bytes 2097152 | tf_op jit(solution)/shard_map/gather_features/all_to_all | solution.py:240
  23.3 1.0 copy-start.1
  29.3 4.7 %collective-permute-start = (bf16[16,128,256]{2,1,0:T(8,128)(2,1)}, bf16[16,128,256]{2,1,0:T(8,128)(2,1)S(1)}, u32[]{:S(2)}, u32[]{:S(2)}) collective-permute-start(bf16[16,128,256]{2,1,0:T(8,128)(2,1)} %get-tuple-element.22), channel_id=1, source_target_pairs={{0,1},{1,0},{2,3},{3,2},{4,5},{5,4},{6,7},{7,6},{8,9},{9,8},{10,11... | collective-permute-start | bytes 3145736 | tf_op jit(solution)/shard_map/sum_over_col/ppermute | solution.py:29
  31.5 12.5 %collective-permute-start.5 = (bf16[16,128,256]{2,1,0:T(8,128)(2,1)}, bf16[16,128,256]{2,1,0:T(8,128)(2,1)S(1)}, u32[]{:S(2)}, u32[]{:S(2)}) collective-permute-start(bf16[16,128,256]{2,1,0:T(8,128)(2,1)} %get-tuple-element.24), channel_id=1, source_target_pairs={{0,1},{1,0},{2,3},{3,2},{4,5},{5,4},{6,7},{7,6},{8,9},{9,8},{10,11... | collective-permute-start | bytes 3145736 | tf_op jit(solution)/shard_map/sum_over_col/ppermute | solution.py:29
  35.5 11.5 %collective-permute-start.3 = (bf16[4,128,256]{2,1,0:T(8,128)(2,1)S(1)}, bf16[4,128,256]{2,1,0:T(8,128)(2,1)S(1)}, u32[]{:S(2)}, u32[]{:S(2)}) collective-permute-start(bf16[4,128,256]{2,1,0:T(8,128)(2,1)S(1)} %get-tuple-element.46), channel_id=1, source_target_pairs={{0,6},{1,7},{2,0},{3,1},{4,2},{5,3},{6,4},{7,5},{8,14},{9,15},{10,... | collective-permute-start | bytes 786440 | tf_op jit(solution)/shard_map/sum_over_col/ppermute | solution.py:29
  38.9 11.2 %collective-permute-start.2 = (bf16[4,128,256]{2,1,0:T(8,128)(2,1)S(1)}, bf16[4,128,256]{2,1,0:T(8,128)(2,1)S(1)}, u32[]{:S(2)}, u32[]{:S(2)}) collective-permute-start(bf16[4,128,256]{2,1,0:T(8,128)(2,1)S(1)} %get-tuple-element.47), channel_id=1, source_target_pairs={{0,2},{1,3},{2,4},{3,5},{4,6},{5,7},{6,0},{7,1},{8,10},{9,11},{10,... | collective-permute-start | bytes 786440 | tf_op jit(solution)/shard_map/sum_over_col/ppermute | solution.py:29
  39.2 16.2 %collective-permute-start.1 = (bf16[4,128,256]{2,1,0:T(8,128)(2,1)S(1)}, bf16[4,128,256]{2,1,0:T(8,128)(2,1)S(1)}, u32[]{:S(2)}, u32[]{:S(2)}) collective-permute-start(bf16[4,128,256]{2,1,0:T(8,128)(2,1)S(1)} %get-tuple-element.48), channel_id=1, source_target_pairs={{0,4},{1,5},{2,6},{3,7},{4,0},{5,1},{6,2},{7,3},{8,12},{9,13},{10,... | collective-permute-start | bytes 786440 | tf_op jit(solution)/shard_map/sum_over_col/ppermute | solution.py:29
  45.5 17.3 %collective-permute-start.8 = (bf16[4,128,256]{2,1,0:T(8,128)(2,1)S(1)}, bf16[4,128,256]{2,1,0:T(8,128)(2,1)S(1)}, u32[]{:S(2)}, u32[]{:S(2)}) collective-permute-start(bf16[4,128,256]{2,1,0:T(8,128)(2,1)S(1)} %get-tuple-element.41), channel_id=1, source_target_pairs={{0,6},{1,7},{2,0},{3,1},{4,2},{5,3},{6,4},{7,5},{8,14},{9,15},{10,... | collective-permute-start | bytes 786440 | tf_op jit(solution)/shard_map/sum_over_col/ppermute | solution.py:29
  46.3 16.5 %collective-permute-start.7 = (bf16[4,128,256]{2,1,0:T(8,128)(2,1)S(1)}, bf16[4,128,256]{2,1,0:T(8,128)(2,1)S(1)}, u32[]{:S(2)}, u32[]{:S(2)}) collective-permute-start(bf16[4,128,256]{2,1,0:T(8,128)(2,1)S(1)} %get-tuple-element.42), channel_id=1, source_target_pairs={{0,2},{1,3},{2,4},{3,5},{4,6},{5,7},{6,0},{7,1},{8,10},{9,11},{10,... | collective-permute-start | bytes 786440 | tf_op jit(solution)/shard_map/sum_over_col/ppermute | solution.py:29
  47.1 19.6 %collective-permute-start.6 = (bf16[4,128,256]{2,1,0:T(8,128)(2,1)S(1)}, bf16[4,128,256]{2,1,0:T(8,128)(2,1)S(1)}, u32[]{:S(2)}, u32[]{:S(2)}) collective-permute-start(bf16[4,128,256]{2,1,0:T(8,128)(2,1)S(1)} %get-tuple-element.43), channel_id=1, source_target_pairs={{0,4},{1,5},{2,6},{3,7},{4,0},{5,1},{6,2},{7,3},{8,12},{9,13},{10,... | collective-permute-start | bytes 786440 | tf_op jit(solution)/shard_map/sum_over_col/ppermute | solution.py:29
  55.5 11.1 %collective-permute-start.9 = (bf16[2,128,256]{2,1,0:T(8,128)(2,1)S(1)}, bf16[2,128,256]{2,1,0:T(8,128)(2,1)S(1)}, u32[]{:S(2)}, u32[]{:S(2)}) collective-permute-start(bf16[2,128,256]{2,1,0:T(8,128)(2,1)S(1)} %get-tuple-element.51), channel_id=1, source_target_pairs={{0,8},{1,9},{2,10},{3,11},{4,12},{5,13},{6,14},{7,15},{8,16},{9,17... | collective-permute-start | bytes 393224 | tf_op jit(solution)/shard_map/sum_over_col/ppermute | solution.py:29
  59.0 13.6 %collective-permute-start.4 = (bf16[2,128,256]{2,1,0:T(8,128)(2,1)S(1)}, bf16[2,128,256]{2,1,0:T(8,128)(2,1)S(1)}, u32[]{:S(2)}, u32[]{:S(2)}) collective-permute-start(bf16[2,128,256]{2,1,0:T(8,128)(2,1)S(1)} %get-tuple-element.52), channel_id=1, source_target_pairs={{0,16},{1,17},{2,18},{3,19},{4,20},{5,21},{6,22},{7,23},{8,24},{9,... | collective-permute-start | bytes 393224 | tf_op jit(solution)/shard_map/sum_over_col/ppermute | solution.py:29
  66.6 11.0 %copy-start.10 = (bf16[2,128,256]{2,1,0:T(8,128)(2,1)}, bf16[2,128,256]{2,1,0:T(8,128)(2,1)S(1)}, u32[]{:S(2)}) copy-start(bf16[2,128,256]{2,1,0:T(8,128)(2,1)S(1)} %collective-permute-done.9) | copy-start | bytes 393220
  67.4 10.2 %collective-permute-start.10 = (bf16[2,128,256]{2,1,0:T(8,128)(2,1)S(1)}, bf16[2,128,256]{2,1,0:T(8,128)(2,1)S(1)}, u32[]{:S(2)}, u32[]{:S(2)}) collective-permute-start(bf16[2,128,256]{2,1,0:T(8,128)(2,1)S(1)} %get-tuple-element.50), channel_id=1, source_target_pairs={{0,24},{1,25},{2,26},{3,27},{4,28},{5,29},{6,30},{7,31},{8,0},{9,1... | collective-permute-start | bytes 393224 | tf_op jit(solution)/shard_map/sum_over_col/ppermute | solution.py:29
  72.6 5.1 %copy-start.11 = (bf16[2,128,256]{2,1,0:T(8,128)(2,1)}, bf16[2,128,256]{2,1,0:T(8,128)(2,1)S(1)}, u32[]{:S(2)}) copy-start(bf16[2,128,256]{2,1,0:T(8,128)(2,1)S(1)} %collective-permute-done.4) | copy-start | bytes 393220
  77.6 0.7 copy-start.12
  80.8 9.7 %collective-permute-start.13 = (bf16[256,256]{1,0:T(8,128)(2,1)}, bf16[256,256]{1,0:T(8,128)(2,1)S(1)}, u32[]{:S(2)}, u32[]{:S(2)}) collective-permute-start(bf16[256,256]{1,0:T(8,128)(2,1)} %get-tuple-element.31), channel_id=1, source_target_pairs={{0,24},{1,25},{2,26},{3,27},{4,28},{5,29},{6,30},{7,31},{8,0},{9,1... | collective-permute-start | bytes 393224 | tf_op jit(solution)/shard_map/gather_gradients/ppermute | solution.py:29
  83.0 12.1 %collective-permute-start.12 = (bf16[256,256]{1,0:T(8,128)(2,1)}, bf16[256,256]{1,0:T(8,128)(2,1)S(1)}, u32[]{:S(2)}, u32[]{:S(2)}) collective-permute-start(bf16[256,256]{1,0:T(8,128)(2,1)} %get-tuple-element.31), channel_id=1, source_target_pairs={{0,16},{1,17},{2,18},{3,19},{4,20},{5,21},{6,22},{7,23},{8,24},{9,... | collective-permute-start | bytes 393224 | tf_op jit(solution)/shard_map/gather_gradients/ppermute | solution.py:29
  86.4 9.1 %collective-permute-start.11 = (bf16[256,256]{1,0:T(8,128)(2,1)}, bf16[256,256]{1,0:T(8,128)(2,1)S(1)}, u32[]{:S(2)}, u32[]{:S(2)}) collective-permute-start(bf16[256,256]{1,0:T(8,128)(2,1)} %get-tuple-element.31), channel_id=1, source_target_pairs={{0,8},{1,9},{2,10},{3,11},{4,12},{5,13},{6,14},{7,15},{8,16},{9,17... | collective-permute-start | bytes 393224 | tf_op jit(solution)/shard_map/gather_gradients/ppermute | solution.py:29
  95.4 25.5 %all-to-all-start.2 = ((f32[32,8,384]{2,1,0:T(8,128)}), f32[32,8,384]{2,1,0:T(8,128)S(1)}, u32[]{:S(2)}, u32[]{:S(2)}) async-start(f32[32,8,384]{2,1,0:T(8,128)} %bitcast.26), calls=%async_computation.2 | async-start | bytes 786432 | tf_op jit(solution)/shard_map/sum_weight_grad/all_to_all | solution.py:268
  105.9 35.0 %copy-start.2 = (bf16[1024,256]{1,0:T(8,128)(2,1)}, bf16[1024,256]{1,0:T(8,128)(2,1)S(1)}, u32[]{:S(2)}) copy-start(bf16[1024,256]{1,0:T(8,128)(2,1)S(1)} %constant_dynamic-update-slice_fusion) | copy-start | bytes 1572868
  105.9 29.8 %collective-permute-start.16 = (bf16[1024,256]{1,0:T(8,128)(2,1)S(1)}, bf16[1024,256]{1,0:T(8,128)(2,1)S(1)}, u32[]{:S(2)}, u32[]{:S(2)}) collective-permute-start(bf16[1024,256]{1,0:T(8,128)(2,1)S(1)} %constant_dynamic-update-slice_fusion), channel_id=1, source_target_pairs={{0,6},{1,7},{2,0},{3,1},{4,2},{5,3},{6,4},{7,5},{8,14},{9,15},{10,... | collective-permute-start | bytes 1572872 | tf_op jit(solution)/shard_map/gather_gradients/ppermute | solution.py:29
  108.5 27.3 %collective-permute-start.15 = (bf16[1024,256]{1,0:T(8,128)(2,1)S(1)}, bf16[1024,256]{1,0:T(8,128)(2,1)S(1)}, u32[]{:S(2)}, u32[]{:S(2)}) collective-permute-start(bf16[1024,256]{1,0:T(8,128)(2,1)S(1)} %constant_dynamic-update-slice_fusion), channel_id=1, source_target_pairs={{0,4},{1,5},{2,6},{3,7},{4,0},{5,1},{6,2},{7,3},{8,12},{9,13},{10,... | collective-permute-start | bytes 1572872 | tf_op jit(solution)/shard_map/gather_gradients/ppermute | solution.py:29
  109.1 28.9 %collective-permute-start.14 = (bf16[1024,256]{1,0:T(8,128)(2,1)S(1)}, bf16[1024,256]{1,0:T(8,128)(2,1)S(1)}, u32[]{:S(2)}, u32[]{:S(2)}) collective-permute-start(bf16[1024,256]{1,0:T(8,128)(2,1)S(1)} %constant_dynamic-update-slice_fusion), channel_id=1, source_target_pairs={{0,2},{1,3},{2,4},{3,5},{4,6},{5,7},{6,0},{7,1},{8,10},{9,11},{10,... | collective-permute-start | bytes 1572872 | tf_op jit(solution)/shard_map/gather_gradients/ppermute | solution.py:29
  129.9 21.1 %all-to-all-start.4 = ((f32[32,8,384]{2,1,0:T(8,128)}), f32[32,8,384]{2,1,0:T(8,128)S(1)}, u32[]{:S(2)}, u32[]{:S(2)}) async-start(f32[32,8,384]{2,1,0:T(8,128)} %broadcast_in_dim.11), calls=%async_computation.4 | async-start | bytes 786432 | tf_op jit(solution)/shard_map/sum_weight_grad/all_to_all | solution.py:272
  135.2 3.3 %collective-permute-start.17 = (bf16[1024,256]{1,0:T(8,128)(2,1)S(1)}, bf16[1024,256]{1,0:T(8,128)(2,1)S(1)}, u32[]{:S(2)}, u32[]{:S(2)}) collective-permute-start(bf16[1024,256]{1,0:T(8,128)(2,1)S(1)} %constant_dynamic-update-slice_fusion), channel_id=1, source_target_pairs={{0,1},{1,0},{2,3},{3,2},{4,5},{5,4},{6,7},{7,6},{8,9},{9,8},{10,11... | collective-permute-start | bytes 1572872 | tf_op jit(solution)/shard_map/gather_gradients/ppermute | solution.py:29
  135.7 5.2 %copy-start.3 = (bf16[1024,256]{1,0:T(8,128)(2,1)}, bf16[1024,256]{1,0:T(8,128)(2,1)S(1)}, u32[]{:S(2)}) copy-start(bf16[1024,256]{1,0:T(8,128)(2,1)S(1)} %collective-permute-done.16) | copy-start | bytes 1572868
  135.7 2.9 %collective-permute-start.20 = (bf16[1024,256]{1,0:T(8,128)(2,1)S(1)}, bf16[1024,256]{1,0:T(8,128)(2,1)S(1)}, u32[]{:S(2)}, u32[]{:S(2)}) collective-permute-start(bf16[1024,256]{1,0:T(8,128)(2,1)S(1)} %collective-permute-done.16), channel_id=1, source_target_pairs={{0,1},{1,0},{2,3},{3,2},{4,5},{5,4},{6,7},{7,6},{8,9},{9,8},{10,11... | collective-permute-start | bytes 1572872 | tf_op jit(solution)/shard_map/gather_gradients/ppermute | solution.py:29
  135.8 5.1 %copy-start.4 = (bf16[1024,256]{1,0:T(8,128)(2,1)}, bf16[1024,256]{1,0:T(8,128)(2,1)S(1)}, u32[]{:S(2)}) copy-start(bf16[1024,256]{1,0:T(8,128)(2,1)S(1)} %collective-permute-done.15) | copy-start | bytes 1572868
  135.8 2.9 %collective-permute-start.19 = (bf16[1024,256]{1,0:T(8,128)(2,1)S(1)}, bf16[1024,256]{1,0:T(8,128)(2,1)S(1)}, u32[]{:S(2)}, u32[]{:S(2)}) collective-permute-start(bf16[1024,256]{1,0:T(8,128)(2,1)S(1)} %collective-permute-done.15), channel_id=1, source_target_pairs={{0,1},{1,0},{2,3},{3,2},{4,5},{5,4},{6,7},{7,6},{8,9},{9,8},{10,11... | collective-permute-start | bytes 1572872 | tf_op jit(solution)/shard_map/gather_gradients/ppermute | solution.py:29
  138.0 2.9 %copy-start.5 = (bf16[1024,256]{1,0:T(8,128)(2,1)}, bf16[1024,256]{1,0:T(8,128)(2,1)S(1)}, u32[]{:S(2)}) copy-start(bf16[1024,256]{1,0:T(8,128)(2,1)S(1)} %collective-permute-done.14) | copy-start | bytes 1572868
  138.0 2.0 %collective-permute-start.18 = (bf16[1024,256]{1,0:T(8,128)(2,1)S(1)}, bf16[1024,256]{1,0:T(8,128)(2,1)S(1)}, u32[]{:S(2)}, u32[]{:S(2)}) collective-permute-start(bf16[1024,256]{1,0:T(8,128)(2,1)S(1)} %collective-permute-done.14), channel_id=1, source_target_pairs={{0,1},{1,0},{2,3},{3,2},{4,5},{5,4},{6,7},{7,6},{8,9},{9,8},{10,11... | collective-permute-start | bytes 1572872 | tf_op jit(solution)/shard_map/gather_gradients/ppermute | solution.py:29
  138.5 2.4 %copy-start.6 = (bf16[1024,256]{1,0:T(8,128)(2,1)}, bf16[1024,256]{1,0:T(8,128)(2,1)S(1)}, u32[]{:S(2)}) copy-start(bf16[1024,256]{1,0:T(8,128)(2,1)S(1)} %collective-permute-done.17) | copy-start | bytes 1572868
  138.6 2.4 %copy-start.7 = (bf16[1024,256]{1,0:T(8,128)(2,1)}, bf16[1024,256]{1,0:T(8,128)(2,1)S(1)}, u32[]{:S(2)}) copy-start(bf16[1024,256]{1,0:T(8,128)(2,1)S(1)} %collective-permute-done.20) | copy-start | bytes 1572868
  138.7 2.2 %copy-start.8 = (bf16[1024,256]{1,0:T(8,128)(2,1)}, bf16[1024,256]{1,0:T(8,128)(2,1)S(1)}, u32[]{:S(2)}) copy-start(bf16[1024,256]{1,0:T(8,128)(2,1)S(1)} %collective-permute-done.19) | copy-start | bytes 1572868
  140.1 0.8 copy-start.9
  151.0 19.6 %all-to-all-start.1 = ((bf16[8,256,256]{2,1,0:T(8,128)(2,1)}), bf16[8,256,256]{2,1,0:T(8,128)(2,1)S(1)}, u32[]{:S(2)}, u32[]{:S(2)}) async-start(bf16[8,256,256]{2,1,0:T(8,128)(2,1)} %bitcast.22), calls=%async_computation.1 | async-start | bytes 2097152 | tf_op jit(solution)/shard_map/sum_over_row/all_to_all | solution.py:280
  170.7 1.0 copy-start

commit v3 on v2

--- a/solution.py
+++ b/solution.py
@@ -17,6 +17,14 @@
 GROUP = 24
 VMEM_LIMIT = 60 * 1024 * 1024
 LANES = 128
+
+
+def row_shift(value, dx, dzl):
+    pairs = []
+    for i in range(N_ROW):
+        x, zl = divmod(i, N_ZL)
+        pairs.append((i, (x + dx) % N_X * N_ZL + (zl ^ dzl)))
+    return lax.ppermute(value, "row", pairs)
 
 
 def col_shift(value, dzh=0, dy=0, dcore=0):
@@ -96,7 +104,7 @@
     width = sources[0].shape[-1]
     sources = [s.reshape(-1, tile, width) for s in sources]
     src_sizes = [s.shape[0] for s in sources]
-    anywhere = pl.BlockSpec(memory_space=pl.ANY)
+    anywhere = pl.BlockSpec(memory_space=pltpu.HBM)
     scalars = pl.BlockSpec(memory_space=pltpu.SMEM)
     return pl.pallas_call(
         functools.partial(tile_kernel, transposed, src_sizes, out_sizes),
@@ -133,13 +141,11 @@
     return dot(high, other) + dot(low, other)
 
 
-def middle_kernel(h0, h1, h2, h3, weight, bias, cotangent, out, grad, total_out, pre_out):
-    total = (
-        h0[...].astype(jnp.float32)
-        + h1[...].astype(jnp.float32)
-        + h2[...].astype(jnp.float32)
-        + h3[...].astype(jnp.float32)
-    )
+def middle_kernel(count, *refs):
+    weight, bias, cotangent, out, grad, total_out, pre_out = refs[count:]
+    total = refs[0][...].astype(jnp.float32)
+    for piece in refs[1:count]:
+        total += piece[...].astype(jnp.float32)
     shifted = split_dot(total, weight[...], (((1,), (0,)), ((), ()))) + bias[...]
     tanh_term = jnp.tanh(GELU_ROOT * (shifted + GELU_CUBIC * shifted * shifted * shifted))
     out[...] = (0.5 * shifted * (1.0 + tanh_term)).astype(jnp.bfloat16)
@@ -156,8 +162,8 @@
     rows, width = cotangent.shape
     vmem = pl.BlockSpec(memory_space=pltpu.VMEM)
     return pl.pallas_call(
-        middle_kernel,
-        in_specs=[vmem] * 7,
+        functools.partial(middle_kernel, len(pieces)),
+        in_specs=[vmem] * (len(pieces) + 3),
         out_specs=[vmem] * 4,
         out_shape=[jax.ShapeDtypeStruct((rows, width), jnp.bfloat16)] * 2
         + [jax.ShapeDtypeStruct((rows, width), jnp.float32)] * 2,
@@ -210,6 +216,35 @@
     )(pieces, weight)
 
 
+def spread_kernel(place, here, there, weight_grad, bias_grad):
+    width = weight_grad.shape[1]
+    chunk = weight_grad.shape[0] // N_COL
+    for core, rows in enumerate((here, there)):
+        for k in range(N_ZH * N_Y):
+            y, zh = divmod(k, N_ZH)
+            owner = (
+                ((place[0] + N_ZH - zh) % N_ZH * N_Y + (place[1] + N_Y - y) % N_Y) * N_CORE
+                + (place[2] + core) % N_CORE
+            )
+            put = pl.ds(pl.multiple_of(owner * chunk, chunk), chunk)
+            weight_grad[put, :] = rows[chunk * k : chunk * (k + 1), :width]
+            bias_grad[put, :] = rows[chunk * k : chunk * (k + 1), width:]
+
+
+def spread(place, here, there, width):
+    rows = here.shape[0] * N_CORE
+    vmem = pl.BlockSpec(memory_space=pltpu.VMEM)
+    return pl.pallas_call(
+        spread_kernel,
+        in_specs=[pl.BlockSpec(memory_space=pltpu.SMEM)] + [vmem] * 2,
+        out_specs=[vmem] * 2,
+        out_shape=[
+            jax.ShapeDtypeStruct((rows, width), jnp.float32),
+            jax.ShapeDtypeStruct((rows, here.shape[1] - width), jnp.float32),
+        ],
+    )(place, here, there)
+
+
 def merge(pieces):
     return sum((p.astype(jnp.float32) for p in pieces[1:]), pieces[0].astype(jnp.float32)).astype(
         jnp.bfloat16
@@ -221,41 +256,46 @@
     tile = adjacency.shape[2]
     scale = 1.0 / math.sqrt(vertices * N_ROW * N_COL)
     live = live_tiles.reshape(1)
-    col_id = lax.axis_index("col")
+    row_id, col_id = lax.axis_index("row"), lax.axis_index("col")
+    my_x, my_zl = row_id // N_ZL, row_id % N_ZL
     my_zh, my_y, my_core = col_id // 8, col_id // 2 % 4, col_id % 2
 
     per = vertices // tile
     r, c = tile_rows[0], tile_cols[0]
-    rc = r // per
+    rc, cc = r // per, c // per
+    c_x, c_zl = cc // 2, cc % 2
     r_zh, r_y, r_core = rc // 8, rc // 2 % 4, rc % 2
     half = (r_core ^ my_core) * 16
     ahead = (r_zh - my_zh) & 3
     part = ((ahead == 3) | (ahead == 0)).astype(jnp.int32)
     place = ((ahead == 1) | (ahead == 0)).astype(jnp.int32)
     put_rows = (half + part * 8 + ((r_y - my_y) & 3) * 2 + place) * per + r % per
+    take_cols = (((my_x - c_x) & 3) * 2 + (c_zl ^ my_zl)) * per + c % per
     take_rows = (half + ((my_y - r_y) & 3) * 4 + ((my_zh - r_zh) & 3)) * per + r % per
 
+    moves = [(dx, dzl) for dx in range(N_X) for dzl in range(N_ZL)]
     with jax.named_scope("gather_features"):
-        copies = jnp.broadcast_to(features, (N_ROW,) + features.shape)
-        source = lax.all_to_all(copies, "row", 0, 0, tiled=True)
+        sources = [features] + [row_shift(features, *m) for m in moves[1:]]
     with jax.named_scope("tiles_forward"):
         parts = tile_sum(
-            adjacency, live, c, put_rows, [source], [8 * per] * 4, False
+            adjacency, live, take_cols, put_rows, sources, [8 * per] * 4, False
         )
     with jax.named_scope("sum_over_col"):
-        sums, pieces = [], []
-        for keep, send in zip(parts[:2], parts[2:]):
-            other = col_shift(send, dcore=1)
-            cut = [slice(2 * per * k, 2 * per * (k + 1)) for k in range(N_Y)]
-            added = [merge([keep[s], other[s]]) for s in cut]
-            arrived = [added[0]] + [col_shift(added[k], dy=k) for k in (2, 1, 3)]
-            if pieces:
-                *arrived, pieces[1] = lax.optimization_barrier((*arrived, pieces[1]))
-            sums = [merge([p[:per] for p in arrived]), merge([p[per:] for p in arrived])]
-            if not pieces:
-                pieces = [col_shift(sums[0], dzh=2), col_shift(sums[1], dzh=1)]
-            else:
-                pieces += [col_shift(sums[0], dzh=3), sums[1]]
+        others = [col_shift(send, dcore=1) for send in parts[2:]]
+
+        def over_y(part, first, size):
+            added = []
+            for k in range(N_Y):
+                rows = slice(2 * per * k + first * per, 2 * per * k + (first + size) * per)
+                added.append(merge([parts[part][rows], others[part][rows]]))
+            return [added[0]] + [col_shift(added[k], dy=k) for k in (2, 1, 3)]
+
+        both = over_y(0, 0, 2)
+        far = col_shift(merge([p[:per] for p in both]), dzh=2)
+        near = col_shift(merge([p[per:] for p in both]), dzh=1)
+        back = over_y(1, 0, 1)
+        *back, near = lax.optimization_barrier((*back, near))
+        pieces = over_y(1, 1, 1) + [far, near, col_shift(merge(back), dzh=3)]
         pieces = [p.reshape(vertices, width) for p in pieces]
     with jax.named_scope("pointwise"):
         layer_out, grad, total, pre_grad = middle(pieces, weight, bias, cotangent)
@@ -268,20 +308,21 @@
         load = jnp.sum(lax.all_to_all(load, "col", 0, 0, tiled=True), axis=0)
         load = jnp.broadcast_to(load, (N_ROW,) + load.shape)
         load = jnp.sum(lax.all_to_all(load, "row", 0, 0, tiled=True), axis=0) * scale
-        load = jnp.broadcast_to(load, (N_COL,) + load.shape)
-        load = lax.all_to_all(load, "col", 0, 0, tiled=True).reshape(width, -1)
-        weight_grad, bias_grad = load[:, :width], load[:, width]
     with jax.named_scope("gather_gradients"):
         here += [col_shift(here[0], dy=k) for k in range(1, N_Y)]
         there = [col_shift(p, dcore=1) for p in here]
     with jax.named_scope("tiles_backward"):
         (back,) = tile_sum(adjacency, live, take_rows, c, here + there, [N_ROW * per], True)
     with jax.named_scope("sum_over_row"):
-        back = lax.all_to_all(
-            back.reshape(N_ROW, vertices, width), "row", 0, 0, tiled=True
-        )
+        back = back.reshape(N_ROW, vertices, width)
+        back = lax.all_to_all(back, "row", 0, 0, tiled=True)
         features_grad = last(back, weight)
-    return layer_out, features_grad, weight_grad, bias_grad
+    with jax.named_scope("sum_weight_grad"):
+        load = jnp.concatenate([load] + [col_shift(load, dzh=k) for k in range(1, N_ZH)])
+        load = jnp.concatenate([load] + [col_shift(load, dy=k) for k in range(1, N_Y)])
+        place = jnp.stack([my_zh, my_y, my_core]).astype(jnp.int32)
+        weight_grad, bias_grad = spread(place, load, col_shift(load, dcore=1), width)
+    return layer_out, features_grad, weight_grad, bias_grad[:, 0]
 
 
 def solution(mesh):

time: 174 us -> 182 us (1.046)
  starting transfers between devices: 63.3 us -> 76.1 us
  blocking collectives: 8.12 us -> 0 us
  Pallas kernels: 16.8 us -> 22.6 us
  waiting for transfers between devices: 69 us -> 66.8 us
    ppermute x21 -> x31, waiting for transfers between devices: 26.7 us -> 59.5 us  [col_shift(): return lax.ppermute(value, 'col', pairs)]
    all_to_all x3 -> x2, waiting for transfers between devices: 31.1 us -> 0.01 us  [the longest x1 0.01 us: shards(): lax.all_to_all(load, 'row', 0, 0, tiled=True)]
    all_to_all x1, waiting for transfers between devices: 11.2 us -> 0.07 us  [shards(): load = jnp.sum(lax.all_to_all(load, 'col', 0, 0, tiled=True), axis=0)]
    ppermute x0 -> x7, starting transfers between devices: none -> 10 us  [row_shift(): return lax.ppermute(value, 'row', pairs)]
    all_to_all x1 -> x0, blocking collectives: 8.12 us -> none  [shards(): lax.all_to_all(load, 'row', 0, 0, tiled=True)]
    ppermute x0 -> x7, waiting for transfers between devices: none -> 7.27 us  [row_shift(): return lax.ppermute(value, 'row', pairs)]
    ppermute x21 -> x31, starting transfers between devices: 38.8 us -> 45.2 us  [col_shift(): return lax.ppermute(value, 'col', pairs)]
    all_to_all x3 -> x2, starting transfers between devices: 15 us -> 11.1 us  [the longest x1 7.3 us: shards(): back = lax.all_to_all(back, 'row', 0, 0, tiled=True)]
  transfers between devices with their start and end apart: 25 -> 41, of which waited for: 14 -> 18; matrix products, arithmetic and copies ran while one was open for 6% -> 6% of each run, Pallas kernels for 4% -> 6%
where the time goes in v3:
time: 182 us; the launch traced here: 181 us
  starting transfers between devices  76.1 us (42%)
  waiting for transfers between devices  66.8 us (37%)
  Pallas kernels  22.6 us (12%)
  other arithmetic  7.23 us (4%)
  local copies, waits for them, and re-layouts  7.13 us (4%)
    ppermute x31, waiting for transfers between devices, col_shift(): return lax.ppermute(value, 'col', pairs)  59.5 us
    ppermute x31, starting transfers between devices, col_shift(): return lax.ppermute(value, 'col', pairs)  45.2 us
    pallas_call x2, Pallas kernels, tile_sum(): pl.pallas_call(functools.partial(tile_kernel, transposed, src_sizes, out_...  13.8 us
    ppermute x7, starting transfers between devices, row_shift(): return lax.ppermute(value, 'row', pairs)  10 us
    all_to_all x1, starting transfers between devices, shards(): load = jnp.sum(lax.all_to_all(load, 'col', 0, 0, tiled=True), axis=0)  9.71 us
    all_to_all x1, starting transfers between devices, shards(): back = lax.all_to_all(back, 'row', 0, 0, tiled=True)  7.3 us
    ppermute x7, waiting for transfers between devices, row_shift(): return lax.ppermute(value, 'row', pairs)  7.27 us
    unnamed x52, local copies, waits for them, and re-layouts  4.89 us
  transfers between devices with their start and end apart: 41, of which 18 were waited for; matrix products, arithmetic and copies ran while one was open for 6% of the time, Pallas kernels for 6%

profile of v3, /device:TPU:1, one launch (start us, length us, event | category | flops | bytes accessed | tf_op | source)
XLA Modules:
  0.0 181.5 jit_solution(12387355463402408731)
XLA Ops:
  0.6 5.0 %collective-permute-start.4 = (bf16[256,256]{1,0:T(8,128)(2,1)}, bf16[256,256]{1,0:T(8,128)(2,1)S(1)}, u32[]{:S(2)}, u32[]{:S(2)}) collective-permute-start(bf16[256,256]{1,0:T(8,128)(2,1)} %param.8), channel_id=1, source_target_pairs={{0,160},{32,128},{64,224},{96,192},{128,32},{160,0},{192,96},{224,... | collective-permute-start | bytes 393224 | tf_op jit(solution)/shard_map/gather_features/ppermute | solution.py:27
  6.6 1.2 collective-permute-start.1
  7.8 1.6 collective-permute-start
  10.1 1.3 multiply_add_fusion
  11.4 1.2 collective-permute-start.6
  12.6 3.8 %collective-permute-done.3 = bf16[256,256]{1,0:T(8,128)(2,1)S(1)} collective-permute-done((bf16[256,256]{1,0:T(8,128)(2,1)}, bf16[256,256]{1,0:T(8,128)(2,1)S(1)}, u32[]{:S(2)}, u32[]{:S(2)}) %collective-permute-start.3) | collective-permute-done | bytes 131104 | tf_op jit(solution)/shard_map/gather_features/ppermute | solution.py:27
  16.4 1.4 fusion.2
  17.8 1.7 collective-permute-done.1
  19.5 1.8 collective-permute-done.5
  21.9 6.9 %tiles_forward.1 = (bf16[16,128,256]{2,1,0:T(8,128)(2,1)}, bf16[16,128,256]{2,1,0:T(8,128)(2,1)}, bf16[16,128,256]{2,1,0:T(8,128)(2,1)}, bf16[16,128,256]{2,1,0:T(8,128)(2,1)}) custom-call(s32[1]{0:T(128)} %bitcast.32.live, s32[192]{0:T(256)} %get-tuple-element.61.take, s32[192]{0:T(256)} %get-tuple-element.62.put, bf16[1,192,128,128]{3,2,1,0:T(8,128)(2,1)} %tiles.3, ...), custom_call_target="tpu_custom_call" | custom-call | flops 1610612736 | bytes 6291456 | tf_op jit(solution)/shard_map/tiles_forward/pallas_call | solution.py:109
  28.8 3.8 %collective-permute-start.11 = (bf16[16,128,256]{2,1,0:T(8,128)(2,1)}, bf16[16,128,256]{2,1,0:T(8,128)(2,1)S(1)}, u32[]{:S(2)}, u32[]{:S(2)}) collective-permute-start(bf16[16,128,256]{2,1,0:T(8,128)(2,1)} %get-tuple-element.26), channel_id=1, source_target_pairs={{0,1},{1,0},{2,3},{3,2},{4,5},{5,4},{6,7},{7,6},{8,9},{9,8},{10,11... | collective-permute-start | bytes 3145736 | tf_op jit(solution)/shard_map/sum_over_col/ppermute | solution.py:37
  32.7 2.4 %collective-permute-done.11 = bf16[16,128,256]{2,1,0:T(8,128)(2,1)S(1)} collective-permute-done((bf16[16,128,256]{2,1,0:T(8,128)(2,1)}, bf16[16,128,256]{2,1,0:T(8,128)(2,1)S(1)}, u32[]{:S(2)}, u32[]{:S(2)}) %collective-permute-start.11) | collective-permute-done | bytes 1048608 | tf_op jit(solution)/shard_map/sum_over_col/ppermute | solution.py:37
  35.1 1.5 add_convert_fusion.3
  36.7 1.5 collective-permute-start.13
  38.8 2.3 %add_convert_fusion.6 = (bf16[2,128,256]{2,1,0:T(8,128)(2,1)S(1)}, bf16[2,128,256]{2,1,0:T(8,128)(2,1)S(1)}, bf16[2,128,256]{2,1,0:T(8,128)(2,1)S(1)}, bf16[2,12...) fusion(bf16[16,128,256]{2,1,0:T(8,128)(2,1)S(1)} %collective-pe, ...), kind=kLoop, calls=%fused_computation.6 | loop fusion | flops 2097152 | bytes 3145728 | tf_op jit(solution)/shard_map/sum_over_col/convert_element_type | solution.py:249
  41.1 1.8 collective-permute-start.18
  42.8 1.4 collective-permute-done.14
  44.9 1.7 collective-permute-done.13
  46.5 3.6 %collective-permute-done.12 = bf16[4,128,256]{2,1,0:T(8,128)(2,1)S(1)} collective-permute-done((bf16[4,128,256]{2,1,0:T(8,128)(2,1)S(1)}, bf16[4,128,256]{2,1,0:T(8,128)(2,1)S(1)}, u32[]{:S(2)}, u32[]{:S(2)}) %collective-permute-start.12) | collective-permute-done | bytes 262176 | tf_op jit(solution)/shard_map/sum_over_col/ppermute | solution.py:37
  50.3 5.6 %collective-permute-start.19 = (bf16[2,128,256]{2,1,0:T(8,128)(2,1)S(1)}, bf16[2,128,256]{2,1,0:T(8,128)(2,1)S(1)}, u32[]{:S(2)}, u32[]{:S(2)}) collective-permute-start(bf16[2,128,256]{2,1,0:T(8,128)(2,1)S(1)} %get-tuple-element.57), channel_id=1, source_target_pairs={{0,8},{1,9},{2,10},{3,11},{4,12},{5,13},{6,14},{7,15},{8,16},{9,17... | collective-permute-start | bytes 393224 | tf_op jit(solution)/shard_map/sum_over_col/ppermute | solution.py:37
  55.9 1.5 collective-permute-start.9
  57.7 6.5 %collective-permute-start.15 = (bf16[2,128,256]{2,1,0:T(8,128)(2,1)S(1)}, bf16[2,128,256]{2,1,0:T(8,128)(2,1)S(1)}, u32[]{:S(2)}, u32[]{:S(2)}) collective-permute-start(bf16[2,128,256]{2,1,0:T(8,128)(2,1)S(1)} %get-tuple-element.58), channel_id=1, source_target_pairs={{0,16},{1,17},{2,18},{3,19},{4,20},{5,21},{6,22},{7,23},{8,24},{9,... | collective-permute-start | bytes 393224 | tf_op jit(solution)/shard_map/sum_over_col/ppermute | solution.py:37
  64.9 4.2 %collective-permute-done.15 = bf16[2,128,256]{2,1,0:T(8,128)(2,1)S(1)} collective-permute-done((bf16[2,128,256]{2,1,0:T(8,128)(2,1)S(1)}, bf16[2,128,256]{2,1,0:T(8,128)(2,1)S(1)}, u32[]{:S(2)}, u32[]{:S(2)}) %collective-permute-start.15) | collective-permute-done | bytes 131104 | tf_op jit(solution)/shard_map/sum_over_col/ppermute | solution.py:37
  69.1 7.7 %collective-permute-done.20 = bf16[2,128,256]{2,1,0:T(8,128)(2,1)S(1)} collective-permute-done((bf16[2,128,256]{2,1,0:T(8,128)(2,1)S(1)}, bf16[2,128,256]{2,1,0:T(8,128)(2,1)S(1)}, u32[]{:S(2)}, u32[]{:S(2)}) %collective-permute-start.20) | collective-permute-done | bytes 131104 | tf_op jit(solution)/shard_map/sum_over_col/ppermute | solution.py:37
  77.4 2.6 %pointwise.1 = (bf16[256,256]{1,0:T(8,128)(2,1)}, bf16[256,256]{1,0:T(8,128)(2,1)}, f32[256,256]{1,0:T(8,128)}, f32[256,256]{1,0:T(8,128)}) custom-call(bf16[256,256]{1,0:T(8,128)(2,1)} %bitcast.42, bf16[256,256]{1,0:T(8,128)(2,1)} %bitcast.54, bf16[256,256]{1,0:T(8,128)(2,1)} %bitcast.53, bf16[256,256]{1,0:T(8,128)(2,1)} %bitcast.52, ...), custom_call_target="tpu_custom_call" | custom-call | tf_op jit(solution)/shard_map/pointwise/pallas_call | solution.py:164
  80.0 2.5 %collective-permute-start.23 = (bf16[256,256]{1,0:T(8,128)(2,1)}, bf16[256,256]{1,0:T(8,128)(2,1)S(1)}, u32[]{:S(2)}, u32[]{:S(2)}) collective-permute-start(bf16[256,256]{1,0:T(8,128)(2,1)} %get-tuple-element.33), channel_id=1, source_target_pairs={{0,24},{1,25},{2,26},{3,27},{4,28},{5,29},{6,30},{7,31},{8,0},{9,1... | collective-permute-start | bytes 393224 | tf_op jit(solution)/shard_map/gather_gradients/ppermute | solution.py:37
  82.5 1.9 %collective-permute-start.22 = (bf16[256,256]{1,0:T(8,128)(2,1)}, bf16[256,256]{1,0:T(8,128)(2,1)S(1)}, u32[]{:S(2)}, u32[]{:S(2)}) collective-permute-start(bf16[256,256]{1,0:T(8,128)(2,1)} %get-tuple-element.33), channel_id=1, source_target_pairs={{0,16},{1,17},{2,18},{3,19},{4,20},{5,21},{6,22},{7,23},{8,24},{9,... | collective-permute-start | bytes 393224 | tf_op jit(solution)/shard_map/gather_gradients/ppermute | solution.py:37
  84.8 2.1 %gather_gradients.1 = f32[256,384]{1,0:T(8,128)} custom-call(f32[256,256]{1,0:T(8,128)} %get-tuple-element.34.total, f32[256,256]{1,0:T(8,128)} %get-tuple-element.35.pre_grad), custom_call_target="tpu_custom_call" | custom-call | tf_op jit(solution)/shard_map/gather_gradients/pallas_call | solution.py:186
  88.8 2.7 %collective-permute-done.22 = bf16[256,256]{1,0:T(8,128)(2,1)S(1)} collective-permute-done((bf16[256,256]{1,0:T(8,128)(2,1)}, bf16[256,256]{1,0:T(8,128)(2,1)S(1)}, u32[]{:S(2)}, u32[]{:S(2)}) %collective-permute-start.22) | collective-permute-done | bytes 131104 | tf_op jit(solution)/shard_map/gather_gradients/ppermute | solution.py:37
  91.5 5.2 %collective-permute-done.21 = bf16[256,256]{1,0:T(8,128)(2,1)S(1)} collective-permute-done((bf16[256,256]{1,0:T(8,128)(2,1)}, bf16[256,256]{1,0:T(8,128)(2,1)S(1)}, u32[]{:S(2)}, u32[]{:S(2)}) %collective-permute-start.21) | collective-permute-done | bytes 131104 | tf_op jit(solution)/shard_map/gather_gradients/ppermute | solution.py:37
  98.3 9.7 %all-to-all-start.1 = ((f32[32,8,384]{2,1,0:T(8,128)}), f32[32,8,384]{2,1,0:T(8,128)S(1)}, u32[]{:S(2)}, u32[]{:S(2)}) async-start(f32[32,8,384]{2,1,0:T(8,128)} %bitcast.35), calls=%async_computation.1 | async-start | bytes 786432 | tf_op jit(solution)/shard_map/sum_weight_grad/all_to_all | solution.py:308
  108.4 1.3 collective-permute-done.26
  109.6 2.8 %collective-permute-start.30 = (bf16[1024,256]{1,0:T(8,128)(2,1)S(1)}, bf16[1024,256]{1,0:T(8,128)(2,1)S(1)}, u32[]{:S(2)}, u32[]{:S(2)}) collective-permute-start(bf16[1024,256]{1,0:T(8,128)(2,1)S(1)} %collective-permute-done.26), channel_id=1, source_target_pairs={{0,1},{1,0},{2,3},{3,2},{4,5},{5,4},{6,7},{7,6},{8,9},{9,8},{10,11... | collective-permute-start | bytes 1572872 | tf_op jit(solution)/shard_map/gather_gradients/ppermute | solution.py:37
  112.4 1.6 collective-permute-start.29
  114.0 12.9 %collective-permute-done.24 = bf16[1024,256]{1,0:T(8,128)(2,1)S(1)} collective-permute-done((bf16[1024,256]{1,0:T(8,128)(2,1)S(1)}, bf16[1024,256]{1,0:T(8,128)(2,1)S(1)}, u32[]{:S(2)}, u32[]{:S(2)}) %collective-permute-start.24) | collective-permute-done | bytes 524320 | tf_op jit(solution)/shard_map/gather_gradients/ppermute | solution.py:37
  128.3 3.8 %all-to-all-start.2 = ((f32[8,8,384]{2,1,0:T(8,128)}), f32[8,8,384]{2,1,0:T(8,128)S(1)}, u32[]{:S(2)}, u32[]{:S(2)}) async-start(f32[8,8,384]{2,1,0:T(8,128)} %broadcast_in_dim.3), calls=%async_computation.2 | async-start | bytes 196608 | tf_op jit(solution)/shard_map/sum_weight_grad/all_to_all | solution.py:310
  133.2 6.9 %tiles_backward.1 = bf16[16,128,256]{2,1,0:T(8,128)(2,1)} custom-call(s32[1]{0:T(128)} %bitcast.33.live, s32[192]{0:T(256)} %get-tuple-element.42.take, s32[192]{0:T(256)} %bitcast.58, bf16[1,192,128,128]{3,2,1,0:T(8,128)(2,1)} %tiles.3, bf16[8,128,256]{2,1,0:T(8,128)(2,1)} %bitcast.36, bf16[8,128,256]{2,1,0:T(8,128)(2,1)} %bitcast.39, ...), custom_call_target="tpu_custom_call" | custom-call | flops 1610612736 | bytes 6291456 | tf_op jit(solution)/shard_map/tiles_backward/pallas_call | solution.py:109
  140.1 7.3 %all-to-all-start = ((bf16[8,256,256]{2,1,0:T(8,128)(2,1)}), bf16[8,256,256]{2,1,0:T(8,128)(2,1)S(1)}, u32[]{:S(2)}, u32[]{:S(2)}) async-start(bf16[8,256,256]{2,1,0:T(8,128)(2,1)} %bitcast.34), calls=%async_computation | async-start | bytes 2097152 | tf_op jit(solution)/shard_map/sum_over_row/all_to_all | solution.py:318
  147.4 2.2 %collective-permute-start.33 = (f32[8,384]{1,0:T(8,128)S(1)}, f32[8,384]{1,0:T(8,128)S(1)}, u32[]{:S(2)}, u32[]{:S(2)}) collective-permute-start(f32[8,384]{1,0:T(8,128)S(1)} %get-tuple-element.59), channel_id=1, source_target_pairs={{0,24},{1,25},{2,26},{3,27},{4,28},{5,29},{6,30},{7,31},{8,0},{9,1... | collective-permute-start | bytes 36872 | tf_op jit(solution)/shard_map/sum_weight_grad/ppermute | solution.py:37
  149.7 2.1 %collective-permute-start.32 = (f32[8,384]{1,0:T(8,128)S(1)}, f32[8,384]{1,0:T(8,128)S(1)}, u32[]{:S(2)}, u32[]{:S(2)}) collective-permute-start(f32[8,384]{1,0:T(8,128)S(1)} %get-tuple-element.59), channel_id=1, source_target_pairs={{0,16},{1,17},{2,18},{3,19},{4,20},{5,21},{6,22},{7,23},{8,24},{9,... | collective-permute-start | bytes 36872 | tf_op jit(solution)/shard_map/sum_weight_grad/ppermute | solution.py:37
  151.8 2.3 %collective-permute-start.31 = (f32[8,384]{1,0:T(8,128)S(1)}, f32[8,384]{1,0:T(8,128)S(1)}, u32[]{:S(2)}, u32[]{:S(2)}) collective-permute-start(f32[8,384]{1,0:T(8,128)S(1)} %get-tuple-element.59), channel_id=1, source_target_pairs={{0,8},{1,9},{2,10},{3,11},{4,12},{5,13},{6,14},{7,15},{8,16},{9,17... | collective-permute-start | bytes 36872 | tf_op jit(solution)/shard_map/sum_weight_grad/ppermute | solution.py:37
  154.0 10.7 %collective-permute-done.32 = f32[8,384]{1,0:T(8,128)S(1)} collective-permute-done((f32[8,384]{1,0:T(8,128)S(1)}, f32[8,384]{1,0:T(8,128)S(1)}, u32[]{:S(2)}, u32[]{:S(2)}) %collective-permute-start.32) | collective-permute-done | bytes 12320 | tf_op jit(solution)/shard_map/sum_weight_grad/ppermute | solution.py:37
  166.3 4.2 %collective-permute-done.34 = f32[32,384]{1,0:T(8,128)S(1)} collective-permute-done((f32[32,384]{1,0:T(8,128)S(1)}, f32[32,384]{1,0:T(8,128)S(1)}, u32[]{:S(2)}, u32[]{:S(2)}) %collective-permute-start.34) | collective-permute-done | bytes 49184 | tf_op jit(solution)/shard_map/sum_weight_grad/ppermute | solution.py:37
  170.6 2.5 %collective-permute-start.37 = (f32[128,384]{1,0:T(8,128)S(1)}, f32[128,384]{1,0:T(8,128)S(1)}, u32[]{:S(2)}, u32[]{:S(2)}) collective-permute-start(f32[128,384]{1,0:T(8,128)S(1)} %constant_dynamic-update-slice_fusion.4.here), channel_id=1, source_target_pairs={{0,1},{1,0},{2,3},{3,2},{4,5},{5,4},{6,7},{7,6},{8,9},{9,8},{10,11... | collective-permute-start | bytes 589832 | tf_op jit(solution)/shard_map/sum_weight_grad/ppermute | solution.py:37
  174.8 1.9 %sum_weight_grad.1 = (f32[256,256]{1,0:T(8,128)}, f32[256,128]{1,0:T(8,128)}) custom-call(s32[3]{0:T(128)} %pad_add_fusion.place, f32[128,384]{1,0:T(8,128)} %copy-done.7, f32[128,384]{1,0:T(8,128)} %copy-done.8), custom_call_target="tpu_custom_call" | custom-call | tf_op jit(solution)/shard_map/sum_weight_grad/pallas_call | solution.py:237
  176.7 1.6 slice_reduce_fusion
  178.3 1.0 copy-done
  179.3 2.2 %sum_over_row.1 = bf16[256,256]{1,0:T(8,128)(2,1)} custom-call(bf16[8,256,256]{2,1,0:T(8,128)(2,1)} %copy-done, bf16[256,256]{1,0:T(8,128)(2,1)} %weight.1), custom_call_target="tpu_custom_call" | custom-call | tf_op jit(solution)/shard_map/sum_over_row/pallas_call | solution.py:210
  (107 shorter events, 14.6 us)
Async XLA Ops:
  0.6 10.8 %collective-permute-start.4 = (bf16[256,256]{1,0:T(8,128)(2,1)}, bf16[256,256]{1,0:T(8,128)(2,1)S(1)}, u32[]{:S(2)}, u32[]{:S(2)}) collective-permute-start(bf16[256,256]{1,0:T(8,128)(2,1)} %param.8), channel_id=1, source_target_pairs={{0,160},{32,128},{64,224},{96,192},{128,32},{160,0},{192,96},{224,... | collective-permute-start | bytes 393224 | tf_op jit(solution)/shard_map/gather_features/ppermute | solution.py:27
  5.6 10.8 %collective-permute-start.3 = (bf16[256,256]{1,0:T(8,128)(2,1)}, bf16[256,256]{1,0:T(8,128)(2,1)S(1)}, u32[]{:S(2)}, u32[]{:S(2)}) collective-permute-start(bf16[256,256]{1,0:T(8,128)(2,1)} %param.8), channel_id=1, source_target_pairs={{0,128},{32,160},{64,192},{96,224},{128,0},{160,32},{192,64},{224,... | collective-permute-start | bytes 393224 | tf_op jit(solution)/shard_map/gather_features/ppermute | solution.py:27
  5.9 11.9 %collective-permute-start.2 = (bf16[256,256]{1,0:T(8,128)(2,1)}, bf16[256,256]{1,0:T(8,128)(2,1)S(1)}, u32[]{:S(2)}, u32[]{:S(2)}) collective-permute-start(bf16[256,256]{1,0:T(8,128)(2,1)} %param.8), channel_id=1, source_target_pairs={{0,96},{32,64},{64,160},{96,128},{128,224},{160,192},{192,32},{224... | collective-permute-start | bytes 393224 | tf_op jit(solution)/shard_map/gather_features/ppermute | solution.py:27
  6.6 12.8 %collective-permute-start.1 = (bf16[256,256]{1,0:T(8,128)(2,1)}, bf16[256,256]{1,0:T(8,128)(2,1)S(1)}, u32[]{:S(2)}, u32[]{:S(2)}) collective-permute-start(bf16[256,256]{1,0:T(8,128)(2,1)} %param.8), channel_id=1, source_target_pairs={{0,64},{32,96},{64,128},{96,160},{128,192},{160,224},{192,0},{224,... | collective-permute-start | bytes 393224 | tf_op jit(solution)/shard_map/gather_features/ppermute | solution.py:27
  7.8 11.6 %collective-permute-start = (bf16[256,256]{1,0:T(8,128)(2,1)}, bf16[256,256]{1,0:T(8,128)(2,1)S(1)}, u32[]{:S(2)}, u32[]{:S(2)}) collective-permute-start(bf16[256,256]{1,0:T(8,128)(2,1)} %param.8), channel_id=1, source_target_pairs={{0,32},{32,0},{64,96},{96,64},{128,160},{160,128},{192,224},{224,1... | collective-permute-start | bytes 393224 | tf_op jit(solution)/shard_map/gather_features/ppermute | solution.py:27
  11.4 8.1 %collective-permute-start.6 = (bf16[256,256]{1,0:T(8,128)(2,1)}, bf16[256,256]{1,0:T(8,128)(2,1)S(1)}, u32[]{:S(2)}, u32[]{:S(2)}) collective-permute-start(bf16[256,256]{1,0:T(8,128)(2,1)} %param.8), channel_id=1, source_target_pairs={{0,224},{32,192},{64,32},{96,0},{128,96},{160,64},{192,160},{224,1... | collective-permute-start | bytes 393224 | tf_op jit(solution)/shard_map/gather_features/ppermute | solution.py:27
  16.4 4.8 %collective-permute-start.5 = (bf16[256,256]{1,0:T(8,128)(2,1)}, bf16[256,256]{1,0:T(8,128)(2,1)S(1)}, u32[]{:S(2)}, u32[]{:S(2)}) collective-permute-start(bf16[256,256]{1,0:T(8,128)(2,1)} %param.8), channel_id=1, source_target_pairs={{0,192},{32,224},{64,0},{96,32},{128,64},{160,96},{192,128},{224,1... | collective-permute-start | bytes 393224 | tf_op jit(solution)/shard_map/gather_features/ppermute | solution.py:27
  28.8 6.3 %collective-permute-start.11 = (bf16[16,128,256]{2,1,0:T(8,128)(2,1)}, bf16[16,128,256]{2,1,0:T(8,128)(2,1)S(1)}, u32[]{:S(2)}, u32[]{:S(2)}) collective-permute-start(bf16[16,128,256]{2,1,0:T(8,128)(2,1)} %get-tuple-element.26), channel_id=1, source_target_pairs={{0,1},{1,0},{2,3},{3,2},{4,5},{5,4},{6,7},{7,6},{8,9},{9,8},{10,11... | collective-permute-start | bytes 3145736 | tf_op jit(solution)/shard_map/sum_over_col/ppermute | solution.py:37
  32.6 6.2 %collective-permute-start.7 = (bf16[16,128,256]{2,1,0:T(8,128)(2,1)}, bf16[16,128,256]{2,1,0:T(8,128)(2,1)S(1)}, u32[]{:S(2)}, u32[]{:S(2)}) collective-permute-start(bf16[16,128,256]{2,1,0:T(8,128)(2,1)} %get-tuple-element.24), channel_id=1, source_target_pairs={{0,1},{1,0},{2,3},{3,2},{4,5},{5,4},{6,7},{7,6},{8,9},{9,8},{10,11... | collective-permute-start | bytes 3145736 | tf_op jit(solution)/shard_map/sum_over_col/ppermute | solution.py:37
  36.6 7.6 %collective-permute-start.14 = (bf16[4,128,256]{2,1,0:T(8,128)(2,1)S(1)}, bf16[4,128,256]{2,1,0:T(8,128)(2,1)S(1)}, u32[]{:S(2)}, u32[]{:S(2)}) collective-permute-start(bf16[4,128,256]{2,1,0:T(8,128)(2,1)S(1)} %get-tuple-element.54), channel_id=1, source_target_pairs={{0,6},{1,7},{2,0},{3,1},{4,2},{5,3},{6,4},{7,5},{8,14},{9,15},{10,... | collective-permute-start | bytes 786440 | tf_op jit(solution)/shard_map/sum_over_col/ppermute | solution.py:37
  36.7 9.8 %collective-permute-start.13 = (bf16[4,128,256]{2,1,0:T(8,128)(2,1)S(1)}, bf16[4,128,256]{2,1,0:T(8,128)(2,1)S(1)}, u32[]{:S(2)}, u32[]{:S(2)}) collective-permute-start(bf16[4,128,256]{2,1,0:T(8,128)(2,1)S(1)} %get-tuple-element.55), channel_id=1, source_target_pairs={{0,2},{1,3},{2,4},{3,5},{4,6},{5,7},{6,0},{7,1},{8,10},{9,11},{10,... | collective-permute-start | bytes 786440 | tf_op jit(solution)/shard_map/sum_over_col/ppermute | solution.py:37
  38.2 12.0 %collective-permute-start.12 = (bf16[4,128,256]{2,1,0:T(8,128)(2,1)S(1)}, bf16[4,128,256]{2,1,0:T(8,128)(2,1)S(1)}, u32[]{:S(2)}, u32[]{:S(2)}) collective-permute-start(bf16[4,128,256]{2,1,0:T(8,128)(2,1)S(1)} %get-tuple-element.56), channel_id=1, source_target_pairs={{0,4},{1,5},{2,6},{3,7},{4,0},{5,1},{6,2},{7,3},{8,12},{9,13},{10,... | collective-permute-start | bytes 786440 | tf_op jit(solution)/shard_map/sum_over_col/ppermute | solution.py:37
  41.1 14.8 %collective-permute-start.18 = (bf16[2,128,256]{2,1,0:T(8,128)(2,1)S(1)}, bf16[2,128,256]{2,1,0:T(8,128)(2,1)S(1)}, u32[]{:S(2)}, u32[]{:S(2)}) collective-permute-start(bf16[2,128,256]{2,1,0:T(8,128)(2,1)S(1)} %get-tuple-element.45), channel_id=1, source_target_pairs={{0,6},{1,7},{2,0},{3,1},{4,2},{5,3},{6,4},{7,5},{8,14},{9,15},{10,... | collective-permute-start | bytes 393224 | tf_op jit(solution)/shard_map/sum_over_col/ppermute | solution.py:37
  42.8 14.5 %collective-permute-start.17 = (bf16[2,128,256]{2,1,0:T(8,128)(2,1)S(1)}, bf16[2,128,256]{2,1,0:T(8,128)(2,1)S(1)}, u32[]{:S(2)}, u32[]{:S(2)}) collective-permute-start(bf16[2,128,256]{2,1,0:T(8,128)(2,1)S(1)} %get-tuple-element.46), channel_id=1, source_target_pairs={{0,2},{1,3},{2,4},{3,5},{4,6},{5,7},{6,0},{7,1},{8,10},{9,11},{10,... | collective-permute-start | bytes 393224 | tf_op jit(solution)/shard_map/sum_over_col/ppermute | solution.py:37
  44.2 13.4 %collective-permute-start.16 = (bf16[2,128,256]{2,1,0:T(8,128)(2,1)S(1)}, bf16[2,128,256]{2,1,0:T(8,128)(2,1)S(1)}, u32[]{:S(2)}, u32[]{:S(2)}) collective-permute-start(bf16[2,128,256]{2,1,0:T(8,128)(2,1)S(1)} %get-tuple-element.47), channel_id=1, source_target_pairs={{0,4},{1,5},{2,6},{3,7},{4,0},{5,1},{6,2},{7,3},{8,12},{9,13},{10,... | collective-permute-start | bytes 393224 | tf_op jit(solution)/shard_map/sum_over_col/ppermute | solution.py:37
  50.3 13.9 %collective-permute-start.19 = (bf16[2,128,256]{2,1,0:T(8,128)(2,1)S(1)}, bf16[2,128,256]{2,1,0:T(8,128)(2,1)S(1)}, u32[]{:S(2)}, u32[]{:S(2)}) collective-permute-start(bf16[2,128,256]{2,1,0:T(8,128)(2,1)S(1)} %get-tuple-element.57), channel_id=1, source_target_pairs={{0,8},{1,9},{2,10},{3,11},{4,12},{5,13},{6,14},{7,15},{8,16},{9,17... | collective-permute-start | bytes 393224 | tf_op jit(solution)/shard_map/sum_over_col/ppermute | solution.py:37
  55.9 9.0 %collective-permute-start.10 = (bf16[2,128,256]{2,1,0:T(8,128)(2,1)S(1)}, bf16[2,128,256]{2,1,0:T(8,128)(2,1)S(1)}, u32[]{:S(2)}, u32[]{:S(2)}) collective-permute-start(bf16[2,128,256]{2,1,0:T(8,128)(2,1)S(1)} %get-tuple-element.49), channel_id=1, source_target_pairs={{0,6},{1,7},{2,0},{3,1},{4,2},{5,3},{6,4},{7,5},{8,14},{9,15},{10,... | collective-permute-start | bytes 393224 | tf_op jit(solution)/shard_map/sum_over_col/ppermute | solution.py:37
  55.9 9.0 %collective-permute-start.9 = (bf16[2,128,256]{2,1,0:T(8,128)(2,1)S(1)}, bf16[2,128,256]{2,1,0:T(8,128)(2,1)S(1)}, u32[]{:S(2)}, u32[]{:S(2)}) collective-permute-start(bf16[2,128,256]{2,1,0:T(8,128)(2,1)S(1)} %get-tuple-element.50), channel_id=1, source_target_pairs={{0,2},{1,3},{2,4},{3,5},{4,6},{5,7},{6,0},{7,1},{8,10},{9,11},{10,... | collective-permute-start | bytes 393224 | tf_op jit(solution)/shard_map/sum_over_col/ppermute | solution.py:37
  57.4 7.6 %collective-permute-start.8 = (bf16[2,128,256]{2,1,0:T(8,128)(2,1)S(1)}, bf16[2,128,256]{2,1,0:T(8,128)(2,1)S(1)}, u32[]{:S(2)}, u32[]{:S(2)}) collective-permute-start(bf16[2,128,256]{2,1,0:T(8,128)(2,1)S(1)} %get-tuple-element.51), channel_id=1, source_target_pairs={{0,4},{1,5},{2,6},{3,7},{4,0},{5,1},{6,2},{7,3},{8,12},{9,13},{10,... | collective-permute-start | bytes 393224 | tf_op jit(solution)/shard_map/sum_over_col/ppermute | solution.py:37
  57.7 11.4 %collective-permute-start.15 = (bf16[2,128,256]{2,1,0:T(8,128)(2,1)S(1)}, bf16[2,128,256]{2,1,0:T(8,128)(2,1)S(1)}, u32[]{:S(2)}, u32[]{:S(2)}) collective-permute-start(bf16[2,128,256]{2,1,0:T(8,128)(2,1)S(1)} %get-tuple-element.58), channel_id=1, source_target_pairs={{0,16},{1,17},{2,18},{3,19},{4,20},{5,21},{6,22},{7,23},{8,24},{9,... | collective-permute-start | bytes 393224 | tf_op jit(solution)/shard_map/sum_over_col/ppermute | solution.py:37
  64.2 12.6 %copy-start.16 = (bf16[2,128,256]{2,1,0:T(8,128)(2,1)}, bf16[2,128,256]{2,1,0:T(8,128)(2,1)S(1)}, u32[]{:S(2)}) copy-start(bf16[2,128,256]{2,1,0:T(8,128)(2,1)S(1)} %collective-permute-done.19) | copy-start | bytes 393220
  64.3 12.5 %collective-permute-start.20 = (bf16[2,128,256]{2,1,0:T(8,128)(2,1)S(1)}, bf16[2,128,256]{2,1,0:T(8,128)(2,1)S(1)}, u32[]{:S(2)}, u32[]{:S(2)}) collective-permute-start(bf16[2,128,256]{2,1,0:T(8,128)(2,1)S(1)} %add_convert_fusion.4), channel_id=1, source_target_pairs={{0,24},{1,25},{2,26},{3,27},{4,28},{5,29},{6,30},{7,31},{8,0},{9,1... | collective-permute-start | bytes 393224 | tf_op jit(solution)/shard_map/sum_over_col/ppermute | solution.py:37
  64.9 11.9 %copy-start.17 = (bf16[2,128,256]{2,1,0:T(8,128)(2,1)}, bf16[2,128,256]{2,1,0:T(8,128)(2,1)S(1)}, u32[]{:S(2)}) copy-start(bf16[2,128,256]{2,1,0:T(8,128)(2,1)S(1)} %collective-permute-done.10) | copy-start | bytes 393220
  64.9 11.9 %copy-start.18 = (bf16[2,128,256]{2,1,0:T(8,128)(2,1)}, bf16[2,128,256]{2,1,0:T(8,128)(2,1)S(1)}, u32[]{:S(2)}) copy-start(bf16[2,128,256]{2,1,0:T(8,128)(2,1)S(1)} %collective-permute-done.9) | copy-start | bytes 393220
  64.9 11.8 %copy-start.19 = (bf16[2,128,256]{2,1,0:T(8,128)(2,1)}, bf16[2,128,256]{2,1,0:T(8,128)(2,1)S(1)}, u32[]{:S(2)}) copy-start(bf16[2,128,256]{2,1,0:T(8,128)(2,1)S(1)} %collective-permute-done.8) | copy-start | bytes 393220
  80.0 8.8 %collective-permute-start.23 = (bf16[256,256]{1,0:T(8,128)(2,1)}, bf16[256,256]{1,0:T(8,128)(2,1)S(1)}, u32[]{:S(2)}, u32[]{:S(2)}) collective-permute-start(bf16[256,256]{1,0:T(8,128)(2,1)} %get-tuple-element.33), channel_id=1, source_target_pairs={{0,24},{1,25},{2,26},{3,27},{4,28},{5,29},{6,30},{7,31},{8,0},{9,1... | collective-permute-start | bytes 393224 | tf_op jit(solution)/shard_map/gather_gradients/ppermute | solution.py:37
  82.5 9.0 %collective-permute-start.22 = (bf16[256,256]{1,0:T(8,128)(2,1)}, bf16[256,256]{1,0:T(8,128)(2,1)S(1)}, u32[]{:S(2)}, u32[]{:S(2)}) collective-permute-start(bf16[256,256]{1,0:T(8,128)(2,1)} %get-tuple-element.33), channel_id=1, source_target_pairs={{0,16},{1,17},{2,18},{3,19},{4,20},{5,21},{6,22},{7,23},{8,24},{9,... | collective-permute-start | bytes 393224 | tf_op jit(solution)/shard_map/gather_gradients/ppermute | solution.py:37
  84.5 12.2 %collective-permute-start.21 = (bf16[256,256]{1,0:T(8,128)(2,1)}, bf16[256,256]{1,0:T(8,128)(2,1)S(1)}, u32[]{:S(2)}, u32[]{:S(2)}) collective-permute-start(bf16[256,256]{1,0:T(8,128)(2,1)} %get-tuple-element.33), channel_id=1, source_target_pairs={{0,8},{1,9},{2,10},{3,11},{4,12},{5,13},{6,14},{7,15},{8,16},{9,17... | collective-permute-start | bytes 393224 | tf_op jit(solution)/shard_map/gather_gradients/ppermute | solution.py:37
  96.8 35.4 %copy-start.1 = (bf16[1024,256]{1,0:T(8,128)(2,1)}, bf16[1024,256]{1,0:T(8,128)(2,1)S(1)}, u32[]{:S(2)}) copy-start(bf16[1024,256]{1,0:T(8,128)(2,1)S(1)} %constant_dynamic-update-slice_fusion) | copy-start | bytes 1572868
  96.8 12.8 %collective-permute-start.26 = (bf16[1024,256]{1,0:T(8,128)(2,1)S(1)}, bf16[1024,256]{1,0:T(8,128)(2,1)S(1)}, u32[]{:S(2)}, u32[]{:S(2)}) collective-permute-start(bf16[1024,256]{1,0:T(8,128)(2,1)S(1)} %constant_dynamic-update-slice_fusion), channel_id=1, source_target_pairs={{0,6},{1,7},{2,0},{3,1},{4,2},{5,3},{6,4},{7,5},{8,14},{9,15},{10,... | collective-permute-start | bytes 1572872 | tf_op jit(solution)/shard_map/gather_gradients/ppermute | solution.py:37
  96.9 15.5 %collective-permute-start.25 = (bf16[1024,256]{1,0:T(8,128)(2,1)S(1)}, bf16[1024,256]{1,0:T(8,128)(2,1)S(1)}, u32[]{:S(2)}, u32[]{:S(2)}) collective-permute-start(bf16[1024,256]{1,0:T(8,128)(2,1)S(1)} %constant_dynamic-update-slice_fusion), channel_id=1, source_target_pairs={{0,4},{1,5},{2,6},{3,7},{4,0},{5,1},{6,2},{7,3},{8,12},{9,13},{10,... | collective-permute-start | bytes 1572872 | tf_op jit(solution)/shard_map/gather_gradients/ppermute | solution.py:37
  97.6 29.3 %collective-permute-start.24 = (bf16[1024,256]{1,0:T(8,128)(2,1)S(1)}, bf16[1024,256]{1,0:T(8,128)(2,1)S(1)}, u32[]{:S(2)}, u32[]{:S(2)}) collective-permute-start(bf16[1024,256]{1,0:T(8,128)(2,1)S(1)} %constant_dynamic-update-slice_fusion), channel_id=1, source_target_pairs={{0,2},{1,3},{2,4},{3,5},{4,6},{5,7},{6,0},{7,1},{8,10},{9,11},{10,... | collective-permute-start | bytes 1572872 | tf_op jit(solution)/shard_map/gather_gradients/ppermute | solution.py:37
  98.3 29.3 %all-to-all-start.1 = ((f32[32,8,384]{2,1,0:T(8,128)}), f32[32,8,384]{2,1,0:T(8,128)S(1)}, u32[]{:S(2)}, u32[]{:S(2)}) async-start(f32[32,8,384]{2,1,0:T(8,128)} %bitcast.35), calls=%async_computation.1 | async-start | bytes 786432 | tf_op jit(solution)/shard_map/sum_weight_grad/all_to_all | solution.py:308
  108.0 24.1 %collective-permute-start.27 = (bf16[1024,256]{1,0:T(8,128)(2,1)S(1)}, bf16[1024,256]{1,0:T(8,128)(2,1)S(1)}, u32[]{:S(2)}, u32[]{:S(2)}) collective-permute-start(bf16[1024,256]{1,0:T(8,128)(2,1)S(1)} %constant_dynamic-update-slice_fusion), channel_id=1, source_target_pairs={{0,1},{1,0},{2,3},{3,2},{4,5},{5,4},{6,7},{7,6},{8,9},{9,8},{10,11... | collective-permute-start | bytes 1572872 | tf_op jit(solution)/shard_map/gather_gradients/ppermute | solution.py:37
  109.6 22.6 %copy-start.2 = (bf16[1024,256]{1,0:T(8,128)(2,1)}, bf16[1024,256]{1,0:T(8,128)(2,1)S(1)}, u32[]{:S(2)}) copy-start(bf16[1024,256]{1,0:T(8,128)(2,1)S(1)} %collective-permute-done.26) | copy-start | bytes 1572868
  109.6 22.6 %collective-permute-start.30 = (bf16[1024,256]{1,0:T(8,128)(2,1)S(1)}, bf16[1024,256]{1,0:T(8,128)(2,1)S(1)}, u32[]{:S(2)}, u32[]{:S(2)}) collective-permute-start(bf16[1024,256]{1,0:T(8,128)(2,1)S(1)} %collective-permute-done.26), channel_id=1, source_target_pairs={{0,1},{1,0},{2,3},{3,2},{4,5},{5,4},{6,7},{7,6},{8,9},{9,8},{10,11... | collective-permute-start | bytes 1572872 | tf_op jit(solution)/shard_map/gather_gradients/ppermute | solution.py:37
  112.4 19.9 %copy-start.3 = (bf16[1024,256]{1,0:T(8,128)(2,1)}, bf16[1024,256]{1,0:T(8,128)(2,1)S(1)}, u32[]{:S(2)}) copy-start(bf16[1024,256]{1,0:T(8,128)(2,1)S(1)} %collective-permute-done.25) | copy-start | bytes 1572868
  112.4 19.8 %collective-permute-start.29 = (bf16[1024,256]{1,0:T(8,128)(2,1)S(1)}, bf16[1024,256]{1,0:T(8,128)(2,1)}, u32[]{:S(2)}, u32[]{:S(2)}) collective-permute-start(bf16[1024,256]{1,0:T(8,128)(2,1)S(1)} %collective-permute-done.25), channel_id=1, source_target_pairs={{0,1},{1,0},{2,3},{3,2},{4,5},{5,4},{6,7},{7,6},{8,9},{9,8},{10,11... | collective-permute-start | bytes 1572872 | tf_op jit(solution)/shard_map/gather_gradients/ppermute | solution.py:37
  127.0 5.2 %collective-permute-start.28 = (bf16[1024,256]{1,0:T(8,128)(2,1)S(1)}, bf16[1024,256]{1,0:T(8,128)(2,1)}, u32[]{:S(2)}, u32[]{:S(2)}) collective-permute-start(bf16[1024,256]{1,0:T(8,128)(2,1)S(1)} %collective-permute-done.24), channel_id=1, source_target_pairs={{0,1},{1,0},{2,3},{3,2},{4,5},{5,4},{6,7},{7,6},{8,9},{9,8},{10,11... | collective-permute-start | bytes 1572872 | tf_op jit(solution)/shard_map/gather_gradients/ppermute | solution.py:37
  128.3 11.8 %all-to-all-start.2 = ((f32[8,8,384]{2,1,0:T(8,128)}), f32[8,8,384]{2,1,0:T(8,128)S(1)}, u32[]{:S(2)}, u32[]{:S(2)}) async-start(f32[8,8,384]{2,1,0:T(8,128)} %broadcast_in_dim.3), calls=%async_computation.2 | async-start | bytes 196608 | tf_op jit(solution)/shard_map/sum_weight_grad/all_to_all | solution.py:310
  140.1 38.2 %all-to-all-start = ((bf16[8,256,256]{2,1,0:T(8,128)(2,1)}), bf16[8,256,256]{2,1,0:T(8,128)(2,1)S(1)}, u32[]{:S(2)}, u32[]{:S(2)}) async-start(bf16[8,256,256]{2,1,0:T(8,128)(2,1)} %bitcast.34), calls=%async_computation | async-start | bytes 2097152 | tf_op jit(solution)/shard_map/sum_over_row/all_to_all | solution.py:318
  147.4 6.6 %collective-permute-start.33 = (f32[8,384]{1,0:T(8,128)S(1)}, f32[8,384]{1,0:T(8,128)S(1)}, u32[]{:S(2)}, u32[]{:S(2)}) collective-permute-start(f32[8,384]{1,0:T(8,128)S(1)} %get-tuple-element.59), channel_id=1, source_target_pairs={{0,24},{1,25},{2,26},{3,27},{4,28},{5,29},{6,30},{7,31},{8,0},{9,1... | collective-permute-start | bytes 36872 | tf_op jit(solution)/shard_map/sum_weight_grad/ppermute | solution.py:37
  149.7 15.1 %collective-permute-start.32 = (f32[8,384]{1,0:T(8,128)S(1)}, f32[8,384]{1,0:T(8,128)S(1)}, u32[]{:S(2)}, u32[]{:S(2)}) collective-permute-start(f32[8,384]{1,0:T(8,128)S(1)} %get-tuple-element.59), channel_id=1, source_target_pairs={{0,16},{1,17},{2,18},{3,19},{4,20},{5,21},{6,22},{7,23},{8,24},{9,... | collective-permute-start | bytes 36872 | tf_op jit(solution)/shard_map/sum_weight_grad/ppermute | solution.py:37
  151.8 13.0 %collective-permute-start.31 = (f32[8,384]{1,0:T(8,128)S(1)}, f32[8,384]{1,0:T(8,128)S(1)}, u32[]{:S(2)}, u32[]{:S(2)}) collective-permute-start(f32[8,384]{1,0:T(8,128)S(1)} %get-tuple-element.59), channel_id=1, source_target_pairs={{0,8},{1,9},{2,10},{3,11},{4,12},{5,13},{6,14},{7,15},{8,16},{9,17... | collective-permute-start | bytes 36872 | tf_op jit(solution)/shard_map/sum_weight_grad/ppermute | solution.py:37
  164.7 5.8 %collective-permute-start.36 = (f32[32,384]{1,0:T(8,128)S(1)}, f32[32,384]{1,0:T(8,128)S(1)}, u32[]{:S(2)}, u32[]{:S(2)}) collective-permute-start(f32[32,384]{1,0:T(8,128)S(1)} %pad_maximum_fusion), channel_id=1, source_target_pairs={{0,6},{1,7},{2,0},{3,1},{4,2},{5,3},{6,4},{7,5},{8,14},{9,15},{10,... | collective-permute-start | bytes 147464 | tf_op jit(solution)/shard_map/sum_weight_grad/ppermute | solution.py:37
  165.5 5.0 %collective-permute-start.35 = (f32[32,384]{1,0:T(8,128)S(1)}, f32[32,384]{1,0:T(8,128)S(1)}, u32[]{:S(2)}, u32[]{:S(2)}) collective-permute-start(f32[32,384]{1,0:T(8,128)S(1)} %pad_maximum_fusion), channel_id=1, source_target_pairs={{0,4},{1,5},{2,6},{3,7},{4,0},{5,1},{6,2},{7,3},{8,12},{9,13},{10,... | collective-permute-start | bytes 147464 | tf_op jit(solution)/shard_map/sum_weight_grad/ppermute | solution.py:37
  165.7 4.8 %collective-permute-start.34 = (f32[32,384]{1,0:T(8,128)S(1)}, f32[32,384]{1,0:T(8,128)S(1)}, u32[]{:S(2)}, u32[]{:S(2)}) collective-permute-start(f32[32,384]{1,0:T(8,128)S(1)} %pad_maximum_fusion), channel_id=1, source_target_pairs={{0,2},{1,3},{2,4},{3,5},{4,6},{5,7},{6,0},{7,1},{8,10},{9,11},{10,... | collective-permute-start | bytes 147464 | tf_op jit(solution)/shard_map/sum_weight_grad/ppermute | solution.py:37
  170.6 3.6 %collective-permute-start.37 = (f32[128,384]{1,0:T(8,128)S(1)}, f32[128,384]{1,0:T(8,128)S(1)}, u32[]{:S(2)}, u32[]{:S(2)}) collective-permute-start(f32[128,384]{1,0:T(8,128)S(1)} %constant_dynamic-update-slice_fusion.4.here), channel_id=1, source_target_pairs={{0,1},{1,0},{2,3},{3,2},{4,5},{5,4},{6,7},{7,6},{8,9},{9,8},{10,11... | collective-permute-start | bytes 589832 | tf_op jit(solution)/shard_map/sum_weight_grad/ppermute | solution.py:37
  (15 other events, 45.0 us)

commit v4 on v3

--- a/solution.py
+++ b/solution.py
@@ -15,7 +15,7 @@
 N_ROW = N_X * N_ZL
 N_COL = N_ZH * N_Y * N_CORE
 GROUP = 24
-VMEM_LIMIT = 60 * 1024 * 1024
+VMEM_LIMIT = 65408 * 1024
 LANES = 128
 
 
@@ -192,10 +192,17 @@
     )(total, pre_grad)
 
 
-def last_kernel(pieces, weight, out):
-    total = pieces[0].astype(jnp.float32)
-    for k in range(1, pieces.shape[0]):
-        total += pieces[k].astype(jnp.float32)
+def last_kernel(pieces, weight, out, held, sems):
+    copies = [
+        pltpu.make_async_copy(pieces.at[k], held.at[k], sems.at[k])
+        for k in range(held.shape[0])
+    ]
+    for copy in copies:
+        copy.start()
+    total = jnp.zeros(out.shape, jnp.float32)
+    for k, copy in enumerate(copies):
+        copy.wait()
+        total += held[k].astype(jnp.float32)
     out[...] = lax.dot_general(
         total.astype(jnp.bfloat16),
         weight[...],
@@ -209,40 +216,15 @@
     vmem = pl.BlockSpec(memory_space=pltpu.VMEM)
     return pl.pallas_call(
         last_kernel,
-        in_specs=[vmem] * 2,
+        in_specs=[pl.BlockSpec(memory_space=pltpu.HBM), vmem],
         out_specs=vmem,
         out_shape=jax.ShapeDtypeStruct((rows, width), jnp.bfloat16),
+        scratch_shapes=[
+            pltpu.VMEM(pieces.shape, jnp.bfloat16),
+            pltpu.SemaphoreType.DMA((pieces.shape[0],)),
+        ],
         compiler_params=pltpu.CompilerParams(vmem_limit_bytes=VMEM_LIMIT),
     )(pieces, weight)
-
-
-def spread_kernel(place, here, there, weight_grad, bias_grad):
-    width = weight_grad.shape[1]
-    chunk = weight_grad.shape[0] // N_COL
-    for core, rows in enumerate((here, there)):
-        for k in range(N_ZH * N_Y):
-            y, zh = divmod(k, N_ZH)
-            owner = (
-                ((place[0] + N_ZH - zh) % N_ZH * N_Y + (place[1] + N_Y - y) % N_Y) * N_CORE
-                + (place[2] + core) % N_CORE
-            )
-            put = pl.ds(pl.multiple_of(owner * chunk, chunk), chunk)
-            weight_grad[put, :] = rows[chunk * k : chunk * (k + 1), :width]
-            bias_grad[put, :] = rows[chunk * k : chunk * (k + 1), width:]
-
-
-def spread(place, here, there, width):
-    rows = here.shape[0] * N_CORE
-    vmem = pl.BlockSpec(memory_space=pltpu.VMEM)
-    return pl.pallas_call(
-        spread_kernel,
-        in_specs=[pl.BlockSpec(memory_space=pltpu.SMEM)] + [vmem] * 2,
-        out_specs=[vmem] * 2,
-        out_shape=[
-            jax.ShapeDtypeStruct((rows, width), jnp.float32),
-            jax.ShapeDtypeStruct((rows, here.shape[1] - width), jnp.float32),
-        ],
-    )(place, here, there)
 
 
 def merge(pieces):
@@ -283,19 +265,19 @@
     with jax.named_scope("sum_over_col"):
         others = [col_shift(send, dcore=1) for send in parts[2:]]
 
-        def over_y(part, first, size):
+        def over_y(keep, other, first, size):
             added = []
             for k in range(N_Y):
                 rows = slice(2 * per * k + first * per, 2 * per * k + (first + size) * per)
-                added.append(merge([parts[part][rows], others[part][rows]]))
+                added.append(merge([keep[rows], other[rows]]))
             return [added[0]] + [col_shift(added[k], dy=k) for k in (2, 1, 3)]
 
-        both = over_y(0, 0, 2)
+        both = over_y(parts[0], others[0], 0, 2)
         far = col_shift(merge([p[:per] for p in both]), dzh=2)
         near = col_shift(merge([p[per:] for p in both]), dzh=1)
-        back = over_y(1, 0, 1)
-        *back, near = lax.optimization_barrier((*back, near))
-        pieces = over_y(1, 1, 1) + [far, near, col_shift(merge(back), dzh=3)]
+        back = over_y(parts[1], others[1], 0, 1)
+        *back, near, others[1] = lax.optimization_barrier((*back, near, others[1]))
+        pieces = over_y(parts[1], others[1], 1, 1) + [far, near, col_shift(merge(back), dzh=3)]
         pieces = [p.reshape(vertices, width) for p in pieces]
     with jax.named_scope("pointwise"):
         layer_out, grad, total, pre_grad = middle(pieces, weight, bias, cotangent)
@@ -318,11 +300,10 @@
         back = lax.all_to_all(back, "row", 0, 0, tiled=True)
         features_grad = last(back, weight)
     with jax.named_scope("sum_weight_grad"):
-        load = jnp.concatenate([load] + [col_shift(load, dzh=k) for k in range(1, N_ZH)])
-        load = jnp.concatenate([load] + [col_shift(load, dy=k) for k in range(1, N_Y)])
-        place = jnp.stack([my_zh, my_y, my_core]).astype(jnp.int32)
-        weight_grad, bias_grad = spread(place, load, col_shift(load, dcore=1), width)
-    return layer_out, features_grad, weight_grad, bias_grad[:, 0]
+        load = jnp.broadcast_to(load, (N_COL,) + load.shape)
+        load = lax.all_to_all(load, "col", 0, 0, tiled=True).reshape(width, -1)
+        weight_grad, bias_grad = load[:, :width], load[:, width]
+    return layer_out, features_grad, weight_grad, bias_grad
 
 
 def solution(mesh):

time: 182 us -> 176 us (0.967)
  waiting for transfers between devices: 66.8 us -> 49.7 us
  blocking collectives: 0 us -> 11.4 us
  local copies, waits for them, and re-layouts: 7.13 us -> 9.26 us
    ppermute x31 -> x24, waiting for transfers between devices: 59.5 us -> 21.7 us  [col_shift(): return lax.ppermute(value, 'col', pairs)]
    all_to_all x1, waiting for transfers between devices: 0.01 us -> 12.9 us  [shards(): back = lax.all_to_all(back, 'row', 0, 0, tiled=True)]
    all_to_all x0 -> x1, blocking collectives: none -> 11.4 us  [shards(): lax.all_to_all(load, 'row', 0, 0, tiled=True)]
    all_to_all x1, waiting for transfers between devices: 0.07 us -> 7.04 us  [shards(): load = jnp.sum(lax.all_to_all(load, 'col', 0, 0, tiled=True), axis=0)]
    all_to_all x1, starting transfers between devices: 9.71 us -> 13.7 us  [shards(): load = jnp.sum(lax.all_to_all(load, 'col', 0, 0, tiled=True), axis=0)]
    all_to_all x1, waiting for transfers between devices: 0.01 us -> 3.87 us  [shards(): load = lax.all_to_all(load, 'col', 0, 0, tiled=True).reshape(width, -1)]
    ppermute x31 -> x24, starting transfers between devices: 45.2 us -> 42.1 us  [col_shift(): return lax.ppermute(value, 'col', pairs)]
    all_to_all x1, starting transfers between devices: 7.3 us -> 4.24 us  [shards(): back = lax.all_to_all(back, 'row', 0, 0, tiled=True)]
  transfers between devices with their start and end apart: 41 -> 34, of which waited for: 18 -> 18; matrix products, arithmetic and copies ran while one was open for 6% -> 8% of each run, Pallas kernels for 6% -> 5%
where the time goes in v4:
time: 176 us; the launch traced here: 177 us
  starting transfers between devices  77.1 us (44%)
  waiting for transfers between devices  49.7 us (28%)
  Pallas kernels  21.6 us (12%)
  blocking collectives  11.4 us (6%)
  local copies, waits for them, and re-layouts  9.26 us (5%)
  other arithmetic  6.34 us (4%)
    ppermute x24, starting transfers between devices, col_shift(): return lax.ppermute(value, 'col', pairs)  42.1 us
    ppermute x24, waiting for transfers between devices, col_shift(): return lax.ppermute(value, 'col', pairs)  21.7 us
    pallas_call x2, Pallas kernels, tile_sum(): pl.pallas_call(functools.partial(tile_kernel, transposed, src_sizes, out_...  13.8 us
    all_to_all x1, starting transfers between devices, shards(): load = jnp.sum(lax.all_to_all(load, 'col', 0, 0, tiled=True), axis=0)  13.7 us
    all_to_all x1, waiting for transfers between devices, shards(): back = lax.all_to_all(back, 'row', 0, 0, tiled=True)  12.9 us
    ppermute x7, starting transfers between devices, row_shift(): return lax.ppermute(value, 'row', pairs)  11.6 us
    all_to_all x1, blocking collectives, shards(): lax.all_to_all(load, 'row', 0, 0, tiled=True)  11.4 us
    all_to_all x1, waiting for transfers between devices, shards(): load = jnp.sum(lax.all_to_all(load, 'col', 0, 0, tiled=True), axis=0)  7.04 us
  transfers between devices with their start and end apart: 34, of which 18 were waited for; matrix products, arithmetic and copies ran while one was open for 8% of the time, Pallas kernels for 5%

profile of v4, /device:TPU:1, one launch (start us, length us, event | category | flops | bytes accessed | tf_op | source)
XLA Modules:
  0.0 177.1 jit_solution(3162096147230767114)
XLA Ops:
  0.6 4.7 %collective-permute-start.6 = (bf16[256,256]{1,0:T(8,128)(2,1)}, bf16[256,256]{1,0:T(8,128)(2,1)}, u32[]{:S(2)}, u32[]{:S(2)}) collective-permute-start(bf16[256,256]{1,0:T(8,128)(2,1)} %param.8), channel_id=1, source_target_pairs={{0,224},{32,192},{64,32},{96,0},{128,96},{160,64},{192,160},{224,1... | collective-permute-start | bytes 393224 | tf_op jit(solution)/shard_map/gather_features/ppermute | solution.py:27
  5.4 1.4 collective-permute-start.2
  6.8 3.7 %collective-permute-start.3 = (bf16[256,256]{1,0:T(8,128)(2,1)}, bf16[256,256]{1,0:T(8,128)(2,1)}, u32[]{:S(2)}, u32[]{:S(2)}) collective-permute-start(bf16[256,256]{1,0:T(8,128)(2,1)} %param.8), channel_id=1, source_target_pairs={{0,128},{32,160},{64,192},{96,224},{128,0},{160,32},{192,64},{224,... | collective-permute-start | bytes 393224 | tf_op jit(solution)/shard_map/gather_features/ppermute | solution.py:27
  11.1 1.3 multiply_add_fusion
  12.4 1.8 %collective-permute-start.5 = (bf16[256,256]{1,0:T(8,128)(2,1)}, bf16[256,256]{1,0:T(8,128)(2,1)}, u32[]{:S(2)}, u32[]{:S(2)}) collective-permute-start(bf16[256,256]{1,0:T(8,128)(2,1)} %param.8), channel_id=1, source_target_pairs={{0,192},{32,224},{64,0},{96,32},{128,64},{160,96},{192,128},{224,1... | collective-permute-start | bytes 393224 | tf_op jit(solution)/shard_map/gather_features/ppermute | solution.py:27
  14.2 1.3 fusion.2
  15.4 2.8 %collective-permute-done.3 = bf16[256,256]{1,0:T(8,128)(2,1)} collective-permute-done((bf16[256,256]{1,0:T(8,128)(2,1)}, bf16[256,256]{1,0:T(8,128)(2,1)}, u32[]{:S(2)}, u32[]{:S(2)}) %collective-permute-start.3) | collective-permute-done | bytes 131104 | tf_op jit(solution)/shard_map/gather_features/ppermute | solution.py:27
  19.7 6.9 %tiles_forward.1 = (bf16[16,128,256]{2,1,0:T(8,128)(2,1)}, bf16[16,128,256]{2,1,0:T(8,128)(2,1)}, bf16[16,128,256]{2,1,0:T(8,128)(2,1)}, bf16[16,128,256]{2,1,0:T(8,128)(2,1)}) custom-call(s32[1]{0:T(128)} %bitcast.30.live, s32[192]{0:T(256)} %get-tuple-element.57.take, s32[192]{0:T(256)} %get-tuple-element.58.put, bf16[1,192,128,128]{3,2,1,0:T(8,128)(2,1)} %tiles.3, ...), custom_call_target="tpu_custom_call" | custom-call | flops 1610612736 | bytes 6291456 | tf_op jit(solution)/shard_map/tiles_forward/pallas_call | solution.py:109
  26.6 1.4 collective-permute-start.11
  28.1 2.4 %collective-permute-done.11 = bf16[16,128,256]{2,1,0:T(8,128)(2,1)S(1)} collective-permute-done((bf16[16,128,256]{2,1,0:T(8,128)(2,1)}, bf16[16,128,256]{2,1,0:T(8,128)(2,1)S(1)}, u32[]{:S(2)}, u32[]{:S(2)}) %collective-permute-start.11) | collective-permute-done | bytes 1048608 | tf_op jit(solution)/shard_map/sum_over_col/ppermute | solution.py:37
  30.5 1.5 add_convert_fusion.3
  32.0 6.5 %collective-permute-start.12 = (bf16[4,128,256]{2,1,0:T(8,128)(2,1)S(1)}, bf16[4,128,256]{2,1,0:T(8,128)(2,1)S(1)}, u32[]{:S(2)}, u32[]{:S(2)}) collective-permute-start(bf16[4,128,256]{2,1,0:T(8,128)(2,1)S(1)} %get-tuple-element.50), channel_id=1, source_target_pairs={{0,4},{1,5},{2,6},{3,7},{4,0},{5,1},{6,2},{7,3},{8,12},{9,13},{10,... | collective-permute-start | bytes 786440 | tf_op jit(solution)/shard_map/sum_over_col/ppermute | solution.py:37
  38.4 2.7 %collective-permute-start.14 = (bf16[4,128,256]{2,1,0:T(8,128)(2,1)S(1)}, bf16[4,128,256]{2,1,0:T(8,128)(2,1)S(1)}, u32[]{:S(2)}, u32[]{:S(2)}) collective-permute-start(bf16[4,128,256]{2,1,0:T(8,128)(2,1)S(1)} %get-tuple-element.48), channel_id=1, source_target_pairs={{0,6},{1,7},{2,0},{3,1},{4,2},{5,3},{6,4},{7,5},{8,14},{9,15},{10,... | collective-permute-start | bytes 786440 | tf_op jit(solution)/shard_map/sum_over_col/ppermute | solution.py:37
  41.1 1.2 add_convert_fusion.11
  43.0 1.8 %collective-permute-done.12 = bf16[4,128,256]{2,1,0:T(8,128)(2,1)S(1)} collective-permute-done((bf16[4,128,256]{2,1,0:T(8,128)(2,1)S(1)}, bf16[4,128,256]{2,1,0:T(8,128)(2,1)S(1)}, u32[]{:S(2)}, u32[]{:S(2)}) %collective-permute-start.12) | collective-permute-done | bytes 262176 | tf_op jit(solution)/shard_map/sum_over_col/ppermute | solution.py:37
  44.9 1.0 collective-permute-start.9
  45.9 5.3 %collective-permute-done.13 = bf16[4,128,256]{2,1,0:T(8,128)(2,1)S(1)} collective-permute-done((bf16[4,128,256]{2,1,0:T(8,128)(2,1)S(1)}, bf16[4,128,256]{2,1,0:T(8,128)(2,1)S(1)}, u32[]{:S(2)}, u32[]{:S(2)}) %collective-permute-start.13) | collective-permute-done | bytes 262176 | tf_op jit(solution)/shard_map/sum_over_col/ppermute | solution.py:37
  51.3 3.0 %collective-permute-start.15 = (bf16[2,128,256]{2,1,0:T(8,128)(2,1)S(1)}, bf16[2,128,256]{2,1,0:T(8,128)(2,1)S(1)}, u32[]{:S(2)}, u32[]{:S(2)}) collective-permute-start(bf16[2,128,256]{2,1,0:T(8,128)(2,1)S(1)} %get-tuple-element.56), channel_id=1, source_target_pairs={{0,8},{1,9},{2,10},{3,11},{4,12},{5,13},{6,14},{7,15},{8,16},{9,17... | collective-permute-start | bytes 393224 | tf_op jit(solution)/shard_map/sum_over_col/ppermute | solution.py:37
  54.4 4.9 %collective-permute-start.19 = (bf16[2,128,256]{2,1,0:T(8,128)(2,1)S(1)}, bf16[2,128,256]{2,1,0:T(8,128)(2,1)S(1)}, u32[]{:S(2)}, u32[]{:S(2)}) collective-permute-start(bf16[2,128,256]{2,1,0:T(8,128)(2,1)S(1)} %get-tuple-element.55), channel_id=1, source_target_pairs={{0,16},{1,17},{2,18},{3,19},{4,20},{5,21},{6,22},{7,23},{8,24},{9,... | collective-permute-start | bytes 393224 | tf_op jit(solution)/shard_map/sum_over_col/ppermute | solution.py:37
  59.3 2.0 %collective-permute-done.15 = bf16[2,128,256]{2,1,0:T(8,128)(2,1)S(1)} collective-permute-done((bf16[2,128,256]{2,1,0:T(8,128)(2,1)S(1)}, bf16[2,128,256]{2,1,0:T(8,128)(2,1)S(1)}, u32[]{:S(2)}, u32[]{:S(2)}) %collective-permute-start.15) | collective-permute-done | bytes 131104 | tf_op jit(solution)/shard_map/sum_over_col/ppermute | solution.py:37
  61.4 3.0 %collective-permute-start.20 = (bf16[2,128,256]{2,1,0:T(8,128)(2,1)S(1)}, bf16[2,128,256]{2,1,0:T(8,128)(2,1)S(1)}, u32[]{:S(2)}, u32[]{:S(2)}) collective-permute-start(bf16[2,128,256]{2,1,0:T(8,128)(2,1)S(1)} %add_convert_fusion.4), channel_id=1, source_target_pairs={{0,24},{1,25},{2,26},{3,27},{4,28},{5,29},{6,30},{7,31},{8,0},{9,1... | collective-permute-start | bytes 393224 | tf_op jit(solution)/shard_map/sum_over_col/ppermute | solution.py:37
  65.4 2.4 %collective-permute-start.18 = (bf16[2,128,256]{2,1,0:T(8,128)(2,1)S(1)}, bf16[2,128,256]{2,1,0:T(8,128)(2,1)S(1)}, u32[]{:S(2)}, u32[]{:S(2)}) collective-permute-start(bf16[2,128,256]{2,1,0:T(8,128)(2,1)S(1)} %get-tuple-element.43), channel_id=1, source_target_pairs={{0,6},{1,7},{2,0},{3,1},{4,2},{5,3},{6,4},{7,5},{8,14},{9,15},{10,... | collective-permute-start | bytes 393224 | tf_op jit(solution)/shard_map/sum_over_col/ppermute | solution.py:37
  67.9 3.2 %collective-permute-done.20 = bf16[2,128,256]{2,1,0:T(8,128)(2,1)S(1)} collective-permute-done((bf16[2,128,256]{2,1,0:T(8,128)(2,1)S(1)}, bf16[2,128,256]{2,1,0:T(8,128)(2,1)S(1)}, u32[]{:S(2)}, u32[]{:S(2)}) %collective-permute-start.20) | collective-permute-done | bytes 131104 | tf_op jit(solution)/shard_map/sum_over_col/ppermute | solution.py:37
  72.5 2.6 %pointwise.1 = (bf16[256,256]{1,0:T(8,128)(2,1)}, bf16[256,256]{1,0:T(8,128)(2,1)}, f32[256,256]{1,0:T(8,128)}, f32[256,256]{1,0:T(8,128)}) custom-call(bf16[256,256]{1,0:T(8,128)(2,1)} %bitcast.42, bf16[256,256]{1,0:T(8,128)(2,1)} %bitcast.47, bf16[256,256]{1,0:T(8,128)(2,1)} %bitcast.48, bf16[256,256]{1,0:T(8,128)(2,1)} %bitcast.49, ...), custom_call_target="tpu_custom_call" | custom-call | tf_op jit(solution)/shard_map/pointwise/pallas_call | solution.py:164
  75.8 7.6 %collective-permute-start.22 = (bf16[256,256]{1,0:T(8,128)(2,1)}, bf16[256,256]{1,0:T(8,128)(2,1)}, u32[]{:S(2)}, u32[]{:S(2)}) collective-permute-start(bf16[256,256]{1,0:T(8,128)(2,1)} %get-tuple-element.33), channel_id=1, source_target_pairs={{0,16},{1,17},{2,18},{3,19},{4,20},{5,21},{6,22},{7,23},{8,24},{9,... | collective-permute-start | bytes 393224 | tf_op jit(solution)/shard_map/gather_gradients/ppermute | solution.py:37
  83.4 1.6 collective-permute-start.23
  85.0 2.1 %gather_gradients.1 = f32[256,384]{1,0:T(8,128)} custom-call(f32[256,256]{1,0:T(8,128)} %get-tuple-element.34.total, f32[256,256]{1,0:T(8,128)} %get-tuple-element.35.pre_grad), custom_call_target="tpu_custom_call" | custom-call | tf_op jit(solution)/shard_map/gather_gradients/pallas_call | solution.py:186
  87.1 1.2 collective-permute-done.22
  88.3 1.9 %collective-permute-done.23 = bf16[256,256]{1,0:T(8,128)(2,1)} collective-permute-done((bf16[256,256]{1,0:T(8,128)(2,1)}, bf16[256,256]{1,0:T(8,128)(2,1)}, u32[]{:S(2)}, u32[]{:S(2)}) %collective-permute-start.23) | collective-permute-done | bytes 131104 | tf_op jit(solution)/shard_map/gather_gradients/ppermute | solution.py:37
  90.2 13.7 %all-to-all-start.1 = ((f32[32,8,384]{2,1,0:T(8,128)}), f32[32,8,384]{2,1,0:T(8,128)S(1)}, u32[]{:S(2)}, u32[]{:S(2)}) async-start(f32[32,8,384]{2,1,0:T(8,128)} %bitcast.33), calls=%async_computation.1 | async-start | bytes 786432 | tf_op jit(solution)/shard_map/sum_weight_grad/all_to_all | solution.py:290
  104.0 0.9 constant_dynamic-update-slice_fusion.3
  104.9 0.9 constant_dynamic-update-slice_fusion.2
  105.8 0.9 constant_dynamic-update-slice_fusion.1
  106.7 0.9 constant_dynamic-update-slice_fusion
  107.7 1.5 collective-permute-start.24
  109.1 2.4 %collective-permute-start.25 = (bf16[1024,256]{1,0:T(8,128)(2,1)S(1)}, bf16[1024,256]{1,0:T(8,128)(2,1)S(1)}, u32[]{:S(2)}, u32[]{:S(2)}) collective-permute-start(bf16[1024,256]{1,0:T(8,128)(2,1)S(1)} %constant_dynamic-update-slice_fusion), channel_id=1, source_target_pairs={{0,4},{1,5},{2,6},{3,7},{4,0},{5,1},{6,2},{7,3},{8,12},{9,13},{10,... | collective-permute-start | bytes 1572872 | tf_op jit(solution)/shard_map/gather_gradients/ppermute | solution.py:37
  111.5 1.2 collective-permute-start.26
  112.7 7.0 %all-to-all-done.1 = f32[32,8,384]{2,1,0:T(8,128)S(1)} async-done(((f32[32,8,384]{2,1,0:T(8,128)}), f32[32,8,384]{2,1,0:T(8,128)S(1)}, u32[]{:S(2)}, u32[]{:S(2)}) %all-to-all-start.1) | async-done | bytes 393248 | tf_op jit(solution)/shard_map/sum_weight_grad/all_to_all | solution.py:290
  119.8 11.4 %all_to_all.20 = f32[8,8,384]{2,1,0:T(8,128)S(1)} all-to-all(f32[8,8,384]{2,1,0:T(8,128)S(1)} %broadcast_in_dim.6), channel_id=1, replica_groups=mesh['row'=8,'col'=32] {'row'}, dimensions={0} | all-to-all | bytes 196608 | tf_op jit(solution)/shard_map/sum_weight_grad/all_to_all | solution.py:292
  132.0 5.5 %all-to-all-start.3 = ((f32[32,8,384]{2,1,0:T(8,128)}), f32[32,8,384]{2,1,0:T(8,128)}, u32[]{:S(2)}, u32[]{:S(2)}) async-start(f32[32,8,384]{2,1,0:T(8,128)} %broadcast_in_dim.7), calls=%async_computation.3 | async-start | bytes 786432 | tf_op jit(solution)/shard_map/sum_weight_grad/all_to_all | solution.py:304
  138.7 0.9 collective-permute-done.27
  142.7 6.9 %tiles_backward.1 = bf16[16,128,256]{2,1,0:T(8,128)(2,1)} custom-call(s32[1]{0:T(128)} %bitcast.31.live, s32[192]{0:T(256)} %get-tuple-element.40.take, s32[192]{0:T(256)} %bitcast.51, bf16[1,192,128,128]{3,2,1,0:T(8,128)(2,1)} %tiles.3, bf16[8,128,256]{2,1,0:T(8,128)(2,1)} %bitcast.34, bf16[8,128,256]{2,1,0:T(8,128)(2,1)} %bitcast.35, ...), custom_call_target="tpu_custom_call" | custom-call | flops 1610612736 | bytes 6291456 | tf_op jit(solution)/shard_map/tiles_backward/pallas_call | solution.py:109
  149.5 3.9 %all-to-all-done.3 = f32[32,8,384]{2,1,0:T(8,128)} async-done(((f32[32,8,384]{2,1,0:T(8,128)}), f32[32,8,384]{2,1,0:T(8,128)}, u32[]{:S(2)}, u32[]{:S(2)}) %all-to-all-start.3) | async-done | bytes 393248 | tf_op jit(solution)/shard_map/sum_weight_grad/all_to_all | solution.py:304
  153.4 4.2 %all-to-all-start = ((bf16[8,256,256]{2,1,0:T(8,128)(2,1)}), bf16[8,256,256]{2,1,0:T(8,128)(2,1)}, u32[]{:S(2)}, u32[]{:S(2)}) async-start(bf16[8,256,256]{2,1,0:T(8,128)(2,1)} %bitcast.32), calls=%async_computation | async-start | bytes 2097152 | tf_op jit(solution)/shard_map/sum_over_row/all_to_all | solution.py:300
  157.6 1.7 slice.152
  159.3 1.6 slice_reduce_fusion
  160.9 12.9 %all-to-all-done.pieces = bf16[8,256,256]{2,1,0:T(8,128)(2,1)} async-done(((bf16[8,256,256]{2,1,0:T(8,128)(2,1)}), bf16[8,256,256]{2,1,0:T(8,128)(2,1)}, u32[]{:S(2)}, u32[]{:S(2)}) %all-to-all-start) | async-done | bytes 1048608 | tf_op jit(solution)/shard_map/sum_over_row/all_to_all | solution.py:300
  173.8 3.1 %sum_over_row.1 = bf16[256,256]{1,0:T(8,128)(2,1)} custom-call(bf16[8,256,256]{2,1,0:T(8,128)(2,1)} %all-to-all-done.pieces, bf16[256,256]{1,0:T(8,128)(2,1)} %weight.1), custom_call_target="tpu_custom_call" | custom-call | tf_op jit(solution)/shard_map/sum_over_row/pallas_call | solution.py:217
  (74 shorter events, 10.7 us)
Async XLA Ops:
  0.6 11.7 %collective-permute-start.6 = (bf16[256,256]{1,0:T(8,128)(2,1)}, bf16[256,256]{1,0:T(8,128)(2,1)}, u32[]{:S(2)}, u32[]{:S(2)}) collective-permute-start(bf16[256,256]{1,0:T(8,128)(2,1)} %param.8), channel_id=1, source_target_pairs={{0,224},{32,192},{64,32},{96,0},{128,96},{160,64},{192,160},{224,1... | collective-permute-start | bytes 393224 | tf_op jit(solution)/shard_map/gather_features/ppermute | solution.py:27
  5.4 7.0 %collective-permute-start = (bf16[256,256]{1,0:T(8,128)(2,1)}, bf16[256,256]{1,0:T(8,128)(2,1)}, u32[]{:S(2)}, u32[]{:S(2)}) collective-permute-start(bf16[256,256]{1,0:T(8,128)(2,1)} %param.8), channel_id=1, source_target_pairs={{0,32},{32,0},{64,96},{96,64},{128,160},{160,128},{192,224},{224,1... | collective-permute-start | bytes 393224 | tf_op jit(solution)/shard_map/gather_features/ppermute | solution.py:27
  5.4 10.1 %collective-permute-start.1 = (bf16[256,256]{1,0:T(8,128)(2,1)}, bf16[256,256]{1,0:T(8,128)(2,1)}, u32[]{:S(2)}, u32[]{:S(2)}) collective-permute-start(bf16[256,256]{1,0:T(8,128)(2,1)} %param.8), channel_id=1, source_target_pairs={{0,64},{32,96},{64,128},{96,160},{128,192},{160,224},{192,0},{224,... | collective-permute-start | bytes 393224 | tf_op jit(solution)/shard_map/gather_features/ppermute | solution.py:27
  5.4 10.1 %collective-permute-start.2 = (bf16[256,256]{1,0:T(8,128)(2,1)}, bf16[256,256]{1,0:T(8,128)(2,1)}, u32[]{:S(2)}, u32[]{:S(2)}) collective-permute-start(bf16[256,256]{1,0:T(8,128)(2,1)} %param.8), channel_id=1, source_target_pairs={{0,96},{32,64},{64,160},{96,128},{128,224},{160,192},{192,32},{224... | collective-permute-start | bytes 393224 | tf_op jit(solution)/shard_map/gather_features/ppermute | solution.py:27
  6.8 11.5 %collective-permute-start.3 = (bf16[256,256]{1,0:T(8,128)(2,1)}, bf16[256,256]{1,0:T(8,128)(2,1)}, u32[]{:S(2)}, u32[]{:S(2)}) collective-permute-start(bf16[256,256]{1,0:T(8,128)(2,1)} %param.8), channel_id=1, source_target_pairs={{0,128},{32,160},{64,192},{96,224},{128,0},{160,32},{192,64},{224,... | collective-permute-start | bytes 393224 | tf_op jit(solution)/shard_map/gather_features/ppermute | solution.py:27
  12.4 6.6 %collective-permute-start.4 = (bf16[256,256]{1,0:T(8,128)(2,1)}, bf16[256,256]{1,0:T(8,128)(2,1)}, u32[]{:S(2)}, u32[]{:S(2)}) collective-permute-start(bf16[256,256]{1,0:T(8,128)(2,1)} %param.8), channel_id=1, source_target_pairs={{0,160},{32,128},{64,224},{96,192},{128,32},{160,0},{192,96},{224,... | collective-permute-start | bytes 393224 | tf_op jit(solution)/shard_map/gather_features/ppermute | solution.py:27
  12.4 7.3 %collective-permute-start.5 = (bf16[256,256]{1,0:T(8,128)(2,1)}, bf16[256,256]{1,0:T(8,128)(2,1)}, u32[]{:S(2)}, u32[]{:S(2)}) collective-permute-start(bf16[256,256]{1,0:T(8,128)(2,1)} %param.8), channel_id=1, source_target_pairs={{0,192},{32,224},{64,0},{96,32},{128,64},{160,96},{192,128},{224,1... | collective-permute-start | bytes 393224 | tf_op jit(solution)/shard_map/gather_features/ppermute | solution.py:27
  26.6 37.8 %copy-start = (bf16[16,128,256]{2,1,0:T(8,128)(2,1)S(1)}, bf16[16,128,256]{2,1,0:T(8,128)(2,1)}, u32[]{:S(2)}) copy-start(bf16[16,128,256]{2,1,0:T(8,128)(2,1)} %get-tuple-element.22) | copy-start | bytes 3145732
  26.6 3.9 %collective-permute-start.11 = (bf16[16,128,256]{2,1,0:T(8,128)(2,1)}, bf16[16,128,256]{2,1,0:T(8,128)(2,1)S(1)}, u32[]{:S(2)}, u32[]{:S(2)}) collective-permute-start(bf16[16,128,256]{2,1,0:T(8,128)(2,1)} %get-tuple-element.25), channel_id=1, source_target_pairs={{0,1},{1,0},{2,3},{3,2},{4,5},{5,4},{6,7},{7,6},{8,9},{9,8},{10,11... | collective-permute-start | bytes 3145736 | tf_op jit(solution)/shard_map/sum_over_col/ppermute | solution.py:37
  28.0 13.1 %collective-permute-start.7 = (bf16[16,128,256]{2,1,0:T(8,128)(2,1)}, bf16[16,128,256]{2,1,0:T(8,128)(2,1)S(1)}, u32[]{:S(2)}, u32[]{:S(2)}) collective-permute-start(bf16[16,128,256]{2,1,0:T(8,128)(2,1)} %get-tuple-element.23), channel_id=1, source_target_pairs={{0,1},{1,0},{2,3},{3,2},{4,5},{5,4},{6,7},{7,6},{8,9},{9,8},{10,11... | collective-permute-start | bytes 3145736 | tf_op jit(solution)/shard_map/sum_over_col/ppermute | solution.py:37
  32.0 12.9 %collective-permute-start.12 = (bf16[4,128,256]{2,1,0:T(8,128)(2,1)S(1)}, bf16[4,128,256]{2,1,0:T(8,128)(2,1)S(1)}, u32[]{:S(2)}, u32[]{:S(2)}) collective-permute-start(bf16[4,128,256]{2,1,0:T(8,128)(2,1)S(1)} %get-tuple-element.50), channel_id=1, source_target_pairs={{0,4},{1,5},{2,6},{3,7},{4,0},{5,1},{6,2},{7,3},{8,12},{9,13},{10,... | collective-permute-start | bytes 786440 | tf_op jit(solution)/shard_map/sum_over_col/ppermute | solution.py:37
  38.4 12.7 %collective-permute-start.13 = (bf16[4,128,256]{2,1,0:T(8,128)(2,1)S(1)}, bf16[4,128,256]{2,1,0:T(8,128)(2,1)S(1)}, u32[]{:S(2)}, u32[]{:S(2)}) collective-permute-start(bf16[4,128,256]{2,1,0:T(8,128)(2,1)S(1)} %get-tuple-element.49), channel_id=1, source_target_pairs={{0,2},{1,3},{2,4},{3,5},{4,6},{5,7},{6,0},{7,1},{8,10},{9,11},{10,... | collective-permute-start | bytes 786440 | tf_op jit(solution)/shard_map/sum_over_col/ppermute | solution.py:37
  38.4 12.7 %collective-permute-start.14 = (bf16[4,128,256]{2,1,0:T(8,128)(2,1)S(1)}, bf16[4,128,256]{2,1,0:T(8,128)(2,1)S(1)}, u32[]{:S(2)}, u32[]{:S(2)}) collective-permute-start(bf16[4,128,256]{2,1,0:T(8,128)(2,1)S(1)} %get-tuple-element.48), channel_id=1, source_target_pairs={{0,6},{1,7},{2,0},{3,1},{4,2},{5,3},{6,4},{7,5},{8,14},{9,15},{10,... | collective-permute-start | bytes 786440 | tf_op jit(solution)/shard_map/sum_over_col/ppermute | solution.py:37
  42.4 16.9 %collective-permute-start.10 = (bf16[2,128,256]{2,1,0:T(8,128)(2,1)S(1)}, bf16[2,128,256]{2,1,0:T(8,128)(2,1)S(1)}, u32[]{:S(2)}, u32[]{:S(2)}) collective-permute-start(bf16[2,128,256]{2,1,0:T(8,128)(2,1)S(1)} %get-tuple-element.51), channel_id=1, source_target_pairs={{0,6},{1,7},{2,0},{3,1},{4,2},{5,3},{6,4},{7,5},{8,14},{9,15},{10,... | collective-permute-start | bytes 393224 | tf_op jit(solution)/shard_map/sum_over_col/ppermute | solution.py:37
  42.5 16.8 %collective-permute-start.8 = (bf16[2,128,256]{2,1,0:T(8,128)(2,1)S(1)}, bf16[2,128,256]{2,1,0:T(8,128)(2,1)S(1)}, u32[]{:S(2)}, u32[]{:S(2)}) collective-permute-start(bf16[2,128,256]{2,1,0:T(8,128)(2,1)S(1)} %get-tuple-element.53), channel_id=1, source_target_pairs={{0,4},{1,5},{2,6},{3,7},{4,0},{5,1},{6,2},{7,3},{8,12},{9,13},{10,... | collective-permute-start | bytes 393224 | tf_op jit(solution)/shard_map/sum_over_col/ppermute | solution.py:37
  44.9 14.4 %collective-permute-start.9 = (bf16[2,128,256]{2,1,0:T(8,128)(2,1)S(1)}, bf16[2,128,256]{2,1,0:T(8,128)(2,1)S(1)}, u32[]{:S(2)}, u32[]{:S(2)}) collective-permute-start(bf16[2,128,256]{2,1,0:T(8,128)(2,1)S(1)} %get-tuple-element.52), channel_id=1, source_target_pairs={{0,2},{1,3},{2,4},{3,5},{4,6},{5,7},{6,0},{7,1},{8,10},{9,11},{10,... | collective-permute-start | bytes 393224 | tf_op jit(solution)/shard_map/sum_over_col/ppermute | solution.py:37
  51.3 10.0 %collective-permute-start.15 = (bf16[2,128,256]{2,1,0:T(8,128)(2,1)S(1)}, bf16[2,128,256]{2,1,0:T(8,128)(2,1)S(1)}, u32[]{:S(2)}, u32[]{:S(2)}) collective-permute-start(bf16[2,128,256]{2,1,0:T(8,128)(2,1)S(1)} %get-tuple-element.56), channel_id=1, source_target_pairs={{0,8},{1,9},{2,10},{3,11},{4,12},{5,13},{6,14},{7,15},{8,16},{9,17... | collective-permute-start | bytes 393224 | tf_op jit(solution)/shard_map/sum_over_col/ppermute | solution.py:37
  54.4 13.5 %collective-permute-start.19 = (bf16[2,128,256]{2,1,0:T(8,128)(2,1)S(1)}, bf16[2,128,256]{2,1,0:T(8,128)(2,1)S(1)}, u32[]{:S(2)}, u32[]{:S(2)}) collective-permute-start(bf16[2,128,256]{2,1,0:T(8,128)(2,1)S(1)} %get-tuple-element.55), channel_id=1, source_target_pairs={{0,16},{1,17},{2,18},{3,19},{4,20},{5,21},{6,22},{7,23},{8,24},{9,... | collective-permute-start | bytes 393224 | tf_op jit(solution)/shard_map/sum_over_col/ppermute | solution.py:37
  61.3 10.5 %copy-start.9 = (bf16[2,128,256]{2,1,0:T(8,128)(2,1)}, bf16[2,128,256]{2,1,0:T(8,128)(2,1)S(1)}, u32[]{:S(2)}) copy-start(bf16[2,128,256]{2,1,0:T(8,128)(2,1)S(1)} %collective-permute-done.15) | copy-start | bytes 393220
  61.4 9.7 %collective-permute-start.20 = (bf16[2,128,256]{2,1,0:T(8,128)(2,1)S(1)}, bf16[2,128,256]{2,1,0:T(8,128)(2,1)S(1)}, u32[]{:S(2)}, u32[]{:S(2)}) collective-permute-start(bf16[2,128,256]{2,1,0:T(8,128)(2,1)S(1)} %add_convert_fusion.4), channel_id=1, source_target_pairs={{0,24},{1,25},{2,26},{3,27},{4,28},{5,29},{6,30},{7,31},{8,0},{9,1... | collective-permute-start | bytes 393224 | tf_op jit(solution)/shard_map/sum_over_col/ppermute | solution.py:37
  65.2 5.9 %collective-permute-start.16 = (bf16[2,128,256]{2,1,0:T(8,128)(2,1)S(1)}, bf16[2,128,256]{2,1,0:T(8,128)(2,1)S(1)}, u32[]{:S(2)}, u32[]{:S(2)}) collective-permute-start(bf16[2,128,256]{2,1,0:T(8,128)(2,1)S(1)} %get-tuple-element.45), channel_id=1, source_target_pairs={{0,4},{1,5},{2,6},{3,7},{4,0},{5,1},{6,2},{7,3},{8,12},{9,13},{10,... | collective-permute-start | bytes 393224 | tf_op jit(solution)/shard_map/sum_over_col/ppermute | solution.py:37
  65.2 6.6 %collective-permute-start.17 = (bf16[2,128,256]{2,1,0:T(8,128)(2,1)S(1)}, bf16[2,128,256]{2,1,0:T(8,128)(2,1)S(1)}, u32[]{:S(2)}, u32[]{:S(2)}) collective-permute-start(bf16[2,128,256]{2,1,0:T(8,128)(2,1)S(1)} %get-tuple-element.44), channel_id=1, source_target_pairs={{0,2},{1,3},{2,4},{3,5},{4,6},{5,7},{6,0},{7,1},{8,10},{9,11},{10,... | collective-permute-start | bytes 393224 | tf_op jit(solution)/shard_map/sum_over_col/ppermute | solution.py:37
  65.4 6.3 %collective-permute-start.18 = (bf16[2,128,256]{2,1,0:T(8,128)(2,1)S(1)}, bf16[2,128,256]{2,1,0:T(8,128)(2,1)S(1)}, u32[]{:S(2)}, u32[]{:S(2)}) collective-permute-start(bf16[2,128,256]{2,1,0:T(8,128)(2,1)S(1)} %get-tuple-element.43), channel_id=1, source_target_pairs={{0,6},{1,7},{2,0},{3,1},{4,2},{5,3},{6,4},{7,5},{8,14},{9,15},{10,... | collective-permute-start | bytes 393224 | tf_op jit(solution)/shard_map/sum_over_col/ppermute | solution.py:37
  67.9 3.9 %copy-start.10 = (bf16[2,128,256]{2,1,0:T(8,128)(2,1)}, bf16[2,128,256]{2,1,0:T(8,128)(2,1)S(1)}, u32[]{:S(2)}) copy-start(bf16[2,128,256]{2,1,0:T(8,128)(2,1)S(1)} %collective-permute-done.19) | copy-start | bytes 393220
  71.1 0.7 copy-start.11
  71.1 0.7 copy-start.12
  71.8 0.7 copy-start.14
  75.1 12.1 %collective-permute-start.21 = (bf16[256,256]{1,0:T(8,128)(2,1)}, bf16[256,256]{1,0:T(8,128)(2,1)}, u32[]{:S(2)}, u32[]{:S(2)}) collective-permute-start(bf16[256,256]{1,0:T(8,128)(2,1)} %get-tuple-element.33), channel_id=1, source_target_pairs={{0,8},{1,9},{2,10},{3,11},{4,12},{5,13},{6,14},{7,15},{8,16},{9,17... | collective-permute-start | bytes 393224 | tf_op jit(solution)/shard_map/gather_gradients/ppermute | solution.py:37
  75.8 12.4 %collective-permute-start.22 = (bf16[256,256]{1,0:T(8,128)(2,1)}, bf16[256,256]{1,0:T(8,128)(2,1)}, u32[]{:S(2)}, u32[]{:S(2)}) collective-permute-start(bf16[256,256]{1,0:T(8,128)(2,1)} %get-tuple-element.33), channel_id=1, source_target_pairs={{0,16},{1,17},{2,18},{3,19},{4,20},{5,21},{6,22},{7,23},{8,24},{9,... | collective-permute-start | bytes 393224 | tf_op jit(solution)/shard_map/gather_gradients/ppermute | solution.py:37
  83.4 6.8 %collective-permute-start.23 = (bf16[256,256]{1,0:T(8,128)(2,1)}, bf16[256,256]{1,0:T(8,128)(2,1)}, u32[]{:S(2)}, u32[]{:S(2)}) collective-permute-start(bf16[256,256]{1,0:T(8,128)(2,1)} %get-tuple-element.33), channel_id=1, source_target_pairs={{0,24},{1,25},{2,26},{3,27},{4,28},{5,29},{6,30},{7,31},{8,0},{9,1... | collective-permute-start | bytes 393224 | tf_op jit(solution)/shard_map/gather_gradients/ppermute | solution.py:37
  90.2 29.5 %all-to-all-start.1 = ((f32[32,8,384]{2,1,0:T(8,128)}), f32[32,8,384]{2,1,0:T(8,128)S(1)}, u32[]{:S(2)}, u32[]{:S(2)}) async-start(f32[32,8,384]{2,1,0:T(8,128)} %bitcast.33), calls=%async_computation.1 | async-start | bytes 786432 | tf_op jit(solution)/shard_map/sum_weight_grad/all_to_all | solution.py:290
  107.6 29.9 %copy-start.1 = (bf16[1024,256]{1,0:T(8,128)(2,1)}, bf16[1024,256]{1,0:T(8,128)(2,1)S(1)}, u32[]{:S(2)}) copy-start(bf16[1024,256]{1,0:T(8,128)(2,1)S(1)} %constant_dynamic-update-slice_fusion) | copy-start | bytes 1572868
  107.7 30.4 %collective-permute-start.24 = (bf16[1024,256]{1,0:T(8,128)(2,1)S(1)}, bf16[1024,256]{1,0:T(8,128)(2,1)S(1)}, u32[]{:S(2)}, u32[]{:S(2)}) collective-permute-start(bf16[1024,256]{1,0:T(8,128)(2,1)S(1)} %constant_dynamic-update-slice_fusion), channel_id=1, source_target_pairs={{0,2},{1,3},{2,4},{3,5},{4,6},{5,7},{6,0},{7,1},{8,10},{9,11},{10,... | collective-permute-start | bytes 1572872 | tf_op jit(solution)/shard_map/gather_gradients/ppermute | solution.py:37
  109.1 29.0 %collective-permute-start.25 = (bf16[1024,256]{1,0:T(8,128)(2,1)S(1)}, bf16[1024,256]{1,0:T(8,128)(2,1)S(1)}, u32[]{:S(2)}, u32[]{:S(2)}) collective-permute-start(bf16[1024,256]{1,0:T(8,128)(2,1)S(1)} %constant_dynamic-update-slice_fusion), channel_id=1, source_target_pairs={{0,4},{1,5},{2,6},{3,7},{4,0},{5,1},{6,2},{7,3},{8,12},{9,13},{10,... | collective-permute-start | bytes 1572872 | tf_op jit(solution)/shard_map/gather_gradients/ppermute | solution.py:37
  111.5 27.0 %collective-permute-start.26 = (bf16[1024,256]{1,0:T(8,128)(2,1)S(1)}, bf16[1024,256]{1,0:T(8,128)(2,1)S(1)}, u32[]{:S(2)}, u32[]{:S(2)}) collective-permute-start(bf16[1024,256]{1,0:T(8,128)(2,1)S(1)} %constant_dynamic-update-slice_fusion), channel_id=1, source_target_pairs={{0,6},{1,7},{2,0},{3,1},{4,2},{5,3},{6,4},{7,5},{8,14},{9,15},{10,... | collective-permute-start | bytes 1572872 | tf_op jit(solution)/shard_map/gather_gradients/ppermute | solution.py:37
  132.0 21.4 %all-to-all-start.3 = ((f32[32,8,384]{2,1,0:T(8,128)}), f32[32,8,384]{2,1,0:T(8,128)}, u32[]{:S(2)}, u32[]{:S(2)}) async-start(f32[32,8,384]{2,1,0:T(8,128)} %broadcast_in_dim.7), calls=%async_computation.3 | async-start | bytes 786432 | tf_op jit(solution)/shard_map/sum_weight_grad/all_to_all | solution.py:304
  137.5 2.0 %collective-permute-start.27 = (bf16[1024,256]{1,0:T(8,128)(2,1)S(1)}, bf16[1024,256]{1,0:T(8,128)(2,1)S(1)}, u32[]{:S(2)}, u32[]{:S(2)}) collective-permute-start(bf16[1024,256]{1,0:T(8,128)(2,1)S(1)} %constant_dynamic-update-slice_fusion), channel_id=1, source_target_pairs={{0,1},{1,0},{2,3},{3,2},{4,5},{5,4},{6,7},{7,6},{8,9},{9,8},{10,11... | collective-permute-start | bytes 1572872 | tf_op jit(solution)/shard_map/gather_gradients/ppermute | solution.py:37
  138.0 1.5 copy-start.2
  138.0 2.3 %collective-permute-start.28 = (bf16[1024,256]{1,0:T(8,128)(2,1)S(1)}, bf16[1024,256]{1,0:T(8,128)(2,1)S(1)}, u32[]{:S(2)}, u32[]{:S(2)}) collective-permute-start(bf16[1024,256]{1,0:T(8,128)(2,1)S(1)} %collective-permute-done.24), channel_id=1, source_target_pairs={{0,1},{1,0},{2,3},{3,2},{4,5},{5,4},{6,7},{7,6},{8,9},{9,8},{10,11... | collective-permute-start | bytes 1572872 | tf_op jit(solution)/shard_map/gather_gradients/ppermute | solution.py:37
  138.2 2.2 %copy-start.3 = (bf16[1024,256]{1,0:T(8,128)(2,1)}, bf16[1024,256]{1,0:T(8,128)(2,1)S(1)}, u32[]{:S(2)}) copy-start(bf16[1024,256]{1,0:T(8,128)(2,1)S(1)} %collective-permute-done.25) | copy-start | bytes 1572868
  138.2 2.9 %collective-permute-start.29 = (bf16[1024,256]{1,0:T(8,128)(2,1)S(1)}, bf16[1024,256]{1,0:T(8,128)(2,1)S(1)}, u32[]{:S(2)}, u32[]{:S(2)}) collective-permute-start(bf16[1024,256]{1,0:T(8,128)(2,1)S(1)} %collective-permute-done.25), channel_id=1, source_target_pairs={{0,1},{1,0},{2,3},{3,2},{4,5},{5,4},{6,7},{7,6},{8,9},{9,8},{10,11... | collective-permute-start | bytes 1572872 | tf_op jit(solution)/shard_map/gather_gradients/ppermute | solution.py:37
  138.6 2.5 %copy-start.4 = (bf16[1024,256]{1,0:T(8,128)(2,1)}, bf16[1024,256]{1,0:T(8,128)(2,1)S(1)}, u32[]{:S(2)}) copy-start(bf16[1024,256]{1,0:T(8,128)(2,1)S(1)} %collective-permute-done.26) | copy-start | bytes 1572868
  138.6 3.3 %collective-permute-start.30 = (bf16[1024,256]{1,0:T(8,128)(2,1)S(1)}, bf16[1024,256]{1,0:T(8,128)(2,1)S(1)}, u32[]{:S(2)}, u32[]{:S(2)}) collective-permute-start(bf16[1024,256]{1,0:T(8,128)(2,1)S(1)} %collective-permute-done.26), channel_id=1, source_target_pairs={{0,1},{1,0},{2,3},{3,2},{4,5},{5,4},{6,7},{7,6},{8,9},{9,8},{10,11... | collective-permute-start | bytes 1572872 | tf_op jit(solution)/shard_map/gather_gradients/ppermute | solution.py:37
  139.6 2.2 %copy-start.5 = (bf16[1024,256]{1,0:T(8,128)(2,1)}, bf16[1024,256]{1,0:T(8,128)(2,1)S(1)}, u32[]{:S(2)}) copy-start(bf16[1024,256]{1,0:T(8,128)(2,1)S(1)} %collective-permute-done.27) | copy-start | bytes 1572868
  140.3 1.5 copy-start.6
  141.1 0.8 copy-start.7
  141.8 0.8 copy-start.8
  153.4 20.4 %all-to-all-start = ((bf16[8,256,256]{2,1,0:T(8,128)(2,1)}), bf16[8,256,256]{2,1,0:T(8,128)(2,1)}, u32[]{:S(2)}, u32[]{:S(2)}) async-start(bf16[8,256,256]{2,1,0:T(8,128)(2,1)} %bitcast.32), calls=%async_computation | async-start | bytes 2097152 | tf_op jit(solution)/shard_map/sum_over_row/all_to_all | solution.py:300
  (1 other events, 0.7 us)

commit v5 on v4

--- a/solution.py
+++ b/solution.py
@@ -15,7 +15,8 @@
 N_ROW = N_X * N_ZL
 N_COL = N_ZH * N_Y * N_CORE
 GROUP = 24
-VMEM_LIMIT = 65408 * 1024
+VMEM_LIMIT = 60 * 1024 * 1024
+VMEM_MOST = 65408 * 1024
 LANES = 128
 
 
@@ -99,7 +100,7 @@
         copy.wait()
 
 
-def tile_sum(adjacency, live, take, put, sources, out_sizes, transposed):
+def tile_sum(adjacency, live, take, put, sources, out_sizes, transposed, vmem):
     slots, tile = adjacency.shape[1], adjacency.shape[2]
     width = sources[0].shape[-1]
     sources = [s.reshape(-1, tile, width) for s in sources]
@@ -123,7 +124,7 @@
             jax.ShapeDtypeStruct((size, tile, width), jnp.bfloat16)
             for size in out_sizes
         ],
-        compiler_params=pltpu.CompilerParams(vmem_limit_bytes=VMEM_LIMIT),
+        compiler_params=pltpu.CompilerParams(vmem_limit_bytes=vmem),
         cost_estimate=pl.CostEstimate(
             flops=2 * slots * tile * tile * width,
             bytes_accessed=slots * tile * tile * 2,
@@ -192,17 +193,10 @@
     )(total, pre_grad)
 
 
-def last_kernel(pieces, weight, out, held, sems):
-    copies = [
-        pltpu.make_async_copy(pieces.at[k], held.at[k], sems.at[k])
-        for k in range(held.shape[0])
-    ]
-    for copy in copies:
-        copy.start()
-    total = jnp.zeros(out.shape, jnp.float32)
-    for k, copy in enumerate(copies):
-        copy.wait()
-        total += held[k].astype(jnp.float32)
+def last_kernel(pieces, weight, out):
+    total = pieces[0].astype(jnp.float32)
+    for k in range(1, pieces.shape[0]):
+        total += pieces[k].astype(jnp.float32)
     out[...] = lax.dot_general(
         total.astype(jnp.bfloat16),
         weight[...],
@@ -216,13 +210,9 @@
     vmem = pl.BlockSpec(memory_space=pltpu.VMEM)
     return pl.pallas_call(
         last_kernel,
-        in_specs=[pl.BlockSpec(memory_space=pltpu.HBM), vmem],
+        in_specs=[vmem] * 2,
         out_specs=vmem,
         out_shape=jax.ShapeDtypeStruct((rows, width), jnp.bfloat16),
-        scratch_shapes=[
-            pltpu.VMEM(pieces.shape, jnp.bfloat16),
-            pltpu.SemaphoreType.DMA((pieces.shape[0],)),
-        ],
         compiler_params=pltpu.CompilerParams(vmem_limit_bytes=VMEM_LIMIT),
     )(pieces, weight)
 
@@ -260,24 +250,22 @@
         sources = [features] + [row_shift(features, *m) for m in moves[1:]]
     with jax.named_scope("tiles_forward"):
         parts = tile_sum(
-            adjacency, live, take_cols, put_rows, sources, [8 * per] * 4, False
+            adjacency, live, take_cols, put_rows, sources, [8 * per] * 4, False, VMEM_MOST
         )
     with jax.named_scope("sum_over_col"):
-        others = [col_shift(send, dcore=1) for send in parts[2:]]
-
-        def over_y(keep, other, first, size):
-            added = []
-            for k in range(N_Y):
-                rows = slice(2 * per * k + first * per, 2 * per * k + (first + size) * per)
-                added.append(merge([keep[rows], other[rows]]))
-            return [added[0]] + [col_shift(added[k], dy=k) for k in (2, 1, 3)]
-
-        both = over_y(parts[0], others[0], 0, 2)
-        far = col_shift(merge([p[:per] for p in both]), dzh=2)
-        near = col_shift(merge([p[per:] for p in both]), dzh=1)
-        back = over_y(parts[1], others[1], 0, 1)
-        *back, near, others[1] = lax.optimization_barrier((*back, near, others[1]))
-        pieces = over_y(parts[1], others[1], 1, 1) + [far, near, col_shift(merge(back), dzh=3)]
+        sums, pieces = [], []
+        for keep, send in zip(parts[:2], parts[2:]):
+            other = col_shift(send, dcore=1)
+            cut = [slice(2 * per * k, 2 * per * (k + 1)) for k in range(N_Y)]
+            added = [merge([keep[s], other[s]]) for s in cut]
+            arrived = [added[0]] + [col_shift(added[k], dy=k) for k in (2, 1, 3)]
+            if pieces:
+                *arrived, pieces[1] = lax.optimization_barrier((*arrived, pieces[1]))
+            sums = [merge([p[:per] for p in arrived]), merge([p[per:] for p in arrived])]
+            if not pieces:
+                pieces = [col_shift(sums[0], dzh=2), col_shift(sums[1], dzh=1)]
+            else:
+                pieces += [col_shift(sums[0], dzh=3), sums[1]]
         pieces = [p.reshape(vertices, width) for p in pieces]
     with jax.named_scope("pointwise"):
         layer_out, grad, total, pre_grad = middle(pieces, weight, bias, cotangent)
@@ -292,9 +280,13 @@
         load = jnp.sum(lax.all_to_all(load, "row", 0, 0, tiled=True), axis=0) * scale
     with jax.named_scope("gather_gradients"):
         here += [col_shift(here[0], dy=k) for k in range(1, N_Y)]
+        *here, load = lax.optimization_barrier((*here, load))
         there = [col_shift(p, dcore=1) for p in here]
+        *there, load = lax.optimization_barrier((*there, load))
     with jax.named_scope("tiles_backward"):
-        (back,) = tile_sum(adjacency, live, take_rows, c, here + there, [N_ROW * per], True)
+        (back,) = tile_sum(
+            adjacency, live, take_rows, c, here + there, [N_ROW * per], True, VMEM_LIMIT
+        )
     with jax.named_scope("sum_over_row"):
         back = back.reshape(N_ROW, vertices, width)
         back = lax.all_to_all(back, "row", 0, 0, tiled=True)

time: 176 us -> 184 us (1.045)
  waiting for transfers between devices: 49.7 us -> 74.6 us
  starting transfers between devices: 77.1 us -> 67.2 us
  local copies, waits for them, and re-layouts: 9.26 us -> 5.59 us
  Pallas kernels: 21.6 us -> 18.1 us
    ppermute x24 -> x21, waiting for transfers between devices: 21.7 us -> 33.2 us  [col_shift(): return lax.ppermute(value, 'col', pairs)]
    all_to_all x1, starting transfers between devices: 13.7 us -> 6.28 us  [shards(): load = jnp.sum(lax.all_to_all(load, 'col', 0, 0, tiled=True), axis=0)]
    all_to_all x1, waiting for transfers between devices: 3.87 us -> 9.6 us  [shards(): load = lax.all_to_all(load, 'col', 0, 0, tiled=True).reshape(width, -1)]
    all_to_all x1, waiting for transfers between devices: 7.04 us -> 10.6 us  [shards(): load = jnp.sum(lax.all_to_all(load, 'col', 0, 0, tiled=True), axis=0)]
    ppermute x7, waiting for transfers between devices: 4.22 us -> 7.36 us  [row_shift(): return lax.ppermute(value, 'row', pairs)]
    pallas_call x2, Pallas kernels: 13.8 us -> 11.4 us  [tile_sum(): pl.pallas_call(functools.partial(tile_kernel, transposed, src_sizes, out_...]
    slice x2, local copies, waits for them, and re-layouts: 3.25 us -> 1.4 us  [shards(): weight_grad, bias_grad = (load[:, :width], load[:, width])]
    ppermute x24 -> x21, starting transfers between devices: 42.1 us -> 40.5 us  [col_shift(): return lax.ppermute(value, 'col', pairs)]
  transfers between devices with their start and end apart: 34 -> 31, of which waited for: 18 -> 20; matrix products, arithmetic and copies ran while one was open for 8% -> 5% of each run, Pallas kernels for 5% -> 4%
where the time goes in v5:
time: 184 us; the launch traced here: 183 us
  waiting for transfers between devices  74.6 us (41%)
  starting transfers between devices  67.2 us (37%)
  Pallas kernels  18.1 us (10%)
  blocking collectives  9.76 us (5%)
  other arithmetic  6.53 us (4%)
  local copies, waits for them, and re-layouts  5.59 us (3%)
    ppermute x21, starting transfers between devices, col_shift(): return lax.ppermute(value, 'col', pairs)  40.5 us
    ppermute x21, waiting for transfers between devices, col_shift(): return lax.ppermute(value, 'col', pairs)  33.2 us
    all_to_all x1, waiting for transfers between devices, shards(): back = lax.all_to_all(back, 'row', 0, 0, tiled=True)  13.8 us
    pallas_call x2, Pallas kernels, tile_sum(): pl.pallas_call(functools.partial(tile_kernel, transposed, src_sizes, out_...  11.4 us
    all_to_all x1, waiting for transfers between devices, shards(): load = jnp.sum(lax.all_to_all(load, 'col', 0, 0, tiled=True), axis=0)  10.6 us
    ppermute x7, starting transfers between devices, row_shift(): return lax.ppermute(value, 'row', pairs)  10 us
    all_to_all x1, blocking collectives, shards(): lax.all_to_all(load, 'row', 0, 0, tiled=True)  9.76 us
    all_to_all x1, waiting for transfers between devices, shards(): load = lax.all_to_all(load, 'col', 0, 0, tiled=True).reshape(width, -1)  9.6 us
  transfers between devices with their start and end apart: 31, of which 20 were waited for; matrix products, arithmetic and copies ran while one was open for 5% of the time, Pallas kernels for 4%

profile of v5, /device:TPU:1, one launch (start us, length us, event | category | flops | bytes accessed | tf_op | source)
XLA Modules:
  0.0 183.3 jit_solution(6566410441620890137)
XLA Ops:
  0.6 5.0 %collective-permute-start.4 = (bf16[256,256]{1,0:T(8,128)(2,1)}, bf16[256,256]{1,0:T(8,128)(2,1)}, u32[]{:S(2)}, u32[]{:S(2)}) collective-permute-start(bf16[256,256]{1,0:T(8,128)(2,1)} %param.8), channel_id=1, source_target_pairs={{0,160},{32,128},{64,224},{96,192},{128,32},{160,0},{192,96},{224,... | collective-permute-start | bytes 393224 | tf_op jit(solution)/shard_map/gather_features/ppermute | solution.py:28
  6.6 1.2 collective-permute-start.1
  7.8 1.6 collective-permute-start
  10.1 1.3 multiply_add_fusion
  11.4 1.2 collective-permute-start.6
  12.6 3.9 %collective-permute-done.3 = bf16[256,256]{1,0:T(8,128)(2,1)} collective-permute-done((bf16[256,256]{1,0:T(8,128)(2,1)}, bf16[256,256]{1,0:T(8,128)(2,1)}, u32[]{:S(2)}, u32[]{:S(2)}) %collective-permute-start.3) | collective-permute-done | bytes 131104 | tf_op jit(solution)/shard_map/gather_features/ppermute | solution.py:28
  16.5 1.3 fusion.2
  17.8 1.8 collective-permute-done.1
  19.6 1.7 collective-permute-done.5
  21.3 5.7 %tiles_forward.1 = (bf16[16,128,256]{2,1,0:T(8,128)(2,1)}, bf16[16,128,256]{2,1,0:T(8,128)(2,1)}, bf16[16,128,256]{2,1,0:T(8,128)(2,1)}, bf16[16,128,256]{2,1,0:T(8,128)(2,1)}) custom-call(s32[1]{0:T(128)} %bitcast.27.live, s32[192]{0:T(256)} %get-tuple-element.73.take, s32[192]{0:T(256)} %get-tuple-element.74.put, bf16[1,192,128,128]{3,2,1,0:T(8,128)(2,1)} %tiles.3, ...), custom_call_target="tpu_custom_call" | custom-call | flops 1610612736 | bytes 6291456 | tf_op jit(solution)/shard_map/tiles_forward/pallas_call | solution.py:110
  27.0 2.9 %collective-permute-start.7 = (bf16[16,128,256]{2,1,0:T(8,128)(2,1)}, bf16[16,128,256]{2,1,0:T(8,128)(2,1)S(1)}, u32[]{:S(2)}, u32[]{:S(2)}) collective-permute-start(bf16[16,128,256]{2,1,0:T(8,128)(2,1)} %get-tuple-element.32), channel_id=1, source_target_pairs={{0,1},{1,0},{2,3},{3,2},{4,5},{5,4},{6,7},{7,6},{8,9},{9,8},{10,11... | collective-permute-start | bytes 3145736 | tf_op jit(solution)/shard_map/sum_over_col/ppermute | solution.py:38
  30.0 2.4 %collective-permute-done.7 = bf16[16,128,256]{2,1,0:T(8,128)(2,1)S(1)} collective-permute-done((bf16[16,128,256]{2,1,0:T(8,128)(2,1)}, bf16[16,128,256]{2,1,0:T(8,128)(2,1)S(1)}, u32[]{:S(2)}, u32[]{:S(2)}) %collective-permute-start.7) | collective-permute-done | bytes 1048608 | tf_op jit(solution)/shard_map/sum_over_col/ppermute | solution.py:38
  32.4 1.5 add_convert_fusion.7
  33.9 1.7 collective-permute-start.10
  35.5 1.6 collective-permute-start.8
  37.2 1.5 add_convert_fusion
  38.7 2.1 %collective-permute-start.15 = (bf16[4,128,256]{2,1,0:T(8,128)(2,1)S(1)}, bf16[4,128,256]{2,1,0:T(8,128)(2,1)S(1)}, u32[]{:S(2)}, u32[]{:S(2)}) collective-permute-start(bf16[4,128,256]{2,1,0:T(8,128)(2,1)S(1)} %get-tuple-element.61), channel_id=1, source_target_pairs={{0,6},{1,7},{2,0},{3,1},{4,2},{5,3},{6,4},{7,5},{8,14},{9,15},{10,... | collective-permute-start | bytes 786440 | tf_op jit(solution)/shard_map/sum_over_col/ppermute | solution.py:38
  41.5 1.6 collective-permute-start.13
  43.1 1.3 collective-permute-done.9
  44.4 4.7 %collective-permute-done.8 = bf16[4,128,256]{2,1,0:T(8,128)(2,1)S(1)} collective-permute-done((bf16[4,128,256]{2,1,0:T(8,128)(2,1)S(1)}, bf16[4,128,256]{2,1,0:T(8,128)(2,1)S(1)}, u32[]{:S(2)}, u32[]{:S(2)}) %collective-permute-start.8) | collective-permute-done | bytes 262176 | tf_op jit(solution)/shard_map/sum_over_col/ppermute | solution.py:38
  49.3 2.7 %collective-permute-start.16 = (bf16[2,128,256]{2,1,0:T(8,128)(2,1)S(1)}, bf16[2,128,256]{2,1,0:T(8,128)(2,1)S(1)}, u32[]{:S(2)}, u32[]{:S(2)}) collective-permute-start(bf16[2,128,256]{2,1,0:T(8,128)(2,1)S(1)} %get-tuple-element.71), channel_id=1, source_target_pairs={{0,8},{1,9},{2,10},{3,11},{4,12},{5,13},{6,14},{7,15},{8,16},{9,17... | collective-permute-start | bytes 393224 | tf_op jit(solution)/shard_map/sum_over_col/ppermute | solution.py:38
  51.9 8.1 %collective-permute-start.11 = (bf16[2,128,256]{2,1,0:T(8,128)(2,1)S(1)}, bf16[2,128,256]{2,1,0:T(8,128)(2,1)S(1)}, u32[]{:S(2)}, u32[]{:S(2)}) collective-permute-start(bf16[2,128,256]{2,1,0:T(8,128)(2,1)S(1)} %get-tuple-element.72), channel_id=1, source_target_pairs={{0,16},{1,17},{2,18},{3,19},{4,20},{5,21},{6,22},{7,23},{8,24},{9,... | collective-permute-start | bytes 393224 | tf_op jit(solution)/shard_map/sum_over_col/ppermute | solution.py:38
  60.1 1.0 collective-permute-done.14
  62.5 7.7 %collective-permute-start.17 = (bf16[2,128,256]{2,1,0:T(8,128)(2,1)S(1)}, bf16[2,128,256]{2,1,0:T(8,128)(2,1)S(1)}, u32[]{:S(2)}, u32[]{:S(2)}) collective-permute-start(bf16[2,128,256]{2,1,0:T(8,128)(2,1)S(1)} %get-tuple-element.70), channel_id=1, source_target_pairs={{0,24},{1,25},{2,26},{3,27},{4,28},{5,29},{6,30},{7,31},{8,0},{9,1... | collective-permute-start | bytes 393224 | tf_op jit(solution)/shard_map/sum_over_col/ppermute | solution.py:38
  70.2 2.8 %collective-permute-done.17 = bf16[2,128,256]{2,1,0:T(8,128)(2,1)S(1)} collective-permute-done((bf16[2,128,256]{2,1,0:T(8,128)(2,1)S(1)}, bf16[2,128,256]{2,1,0:T(8,128)(2,1)S(1)}, u32[]{:S(2)}, u32[]{:S(2)}) %collective-permute-start.17) | collective-permute-done | bytes 131104 | tf_op jit(solution)/shard_map/sum_over_col/ppermute | solution.py:38
  73.6 2.5 %pointwise.1 = (bf16[256,256]{1,0:T(8,128)(2,1)}, bf16[256,256]{1,0:T(8,128)(2,1)}, f32[256,256]{1,0:T(8,128)}, f32[256,256]{1,0:T(8,128)}) custom-call(bf16[256,256]{1,0:T(8,128)(2,1)} %bitcast.43, bf16[256,256]{1,0:T(8,128)(2,1)} %bitcast.42, bf16[256,256]{1,0:T(8,128)(2,1)} %bitcast.44, bf16[256,256]{1,0:T(8,128)(2,1)} %bitcast.40, ...), custom_call_target="tpu_custom_call" | custom-call | tf_op jit(solution)/shard_map/pointwise/pallas_call | solution.py:165
  76.1 5.0 %collective-permute-start.20 = (bf16[256,256]{1,0:T(8,128)(2,1)}, bf16[256,256]{1,0:T(8,128)(2,1)S(1)}, u32[]{:S(2)}, u32[]{:S(2)}) collective-permute-start(bf16[256,256]{1,0:T(8,128)(2,1)} %get-tuple-element.41), channel_id=1, source_target_pairs={{0,24},{1,25},{2,26},{3,27},{4,28},{5,29},{6,30},{7,31},{8,0},{9,1... | collective-permute-start | bytes 393224 | tf_op jit(solution)/shard_map/gather_gradients/ppermute | solution.py:38
  81.1 2.1 %collective-permute-start.19 = (bf16[256,256]{1,0:T(8,128)(2,1)}, bf16[256,256]{1,0:T(8,128)(2,1)S(1)}, u32[]{:S(2)}, u32[]{:S(2)}) collective-permute-start(bf16[256,256]{1,0:T(8,128)(2,1)} %get-tuple-element.41), channel_id=1, source_target_pairs={{0,16},{1,17},{2,18},{3,19},{4,20},{5,21},{6,22},{7,23},{8,24},{9,... | collective-permute-start | bytes 393224 | tf_op jit(solution)/shard_map/gather_gradients/ppermute | solution.py:38
  83.2 2.1 %gather_gradients.1 = f32[256,384]{1,0:T(8,128)} custom-call(f32[256,256]{1,0:T(8,128)} %get-tuple-element.42.total, f32[256,256]{1,0:T(8,128)} %get-tuple-element.43.pre_grad), custom_call_target="tpu_custom_call" | custom-call | tf_op jit(solution)/shard_map/gather_gradients/pallas_call | solution.py:187
  85.3 6.5 %collective-permute-done.20 = bf16[256,256]{1,0:T(8,128)(2,1)S(1)} collective-permute-done((bf16[256,256]{1,0:T(8,128)(2,1)}, bf16[256,256]{1,0:T(8,128)(2,1)S(1)}, u32[]{:S(2)}, u32[]{:S(2)}) %collective-permute-start.20) | collective-permute-done | bytes 131104 | tf_op jit(solution)/shard_map/gather_gradients/ppermute | solution.py:38
  91.8 2.8 %collective-permute-done.19 = bf16[256,256]{1,0:T(8,128)(2,1)S(1)} collective-permute-done((bf16[256,256]{1,0:T(8,128)(2,1)}, bf16[256,256]{1,0:T(8,128)(2,1)S(1)}, u32[]{:S(2)}, u32[]{:S(2)}) %collective-permute-start.19) | collective-permute-done | bytes 131104 | tf_op jit(solution)/shard_map/gather_gradients/ppermute | solution.py:38
  94.5 6.3 %all-to-all-start = ((f32[32,8,384]{2,1,0:T(8,128)}), f32[32,8,384]{2,1,0:T(8,128)S(1)}, u32[]{:S(2)}, u32[]{:S(2)}) async-start(f32[32,8,384]{2,1,0:T(8,128)} %bitcast.30), calls=%async_computation | async-start | bytes 786432 | tf_op jit(solution)/shard_map/sum_weight_grad/all_to_all | solution.py:278
  100.8 0.9 constant_dynamic-update-slice_fusion.3
  101.8 2.7 %collective-permute-start.23 = (bf16[1024,256]{1,0:T(8,128)(2,1)S(1)}, bf16[1024,256]{1,0:T(8,128)(2,1)S(1)}, u32[]{:S(2)}, u32[]{:S(2)}) collective-permute-start(bf16[1024,256]{1,0:T(8,128)(2,1)S(1)} %constant_dynamic-update-slice_fusion), channel_id=1, source_target_pairs={{0,6},{1,7},{2,0},{3,1},{4,2},{5,3},{6,4},{7,5},{8,14},{9,15},{10,... | collective-permute-start | bytes 1572872 | tf_op jit(solution)/shard_map/gather_gradients/ppermute | solution.py:38
  105.6 10.6 %all-to-all-done = f32[32,8,384]{2,1,0:T(8,128)S(1)} async-done(((f32[32,8,384]{2,1,0:T(8,128)}), f32[32,8,384]{2,1,0:T(8,128)S(1)}, u32[]{:S(2)}, u32[]{:S(2)}) %all-to-all-start) | async-done | bytes 393248 | tf_op jit(solution)/shard_map/sum_weight_grad/all_to_all | solution.py:278
  116.3 9.8 %all_to_all.20 = f32[8,8,384]{2,1,0:T(8,128)S(1)} all-to-all(f32[8,8,384]{2,1,0:T(8,128)S(1)} %broadcast_in_dim.6), channel_id=1, replica_groups=mesh['row'=8,'col'=32] {'row'}, dimensions={0} | all-to-all | bytes 196608 | tf_op jit(solution)/shard_map/sum_weight_grad/all_to_all | solution.py:280
  126.1 3.6 %collective-permute-done.23 = bf16[1024,256]{1,0:T(8,128)(2,1)S(1)} collective-permute-done((bf16[1024,256]{1,0:T(8,128)(2,1)S(1)}, bf16[1024,256]{1,0:T(8,128)(2,1)S(1)}, u32[]{:S(2)}, u32[]{:S(2)}) %collective-permute-start.23) | collective-permute-done | bytes 524320 | tf_op jit(solution)/shard_map/gather_gradients/ppermute | solution.py:38
  129.7 3.7 %collective-permute-done.21 = bf16[1024,256]{1,0:T(8,128)(2,1)S(1)} collective-permute-done((bf16[1024,256]{1,0:T(8,128)(2,1)S(1)}, bf16[1024,256]{1,0:T(8,128)(2,1)S(1)}, u32[]{:S(2)}, u32[]{:S(2)}) %collective-permute-start.21) | collective-permute-done | bytes 524320 | tf_op jit(solution)/shard_map/gather_gradients/ppermute | solution.py:38
  134.4 1.0 collective-permute-done.24
  135.4 1.5 collective-permute-done.25
  137.7 0.8 copy-done.7
  139.2 6.1 %all-to-all-start.3 = ((f32[32,8,384]{2,1,0:T(8,128)}), f32[32,8,384]{2,1,0:T(8,128)S(1)}, u32[]{:S(2)}, u32[]{:S(2)}) async-start(f32[32,8,384]{2,1,0:T(8,128)} %broadcast_in_dim.7), calls=%async_computation.3 | async-start | bytes 786432 | tf_op jit(solution)/shard_map/sum_weight_grad/all_to_all | solution.py:296
  145.4 5.6 %tiles_backward.1 = bf16[16,128,256]{2,1,0:T(8,128)(2,1)} custom-call(s32[1]{0:T(128)} %bitcast.28.live, s32[192]{0:T(256)} %get-tuple-element.58.take, s32[192]{0:T(256)} %bitcast.46, bf16[1,192,128,128]{3,2,1,0:T(8,128)(2,1)} %tiles.3, bf16[8,128,256]{2,1,0:T(8,128)(2,1)} %bitcast.33, bf16[8,128,256]{2,1,0:T(8,128)(2,1)} %bitcast.36, ...), custom_call_target="tpu_custom_call" | custom-call | flops 1610612736 | bytes 6291456 | tf_op jit(solution)/shard_map/tiles_backward/pallas_call | solution.py:110
  151.1 9.6 %all-to-all-done.3 = f32[32,8,384]{2,1,0:T(8,128)S(1)} async-done(((f32[32,8,384]{2,1,0:T(8,128)}), f32[32,8,384]{2,1,0:T(8,128)S(1)}, u32[]{:S(2)}, u32[]{:S(2)}) %all-to-all-start.3) | async-done | bytes 393248 | tf_op jit(solution)/shard_map/sum_weight_grad/all_to_all | solution.py:296
  160.7 4.3 %all-to-all-start.2 = ((bf16[8,256,256]{2,1,0:T(8,128)(2,1)}), bf16[8,256,256]{2,1,0:T(8,128)(2,1)S(1)}, u32[]{:S(2)}, u32[]{:S(2)}) async-start(bf16[8,256,256]{2,1,0:T(8,128)(2,1)} %bitcast.29), calls=%async_computation.2 | async-start | bytes 2097152 | tf_op jit(solution)/shard_map/sum_over_row/all_to_all | solution.py:292
  166.4 13.8 %all-to-all-done.2.pieces = bf16[8,256,256]{2,1,0:T(8,128)(2,1)S(1)} async-done(((bf16[8,256,256]{2,1,0:T(8,128)(2,1)}), bf16[8,256,256]{2,1,0:T(8,128)(2,1)S(1)}, u32[]{:S(2)}, u32[]{:S(2)}) %all-to-all-start.2) | async-done | bytes 1048608 | tf_op jit(solution)/shard_map/sum_over_row/all_to_all | solution.py:292
  180.1 1.0 copy-done
  181.1 2.2 %sum_over_row.1 = bf16[256,256]{1,0:T(8,128)(2,1)} custom-call(bf16[8,256,256]{2,1,0:T(8,128)(2,1)} %copy-done, bf16[256,256]{1,0:T(8,128)(2,1)} %weight.1), custom_call_target="tpu_custom_call" | custom-call | tf_op jit(solution)/shard_map/sum_over_row/pallas_call | solution.py:211
  (59 shorter events, 9.2 us)
Async XLA Ops:
  0.6 10.8 %collective-permute-start.4 = (bf16[256,256]{1,0:T(8,128)(2,1)}, bf16[256,256]{1,0:T(8,128)(2,1)}, u32[]{:S(2)}, u32[]{:S(2)}) collective-permute-start(bf16[256,256]{1,0:T(8,128)(2,1)} %param.8), channel_id=1, source_target_pairs={{0,160},{32,128},{64,224},{96,192},{128,32},{160,0},{192,96},{224,... | collective-permute-start | bytes 393224 | tf_op jit(solution)/shard_map/gather_features/ppermute | solution.py:28
  5.6 10.9 %collective-permute-start.3 = (bf16[256,256]{1,0:T(8,128)(2,1)}, bf16[256,256]{1,0:T(8,128)(2,1)}, u32[]{:S(2)}, u32[]{:S(2)}) collective-permute-start(bf16[256,256]{1,0:T(8,128)(2,1)} %param.8), channel_id=1, source_target_pairs={{0,128},{32,160},{64,192},{96,224},{128,0},{160,32},{192,64},{224,... | collective-permute-start | bytes 393224 | tf_op jit(solution)/shard_map/gather_features/ppermute | solution.py:28
  5.9 11.9 %collective-permute-start.2 = (bf16[256,256]{1,0:T(8,128)(2,1)}, bf16[256,256]{1,0:T(8,128)(2,1)}, u32[]{:S(2)}, u32[]{:S(2)}) collective-permute-start(bf16[256,256]{1,0:T(8,128)(2,1)} %param.8), channel_id=1, source_target_pairs={{0,96},{32,64},{64,160},{96,128},{128,224},{160,192},{192,32},{224... | collective-permute-start | bytes 393224 | tf_op jit(solution)/shard_map/gather_features/ppermute | solution.py:28
  6.6 12.9 %collective-permute-start.1 = (bf16[256,256]{1,0:T(8,128)(2,1)}, bf16[256,256]{1,0:T(8,128)(2,1)}, u32[]{:S(2)}, u32[]{:S(2)}) collective-permute-start(bf16[256,256]{1,0:T(8,128)(2,1)} %param.8), channel_id=1, source_target_pairs={{0,64},{32,96},{64,128},{96,160},{128,192},{160,224},{192,0},{224,... | collective-permute-start | bytes 393224 | tf_op jit(solution)/shard_map/gather_features/ppermute | solution.py:28
  7.8 11.7 %collective-permute-start = (bf16[256,256]{1,0:T(8,128)(2,1)}, bf16[256,256]{1,0:T(8,128)(2,1)}, u32[]{:S(2)}, u32[]{:S(2)}) collective-permute-start(bf16[256,256]{1,0:T(8,128)(2,1)} %param.8), channel_id=1, source_target_pairs={{0,32},{32,0},{64,96},{96,64},{128,160},{160,128},{192,224},{224,1... | collective-permute-start | bytes 393224 | tf_op jit(solution)/shard_map/gather_features/ppermute | solution.py:28
  11.4 8.2 %collective-permute-start.6 = (bf16[256,256]{1,0:T(8,128)(2,1)}, bf16[256,256]{1,0:T(8,128)(2,1)}, u32[]{:S(2)}, u32[]{:S(2)}) collective-permute-start(bf16[256,256]{1,0:T(8,128)(2,1)} %param.8), channel_id=1, source_target_pairs={{0,224},{32,192},{64,32},{96,0},{128,96},{160,64},{192,160},{224,1... | collective-permute-start | bytes 393224 | tf_op jit(solution)/shard_map/gather_features/ppermute | solution.py:28
  16.5 4.7 %collective-permute-start.5 = (bf16[256,256]{1,0:T(8,128)(2,1)}, bf16[256,256]{1,0:T(8,128)(2,1)}, u32[]{:S(2)}, u32[]{:S(2)}) collective-permute-start(bf16[256,256]{1,0:T(8,128)(2,1)} %param.8), channel_id=1, source_target_pairs={{0,192},{32,224},{64,0},{96,32},{128,64},{160,96},{192,128},{224,1... | collective-permute-start | bytes 393224 | tf_op jit(solution)/shard_map/gather_features/ppermute | solution.py:28
  27.0 5.4 %collective-permute-start.7 = (bf16[16,128,256]{2,1,0:T(8,128)(2,1)}, bf16[16,128,256]{2,1,0:T(8,128)(2,1)S(1)}, u32[]{:S(2)}, u32[]{:S(2)}) collective-permute-start(bf16[16,128,256]{2,1,0:T(8,128)(2,1)} %get-tuple-element.32), channel_id=1, source_target_pairs={{0,1},{1,0},{2,3},{3,2},{4,5},{5,4},{6,7},{7,6},{8,9},{9,8},{10,11... | collective-permute-start | bytes 3145736 | tf_op jit(solution)/shard_map/sum_over_col/ppermute | solution.py:38
  29.9 7.3 %collective-permute-start.12 = (bf16[16,128,256]{2,1,0:T(8,128)(2,1)}, bf16[16,128,256]{2,1,0:T(8,128)(2,1)S(1)}, u32[]{:S(2)}, u32[]{:S(2)}) collective-permute-start(bf16[16,128,256]{2,1,0:T(8,128)(2,1)} %get-tuple-element.34), channel_id=1, source_target_pairs={{0,1},{1,0},{2,3},{3,2},{4,5},{5,4},{6,7},{7,6},{8,9},{9,8},{10,11... | collective-permute-start | bytes 3145736 | tf_op jit(solution)/shard_map/sum_over_col/ppermute | solution.py:38
  33.9 7.6 %collective-permute-start.10 = (bf16[4,128,256]{2,1,0:T(8,128)(2,1)S(1)}, bf16[4,128,256]{2,1,0:T(8,128)(2,1)S(1)}, u32[]{:S(2)}, u32[]{:S(2)}) collective-permute-start(bf16[4,128,256]{2,1,0:T(8,128)(2,1)S(1)} %get-tuple-element.66), channel_id=1, source_target_pairs={{0,6},{1,7},{2,0},{3,1},{4,2},{5,3},{6,4},{7,5},{8,14},{9,15},{10,... | collective-permute-start | bytes 786440 | tf_op jit(solution)/shard_map/sum_over_col/ppermute | solution.py:38
  35.5 8.9 %collective-permute-start.9 = (bf16[4,128,256]{2,1,0:T(8,128)(2,1)S(1)}, bf16[4,128,256]{2,1,0:T(8,128)(2,1)S(1)}, u32[]{:S(2)}, u32[]{:S(2)}) collective-permute-start(bf16[4,128,256]{2,1,0:T(8,128)(2,1)S(1)} %get-tuple-element.67), channel_id=1, source_target_pairs={{0,2},{1,3},{2,4},{3,5},{4,6},{5,7},{6,0},{7,1},{8,10},{9,11},{10,... | collective-permute-start | bytes 786440 | tf_op jit(solution)/shard_map/sum_over_col/ppermute | solution.py:38
  35.5 13.6 %collective-permute-start.8 = (bf16[4,128,256]{2,1,0:T(8,128)(2,1)S(1)}, bf16[4,128,256]{2,1,0:T(8,128)(2,1)S(1)}, u32[]{:S(2)}, u32[]{:S(2)}) collective-permute-start(bf16[4,128,256]{2,1,0:T(8,128)(2,1)S(1)} %get-tuple-element.68), channel_id=1, source_target_pairs={{0,4},{1,5},{2,6},{3,7},{4,0},{5,1},{6,2},{7,3},{8,12},{9,13},{10,... | collective-permute-start | bytes 786440 | tf_op jit(solution)/shard_map/sum_over_col/ppermute | solution.py:38
  38.7 21.4 %collective-permute-start.15 = (bf16[4,128,256]{2,1,0:T(8,128)(2,1)S(1)}, bf16[4,128,256]{2,1,0:T(8,128)(2,1)S(1)}, u32[]{:S(2)}, u32[]{:S(2)}) collective-permute-start(bf16[4,128,256]{2,1,0:T(8,128)(2,1)S(1)} %get-tuple-element.61), channel_id=1, source_target_pairs={{0,6},{1,7},{2,0},{3,1},{4,2},{5,3},{6,4},{7,5},{8,14},{9,15},{10,... | collective-permute-start | bytes 786440 | tf_op jit(solution)/shard_map/sum_over_col/ppermute | solution.py:38
  40.8 20.2 %collective-permute-start.14 = (bf16[4,128,256]{2,1,0:T(8,128)(2,1)S(1)}, bf16[4,128,256]{2,1,0:T(8,128)(2,1)S(1)}, u32[]{:S(2)}, u32[]{:S(2)}) collective-permute-start(bf16[4,128,256]{2,1,0:T(8,128)(2,1)S(1)} %get-tuple-element.62), channel_id=1, source_target_pairs={{0,2},{1,3},{2,4},{3,5},{4,6},{5,7},{6,0},{7,1},{8,10},{9,11},{10,... | collective-permute-start | bytes 786440 | tf_op jit(solution)/shard_map/sum_over_col/ppermute | solution.py:38
  41.5 19.6 %collective-permute-start.13 = (bf16[4,128,256]{2,1,0:T(8,128)(2,1)S(1)}, bf16[4,128,256]{2,1,0:T(8,128)(2,1)S(1)}, u32[]{:S(2)}, u32[]{:S(2)}) collective-permute-start(bf16[4,128,256]{2,1,0:T(8,128)(2,1)S(1)} %get-tuple-element.63), channel_id=1, source_target_pairs={{0,4},{1,5},{2,6},{3,7},{4,0},{5,1},{6,2},{7,3},{8,12},{9,13},{10,... | collective-permute-start | bytes 786440 | tf_op jit(solution)/shard_map/sum_over_col/ppermute | solution.py:38
  49.3 12.4 %collective-permute-start.16 = (bf16[2,128,256]{2,1,0:T(8,128)(2,1)S(1)}, bf16[2,128,256]{2,1,0:T(8,128)(2,1)S(1)}, u32[]{:S(2)}, u32[]{:S(2)}) collective-permute-start(bf16[2,128,256]{2,1,0:T(8,128)(2,1)S(1)} %get-tuple-element.71), channel_id=1, source_target_pairs={{0,8},{1,9},{2,10},{3,11},{4,12},{5,13},{6,14},{7,15},{8,16},{9,17... | collective-permute-start | bytes 393224 | tf_op jit(solution)/shard_map/sum_over_col/ppermute | solution.py:38
  51.9 18.3 %collective-permute-start.11 = (bf16[2,128,256]{2,1,0:T(8,128)(2,1)S(1)}, bf16[2,128,256]{2,1,0:T(8,128)(2,1)S(1)}, u32[]{:S(2)}, u32[]{:S(2)}) collective-permute-start(bf16[2,128,256]{2,1,0:T(8,128)(2,1)S(1)} %get-tuple-element.72), channel_id=1, source_target_pairs={{0,16},{1,17},{2,18},{3,19},{4,20},{5,21},{6,22},{7,23},{8,24},{9,... | collective-permute-start | bytes 393224 | tf_op jit(solution)/shard_map/sum_over_col/ppermute | solution.py:38
  61.7 11.3 %copy-start.8 = (bf16[2,128,256]{2,1,0:T(8,128)(2,1)}, bf16[2,128,256]{2,1,0:T(8,128)(2,1)S(1)}, u32[]{:S(2)}) copy-start(bf16[2,128,256]{2,1,0:T(8,128)(2,1)S(1)} %collective-permute-done.16) | copy-start | bytes 393220
  62.5 10.5 %collective-permute-start.17 = (bf16[2,128,256]{2,1,0:T(8,128)(2,1)S(1)}, bf16[2,128,256]{2,1,0:T(8,128)(2,1)S(1)}, u32[]{:S(2)}, u32[]{:S(2)}) collective-permute-start(bf16[2,128,256]{2,1,0:T(8,128)(2,1)S(1)} %get-tuple-element.70), channel_id=1, source_target_pairs={{0,24},{1,25},{2,26},{3,27},{4,28},{5,29},{6,30},{7,31},{8,0},{9,1... | collective-permute-start | bytes 393224 | tf_op jit(solution)/shard_map/sum_over_col/ppermute | solution.py:38
  70.2 2.8 %copy-start.9 = (bf16[2,128,256]{2,1,0:T(8,128)(2,1)}, bf16[2,128,256]{2,1,0:T(8,128)(2,1)S(1)}, u32[]{:S(2)}) copy-start(bf16[2,128,256]{2,1,0:T(8,128)(2,1)S(1)} %collective-permute-done.11) | copy-start | bytes 393220
  73.0 0.7 copy-start.10
  76.1 15.6 %collective-permute-start.20 = (bf16[256,256]{1,0:T(8,128)(2,1)}, bf16[256,256]{1,0:T(8,128)(2,1)S(1)}, u32[]{:S(2)}, u32[]{:S(2)}) collective-permute-start(bf16[256,256]{1,0:T(8,128)(2,1)} %get-tuple-element.41), channel_id=1, source_target_pairs={{0,24},{1,25},{2,26},{3,27},{4,28},{5,29},{6,30},{7,31},{8,0},{9,1... | collective-permute-start | bytes 393224 | tf_op jit(solution)/shard_map/gather_gradients/ppermute | solution.py:38
  81.1 13.5 %collective-permute-start.19 = (bf16[256,256]{1,0:T(8,128)(2,1)}, bf16[256,256]{1,0:T(8,128)(2,1)S(1)}, u32[]{:S(2)}, u32[]{:S(2)}) collective-permute-start(bf16[256,256]{1,0:T(8,128)(2,1)} %get-tuple-element.41), channel_id=1, source_target_pairs={{0,16},{1,17},{2,18},{3,19},{4,20},{5,21},{6,22},{7,23},{8,24},{9,... | collective-permute-start | bytes 393224 | tf_op jit(solution)/shard_map/gather_gradients/ppermute | solution.py:38
  83.1 11.4 %collective-permute-start.18 = (bf16[256,256]{1,0:T(8,128)(2,1)}, bf16[256,256]{1,0:T(8,128)(2,1)S(1)}, u32[]{:S(2)}, u32[]{:S(2)}) collective-permute-start(bf16[256,256]{1,0:T(8,128)(2,1)} %get-tuple-element.41), channel_id=1, source_target_pairs={{0,8},{1,9},{2,10},{3,11},{4,12},{5,13},{6,14},{7,15},{8,16},{9,17... | collective-permute-start | bytes 393224 | tf_op jit(solution)/shard_map/gather_gradients/ppermute | solution.py:38
  94.5 21.7 %all-to-all-start = ((f32[32,8,384]{2,1,0:T(8,128)}), f32[32,8,384]{2,1,0:T(8,128)S(1)}, u32[]{:S(2)}, u32[]{:S(2)}) async-start(f32[32,8,384]{2,1,0:T(8,128)} %bitcast.30), calls=%async_computation | async-start | bytes 786432 | tf_op jit(solution)/shard_map/sum_weight_grad/all_to_all | solution.py:278
  101.8 43.6 %copy-start.1 = (bf16[1024,256]{1,0:T(8,128)(2,1)}, bf16[1024,256]{1,0:T(8,128)(2,1)S(1)}, u32[]{:S(2)}) copy-start(bf16[1024,256]{1,0:T(8,128)(2,1)S(1)} %constant_dynamic-update-slice_fusion) | copy-start | bytes 1572868
  101.8 27.9 %collective-permute-start.23 = (bf16[1024,256]{1,0:T(8,128)(2,1)S(1)}, bf16[1024,256]{1,0:T(8,128)(2,1)S(1)}, u32[]{:S(2)}, u32[]{:S(2)}) collective-permute-start(bf16[1024,256]{1,0:T(8,128)(2,1)S(1)} %constant_dynamic-update-slice_fusion), channel_id=1, source_target_pairs={{0,6},{1,7},{2,0},{3,1},{4,2},{5,3},{6,4},{7,5},{8,14},{9,15},{10,... | collective-permute-start | bytes 1572872 | tf_op jit(solution)/shard_map/gather_gradients/ppermute | solution.py:38
  104.5 25.2 %collective-permute-start.22 = (bf16[1024,256]{1,0:T(8,128)(2,1)S(1)}, bf16[1024,256]{1,0:T(8,128)(2,1)S(1)}, u32[]{:S(2)}, u32[]{:S(2)}) collective-permute-start(bf16[1024,256]{1,0:T(8,128)(2,1)S(1)} %constant_dynamic-update-slice_fusion), channel_id=1, source_target_pairs={{0,4},{1,5},{2,6},{3,7},{4,0},{5,1},{6,2},{7,3},{8,12},{9,13},{10,... | collective-permute-start | bytes 1572872 | tf_op jit(solution)/shard_map/gather_gradients/ppermute | solution.py:38
  105.1 28.3 %collective-permute-start.21 = (bf16[1024,256]{1,0:T(8,128)(2,1)S(1)}, bf16[1024,256]{1,0:T(8,128)(2,1)S(1)}, u32[]{:S(2)}, u32[]{:S(2)}) collective-permute-start(bf16[1024,256]{1,0:T(8,128)(2,1)S(1)} %constant_dynamic-update-slice_fusion), channel_id=1, source_target_pairs={{0,2},{1,3},{2,4},{3,5},{4,6},{5,7},{6,0},{7,1},{8,10},{9,11},{10,... | collective-permute-start | bytes 1572872 | tf_op jit(solution)/shard_map/gather_gradients/ppermute | solution.py:38
  129.7 15.7 %copy-start.2 = (bf16[1024,256]{1,0:T(8,128)(2,1)}, bf16[1024,256]{1,0:T(8,128)(2,1)S(1)}, u32[]{:S(2)}) copy-start(bf16[1024,256]{1,0:T(8,128)(2,1)S(1)} %collective-permute-done.23) | copy-start | bytes 1572868
  129.7 15.7 %copy-start.3 = (bf16[1024,256]{1,0:T(8,128)(2,1)}, bf16[1024,256]{1,0:T(8,128)(2,1)S(1)}, u32[]{:S(2)}) copy-start(bf16[1024,256]{1,0:T(8,128)(2,1)S(1)} %collective-permute-done.22) | copy-start | bytes 1572868
  133.4 12.0 %copy-start.4 = (bf16[1024,256]{1,0:T(8,128)(2,1)}, bf16[1024,256]{1,0:T(8,128)(2,1)S(1)}, u32[]{:S(2)}) copy-start(bf16[1024,256]{1,0:T(8,128)(2,1)S(1)} %collective-permute-done.21) | copy-start | bytes 1572868
  133.4 2.0 %collective-permute-start.24 = (bf16[1024,256]{1,0:T(8,128)(2,1)S(1)}, bf16[1024,256]{1,0:T(8,128)(2,1)S(1)}, u32[]{:S(2)}, u32[]{:S(2)}) collective-permute-start(bf16[1024,256]{1,0:T(8,128)(2,1)S(1)} %constant_dynamic-update-slice_fusion), channel_id=1, source_target_pairs={{0,1},{1,0},{2,3},{3,2},{4,5},{5,4},{6,7},{7,6},{8,9},{9,8},{10,11... | collective-permute-start | bytes 1572872 | tf_op jit(solution)/shard_map/gather_gradients/ppermute | solution.py:38
  133.9 3.0 %collective-permute-start.25 = (bf16[1024,256]{1,0:T(8,128)(2,1)S(1)}, bf16[1024,256]{1,0:T(8,128)(2,1)S(1)}, u32[]{:S(2)}, u32[]{:S(2)}) collective-permute-start(bf16[1024,256]{1,0:T(8,128)(2,1)S(1)} %collective-permute-done.21), channel_id=1, source_target_pairs={{0,1},{1,0},{2,3},{3,2},{4,5},{5,4},{6,7},{7,6},{8,9},{9,8},{10,11... | collective-permute-start | bytes 1572872 | tf_op jit(solution)/shard_map/gather_gradients/ppermute | solution.py:38
  133.9 3.8 %collective-permute-start.26 = (bf16[1024,256]{1,0:T(8,128)(2,1)S(1)}, bf16[1024,256]{1,0:T(8,128)(2,1)S(1)}, u32[]{:S(2)}, u32[]{:S(2)}) collective-permute-start(bf16[1024,256]{1,0:T(8,128)(2,1)S(1)} %collective-permute-done.22), channel_id=1, source_target_pairs={{0,1},{1,0},{2,3},{3,2},{4,5},{5,4},{6,7},{7,6},{8,9},{9,8},{10,11... | collective-permute-start | bytes 1572872 | tf_op jit(solution)/shard_map/gather_gradients/ppermute | solution.py:38
  134.4 4.1 %collective-permute-start.27 = (bf16[1024,256]{1,0:T(8,128)(2,1)S(1)}, bf16[1024,256]{1,0:T(8,128)(2,1)}, u32[]{:S(2)}, u32[]{:S(2)}) collective-permute-start(bf16[1024,256]{1,0:T(8,128)(2,1)S(1)} %collective-permute-done.23), channel_id=1, source_target_pairs={{0,1},{1,0},{2,3},{3,2},{4,5},{5,4},{6,7},{7,6},{8,9},{9,8},{10,11... | collective-permute-start | bytes 1572872 | tf_op jit(solution)/shard_map/gather_gradients/ppermute | solution.py:38
  135.4 10.0 %copy-start.5 = (bf16[1024,256]{1,0:T(8,128)(2,1)}, bf16[1024,256]{1,0:T(8,128)(2,1)S(1)}, u32[]{:S(2)}) copy-start(bf16[1024,256]{1,0:T(8,128)(2,1)S(1)} %collective-permute-done.24) | copy-start | bytes 1572868
  136.9 8.5 %copy-start.6 = (bf16[1024,256]{1,0:T(8,128)(2,1)}, bf16[1024,256]{1,0:T(8,128)(2,1)S(1)}, u32[]{:S(2)}) copy-start(bf16[1024,256]{1,0:T(8,128)(2,1)S(1)} %collective-permute-done.25) | copy-start | bytes 1572868
  137.7 0.8 copy-start.7
  139.2 21.4 %all-to-all-start.3 = ((f32[32,8,384]{2,1,0:T(8,128)}), f32[32,8,384]{2,1,0:T(8,128)S(1)}, u32[]{:S(2)}, u32[]{:S(2)}) async-start(f32[32,8,384]{2,1,0:T(8,128)} %broadcast_in_dim.7), calls=%async_computation.3 | async-start | bytes 786432 | tf_op jit(solution)/shard_map/sum_weight_grad/all_to_all | solution.py:296
  160.7 19.5 %all-to-all-start.2 = ((bf16[8,256,256]{2,1,0:T(8,128)(2,1)}), bf16[8,256,256]{2,1,0:T(8,128)(2,1)S(1)}, u32[]{:S(2)}, u32[]{:S(2)}) async-start(bf16[8,256,256]{2,1,0:T(8,128)(2,1)} %bitcast.29), calls=%async_computation.2 | async-start | bytes 2097152 | tf_op jit(solution)/shard_map/sum_over_row/all_to_all | solution.py:292
  180.1 1.0 copy-start

commit v6 on v5

--- a/solution.py
+++ b/solution.py
@@ -14,6 +14,7 @@
 N_X, N_ZL, N_ZH, N_Y, N_CORE = 4, 2, 4, 4, 2
 N_ROW = N_X * N_ZL
 N_COL = N_ZH * N_Y * N_CORE
+PIECE = 8
 GROUP = 24
 VMEM_LIMIT = 60 * 1024 * 1024
 VMEM_MOST = 65408 * 1024
@@ -62,39 +63,55 @@
     def _(g):
         tile_copy(g).start()
 
-    @pl.loop(0, acc.shape[0])
+    @pl.loop(0, acc.shape[0] // 4)
     def _(i):
-        acc[i] = jnp.zeros(acc.shape[1:], jnp.float32)
+        for j in range(4):
+            acc[i * 4 + j] = jnp.zeros(acc.shape[1:], jnp.float32)
 
     for copy in copies:
         copy.wait()
 
-    @pl.loop(0, groups)
+    def product(slot):
+        value = lax.dot_general(
+            held[slot],
+            src[take[slot]],
+            (((0 if transposed else 1,), (0,)), ((), ())),
+            preferred_element_type=jnp.float32,
+        )
+        acc[put[slot]] += value
+
+    @pl.loop(0, groups // 2)
     def _(g):
-        tile_copy(g).wait()
-
+        tile_copy(2 * g).wait()
+        tile_copy(2 * g + 1).wait()
+        for j in range(2 * GROUP):
+            product(2 * g * GROUP + j)
+
+    @pl.when(groups % 2 == 1)
+    def _():
+        tile_copy(groups - 1).wait()
         for j in range(GROUP):
-            slot = g * GROUP + j
-            product = lax.dot_general(
-                held[slot],
-                src[take[slot]],
-                (((0 if transposed else 1,), (0,)), ((), ())),
-                preferred_element_type=jnp.float32,
-            )
-            acc[put[slot]] += product
+            product((groups - 1) * GROUP + j)
 
     copies, first = [], 0
     for k, size in enumerate(out_sizes):
-        start = first
-
-        @pl.loop(0, size)
-        def _(i):
-            staged[start + i] = acc[start + i].astype(jnp.bfloat16)
-
-        copies.append(
-            pltpu.make_async_copy(staged.at[pl.ds(start, size)], outs[k], out_sems.at[k])
-        )
-        copies[-1].start()
+        for part in range(0, size, PIECE):
+            start = first + part
+
+            @pl.loop(0, PIECE // 4)
+            def _(i):
+                for j in range(4):
+                    row = start + i * 4 + j
+                    staged[row] = acc[row].astype(jnp.bfloat16)
+
+            copies.append(
+                pltpu.make_async_copy(
+                    staged.at[pl.ds(start, PIECE)],
+                    outs[k].at[pl.ds(part, PIECE)],
+                    out_sems.at[start // PIECE],
+                )
+            )
+            copies[-1].start()
         first += size
     for copy in copies:
         copy.wait()
@@ -118,7 +135,7 @@
             pltpu.VMEM((sum(out_sizes), tile, width), jnp.bfloat16),
             pltpu.SemaphoreType.DMA((slots // GROUP,)),
             pltpu.SemaphoreType.DMA((len(sources),)),
-            pltpu.SemaphoreType.DMA((len(out_sizes),)),
+            pltpu.SemaphoreType.DMA((sum(out_sizes) // PIECE,)),
         ],
         out_shape=[
             jax.ShapeDtypeStruct((size, tile, width), jnp.bfloat16)
@@ -280,9 +297,7 @@
         load = jnp.sum(lax.all_to_all(load, "row", 0, 0, tiled=True), axis=0) * scale
     with jax.named_scope("gather_gradients"):
         here += [col_shift(here[0], dy=k) for k in range(1, N_Y)]
-        *here, load = lax.optimization_barrier((*here, load))
         there = [col_shift(p, dcore=1) for p in here]
-        *there, load = lax.optimization_barrier((*there, load))
     with jax.named_scope("tiles_backward"):
         (back,) = tile_sum(
             adjacency, live, take_rows, c, here + there, [N_ROW * per], True, VMEM_LIMIT

time: 184 us -> 173 us (0.940)
  waiting for transfers between devices: 74.6 us -> 68.1 us
  starting transfers between devices: 67.2 us -> 61.7 us
  blocking collectives: 9.76 us -> 12.8 us
    ppermute x21, starting transfers between devices: 40.5 us -> 33.4 us  [col_shift(): return lax.ppermute(value, 'col', pairs)]
    all_to_all x1, waiting for transfers between devices: 9.6 us -> 5.72 us  [shards(): load = lax.all_to_all(load, 'col', 0, 0, tiled=True).reshape(width, -1)]
    ppermute x21, waiting for transfers between devices: 33.2 us -> 29.6 us  [col_shift(): return lax.ppermute(value, 'col', pairs)]
    all_to_all x1, starting transfers between devices: 6.28 us -> 9.54 us  [shards(): load = jnp.sum(lax.all_to_all(load, 'col', 0, 0, tiled=True), axis=0)]
    all_to_all x1, blocking collectives: 9.76 us -> 12.8 us  [shards(): lax.all_to_all(load, 'row', 0, 0, tiled=True)]
  transfers between devices with their start and end apart: 31 -> 31, of which waited for: 20 -> 19; matrix products, arithmetic and copies ran while one was open for 5% -> 6% of each run, Pallas kernels for 4% -> 4%
where the time goes in v6:
time: 173 us
  waiting for transfers between devices  68.1 us (39%)
  starting transfers between devices  61.7 us (36%)
  Pallas kernels  16.7 us (10%)
  blocking collectives  12.8 us (7%)
  other arithmetic  6.54 us (4%)
  local copies, waits for them, and re-layouts  5.59 us (3%)
    ppermute x21, starting transfers between devices, col_shift(): return lax.ppermute(value, 'col', pairs)  33.4 us
    ppermute x21, waiting for transfers between devices, col_shift(): return lax.ppermute(value, 'col', pairs)  29.6 us
    all_to_all x1, waiting for transfers between devices, shards(): back = lax.all_to_all(back, 'row', 0, 0, tiled=True)  14.8 us
    all_to_all x1, blocking collectives, shards(): lax.all_to_all(load, 'row', 0, 0, tiled=True)  12.8 us
    all_to_all x1, waiting for transfers between devices, shards(): load = jnp.sum(lax.all_to_all(load, 'col', 0, 0, tiled=True), axis=0)  10.6 us
    ppermute x7, starting transfers between devices, row_shift(): return lax.ppermute(value, 'row', pairs)  10 us
    pallas_call x2, Pallas kernels, tile_sum(): pl.pallas_call(functools.partial(tile_kernel, transposed, src_sizes, out_...  10 us
    all_to_all x1, starting transfers between devices, shards(): load = jnp.sum(lax.all_to_all(load, 'col', 0, 0, tiled=True), axis=0)  9.54 us
  transfers between devices with their start and end apart: 31, of which 19 were waited for; matrix products, arithmetic and copies ran while one was open for 6% of the time, Pallas kernels for 4%

profile of v6, /device:TPU:1, one launch (start us, length us, event | category | flops | bytes accessed | tf_op | source)
XLA Modules:
  0.0 173.0 jit_solution(4011436714560737007)
XLA Ops:
  0.6 5.0 %collective-permute-start.4 = (bf16[256,256]{1,0:T(8,128)(2,1)}, bf16[256,256]{1,0:T(8,128)(2,1)}, u32[]{:S(2)}, u32[]{:S(2)}) collective-permute-start(bf16[256,256]{1,0:T(8,128)(2,1)} %param.8), channel_id=1, source_target_pairs={{0,160},{32,128},{64,224},{96,192},{128,32},{160,0},{192,96},{224,... | collective-permute-start | bytes 393224 | tf_op jit(solution)/shard_map/gather_features/ppermute | solution.py:29
  6.6 1.2 collective-permute-start.1
  7.8 1.6 collective-permute-start
  10.1 1.3 multiply_add_fusion
  11.4 1.2 collective-permute-start.6
  12.6 3.9 %collective-permute-done.3 = bf16[256,256]{1,0:T(8,128)(2,1)} collective-permute-done((bf16[256,256]{1,0:T(8,128)(2,1)}, bf16[256,256]{1,0:T(8,128)(2,1)}, u32[]{:S(2)}, u32[]{:S(2)}) %collective-permute-start.3) | collective-permute-done | bytes 131104 | tf_op jit(solution)/shard_map/gather_features/ppermute | solution.py:29
  16.5 1.3 fusion.2
  17.8 1.8 %collective-permute-done.1 = bf16[256,256]{1,0:T(8,128)(2,1)} collective-permute-done((bf16[256,256]{1,0:T(8,128)(2,1)}, bf16[256,256]{1,0:T(8,128)(2,1)}, u32[]{:S(2)}, u32[]{:S(2)}) %collective-permute-start.1) | collective-permute-done | bytes 131104 | tf_op jit(solution)/shard_map/gather_features/ppermute | solution.py:29
  19.6 1.7 collective-permute-done.5
  21.3 5.1 %tiles_forward.1 = (bf16[16,128,256]{2,1,0:T(8,128)(2,1)}, bf16[16,128,256]{2,1,0:T(8,128)(2,1)}, bf16[16,128,256]{2,1,0:T(8,128)(2,1)}, bf16[16,128,256]{2,1,0:T(8,128)(2,1)}) custom-call(s32[1]{0:T(128)} %bitcast.27.live, s32[192]{0:T(256)} %get-tuple-element.53.take, s32[192]{0:T(256)} %get-tuple-element.54.put, bf16[1,192,128,128]{3,2,1,0:T(8,128)(2,1)} %tiles.3, ...), custom_call_target="tpu_custom_call" | custom-call | flops 1610612736 | bytes 6291456 | tf_op jit(solution)/shard_map/tiles_forward/pallas_call | solution.py:127
  26.3 1.7 collective-permute-start.7
  28.1 2.4 %collective-permute-done.7 = bf16[16,128,256]{2,1,0:T(8,128)(2,1)S(1)} collective-permute-done((bf16[16,128,256]{2,1,0:T(8,128)(2,1)}, bf16[16,128,256]{2,1,0:T(8,128)(2,1)S(1)}, u32[]{:S(2)}, u32[]{:S(2)}) %collective-permute-start.7) | collective-permute-done | bytes 1048608 | tf_op jit(solution)/shard_map/sum_over_col/ppermute | solution.py:39
  30.5 1.5 add_convert_fusion.7
  32.0 6.4 %collective-permute-start.10 = (bf16[4,128,256]{2,1,0:T(8,128)(2,1)S(1)}, bf16[4,128,256]{2,1,0:T(8,128)(2,1)S(1)}, u32[]{:S(2)}, u32[]{:S(2)}) collective-permute-start(bf16[4,128,256]{2,1,0:T(8,128)(2,1)S(1)} %get-tuple-element.46), channel_id=1, source_target_pairs={{0,6},{1,7},{2,0},{3,1},{4,2},{5,3},{6,4},{7,5},{8,14},{9,15},{10,... | collective-permute-start | bytes 786440 | tf_op jit(solution)/shard_map/sum_over_col/ppermute | solution.py:39
  38.5 1.3 collective-permute-start.8
  39.7 1.5 add_convert_fusion
  41.3 1.5 collective-permute-start.15
  43.4 5.9 %collective-permute-done.10 = bf16[4,128,256]{2,1,0:T(8,128)(2,1)S(1)} collective-permute-done((bf16[4,128,256]{2,1,0:T(8,128)(2,1)S(1)}, bf16[4,128,256]{2,1,0:T(8,128)(2,1)S(1)}, u32[]{:S(2)}, u32[]{:S(2)}) %collective-permute-start.10) | collective-permute-done | bytes 262176 | tf_op jit(solution)/shard_map/sum_over_col/ppermute | solution.py:39
  49.3 2.6 %collective-permute-done.9 = bf16[4,128,256]{2,1,0:T(8,128)(2,1)S(1)} collective-permute-done((bf16[4,128,256]{2,1,0:T(8,128)(2,1)S(1)}, bf16[4,128,256]{2,1,0:T(8,128)(2,1)S(1)}, u32[]{:S(2)}, u32[]{:S(2)}) %collective-permute-start.9) | collective-permute-done | bytes 262176 | tf_op jit(solution)/shard_map/sum_over_col/ppermute | solution.py:39
  52.7 5.4 %collective-permute-start.11 = (bf16[2,128,256]{2,1,0:T(8,128)(2,1)S(1)}, bf16[2,128,256]{2,1,0:T(8,128)(2,1)S(1)}, u32[]{:S(2)}, u32[]{:S(2)}) collective-permute-start(bf16[2,128,256]{2,1,0:T(8,128)(2,1)S(1)} %get-tuple-element.52), channel_id=1, source_target_pairs={{0,16},{1,17},{2,18},{3,19},{4,20},{5,21},{6,22},{7,23},{8,24},{9,... | collective-permute-start | bytes 393224 | tf_op jit(solution)/shard_map/sum_over_col/ppermute | solution.py:39
  58.1 2.4 %collective-permute-done.15 = bf16[4,128,256]{2,1,0:T(8,128)(2,1)S(1)} collective-permute-done((bf16[4,128,256]{2,1,0:T(8,128)(2,1)S(1)}, bf16[4,128,256]{2,1,0:T(8,128)(2,1)S(1)}, u32[]{:S(2)}, u32[]{:S(2)}) %collective-permute-start.15) | collective-permute-done | bytes 262176 | tf_op jit(solution)/shard_map/sum_over_col/ppermute | solution.py:39
  60.5 3.2 %collective-permute-done.14 = bf16[4,128,256]{2,1,0:T(8,128)(2,1)S(1)} collective-permute-done((bf16[4,128,256]{2,1,0:T(8,128)(2,1)S(1)}, bf16[4,128,256]{2,1,0:T(8,128)(2,1)S(1)}, u32[]{:S(2)}, u32[]{:S(2)}) %collective-permute-start.14) | collective-permute-done | bytes 262176 | tf_op jit(solution)/shard_map/sum_over_col/ppermute | solution.py:39
  63.7 0.8 add_convert_fusion.8
  64.5 3.4 %collective-permute-start.17 = (bf16[2,128,256]{2,1,0:T(8,128)(2,1)S(1)}, bf16[2,128,256]{2,1,0:T(8,128)(2,1)S(1)}, u32[]{:S(2)}, u32[]{:S(2)}) collective-permute-start(bf16[2,128,256]{2,1,0:T(8,128)(2,1)S(1)} %get-tuple-element.50), channel_id=1, source_target_pairs={{0,24},{1,25},{2,26},{3,27},{4,28},{5,29},{6,30},{7,31},{8,0},{9,1... | collective-permute-start | bytes 393224 | tf_op jit(solution)/shard_map/sum_over_col/ppermute | solution.py:39
  68.0 2.8 %collective-permute-done.17 = bf16[2,128,256]{2,1,0:T(8,128)(2,1)S(1)} collective-permute-done((bf16[2,128,256]{2,1,0:T(8,128)(2,1)S(1)}, bf16[2,128,256]{2,1,0:T(8,128)(2,1)S(1)}, u32[]{:S(2)}, u32[]{:S(2)}) %collective-permute-start.17) | collective-permute-done | bytes 131104 | tf_op jit(solution)/shard_map/sum_over_col/ppermute | solution.py:39
  71.4 2.5 %pointwise.1 = (bf16[256,256]{1,0:T(8,128)(2,1)}, bf16[256,256]{1,0:T(8,128)(2,1)}, f32[256,256]{1,0:T(8,128)}, f32[256,256]{1,0:T(8,128)}) custom-call(bf16[256,256]{1,0:T(8,128)(2,1)} %bitcast.44, bf16[256,256]{1,0:T(8,128)(2,1)} %bitcast.43, bf16[256,256]{1,0:T(8,128)(2,1)} %bitcast.45, bf16[256,256]{1,0:T(8,128)(2,1)} %bitcast.41, ...), custom_call_target="tpu_custom_call" | custom-call | tf_op jit(solution)/shard_map/pointwise/pallas_call | solution.py:182
  73.9 4.4 %collective-permute-start.20 = (bf16[256,256]{1,0:T(8,128)(2,1)}, bf16[256,256]{1,0:T(8,128)(2,1)S(1)}, u32[]{:S(2)}, u32[]{:S(2)}) collective-permute-start(bf16[256,256]{1,0:T(8,128)(2,1)} %get-tuple-element.31), channel_id=1, source_target_pairs={{0,24},{1,25},{2,26},{3,27},{4,28},{5,29},{6,30},{7,31},{8,0},{9,1... | collective-permute-start | bytes 393224 | tf_op jit(solution)/shard_map/gather_gradients/ppermute | solution.py:39
  78.3 1.9 %collective-permute-start.19 = (bf16[256,256]{1,0:T(8,128)(2,1)}, bf16[256,256]{1,0:T(8,128)(2,1)S(1)}, u32[]{:S(2)}, u32[]{:S(2)}) collective-permute-start(bf16[256,256]{1,0:T(8,128)(2,1)} %get-tuple-element.31), channel_id=1, source_target_pairs={{0,16},{1,17},{2,18},{3,19},{4,20},{5,21},{6,22},{7,23},{8,24},{9,... | collective-permute-start | bytes 393224 | tf_op jit(solution)/shard_map/gather_gradients/ppermute | solution.py:39
  80.2 1.1 collective-permute-start.18
  81.2 2.1 %gather_gradients.1 = f32[256,384]{1,0:T(8,128)} custom-call(f32[256,256]{1,0:T(8,128)} %get-tuple-element.32.total, f32[256,256]{1,0:T(8,128)} %get-tuple-element.33.pre_grad), custom_call_target="tpu_custom_call" | custom-call | tf_op jit(solution)/shard_map/gather_gradients/pallas_call | solution.py:204
  83.3 0.9 collective-permute-done.20
  84.2 5.5 %collective-permute-done.19 = bf16[256,256]{1,0:T(8,128)(2,1)S(1)} collective-permute-done((bf16[256,256]{1,0:T(8,128)(2,1)}, bf16[256,256]{1,0:T(8,128)(2,1)S(1)}, u32[]{:S(2)}, u32[]{:S(2)}) %collective-permute-start.19) | collective-permute-done | bytes 131104 | tf_op jit(solution)/shard_map/gather_gradients/ppermute | solution.py:39
  89.7 0.8 collective-permute-done.18
  90.5 9.5 %all-to-all-start.1 = ((f32[32,8,384]{2,1,0:T(8,128)}), f32[32,8,384]{2,1,0:T(8,128)S(1)}, u32[]{:S(2)}, u32[]{:S(2)}) async-start(f32[32,8,384]{2,1,0:T(8,128)} %bitcast.32), calls=%async_computation.1 | async-start | bytes 786432 | tf_op jit(solution)/shard_map/sum_weight_grad/all_to_all | solution.py:295
  100.0 0.9 constant_dynamic-update-slice_fusion.3
  101.0 2.7 %collective-permute-start.23 = (bf16[1024,256]{1,0:T(8,128)(2,1)S(1)}, bf16[1024,256]{1,0:T(8,128)(2,1)S(1)}, u32[]{:S(2)}, u32[]{:S(2)}) collective-permute-start(bf16[1024,256]{1,0:T(8,128)(2,1)S(1)} %constant_dynamic-update-slice_fusion), channel_id=1, source_target_pairs={{0,6},{1,7},{2,0},{3,1},{4,2},{5,3},{6,4},{7,5},{8,14},{9,15},{10,... | collective-permute-start | bytes 1572872 | tf_op jit(solution)/shard_map/gather_gradients/ppermute | solution.py:39
  104.8 10.6 %all-to-all-done.1 = f32[32,8,384]{2,1,0:T(8,128)S(1)} async-done(((f32[32,8,384]{2,1,0:T(8,128)}), f32[32,8,384]{2,1,0:T(8,128)S(1)}, u32[]{:S(2)}, u32[]{:S(2)}) %all-to-all-start.1) | async-done | bytes 393248 | tf_op jit(solution)/shard_map/sum_weight_grad/all_to_all | solution.py:295
  115.5 12.8 %all_to_all.20 = f32[8,8,384]{2,1,0:T(8,128)S(1)} all-to-all(f32[8,8,384]{2,1,0:T(8,128)S(1)} %broadcast_in_dim.6), channel_id=1, replica_groups=mesh['row'=8,'col'=32] {'row'}, dimensions={0} | all-to-all | bytes 196608 | tf_op jit(solution)/shard_map/sum_weight_grad/all_to_all | solution.py:297
  128.4 0.8 broadcast_in_dim.7
  129.1 5.2 %all-to-all-start.3 = ((f32[32,8,384]{2,1,0:T(8,128)}), f32[32,8,384]{2,1,0:T(8,128)S(1)}, u32[]{:S(2)}, u32[]{:S(2)}) async-start(f32[32,8,384]{2,1,0:T(8,128)} %broadcast_in_dim.7), calls=%async_computation.3 | async-start | bytes 786432 | tf_op jit(solution)/shard_map/sum_weight_grad/all_to_all | solution.py:311
  135.4 0.9 collective-permute-done.24
  138.5 0.8 copy-done.8
  139.4 4.9 %tiles_backward.1 = bf16[16,128,256]{2,1,0:T(8,128)(2,1)} custom-call(s32[1]{0:T(128)} %bitcast.28.live, s32[192]{0:T(256)} %get-tuple-element.38.take, s32[192]{0:T(256)} %bitcast.47, bf16[1,192,128,128]{3,2,1,0:T(8,128)(2,1)} %tiles.3, bf16[8,128,256]{2,1,0:T(8,128)(2,1)} %bitcast.33, bf16[8,128,256]{2,1,0:T(8,128)(2,1)} %bitcast.36, ...), custom_call_target="tpu_custom_call" | custom-call | flops 1610612736 | bytes 6291456 | tf_op jit(solution)/shard_map/tiles_backward/pallas_call | solution.py:127
  144.3 5.7 %all-to-all-done.3 = f32[32,8,384]{2,1,0:T(8,128)S(1)} async-done(((f32[32,8,384]{2,1,0:T(8,128)}), f32[32,8,384]{2,1,0:T(8,128)S(1)}, u32[]{:S(2)}, u32[]{:S(2)}) %all-to-all-start.3) | async-done | bytes 393248 | tf_op jit(solution)/shard_map/sum_weight_grad/all_to_all | solution.py:311
  150.0 3.6 %all-to-all-start = ((bf16[8,256,256]{2,1,0:T(8,128)(2,1)}), bf16[8,256,256]{2,1,0:T(8,128)(2,1)S(1)}, u32[]{:S(2)}, u32[]{:S(2)}) async-start(bf16[8,256,256]{2,1,0:T(8,128)(2,1)} %bitcast.29), calls=%async_computation | async-start | bytes 2097152 | tf_op jit(solution)/shard_map/sum_over_row/all_to_all | solution.py:307
  155.0 14.8 %all-to-all-done.pieces = bf16[8,256,256]{2,1,0:T(8,128)(2,1)S(1)} async-done(((bf16[8,256,256]{2,1,0:T(8,128)(2,1)}), bf16[8,256,256]{2,1,0:T(8,128)(2,1)S(1)}, u32[]{:S(2)}, u32[]{:S(2)}) %all-to-all-start) | async-done | bytes 1048608 | tf_op jit(solution)/shard_map/sum_over_row/all_to_all | solution.py:307
  169.8 1.0 copy-done
  170.8 2.2 %sum_over_row.1 = bf16[256,256]{1,0:T(8,128)(2,1)} custom-call(bf16[8,256,256]{2,1,0:T(8,128)(2,1)} %copy-done, bf16[256,256]{1,0:T(8,128)(2,1)} %weight.1), custom_call_target="tpu_custom_call" | custom-call | tf_op jit(solution)/shard_map/sum_over_row/pallas_call | solution.py:228
  (61 shorter events, 9.3 us)
Async XLA Ops:
  0.6 10.8 %collective-permute-start.4 = (bf16[256,256]{1,0:T(8,128)(2,1)}, bf16[256,256]{1,0:T(8,128)(2,1)}, u32[]{:S(2)}, u32[]{:S(2)}) collective-permute-start(bf16[256,256]{1,0:T(8,128)(2,1)} %param.8), channel_id=1, source_target_pairs={{0,160},{32,128},{64,224},{96,192},{128,32},{160,0},{192,96},{224,... | collective-permute-start | bytes 393224 | tf_op jit(solution)/shard_map/gather_features/ppermute | solution.py:29
  5.6 10.9 %collective-permute-start.3 = (bf16[256,256]{1,0:T(8,128)(2,1)}, bf16[256,256]{1,0:T(8,128)(2,1)}, u32[]{:S(2)}, u32[]{:S(2)}) collective-permute-start(bf16[256,256]{1,0:T(8,128)(2,1)} %param.8), channel_id=1, source_target_pairs={{0,128},{32,160},{64,192},{96,224},{128,0},{160,32},{192,64},{224,... | collective-permute-start | bytes 393224 | tf_op jit(solution)/shard_map/gather_features/ppermute | solution.py:29
  5.9 11.9 %collective-permute-start.2 = (bf16[256,256]{1,0:T(8,128)(2,1)}, bf16[256,256]{1,0:T(8,128)(2,1)}, u32[]{:S(2)}, u32[]{:S(2)}) collective-permute-start(bf16[256,256]{1,0:T(8,128)(2,1)} %param.8), channel_id=1, source_target_pairs={{0,96},{32,64},{64,160},{96,128},{128,224},{160,192},{192,32},{224... | collective-permute-start | bytes 393224 | tf_op jit(solution)/shard_map/gather_features/ppermute | solution.py:29
  6.6 12.9 %collective-permute-start.1 = (bf16[256,256]{1,0:T(8,128)(2,1)}, bf16[256,256]{1,0:T(8,128)(2,1)}, u32[]{:S(2)}, u32[]{:S(2)}) collective-permute-start(bf16[256,256]{1,0:T(8,128)(2,1)} %param.8), channel_id=1, source_target_pairs={{0,64},{32,96},{64,128},{96,160},{128,192},{160,224},{192,0},{224,... | collective-permute-start | bytes 393224 | tf_op jit(solution)/shard_map/gather_features/ppermute | solution.py:29
  7.8 11.7 %collective-permute-start = (bf16[256,256]{1,0:T(8,128)(2,1)}, bf16[256,256]{1,0:T(8,128)(2,1)}, u32[]{:S(2)}, u32[]{:S(2)}) collective-permute-start(bf16[256,256]{1,0:T(8,128)(2,1)} %param.8), channel_id=1, source_target_pairs={{0,32},{32,0},{64,96},{96,64},{128,160},{160,128},{192,224},{224,1... | collective-permute-start | bytes 393224 | tf_op jit(solution)/shard_map/gather_features/ppermute | solution.py:29
  11.4 8.2 %collective-permute-start.6 = (bf16[256,256]{1,0:T(8,128)(2,1)}, bf16[256,256]{1,0:T(8,128)(2,1)}, u32[]{:S(2)}, u32[]{:S(2)}) collective-permute-start(bf16[256,256]{1,0:T(8,128)(2,1)} %param.8), channel_id=1, source_target_pairs={{0,224},{32,192},{64,32},{96,0},{128,96},{160,64},{192,160},{224,1... | collective-permute-start | bytes 393224 | tf_op jit(solution)/shard_map/gather_features/ppermute | solution.py:29
  16.5 4.7 %collective-permute-start.5 = (bf16[256,256]{1,0:T(8,128)(2,1)}, bf16[256,256]{1,0:T(8,128)(2,1)}, u32[]{:S(2)}, u32[]{:S(2)}) collective-permute-start(bf16[256,256]{1,0:T(8,128)(2,1)} %param.8), channel_id=1, source_target_pairs={{0,192},{32,224},{64,0},{96,32},{128,64},{160,96},{192,128},{224,1... | collective-permute-start | bytes 393224 | tf_op jit(solution)/shard_map/gather_features/ppermute | solution.py:29
  26.3 4.2 %collective-permute-start.7 = (bf16[16,128,256]{2,1,0:T(8,128)(2,1)}, bf16[16,128,256]{2,1,0:T(8,128)(2,1)S(1)}, u32[]{:S(2)}, u32[]{:S(2)}) collective-permute-start(bf16[16,128,256]{2,1,0:T(8,128)(2,1)} %get-tuple-element.22), channel_id=1, source_target_pairs={{0,1},{1,0},{2,3},{3,2},{4,5},{5,4},{6,7},{7,6},{8,9},{9,8},{10,11... | collective-permute-start | bytes 3145736 | tf_op jit(solution)/shard_map/sum_over_col/ppermute | solution.py:39
  28.0 11.7 %collective-permute-start.12 = (bf16[16,128,256]{2,1,0:T(8,128)(2,1)}, bf16[16,128,256]{2,1,0:T(8,128)(2,1)S(1)}, u32[]{:S(2)}, u32[]{:S(2)}) collective-permute-start(bf16[16,128,256]{2,1,0:T(8,128)(2,1)} %get-tuple-element.24), channel_id=1, source_target_pairs={{0,1},{1,0},{2,3},{3,2},{4,5},{5,4},{6,7},{7,6},{8,9},{9,8},{10,11... | collective-permute-start | bytes 3145736 | tf_op jit(solution)/shard_map/sum_over_col/ppermute | solution.py:39
  32.0 17.2 %collective-permute-start.10 = (bf16[4,128,256]{2,1,0:T(8,128)(2,1)S(1)}, bf16[4,128,256]{2,1,0:T(8,128)(2,1)S(1)}, u32[]{:S(2)}, u32[]{:S(2)}) collective-permute-start(bf16[4,128,256]{2,1,0:T(8,128)(2,1)S(1)} %get-tuple-element.46), channel_id=1, source_target_pairs={{0,6},{1,7},{2,0},{3,1},{4,2},{5,3},{6,4},{7,5},{8,14},{9,15},{10,... | collective-permute-start | bytes 786440 | tf_op jit(solution)/shard_map/sum_over_col/ppermute | solution.py:39
  38.5 13.4 %collective-permute-start.9 = (bf16[4,128,256]{2,1,0:T(8,128)(2,1)S(1)}, bf16[4,128,256]{2,1,0:T(8,128)(2,1)S(1)}, u32[]{:S(2)}, u32[]{:S(2)}) collective-permute-start(bf16[4,128,256]{2,1,0:T(8,128)(2,1)S(1)} %get-tuple-element.47), channel_id=1, source_target_pairs={{0,2},{1,3},{2,4},{3,5},{4,6},{5,7},{6,0},{7,1},{8,10},{9,11},{10,... | collective-permute-start | bytes 786440 | tf_op jit(solution)/shard_map/sum_over_col/ppermute | solution.py:39
  38.5 13.4 %collective-permute-start.8 = (bf16[4,128,256]{2,1,0:T(8,128)(2,1)S(1)}, bf16[4,128,256]{2,1,0:T(8,128)(2,1)S(1)}, u32[]{:S(2)}, u32[]{:S(2)}) collective-permute-start(bf16[4,128,256]{2,1,0:T(8,128)(2,1)S(1)} %get-tuple-element.48), channel_id=1, source_target_pairs={{0,4},{1,5},{2,6},{3,7},{4,0},{5,1},{6,2},{7,3},{8,12},{9,13},{10,... | collective-permute-start | bytes 786440 | tf_op jit(solution)/shard_map/sum_over_col/ppermute | solution.py:39
  41.3 19.2 %collective-permute-start.15 = (bf16[4,128,256]{2,1,0:T(8,128)(2,1)S(1)}, bf16[4,128,256]{2,1,0:T(8,128)(2,1)S(1)}, u32[]{:S(2)}, u32[]{:S(2)}) collective-permute-start(bf16[4,128,256]{2,1,0:T(8,128)(2,1)S(1)} %get-tuple-element.41), channel_id=1, source_target_pairs={{0,6},{1,7},{2,0},{3,1},{4,2},{5,3},{6,4},{7,5},{8,14},{9,15},{10,... | collective-permute-start | bytes 786440 | tf_op jit(solution)/shard_map/sum_over_col/ppermute | solution.py:39
  42.7 21.0 %collective-permute-start.14 = (bf16[4,128,256]{2,1,0:T(8,128)(2,1)S(1)}, bf16[4,128,256]{2,1,0:T(8,128)(2,1)S(1)}, u32[]{:S(2)}, u32[]{:S(2)}) collective-permute-start(bf16[4,128,256]{2,1,0:T(8,128)(2,1)S(1)} %get-tuple-element.42), channel_id=1, source_target_pairs={{0,2},{1,3},{2,4},{3,5},{4,6},{5,7},{6,0},{7,1},{8,10},{9,11},{10,... | collective-permute-start | bytes 786440 | tf_op jit(solution)/shard_map/sum_over_col/ppermute | solution.py:39
  49.3 14.5 %collective-permute-start.13 = (bf16[4,128,256]{2,1,0:T(8,128)(2,1)S(1)}, bf16[4,128,256]{2,1,0:T(8,128)(2,1)S(1)}, u32[]{:S(2)}, u32[]{:S(2)}) collective-permute-start(bf16[4,128,256]{2,1,0:T(8,128)(2,1)S(1)} %get-tuple-element.43), channel_id=1, source_target_pairs={{0,4},{1,5},{2,6},{3,7},{4,0},{5,1},{6,2},{7,3},{8,12},{9,13},{10,... | collective-permute-start | bytes 786440 | tf_op jit(solution)/shard_map/sum_over_col/ppermute | solution.py:39
  52.1 11.7 %collective-permute-start.16 = (bf16[2,128,256]{2,1,0:T(8,128)(2,1)S(1)}, bf16[2,128,256]{2,1,0:T(8,128)(2,1)S(1)}, u32[]{:S(2)}, u32[]{:S(2)}) collective-permute-start(bf16[2,128,256]{2,1,0:T(8,128)(2,1)S(1)} %get-tuple-element.51), channel_id=1, source_target_pairs={{0,8},{1,9},{2,10},{3,11},{4,12},{5,13},{6,14},{7,15},{8,16},{9,17... | collective-permute-start | bytes 393224 | tf_op jit(solution)/shard_map/sum_over_col/ppermute | solution.py:39
  52.7 15.2 %collective-permute-start.11 = (bf16[2,128,256]{2,1,0:T(8,128)(2,1)S(1)}, bf16[2,128,256]{2,1,0:T(8,128)(2,1)S(1)}, u32[]{:S(2)}, u32[]{:S(2)}) collective-permute-start(bf16[2,128,256]{2,1,0:T(8,128)(2,1)S(1)} %get-tuple-element.52), channel_id=1, source_target_pairs={{0,16},{1,17},{2,18},{3,19},{4,20},{5,21},{6,22},{7,23},{8,24},{9,... | collective-permute-start | bytes 393224 | tf_op jit(solution)/shard_map/sum_over_col/ppermute | solution.py:39
  63.7 7.0 %copy-start.9 = (bf16[2,128,256]{2,1,0:T(8,128)(2,1)}, bf16[2,128,256]{2,1,0:T(8,128)(2,1)S(1)}, u32[]{:S(2)}) copy-start(bf16[2,128,256]{2,1,0:T(8,128)(2,1)S(1)} %collective-permute-done.16) | copy-start | bytes 393220
  64.5 6.2 %collective-permute-start.17 = (bf16[2,128,256]{2,1,0:T(8,128)(2,1)S(1)}, bf16[2,128,256]{2,1,0:T(8,128)(2,1)S(1)}, u32[]{:S(2)}, u32[]{:S(2)}) collective-permute-start(bf16[2,128,256]{2,1,0:T(8,128)(2,1)S(1)} %get-tuple-element.50), channel_id=1, source_target_pairs={{0,24},{1,25},{2,26},{3,27},{4,28},{5,29},{6,30},{7,31},{8,0},{9,1... | collective-permute-start | bytes 393224 | tf_op jit(solution)/shard_map/sum_over_col/ppermute | solution.py:39
  68.0 2.8 %copy-start.10 = (bf16[2,128,256]{2,1,0:T(8,128)(2,1)}, bf16[2,128,256]{2,1,0:T(8,128)(2,1)S(1)}, u32[]{:S(2)}) copy-start(bf16[2,128,256]{2,1,0:T(8,128)(2,1)S(1)} %collective-permute-done.11) | copy-start | bytes 393220
  70.8 0.7 copy-start.11
  73.9 10.3 %collective-permute-start.20 = (bf16[256,256]{1,0:T(8,128)(2,1)}, bf16[256,256]{1,0:T(8,128)(2,1)S(1)}, u32[]{:S(2)}, u32[]{:S(2)}) collective-permute-start(bf16[256,256]{1,0:T(8,128)(2,1)} %get-tuple-element.31), channel_id=1, source_target_pairs={{0,24},{1,25},{2,26},{3,27},{4,28},{5,29},{6,30},{7,31},{8,0},{9,1... | collective-permute-start | bytes 393224 | tf_op jit(solution)/shard_map/gather_gradients/ppermute | solution.py:39
  78.3 11.4 %collective-permute-start.19 = (bf16[256,256]{1,0:T(8,128)(2,1)}, bf16[256,256]{1,0:T(8,128)(2,1)S(1)}, u32[]{:S(2)}, u32[]{:S(2)}) collective-permute-start(bf16[256,256]{1,0:T(8,128)(2,1)} %get-tuple-element.31), channel_id=1, source_target_pairs={{0,16},{1,17},{2,18},{3,19},{4,20},{5,21},{6,22},{7,23},{8,24},{9,... | collective-permute-start | bytes 393224 | tf_op jit(solution)/shard_map/gather_gradients/ppermute | solution.py:39
  80.2 10.3 %collective-permute-start.18 = (bf16[256,256]{1,0:T(8,128)(2,1)}, bf16[256,256]{1,0:T(8,128)(2,1)S(1)}, u32[]{:S(2)}, u32[]{:S(2)}) collective-permute-start(bf16[256,256]{1,0:T(8,128)(2,1)} %get-tuple-element.31), channel_id=1, source_target_pairs={{0,8},{1,9},{2,10},{3,11},{4,12},{5,13},{6,14},{7,15},{8,16},{9,17... | collective-permute-start | bytes 393224 | tf_op jit(solution)/shard_map/gather_gradients/ppermute | solution.py:39
  90.5 25.0 %all-to-all-start.1 = ((f32[32,8,384]{2,1,0:T(8,128)}), f32[32,8,384]{2,1,0:T(8,128)S(1)}, u32[]{:S(2)}, u32[]{:S(2)}) async-start(f32[32,8,384]{2,1,0:T(8,128)} %bitcast.32), calls=%async_computation.1 | async-start | bytes 786432 | tf_op jit(solution)/shard_map/sum_weight_grad/all_to_all | solution.py:295
  101.0 38.3 %copy-start.1 = (bf16[1024,256]{1,0:T(8,128)(2,1)}, bf16[1024,256]{1,0:T(8,128)(2,1)S(1)}, u32[]{:S(2)}) copy-start(bf16[1024,256]{1,0:T(8,128)(2,1)S(1)} %constant_dynamic-update-slice_fusion) | copy-start | bytes 1572868
  101.0 33.6 %collective-permute-start.23 = (bf16[1024,256]{1,0:T(8,128)(2,1)S(1)}, bf16[1024,256]{1,0:T(8,128)(2,1)S(1)}, u32[]{:S(2)}, u32[]{:S(2)}) collective-permute-start(bf16[1024,256]{1,0:T(8,128)(2,1)S(1)} %constant_dynamic-update-slice_fusion), channel_id=1, source_target_pairs={{0,6},{1,7},{2,0},{3,1},{4,2},{5,3},{6,4},{7,5},{8,14},{9,15},{10,... | collective-permute-start | bytes 1572872 | tf_op jit(solution)/shard_map/gather_gradients/ppermute | solution.py:39
  103.7 31.2 %collective-permute-start.22 = (bf16[1024,256]{1,0:T(8,128)(2,1)S(1)}, bf16[1024,256]{1,0:T(8,128)(2,1)S(1)}, u32[]{:S(2)}, u32[]{:S(2)}) collective-permute-start(bf16[1024,256]{1,0:T(8,128)(2,1)S(1)} %constant_dynamic-update-slice_fusion), channel_id=1, source_target_pairs={{0,4},{1,5},{2,6},{3,7},{4,0},{5,1},{6,2},{7,3},{8,12},{9,13},{10,... | collective-permute-start | bytes 1572872 | tf_op jit(solution)/shard_map/gather_gradients/ppermute | solution.py:39
  104.3 30.9 %collective-permute-start.21 = (bf16[1024,256]{1,0:T(8,128)(2,1)S(1)}, bf16[1024,256]{1,0:T(8,128)(2,1)S(1)}, u32[]{:S(2)}, u32[]{:S(2)}) collective-permute-start(bf16[1024,256]{1,0:T(8,128)(2,1)S(1)} %constant_dynamic-update-slice_fusion), channel_id=1, source_target_pairs={{0,2},{1,3},{2,4},{3,5},{4,6},{5,7},{6,0},{7,1},{8,10},{9,11},{10,... | collective-permute-start | bytes 1572872 | tf_op jit(solution)/shard_map/gather_gradients/ppermute | solution.py:39
  129.1 20.9 %all-to-all-start.3 = ((f32[32,8,384]{2,1,0:T(8,128)}), f32[32,8,384]{2,1,0:T(8,128)S(1)}, u32[]{:S(2)}, u32[]{:S(2)}) async-start(f32[32,8,384]{2,1,0:T(8,128)} %broadcast_in_dim.7), calls=%async_computation.3 | async-start | bytes 786432 | tf_op jit(solution)/shard_map/sum_weight_grad/all_to_all | solution.py:311
  134.3 2.0 %collective-permute-start.24 = (bf16[1024,256]{1,0:T(8,128)(2,1)S(1)}, bf16[1024,256]{1,0:T(8,128)(2,1)S(1)}, u32[]{:S(2)}, u32[]{:S(2)}) collective-permute-start(bf16[1024,256]{1,0:T(8,128)(2,1)S(1)} %constant_dynamic-update-slice_fusion), channel_id=1, source_target_pairs={{0,1},{1,0},{2,3},{3,2},{4,5},{5,4},{6,7},{7,6},{8,9},{9,8},{10,11... | collective-permute-start | bytes 1572872 | tf_op jit(solution)/shard_map/gather_gradients/ppermute | solution.py:39
  134.6 4.7 %copy-start.2 = (bf16[1024,256]{1,0:T(8,128)(2,1)}, bf16[1024,256]{1,0:T(8,128)(2,1)S(1)}, u32[]{:S(2)}) copy-start(bf16[1024,256]{1,0:T(8,128)(2,1)S(1)} %collective-permute-done.23) | copy-start | bytes 1572868
  134.6 2.4 %collective-permute-start.27 = (bf16[1024,256]{1,0:T(8,128)(2,1)S(1)}, bf16[1024,256]{1,0:T(8,128)(2,1)S(1)}, u32[]{:S(2)}, u32[]{:S(2)}) collective-permute-start(bf16[1024,256]{1,0:T(8,128)(2,1)S(1)} %collective-permute-done.23), channel_id=1, source_target_pairs={{0,1},{1,0},{2,3},{3,2},{4,5},{5,4},{6,7},{7,6},{8,9},{9,8},{10,11... | collective-permute-start | bytes 1572872 | tf_op jit(solution)/shard_map/gather_gradients/ppermute | solution.py:39
  134.9 4.4 %copy-start.3 = (bf16[1024,256]{1,0:T(8,128)(2,1)}, bf16[1024,256]{1,0:T(8,128)(2,1)S(1)}, u32[]{:S(2)}) copy-start(bf16[1024,256]{1,0:T(8,128)(2,1)S(1)} %collective-permute-done.22) | copy-start | bytes 1572868
  134.9 2.9 %collective-permute-start.26 = (bf16[1024,256]{1,0:T(8,128)(2,1)S(1)}, bf16[1024,256]{1,0:T(8,128)(2,1)S(1)}, u32[]{:S(2)}, u32[]{:S(2)}) collective-permute-start(bf16[1024,256]{1,0:T(8,128)(2,1)S(1)} %collective-permute-done.22), channel_id=1, source_target_pairs={{0,1},{1,0},{2,3},{3,2},{4,5},{5,4},{6,7},{7,6},{8,9},{9,8},{10,11... | collective-permute-start | bytes 1572872 | tf_op jit(solution)/shard_map/gather_gradients/ppermute | solution.py:39
  135.1 4.2 %copy-start.4 = (bf16[1024,256]{1,0:T(8,128)(2,1)}, bf16[1024,256]{1,0:T(8,128)(2,1)S(1)}, u32[]{:S(2)}) copy-start(bf16[1024,256]{1,0:T(8,128)(2,1)S(1)} %collective-permute-done.21) | copy-start | bytes 1572868
  135.1 3.4 %collective-permute-start.25 = (bf16[1024,256]{1,0:T(8,128)(2,1)S(1)}, bf16[1024,256]{1,0:T(8,128)(2,1)S(1)}, u32[]{:S(2)}, u32[]{:S(2)}) collective-permute-start(bf16[1024,256]{1,0:T(8,128)(2,1)S(1)} %collective-permute-done.21), channel_id=1, source_target_pairs={{0,1},{1,0},{2,3},{3,2},{4,5},{5,4},{6,7},{7,6},{8,9},{9,8},{10,11... | collective-permute-start | bytes 1572872 | tf_op jit(solution)/shard_map/gather_gradients/ppermute | solution.py:39
  136.3 3.1 %copy-start.5 = (bf16[1024,256]{1,0:T(8,128)(2,1)}, bf16[1024,256]{1,0:T(8,128)(2,1)S(1)}, u32[]{:S(2)}) copy-start(bf16[1024,256]{1,0:T(8,128)(2,1)S(1)} %collective-permute-done.24) | copy-start | bytes 1572868
  137.0 2.3 %copy-start.6 = (bf16[1024,256]{1,0:T(8,128)(2,1)}, bf16[1024,256]{1,0:T(8,128)(2,1)S(1)}, u32[]{:S(2)}) copy-start(bf16[1024,256]{1,0:T(8,128)(2,1)S(1)} %collective-permute-done.27) | copy-start | bytes 1572868
  137.8 1.6 copy-start.7
  138.5 0.8 copy-start.8
  150.0 19.8 %all-to-all-start = ((bf16[8,256,256]{2,1,0:T(8,128)(2,1)}), bf16[8,256,256]{2,1,0:T(8,128)(2,1)S(1)}, u32[]{:S(2)}, u32[]{:S(2)}) async-start(bf16[8,256,256]{2,1,0:T(8,128)(2,1)} %bitcast.29), calls=%async_computation | async-start | bytes 2097152 | tf_op jit(solution)/shard_map/sum_over_row/all_to_all | solution.py:307
  169.8 1.0 copy-start

commit v7 on v6

--- a/solution.py
+++ b/solution.py
@@ -193,9 +193,9 @@
     width = total.shape[1]
     rows = (((0,), (0,)), ((), ()))
     rounded = pre_grad[...].astype(jnp.bfloat16)
-    load[:, :width] = split_dot(total[...], rounded, rows)
+    load[:, :width] = split_dot(total[...], rounded, rows).astype(load.dtype)
     ones = jnp.ones((total.shape[0], LANES), jnp.bfloat16)
-    load[:, width:] = split_dot(pre_grad[...], ones, rows)
+    load[:, width:] = split_dot(pre_grad[...], ones, rows).astype(load.dtype)
 
 
 def loads(total, pre_grad):
@@ -205,7 +205,7 @@
         load_kernel,
         in_specs=[vmem] * 2,
         out_specs=vmem,
-        out_shape=jax.ShapeDtypeStruct((width, width + LANES), jnp.float32),
+        out_shape=jax.ShapeDtypeStruct((width, width + LANES), jnp.bfloat16),
         compiler_params=pltpu.CompilerParams(vmem_limit_bytes=VMEM_LIMIT),
     )(total, pre_grad)
 
@@ -292,12 +292,15 @@
         *near, load = lax.optimization_barrier((*near, load))
         here = [jnp.concatenate([grad] + near)]
     with jax.named_scope("sum_weight_grad"):
-        load = jnp.sum(lax.all_to_all(load, "col", 0, 0, tiled=True), axis=0)
+        load = lax.all_to_all(load, "col", 0, 0, tiled=True)
+        load = jnp.sum(load.astype(jnp.float32), axis=0)
+        there = [col_shift(here[0], dcore=1)]
+        there[0], load = lax.optimization_barrier((there[0], load))
         load = jnp.broadcast_to(load, (N_ROW,) + load.shape)
         load = jnp.sum(lax.all_to_all(load, "row", 0, 0, tiled=True), axis=0) * scale
     with jax.named_scope("gather_gradients"):
         here += [col_shift(here[0], dy=k) for k in range(1, N_Y)]
-        there = [col_shift(p, dcore=1) for p in here]
+        there += [col_shift(p, dcore=1) for p in here[1:]]
     with jax.named_scope("tiles_backward"):
         (back,) = tile_sum(
             adjacency, live, take_rows, c, here + there, [N_ROW * per], True, VMEM_LIMIT

time: 173 us -> 173 us (level)
  starting transfers between devices: 61.7 us -> 72.2 us
  waiting for transfers between devices: 68.1 us -> 58.5 us
  blocking collectives: 12.8 us -> 9.25 us
    ppermute x21, starting transfers between devices: 33.4 us -> 41.1 us  [col_shift(): return lax.ppermute(value, 'col', pairs)]
    all_to_all x1, blocking collectives: 12.8 us -> 9.25 us  [shards(): lax.all_to_all(load, 'row', 0, 0, tiled=True)]
    ppermute x7, waiting for transfers between devices: 7.36 us -> 4.07 us  [row_shift(): return lax.ppermute(value, 'row', pairs)]
    ppermute x21, waiting for transfers between devices: 29.6 us -> 26.6 us  [col_shift(): return lax.ppermute(value, 'col', pairs)]
    all_to_all x1, waiting for transfers between devices: 10.6 us -> 7.74 us  [shards(): load = lax.all_to_all(load, 'col', 0, 0, tiled=True)]
    all_to_all x1, starting transfers between devices: 9.54 us -> 12.2 us  [shards(): load = lax.all_to_all(load, 'col', 0, 0, tiled=True)]
  transfers between devices with their start and end apart: 31 -> 31, of which waited for: 19 -> 15; matrix products, arithmetic and copies ran while one was open for 6% -> 6% of each run, Pallas kernels for 4% -> 4%
where the time goes in v7:
time: 173 us; the launch traced here: 172 us
  starting transfers between devices  72.2 us (42%)
  waiting for transfers between devices  58.5 us (34%)
  Pallas kernels  18 us (10%)
  blocking collectives  9.25 us (5%)
  other arithmetic  6.54 us (4%)
  local copies, waits for them, and re-layouts  5.63 us (3%)
    ppermute x21, starting transfers between devices, col_shift(): return lax.ppermute(value, 'col', pairs)  41.1 us
    ppermute x21, waiting for transfers between devices, col_shift(): return lax.ppermute(value, 'col', pairs)  26.6 us
    all_to_all x1, waiting for transfers between devices, shards(): back = lax.all_to_all(back, 'row', 0, 0, tiled=True)  14.7 us
    all_to_all x1, starting transfers between devices, shards(): load = lax.all_to_all(load, 'col', 0, 0, tiled=True)  12.2 us
    pallas_call x2, Pallas kernels, tile_sum(): pl.pallas_call(functools.partial(tile_kernel, transposed, src_sizes, out_...  11.3 us
    ppermute x7, starting transfers between devices, row_shift(): return lax.ppermute(value, 'row', pairs)  10.4 us
    all_to_all x1, blocking collectives, shards(): lax.all_to_all(load, 'row', 0, 0, tiled=True)  9.25 us
    all_to_all x1, waiting for transfers between devices, shards(): load = lax.all_to_all(load, 'col', 0, 0, tiled=True)  7.74 us
  transfers between devices with their start and end apart: 31, of which 15 were waited for; matrix products, arithmetic and copies ran while one was open for 6% of the time, Pallas kernels for 4%

profile of v7, /device:TPU:1, one launch (start us, length us, event | category | flops | bytes accessed | tf_op | source)
XLA Modules:
  0.0 171.6 jit_solution(2838699447375259038)
XLA Ops:
  0.6 2.6 %collective-permute-start = (bf16[256,256]{1,0:T(8,128)(2,1)}, bf16[256,256]{1,0:T(8,128)(2,1)}, u32[]{:S(2)}, u32[]{:S(2)}) collective-permute-start(bf16[256,256]{1,0:T(8,128)(2,1)} %param.8), channel_id=1, source_target_pairs={{0,32},{32,0},{64,96},{96,64},{128,160},{160,128},{192,224},{224,1... | collective-permute-start | bytes 393224 | tf_op jit(solution)/shard_map/gather_features/ppermute | solution.py:29
  3.2 1.2 collective-permute-start.1
  4.4 1.0 collective-permute-start.2
  5.4 1.4 collective-permute-start.3
  6.9 2.6 %collective-permute-start.4 = (bf16[256,256]{1,0:T(8,128)(2,1)}, bf16[256,256]{1,0:T(8,128)(2,1)}, u32[]{:S(2)}, u32[]{:S(2)}) collective-permute-start(bf16[256,256]{1,0:T(8,128)(2,1)} %param.8), channel_id=1, source_target_pairs={{0,160},{32,128},{64,224},{96,192},{128,32},{160,0},{192,96},{224,... | collective-permute-start | bytes 393224 | tf_op jit(solution)/shard_map/gather_features/ppermute | solution.py:29
  10.2 1.3 multiply_add_fusion
  11.4 1.5 collective-permute-start.5
  13.0 1.3 fusion.2
  14.3 4.0 %collective-permute-done.3 = bf16[256,256]{1,0:T(8,128)(2,1)} collective-permute-done((bf16[256,256]{1,0:T(8,128)(2,1)}, bf16[256,256]{1,0:T(8,128)(2,1)}, u32[]{:S(2)}, u32[]{:S(2)}) %collective-permute-start.3) | collective-permute-done | bytes 131104 | tf_op jit(solution)/shard_map/gather_features/ppermute | solution.py:29
  18.3 5.7 %tiles_forward.1 = (bf16[16,128,256]{2,1,0:T(8,128)(2,1)}, bf16[16,128,256]{2,1,0:T(8,128)(2,1)}, bf16[16,128,256]{2,1,0:T(8,128)(2,1)}, bf16[16,128,256]{2,1,0:T(8,128)(2,1)}) custom-call(s32[1]{0:T(128)} %bitcast.27.live, s32[192]{0:T(256)} %get-tuple-element.57.take, s32[192]{0:T(256)} %get-tuple-element.58.put, bf16[1,192,128,128]{3,2,1,0:T(8,128)(2,1)} %tiles.3, ...), custom_call_target="tpu_custom_call" | custom-call | flops 1610612736 | bytes 6291456 | tf_op jit(solution)/shard_map/tiles_forward/pallas_call | solution.py:127
  24.1 5.3 %collective-permute-start.7 = (bf16[16,128,256]{2,1,0:T(8,128)(2,1)}, bf16[16,128,256]{2,1,0:T(8,128)(2,1)S(1)}, u32[]{:S(2)}, u32[]{:S(2)}) collective-permute-start(bf16[16,128,256]{2,1,0:T(8,128)(2,1)} %get-tuple-element.24), channel_id=1, source_target_pairs={{0,1},{1,0},{2,3},{3,2},{4,5},{5,4},{6,7},{7,6},{8,9},{9,8},{10,11... | collective-permute-start | bytes 3145736 | tf_op jit(solution)/shard_map/sum_over_col/ppermute | solution.py:39
  29.5 2.4 %collective-permute-done.7 = bf16[16,128,256]{2,1,0:T(8,128)(2,1)S(1)} collective-permute-done((bf16[16,128,256]{2,1,0:T(8,128)(2,1)}, bf16[16,128,256]{2,1,0:T(8,128)(2,1)S(1)}, u32[]{:S(2)}, u32[]{:S(2)}) %collective-permute-start.7) | collective-permute-done | bytes 1048608 | tf_op jit(solution)/shard_map/sum_over_col/ppermute | solution.py:39
  31.9 1.5 add_convert_fusion.7
  33.4 5.0 %collective-permute-start.10 = (bf16[4,128,256]{2,1,0:T(8,128)(2,1)S(1)}, bf16[4,128,256]{2,1,0:T(8,128)(2,1)S(1)}, u32[]{:S(2)}, u32[]{:S(2)}) collective-permute-start(bf16[4,128,256]{2,1,0:T(8,128)(2,1)S(1)} %get-tuple-element.50), channel_id=1, source_target_pairs={{0,6},{1,7},{2,0},{3,1},{4,2},{5,3},{6,4},{7,5},{8,14},{9,15},{10,... | collective-permute-start | bytes 786440 | tf_op jit(solution)/shard_map/sum_over_col/ppermute | solution.py:39
  38.4 1.3 collective-permute-start.8
  39.7 1.5 add_convert_fusion
  41.2 1.8 %collective-permute-start.13 = (bf16[4,128,256]{2,1,0:T(8,128)(2,1)S(1)}, bf16[4,128,256]{2,1,0:T(8,128)(2,1)S(1)}, u32[]{:S(2)}, u32[]{:S(2)}) collective-permute-start(bf16[4,128,256]{2,1,0:T(8,128)(2,1)S(1)} %get-tuple-element.47), channel_id=1, source_target_pairs={{0,4},{1,5},{2,6},{3,7},{4,0},{5,1},{6,2},{7,3},{8,12},{9,13},{10,... | collective-permute-start | bytes 786440 | tf_op jit(solution)/shard_map/sum_over_col/ppermute | solution.py:39
  43.3 11.6 %collective-permute-done.10 = bf16[4,128,256]{2,1,0:T(8,128)(2,1)S(1)} collective-permute-done((bf16[4,128,256]{2,1,0:T(8,128)(2,1)S(1)}, bf16[4,128,256]{2,1,0:T(8,128)(2,1)S(1)}, u32[]{:S(2)}, u32[]{:S(2)}) %collective-permute-start.10) | collective-permute-done | bytes 262176 | tf_op jit(solution)/shard_map/sum_over_col/ppermute | solution.py:39
  54.9 3.4 %collective-permute-start.15 = (bf16[4,128,256]{2,1,0:T(8,128)(2,1)S(1)}, bf16[4,128,256]{2,1,0:T(8,128)(2,1)S(1)}, u32[]{:S(2)}, u32[]{:S(2)}) collective-permute-start(bf16[4,128,256]{2,1,0:T(8,128)(2,1)S(1)} %get-tuple-element.45), channel_id=1, source_target_pairs={{0,6},{1,7},{2,0},{3,1},{4,2},{5,3},{6,4},{7,5},{8,14},{9,15},{10,... | collective-permute-start | bytes 786440 | tf_op jit(solution)/shard_map/sum_over_col/ppermute | solution.py:39
  58.6 4.6 %collective-permute-start.11 = (bf16[2,128,256]{2,1,0:T(8,128)(2,1)S(1)}, bf16[2,128,256]{2,1,0:T(8,128)(2,1)S(1)}, u32[]{:S(2)}, u32[]{:S(2)}) collective-permute-start(bf16[2,128,256]{2,1,0:T(8,128)(2,1)S(1)} %get-tuple-element.56), channel_id=1, source_target_pairs={{0,16},{1,17},{2,18},{3,19},{4,20},{5,21},{6,22},{7,23},{8,24},{9,... | collective-permute-start | bytes 393224 | tf_op jit(solution)/shard_map/sum_over_col/ppermute | solution.py:39
  63.6 0.9 collective-permute-done.16
  65.4 2.2 %collective-permute-start.17 = (bf16[2,128,256]{2,1,0:T(8,128)(2,1)S(1)}, bf16[2,128,256]{2,1,0:T(8,128)(2,1)S(1)}, u32[]{:S(2)}, u32[]{:S(2)}) collective-permute-start(bf16[2,128,256]{2,1,0:T(8,128)(2,1)S(1)} %get-tuple-element.54), channel_id=1, source_target_pairs={{0,24},{1,25},{2,26},{3,27},{4,28},{5,29},{6,30},{7,31},{8,0},{9,1... | collective-permute-start | bytes 393224 | tf_op jit(solution)/shard_map/sum_over_col/ppermute | solution.py:39
  67.6 3.3 %collective-permute-done.11 = bf16[2,128,256]{2,1,0:T(8,128)(2,1)S(1)} collective-permute-done((bf16[2,128,256]{2,1,0:T(8,128)(2,1)S(1)}, bf16[2,128,256]{2,1,0:T(8,128)(2,1)S(1)}, u32[]{:S(2)}, u32[]{:S(2)}) %collective-permute-start.11) | collective-permute-done | bytes 131104 | tf_op jit(solution)/shard_map/sum_over_col/ppermute | solution.py:39
  70.9 2.1 %collective-permute-done.17 = bf16[2,128,256]{2,1,0:T(8,128)(2,1)S(1)} collective-permute-done((bf16[2,128,256]{2,1,0:T(8,128)(2,1)S(1)}, bf16[2,128,256]{2,1,0:T(8,128)(2,1)S(1)}, u32[]{:S(2)}, u32[]{:S(2)}) %collective-permute-start.17) | collective-permute-done | bytes 131104 | tf_op jit(solution)/shard_map/sum_over_col/ppermute | solution.py:39
  73.6 2.5 %pointwise.1 = (bf16[256,256]{1,0:T(8,128)(2,1)}, bf16[256,256]{1,0:T(8,128)(2,1)}, f32[256,256]{1,0:T(8,128)}, f32[256,256]{1,0:T(8,128)}) custom-call(bf16[256,256]{1,0:T(8,128)(2,1)} %bitcast.44, bf16[256,256]{1,0:T(8,128)(2,1)} %bitcast.43, bf16[256,256]{1,0:T(8,128)(2,1)} %bitcast.45, bf16[256,256]{1,0:T(8,128)(2,1)} %bitcast.41, ...), custom_call_target="tpu_custom_call" | custom-call | tf_op jit(solution)/shard_map/pointwise/pallas_call | solution.py:182
  76.1 1.7 collective-permute-start.18
  77.8 2.3 %collective-permute-start.19 = (bf16[256,256]{1,0:T(8,128)(2,1)}, bf16[256,256]{1,0:T(8,128)(2,1)S(1)}, u32[]{:S(2)}, u32[]{:S(2)}) collective-permute-start(bf16[256,256]{1,0:T(8,128)(2,1)} %get-tuple-element.33), channel_id=1, source_target_pairs={{0,16},{1,17},{2,18},{3,19},{4,20},{5,21},{6,22},{7,23},{8,24},{9,... | collective-permute-start | bytes 393224 | tf_op jit(solution)/shard_map/gather_gradients/ppermute | solution.py:39
  80.1 1.0 collective-permute-start.20
  81.1 2.0 %gather_gradients.1 = bf16[256,384]{1,0:T(8,128)(2,1)} custom-call(f32[256,256]{1,0:T(8,128)} %get-tuple-element.34.total, f32[256,256]{1,0:T(8,128)} %get-tuple-element.35.pre_grad), custom_call_target="tpu_custom_call" | custom-call | tf_op jit(solution)/shard_map/gather_gradients/pallas_call | solution.py:204
  83.1 0.9 constant_dynamic-update-slice_fusion.3
  84.1 1.7 %collective-permute-done.19 = bf16[256,256]{1,0:T(8,128)(2,1)S(1)} collective-permute-done((bf16[256,256]{1,0:T(8,128)(2,1)}, bf16[256,256]{1,0:T(8,128)(2,1)S(1)}, u32[]{:S(2)}, u32[]{:S(2)}) %collective-permute-start.19) | collective-permute-done | bytes 131104 | tf_op jit(solution)/shard_map/gather_gradients/ppermute | solution.py:39
  85.8 1.9 %collective-permute-done.20 = bf16[256,256]{1,0:T(8,128)(2,1)S(1)} collective-permute-done((bf16[256,256]{1,0:T(8,128)(2,1)}, bf16[256,256]{1,0:T(8,128)(2,1)S(1)}, u32[]{:S(2)}, u32[]{:S(2)}) %collective-permute-start.20) | collective-permute-done | bytes 131104 | tf_op jit(solution)/shard_map/gather_gradients/ppermute | solution.py:39
  87.7 5.1 %collective-permute-start.24 = (bf16[1024,256]{1,0:T(8,128)(2,1)S(1)}, bf16[1024,256]{1,0:T(8,128)(2,1)S(1)}, u32[]{:S(2)}, u32[]{:S(2)}) collective-permute-start(bf16[1024,256]{1,0:T(8,128)(2,1)S(1)} %constant_dynamic-update-slice_fusion), channel_id=1, source_target_pairs={{0,1},{1,0},{2,3},{3,2},{4,5},{5,4},{6,7},{7,6},{8,9},{9,8},{10,11... | collective-permute-start | bytes 1572872 | tf_op jit(solution)/shard_map/sum_weight_grad/ppermute | solution.py:39
  92.9 12.2 %all-to-all-start = ((bf16[32,8,384]{2,1,0:T(8,128)(2,1)}), bf16[32,8,384]{2,1,0:T(8,128)(2,1)S(1)}, u32[]{:S(2)}, u32[]{:S(2)}) async-start(bf16[32,8,384]{2,1,0:T(8,128)(2,1)} %bitcast.33), calls=%async_computation | async-start | bytes 393216 | tf_op jit(solution)/shard_map/sum_weight_grad/all_to_all | solution.py:295
  105.1 1.5 collective-permute-start.21
  106.5 2.4 %collective-permute-start.22 = (bf16[1024,256]{1,0:T(8,128)(2,1)S(1)}, bf16[1024,256]{1,0:T(8,128)(2,1)S(1)}, u32[]{:S(2)}, u32[]{:S(2)}) collective-permute-start(bf16[1024,256]{1,0:T(8,128)(2,1)S(1)} %constant_dynamic-update-slice_fusion), channel_id=1, source_target_pairs={{0,4},{1,5},{2,6},{3,7},{4,0},{5,1},{6,2},{7,3},{8,12},{9,13},{10,... | collective-permute-start | bytes 1572872 | tf_op jit(solution)/shard_map/gather_gradients/ppermute | solution.py:39
  108.9 1.2 collective-permute-start.23
  110.1 7.7 %all-to-all-done = bf16[32,8,384]{2,1,0:T(8,128)(2,1)S(1)} async-done(((bf16[32,8,384]{2,1,0:T(8,128)(2,1)}), bf16[32,8,384]{2,1,0:T(8,128)(2,1)S(1)}, u32[]{:S(2)}, u32[]{:S(2)}) %all-to-all-start) | async-done | bytes 196640 | tf_op jit(solution)/shard_map/sum_weight_grad/all_to_all | solution.py:295
  118.0 9.2 %all_to_all.20 = f32[8,8,384]{2,1,0:T(8,128)S(1)} all-to-all(f32[8,8,384]{2,1,0:T(8,128)S(1)} %broadcast_in_dim.6), channel_id=1, replica_groups=mesh['row'=8,'col'=32] {'row'}, dimensions={0} | all-to-all | bytes 196608 | tf_op jit(solution)/shard_map/sum_weight_grad/all_to_all | solution.py:300
  128.0 5.0 %all-to-all-start.3 = ((f32[32,8,384]{2,1,0:T(8,128)}), f32[32,8,384]{2,1,0:T(8,128)S(1)}, u32[]{:S(2)}, u32[]{:S(2)}) async-start(f32[32,8,384]{2,1,0:T(8,128)} %broadcast_in_dim.7), calls=%async_computation.3 | async-start | bytes 786432 | tf_op jit(solution)/shard_map/sum_weight_grad/all_to_all | solution.py:314
  133.4 1.2 collective-permute-start.26
  135.0 1.1 collective-permute-done.26
  137.8 5.6 %tiles_backward.1 = bf16[16,128,256]{2,1,0:T(8,128)(2,1)} custom-call(s32[1]{0:T(128)} %bitcast.28.live, s32[192]{0:T(256)} %get-tuple-element.42.take, s32[192]{0:T(256)} %bitcast.47, bf16[1,192,128,128]{3,2,1,0:T(8,128)(2,1)} %tiles.3, bf16[8,128,256]{2,1,0:T(8,128)(2,1)} %bitcast.32, bf16[8,128,256]{2,1,0:T(8,128)(2,1)} %bitcast.35, ...), custom_call_target="tpu_custom_call" | custom-call | flops 1610612736 | bytes 6291456 | tf_op jit(solution)/shard_map/tiles_backward/pallas_call | solution.py:127
  143.4 5.4 %all-to-all-done.3 = f32[32,8,384]{2,1,0:T(8,128)S(1)} async-done(((f32[32,8,384]{2,1,0:T(8,128)}), f32[32,8,384]{2,1,0:T(8,128)S(1)}, u32[]{:S(2)}, u32[]{:S(2)}) %all-to-all-start.3) | async-done | bytes 393248 | tf_op jit(solution)/shard_map/sum_weight_grad/all_to_all | solution.py:314
  148.8 3.6 %all-to-all-start.1 = ((bf16[8,256,256]{2,1,0:T(8,128)(2,1)}), bf16[8,256,256]{2,1,0:T(8,128)(2,1)S(1)}, u32[]{:S(2)}, u32[]{:S(2)}) async-start(bf16[8,256,256]{2,1,0:T(8,128)(2,1)} %bitcast.29), calls=%async_computation.1 | async-start | bytes 2097152 | tf_op jit(solution)/shard_map/sum_over_row/all_to_all | solution.py:310
  153.8 14.7 %all-to-all-done.1.pieces = bf16[8,256,256]{2,1,0:T(8,128)(2,1)S(1)} async-done(((bf16[8,256,256]{2,1,0:T(8,128)(2,1)}), bf16[8,256,256]{2,1,0:T(8,128)(2,1)S(1)}, u32[]{:S(2)}, u32[]{:S(2)}) %all-to-all-start.1) | async-done | bytes 1048608 | tf_op jit(solution)/shard_map/sum_over_row/all_to_all | solution.py:310
  168.5 1.0 copy-done
  169.5 2.2 %sum_over_row.1 = bf16[256,256]{1,0:T(8,128)(2,1)} custom-call(bf16[8,256,256]{2,1,0:T(8,128)(2,1)} %copy-done, bf16[256,256]{1,0:T(8,128)(2,1)} %weight.1), custom_call_target="tpu_custom_call" | custom-call | tf_op jit(solution)/shard_map/sum_over_row/pallas_call | solution.py:228
  (61 shorter events, 7.4 us)
Async XLA Ops:
  0.6 10.8 %collective-permute-start = (bf16[256,256]{1,0:T(8,128)(2,1)}, bf16[256,256]{1,0:T(8,128)(2,1)}, u32[]{:S(2)}, u32[]{:S(2)}) collective-permute-start(bf16[256,256]{1,0:T(8,128)(2,1)} %param.8), channel_id=1, source_target_pairs={{0,32},{32,0},{64,96},{96,64},{128,160},{160,128},{192,224},{224,1... | collective-permute-start | bytes 393224 | tf_op jit(solution)/shard_map/gather_features/ppermute | solution.py:29
  3.2 9.7 %collective-permute-start.1 = (bf16[256,256]{1,0:T(8,128)(2,1)}, bf16[256,256]{1,0:T(8,128)(2,1)}, u32[]{:S(2)}, u32[]{:S(2)}) collective-permute-start(bf16[256,256]{1,0:T(8,128)(2,1)} %param.8), channel_id=1, source_target_pairs={{0,64},{32,96},{64,128},{96,160},{128,192},{160,224},{192,0},{224,... | collective-permute-start | bytes 393224 | tf_op jit(solution)/shard_map/gather_features/ppermute | solution.py:29
  4.4 9.9 %collective-permute-start.2 = (bf16[256,256]{1,0:T(8,128)(2,1)}, bf16[256,256]{1,0:T(8,128)(2,1)}, u32[]{:S(2)}, u32[]{:S(2)}) collective-permute-start(bf16[256,256]{1,0:T(8,128)(2,1)} %param.8), channel_id=1, source_target_pairs={{0,96},{32,64},{64,160},{96,128},{128,224},{160,192},{192,32},{224... | collective-permute-start | bytes 393224 | tf_op jit(solution)/shard_map/gather_features/ppermute | solution.py:29
  5.4 12.9 %collective-permute-start.3 = (bf16[256,256]{1,0:T(8,128)(2,1)}, bf16[256,256]{1,0:T(8,128)(2,1)}, u32[]{:S(2)}, u32[]{:S(2)}) collective-permute-start(bf16[256,256]{1,0:T(8,128)(2,1)} %param.8), channel_id=1, source_target_pairs={{0,128},{32,160},{64,192},{96,224},{128,0},{160,32},{192,64},{224,... | collective-permute-start | bytes 393224 | tf_op jit(solution)/shard_map/gather_features/ppermute | solution.py:29
  6.9 11.5 %collective-permute-start.4 = (bf16[256,256]{1,0:T(8,128)(2,1)}, bf16[256,256]{1,0:T(8,128)(2,1)}, u32[]{:S(2)}, u32[]{:S(2)}) collective-permute-start(bf16[256,256]{1,0:T(8,128)(2,1)} %param.8), channel_id=1, source_target_pairs={{0,160},{32,128},{64,224},{96,192},{128,32},{160,0},{192,96},{224,... | collective-permute-start | bytes 393224 | tf_op jit(solution)/shard_map/gather_features/ppermute | solution.py:29
  11.4 6.9 %collective-permute-start.5 = (bf16[256,256]{1,0:T(8,128)(2,1)}, bf16[256,256]{1,0:T(8,128)(2,1)}, u32[]{:S(2)}, u32[]{:S(2)}) collective-permute-start(bf16[256,256]{1,0:T(8,128)(2,1)} %param.8), channel_id=1, source_target_pairs={{0,192},{32,224},{64,0},{96,32},{128,64},{160,96},{192,128},{224,1... | collective-permute-start | bytes 393224 | tf_op jit(solution)/shard_map/gather_features/ppermute | solution.py:29
  12.9 5.4 %collective-permute-start.6 = (bf16[256,256]{1,0:T(8,128)(2,1)}, bf16[256,256]{1,0:T(8,128)(2,1)}, u32[]{:S(2)}, u32[]{:S(2)}) collective-permute-start(bf16[256,256]{1,0:T(8,128)(2,1)} %param.8), channel_id=1, source_target_pairs={{0,224},{32,192},{64,32},{96,0},{128,96},{160,64},{192,160},{224,1... | collective-permute-start | bytes 393224 | tf_op jit(solution)/shard_map/gather_features/ppermute | solution.py:29
  24.1 7.8 %collective-permute-start.7 = (bf16[16,128,256]{2,1,0:T(8,128)(2,1)}, bf16[16,128,256]{2,1,0:T(8,128)(2,1)S(1)}, u32[]{:S(2)}, u32[]{:S(2)}) collective-permute-start(bf16[16,128,256]{2,1,0:T(8,128)(2,1)} %get-tuple-element.24), channel_id=1, source_target_pairs={{0,1},{1,0},{2,3},{3,2},{4,5},{5,4},{6,7},{7,6},{8,9},{9,8},{10,11... | collective-permute-start | bytes 3145736 | tf_op jit(solution)/shard_map/sum_over_col/ppermute | solution.py:39
  29.4 10.3 %collective-permute-start.12 = (bf16[16,128,256]{2,1,0:T(8,128)(2,1)}, bf16[16,128,256]{2,1,0:T(8,128)(2,1)S(1)}, u32[]{:S(2)}, u32[]{:S(2)}) collective-permute-start(bf16[16,128,256]{2,1,0:T(8,128)(2,1)} %get-tuple-element.26), channel_id=1, source_target_pairs={{0,1},{1,0},{2,3},{3,2},{4,5},{5,4},{6,7},{7,6},{8,9},{9,8},{10,11... | collective-permute-start | bytes 3145736 | tf_op jit(solution)/shard_map/sum_over_col/ppermute | solution.py:39
  33.4 21.5 %collective-permute-start.10 = (bf16[4,128,256]{2,1,0:T(8,128)(2,1)S(1)}, bf16[4,128,256]{2,1,0:T(8,128)(2,1)S(1)}, u32[]{:S(2)}, u32[]{:S(2)}) collective-permute-start(bf16[4,128,256]{2,1,0:T(8,128)(2,1)S(1)} %get-tuple-element.50), channel_id=1, source_target_pairs={{0,6},{1,7},{2,0},{3,1},{4,2},{5,3},{6,4},{7,5},{8,14},{9,15},{10,... | collective-permute-start | bytes 786440 | tf_op jit(solution)/shard_map/sum_over_col/ppermute | solution.py:39
  38.4 20.0 %collective-permute-start.9 = (bf16[4,128,256]{2,1,0:T(8,128)(2,1)S(1)}, bf16[4,128,256]{2,1,0:T(8,128)(2,1)S(1)}, u32[]{:S(2)}, u32[]{:S(2)}) collective-permute-start(bf16[4,128,256]{2,1,0:T(8,128)(2,1)S(1)} %get-tuple-element.51), channel_id=1, source_target_pairs={{0,2},{1,3},{2,4},{3,5},{4,6},{5,7},{6,0},{7,1},{8,10},{9,11},{10,... | collective-permute-start | bytes 786440 | tf_op jit(solution)/shard_map/sum_over_col/ppermute | solution.py:39
  38.4 20.0 %collective-permute-start.8 = (bf16[4,128,256]{2,1,0:T(8,128)(2,1)S(1)}, bf16[4,128,256]{2,1,0:T(8,128)(2,1)S(1)}, u32[]{:S(2)}, u32[]{:S(2)}) collective-permute-start(bf16[4,128,256]{2,1,0:T(8,128)(2,1)S(1)} %get-tuple-element.52), channel_id=1, source_target_pairs={{0,4},{1,5},{2,6},{3,7},{4,0},{5,1},{6,2},{7,3},{8,12},{9,13},{10,... | collective-permute-start | bytes 786440 | tf_op jit(solution)/shard_map/sum_over_col/ppermute | solution.py:39
  41.2 22.0 %collective-permute-start.13 = (bf16[4,128,256]{2,1,0:T(8,128)(2,1)S(1)}, bf16[4,128,256]{2,1,0:T(8,128)(2,1)S(1)}, u32[]{:S(2)}, u32[]{:S(2)}) collective-permute-start(bf16[4,128,256]{2,1,0:T(8,128)(2,1)S(1)} %get-tuple-element.47), channel_id=1, source_target_pairs={{0,4},{1,5},{2,6},{3,7},{4,0},{5,1},{6,2},{7,3},{8,12},{9,13},{10,... | collective-permute-start | bytes 786440 | tf_op jit(solution)/shard_map/sum_over_col/ppermute | solution.py:39
  42.9 20.7 %collective-permute-start.14 = (bf16[4,128,256]{2,1,0:T(8,128)(2,1)S(1)}, bf16[4,128,256]{2,1,0:T(8,128)(2,1)S(1)}, u32[]{:S(2)}, u32[]{:S(2)}) collective-permute-start(bf16[4,128,256]{2,1,0:T(8,128)(2,1)S(1)} %get-tuple-element.46), channel_id=1, source_target_pairs={{0,2},{1,3},{2,4},{3,5},{4,6},{5,7},{6,0},{7,1},{8,10},{9,11},{10,... | collective-permute-start | bytes 786440 | tf_op jit(solution)/shard_map/sum_over_col/ppermute | solution.py:39
  54.9 8.7 %collective-permute-start.15 = (bf16[4,128,256]{2,1,0:T(8,128)(2,1)S(1)}, bf16[4,128,256]{2,1,0:T(8,128)(2,1)S(1)}, u32[]{:S(2)}, u32[]{:S(2)}) collective-permute-start(bf16[4,128,256]{2,1,0:T(8,128)(2,1)S(1)} %get-tuple-element.45), channel_id=1, source_target_pairs={{0,6},{1,7},{2,0},{3,1},{4,2},{5,3},{6,4},{7,5},{8,14},{9,15},{10,... | collective-permute-start | bytes 786440 | tf_op jit(solution)/shard_map/sum_over_col/ppermute | solution.py:39
  58.5 6.1 %collective-permute-start.16 = (bf16[2,128,256]{2,1,0:T(8,128)(2,1)S(1)}, bf16[2,128,256]{2,1,0:T(8,128)(2,1)S(1)}, u32[]{:S(2)}, u32[]{:S(2)}) collective-permute-start(bf16[2,128,256]{2,1,0:T(8,128)(2,1)S(1)} %get-tuple-element.55), channel_id=1, source_target_pairs={{0,8},{1,9},{2,10},{3,11},{4,12},{5,13},{6,14},{7,15},{8,16},{9,17... | collective-permute-start | bytes 393224 | tf_op jit(solution)/shard_map/sum_over_col/ppermute | solution.py:39
  58.6 12.3 %collective-permute-start.11 = (bf16[2,128,256]{2,1,0:T(8,128)(2,1)S(1)}, bf16[2,128,256]{2,1,0:T(8,128)(2,1)S(1)}, u32[]{:S(2)}, u32[]{:S(2)}) collective-permute-start(bf16[2,128,256]{2,1,0:T(8,128)(2,1)S(1)} %get-tuple-element.56), channel_id=1, source_target_pairs={{0,16},{1,17},{2,18},{3,19},{4,20},{5,21},{6,22},{7,23},{8,24},{9,... | collective-permute-start | bytes 393224 | tf_op jit(solution)/shard_map/sum_over_col/ppermute | solution.py:39
  64.6 8.4 %copy-start.9 = (bf16[2,128,256]{2,1,0:T(8,128)(2,1)}, bf16[2,128,256]{2,1,0:T(8,128)(2,1)S(1)}, u32[]{:S(2)}) copy-start(bf16[2,128,256]{2,1,0:T(8,128)(2,1)S(1)} %collective-permute-done.16) | copy-start | bytes 393220
  65.4 7.6 %collective-permute-start.17 = (bf16[2,128,256]{2,1,0:T(8,128)(2,1)S(1)}, bf16[2,128,256]{2,1,0:T(8,128)(2,1)S(1)}, u32[]{:S(2)}, u32[]{:S(2)}) collective-permute-start(bf16[2,128,256]{2,1,0:T(8,128)(2,1)S(1)} %get-tuple-element.54), channel_id=1, source_target_pairs={{0,24},{1,25},{2,26},{3,27},{4,28},{5,29},{6,30},{7,31},{8,0},{9,1... | collective-permute-start | bytes 393224 | tf_op jit(solution)/shard_map/sum_over_col/ppermute | solution.py:39
  70.9 2.1 %copy-start.10 = (bf16[2,128,256]{2,1,0:T(8,128)(2,1)}, bf16[2,128,256]{2,1,0:T(8,128)(2,1)S(1)}, u32[]{:S(2)}) copy-start(bf16[2,128,256]{2,1,0:T(8,128)(2,1)S(1)} %collective-permute-done.11) | copy-start | bytes 393220
  72.9 0.6 copy-start.11
  76.1 8.0 %collective-permute-start.18 = (bf16[256,256]{1,0:T(8,128)(2,1)}, bf16[256,256]{1,0:T(8,128)(2,1)S(1)}, u32[]{:S(2)}, u32[]{:S(2)}) collective-permute-start(bf16[256,256]{1,0:T(8,128)(2,1)} %get-tuple-element.33), channel_id=1, source_target_pairs={{0,8},{1,9},{2,10},{3,11},{4,12},{5,13},{6,14},{7,15},{8,16},{9,17... | collective-permute-start | bytes 393224 | tf_op jit(solution)/shard_map/gather_gradients/ppermute | solution.py:39
  77.8 8.0 %collective-permute-start.19 = (bf16[256,256]{1,0:T(8,128)(2,1)}, bf16[256,256]{1,0:T(8,128)(2,1)S(1)}, u32[]{:S(2)}, u32[]{:S(2)}) collective-permute-start(bf16[256,256]{1,0:T(8,128)(2,1)} %get-tuple-element.33), channel_id=1, source_target_pairs={{0,16},{1,17},{2,18},{3,19},{4,20},{5,21},{6,22},{7,23},{8,24},{9,... | collective-permute-start | bytes 393224 | tf_op jit(solution)/shard_map/gather_gradients/ppermute | solution.py:39
  80.1 7.6 %collective-permute-start.20 = (bf16[256,256]{1,0:T(8,128)(2,1)}, bf16[256,256]{1,0:T(8,128)(2,1)S(1)}, u32[]{:S(2)}, u32[]{:S(2)}) collective-permute-start(bf16[256,256]{1,0:T(8,128)(2,1)} %get-tuple-element.33), channel_id=1, source_target_pairs={{0,24},{1,25},{2,26},{3,27},{4,28},{5,29},{6,30},{7,31},{8,0},{9,1... | collective-permute-start | bytes 393224 | tf_op jit(solution)/shard_map/gather_gradients/ppermute | solution.py:39
  87.7 50.0 %copy-start.1 = (bf16[1024,256]{1,0:T(8,128)(2,1)}, bf16[1024,256]{1,0:T(8,128)(2,1)S(1)}, u32[]{:S(2)}) copy-start(bf16[1024,256]{1,0:T(8,128)(2,1)S(1)} %constant_dynamic-update-slice_fusion) | copy-start | bytes 1572868
  87.7 30.2 %collective-permute-start.24 = (bf16[1024,256]{1,0:T(8,128)(2,1)S(1)}, bf16[1024,256]{1,0:T(8,128)(2,1)S(1)}, u32[]{:S(2)}, u32[]{:S(2)}) collective-permute-start(bf16[1024,256]{1,0:T(8,128)(2,1)S(1)} %constant_dynamic-update-slice_fusion), channel_id=1, source_target_pairs={{0,1},{1,0},{2,3},{3,2},{4,5},{5,4},{6,7},{7,6},{8,9},{9,8},{10,11... | collective-permute-start | bytes 1572872 | tf_op jit(solution)/shard_map/sum_weight_grad/ppermute | solution.py:39
  92.9 25.0 %all-to-all-start = ((bf16[32,8,384]{2,1,0:T(8,128)(2,1)}), bf16[32,8,384]{2,1,0:T(8,128)(2,1)S(1)}, u32[]{:S(2)}, u32[]{:S(2)}) async-start(bf16[32,8,384]{2,1,0:T(8,128)(2,1)} %bitcast.33), calls=%async_computation | async-start | bytes 393216 | tf_op jit(solution)/shard_map/sum_weight_grad/all_to_all | solution.py:295
  105.1 27.9 %collective-permute-start.21 = (bf16[1024,256]{1,0:T(8,128)(2,1)S(1)}, bf16[1024,256]{1,0:T(8,128)(2,1)S(1)}, u32[]{:S(2)}, u32[]{:S(2)}) collective-permute-start(bf16[1024,256]{1,0:T(8,128)(2,1)S(1)} %constant_dynamic-update-slice_fusion), channel_id=1, source_target_pairs={{0,2},{1,3},{2,4},{3,5},{4,6},{5,7},{6,0},{7,1},{8,10},{9,11},{10,... | collective-permute-start | bytes 1572872 | tf_op jit(solution)/shard_map/gather_gradients/ppermute | solution.py:39
  106.5 26.9 %collective-permute-start.22 = (bf16[1024,256]{1,0:T(8,128)(2,1)S(1)}, bf16[1024,256]{1,0:T(8,128)(2,1)S(1)}, u32[]{:S(2)}, u32[]{:S(2)}) collective-permute-start(bf16[1024,256]{1,0:T(8,128)(2,1)S(1)} %constant_dynamic-update-slice_fusion), channel_id=1, source_target_pairs={{0,4},{1,5},{2,6},{3,7},{4,0},{5,1},{6,2},{7,3},{8,12},{9,13},{10,... | collective-permute-start | bytes 1572872 | tf_op jit(solution)/shard_map/gather_gradients/ppermute | solution.py:39
  108.9 25.7 %collective-permute-start.23 = (bf16[1024,256]{1,0:T(8,128)(2,1)S(1)}, bf16[1024,256]{1,0:T(8,128)(2,1)S(1)}, u32[]{:S(2)}, u32[]{:S(2)}) collective-permute-start(bf16[1024,256]{1,0:T(8,128)(2,1)S(1)} %constant_dynamic-update-slice_fusion), channel_id=1, source_target_pairs={{0,6},{1,7},{2,0},{3,1},{4,2},{5,3},{6,4},{7,5},{8,14},{9,15},{10,... | collective-permute-start | bytes 1572872 | tf_op jit(solution)/shard_map/gather_gradients/ppermute | solution.py:39
  117.9 19.8 %copy-start.2 = (bf16[1024,256]{1,0:T(8,128)(2,1)}, bf16[1024,256]{1,0:T(8,128)(2,1)S(1)}, u32[]{:S(2)}) copy-start(bf16[1024,256]{1,0:T(8,128)(2,1)S(1)} %collective-permute-done.24) | copy-start | bytes 1572868
  128.0 20.8 %all-to-all-start.3 = ((f32[32,8,384]{2,1,0:T(8,128)}), f32[32,8,384]{2,1,0:T(8,128)S(1)}, u32[]{:S(2)}, u32[]{:S(2)}) async-start(f32[32,8,384]{2,1,0:T(8,128)} %broadcast_in_dim.7), calls=%async_computation.3 | async-start | bytes 786432 | tf_op jit(solution)/shard_map/sum_weight_grad/all_to_all | solution.py:314
  133.0 4.7 %copy-start.3 = (bf16[1024,256]{1,0:T(8,128)(2,1)}, bf16[1024,256]{1,0:T(8,128)(2,1)S(1)}, u32[]{:S(2)}) copy-start(bf16[1024,256]{1,0:T(8,128)(2,1)S(1)} %collective-permute-done.21) | copy-start | bytes 1572868
  133.0 2.0 %collective-permute-start.25 = (bf16[1024,256]{1,0:T(8,128)(2,1)S(1)}, bf16[1024,256]{1,0:T(8,128)(2,1)S(1)}, u32[]{:S(2)}, u32[]{:S(2)}) collective-permute-start(bf16[1024,256]{1,0:T(8,128)(2,1)S(1)} %collective-permute-done.21), channel_id=1, source_target_pairs={{0,1},{1,0},{2,3},{3,2},{4,5},{5,4},{6,7},{7,6},{8,9},{9,8},{10,11... | collective-permute-start | bytes 1572872 | tf_op jit(solution)/shard_map/gather_gradients/ppermute | solution.py:39
  133.4 4.3 %copy-start.4 = (bf16[1024,256]{1,0:T(8,128)(2,1)}, bf16[1024,256]{1,0:T(8,128)(2,1)S(1)}, u32[]{:S(2)}) copy-start(bf16[1024,256]{1,0:T(8,128)(2,1)S(1)} %collective-permute-done.22) | copy-start | bytes 1572868
  133.4 2.7 %collective-permute-start.26 = (bf16[1024,256]{1,0:T(8,128)(2,1)S(1)}, bf16[1024,256]{1,0:T(8,128)(2,1)S(1)}, u32[]{:S(2)}, u32[]{:S(2)}) collective-permute-start(bf16[1024,256]{1,0:T(8,128)(2,1)S(1)} %collective-permute-done.22), channel_id=1, source_target_pairs={{0,1},{1,0},{2,3},{3,2},{4,5},{5,4},{6,7},{7,6},{8,9},{9,8},{10,11... | collective-permute-start | bytes 1572872 | tf_op jit(solution)/shard_map/gather_gradients/ppermute | solution.py:39
  134.6 3.1 %copy-start.5 = (bf16[1024,256]{1,0:T(8,128)(2,1)}, bf16[1024,256]{1,0:T(8,128)(2,1)S(1)}, u32[]{:S(2)}) copy-start(bf16[1024,256]{1,0:T(8,128)(2,1)S(1)} %collective-permute-done.23) | copy-start | bytes 1572868
  134.6 2.3 %collective-permute-start.27 = (bf16[1024,256]{1,0:T(8,128)(2,1)S(1)}, bf16[1024,256]{1,0:T(8,128)(2,1)S(1)}, u32[]{:S(2)}, u32[]{:S(2)}) collective-permute-start(bf16[1024,256]{1,0:T(8,128)(2,1)S(1)} %collective-permute-done.23), channel_id=1, source_target_pairs={{0,1},{1,0},{2,3},{3,2},{4,5},{5,4},{6,7},{7,6},{8,9},{9,8},{10,11... | collective-permute-start | bytes 1572872 | tf_op jit(solution)/shard_map/gather_gradients/ppermute | solution.py:39
  135.0 2.8 %copy-start.6 = (bf16[1024,256]{1,0:T(8,128)(2,1)}, bf16[1024,256]{1,0:T(8,128)(2,1)S(1)}, u32[]{:S(2)}) copy-start(bf16[1024,256]{1,0:T(8,128)(2,1)S(1)} %collective-permute-done.25) | copy-start | bytes 1572868
  136.2 1.6 copy-start.7
  136.9 0.8 copy-start.8
  148.8 19.7 %all-to-all-start.1 = ((bf16[8,256,256]{2,1,0:T(8,128)(2,1)}), bf16[8,256,256]{2,1,0:T(8,128)(2,1)S(1)}, u32[]{:S(2)}, u32[]{:S(2)}) async-start(bf16[8,256,256]{2,1,0:T(8,128)(2,1)} %bitcast.29), calls=%async_computation.1 | async-start | bytes 2097152 | tf_op jit(solution)/shard_map/sum_over_row/all_to_all | solution.py:310
  168.5 1.0 copy-start

commit v8 on v7

--- a/solution.py
+++ b/solution.py
@@ -294,13 +294,11 @@
     with jax.named_scope("sum_weight_grad"):
         load = lax.all_to_all(load, "col", 0, 0, tiled=True)
         load = jnp.sum(load.astype(jnp.float32), axis=0)
-        there = [col_shift(here[0], dcore=1)]
-        there[0], load = lax.optimization_barrier((there[0], load))
         load = jnp.broadcast_to(load, (N_ROW,) + load.shape)
         load = jnp.sum(lax.all_to_all(load, "row", 0, 0, tiled=True), axis=0) * scale
     with jax.named_scope("gather_gradients"):
         here += [col_shift(here[0], dy=k) for k in range(1, N_Y)]
-        there += [col_shift(p, dcore=1) for p in here[1:]]
+        there = [col_shift(p, dcore=1) for p in here]
     with jax.named_scope("tiles_backward"):
         (back,) = tile_sum(
             adjacency, live, take_rows, c, here + there, [N_ROW * per], True, VMEM_LIMIT

time: 173 us -> 173 us (level)
  waiting for transfers between devices: 58.5 us -> 48.9 us
  starting transfers between devices: 72.2 us -> 78.1 us
  Pallas kernels: 18 us -> 20 us
    all_to_all x1, starting transfers between devices: 12.2 us -> 18.6 us  [shards(): load = lax.all_to_all(load, 'col', 0, 0, tiled=True)]
    ppermute x21, waiting for transfers between devices: 26.6 us -> 21.4 us  [col_shift(): return lax.ppermute(value, 'col', pairs)]
    all_to_all x1, waiting for transfers between devices: 14.7 us -> 12.6 us  [shards(): back = lax.all_to_all(back, 'row', 0, 0, tiled=True)]
    pallas_call x2, Pallas kernels: 11.3 us -> 13.3 us  [tile_sum(): pl.pallas_call(functools.partial(tile_kernel, transposed, src_sizes, out_...]
  transfers between devices with their start and end apart: 31 -> 31, of which waited for: 15 -> 16; matrix products, arithmetic and copies ran while one was open for 6% -> 6% of each run, Pallas kernels for 4% -> 5%
where the time goes in v8:
time: 173 us; the launch traced here: 171 us
  starting transfers between devices  78.1 us (45%)
  waiting for transfers between devices  48.9 us (28%)
  Pallas kernels  20 us (12%)
  blocking collectives  10.1 us (6%)
  other arithmetic  6.54 us (4%)
  local copies, waits for them, and re-layouts  5.63 us (3%)
    ppermute x21, starting transfers between devices, col_shift(): return lax.ppermute(value, 'col', pairs)  40.7 us
    ppermute x21, waiting for transfers between devices, col_shift(): return lax.ppermute(value, 'col', pairs)  21.4 us
    all_to_all x1, starting transfers between devices, shards(): load = lax.all_to_all(load, 'col', 0, 0, tiled=True)  18.6 us
    pallas_call x2, Pallas kernels, tile_sum(): pl.pallas_call(functools.partial(tile_kernel, transposed, src_sizes, out_...  13.3 us
    all_to_all x1, waiting for transfers between devices, shards(): back = lax.all_to_all(back, 'row', 0, 0, tiled=True)  12.6 us
    ppermute x7, starting transfers between devices, row_shift(): return lax.ppermute(value, 'row', pairs)  10.4 us
    all_to_all x1, blocking collectives, shards(): lax.all_to_all(load, 'row', 0, 0, tiled=True)  10.1 us
    all_to_all x1, waiting for transfers between devices, shards(): load = lax.all_to_all(load, 'col', 0, 0, tiled=True)  6.76 us
  transfers between devices with their start and end apart: 31, of which 16 were waited for; matrix products, arithmetic and copies ran while one was open for 6% of the time, Pallas kernels for 5%

profile of v8, /device:TPU:1, one launch (start us, length us, event | category | flops | bytes accessed | tf_op | source)
XLA Modules:
  0.0 170.7 jit_solution(11297741173192048389)
XLA Ops:
  0.6 2.6 %collective-permute-start = (bf16[256,256]{1,0:T(8,128)(2,1)}, bf16[256,256]{1,0:T(8,128)(2,1)}, u32[]{:S(2)}, u32[]{:S(2)}) collective-permute-start(bf16[256,256]{1,0:T(8,128)(2,1)} %param.8), channel_id=1, source_target_pairs={{0,32},{32,0},{64,96},{96,64},{128,160},{160,128},{192,224},{224,1... | collective-permute-start | bytes 393224 | tf_op jit(solution)/shard_map/gather_features/ppermute | solution.py:29
  3.2 1.2 collective-permute-start.1
  4.4 1.0 collective-permute-start.2
  5.4 1.4 collective-permute-start.3
  6.9 2.6 %collective-permute-start.4 = (bf16[256,256]{1,0:T(8,128)(2,1)}, bf16[256,256]{1,0:T(8,128)(2,1)}, u32[]{:S(2)}, u32[]{:S(2)}) collective-permute-start(bf16[256,256]{1,0:T(8,128)(2,1)} %param.8), channel_id=1, source_target_pairs={{0,160},{32,128},{64,224},{96,192},{128,32},{160,0},{192,96},{224,... | collective-permute-start | bytes 393224 | tf_op jit(solution)/shard_map/gather_features/ppermute | solution.py:29
  10.2 1.3 multiply_add_fusion
  11.4 1.5 collective-permute-start.5
  13.0 1.3 fusion.2
  14.3 4.0 %collective-permute-done.3 = bf16[256,256]{1,0:T(8,128)(2,1)} collective-permute-done((bf16[256,256]{1,0:T(8,128)(2,1)}, bf16[256,256]{1,0:T(8,128)(2,1)}, u32[]{:S(2)}, u32[]{:S(2)}) %collective-permute-start.3) | collective-permute-done | bytes 131104 | tf_op jit(solution)/shard_map/gather_features/ppermute | solution.py:29
  18.3 6.7 %tiles_forward.1 = (bf16[16,128,256]{2,1,0:T(8,128)(2,1)}, bf16[16,128,256]{2,1,0:T(8,128)(2,1)}, bf16[16,128,256]{2,1,0:T(8,128)(2,1)}, bf16[16,128,256]{2,1,0:T(8,128)(2,1)}) custom-call(s32[1]{0:T(128)} %bitcast.27.live, s32[192]{0:T(256)} %get-tuple-element.53.take, s32[192]{0:T(256)} %get-tuple-element.54.put, bf16[1,192,128,128]{3,2,1,0:T(8,128)(2,1)} %tiles.3, ...), custom_call_target="tpu_custom_call" | custom-call | flops 1610612736 | bytes 6291456 | tf_op jit(solution)/shard_map/tiles_forward/pallas_call | solution.py:127
  25.0 3.4 %collective-permute-start.7 = (bf16[16,128,256]{2,1,0:T(8,128)(2,1)}, bf16[16,128,256]{2,1,0:T(8,128)(2,1)S(1)}, u32[]{:S(2)}, u32[]{:S(2)}) collective-permute-start(bf16[16,128,256]{2,1,0:T(8,128)(2,1)} %get-tuple-element.22), channel_id=1, source_target_pairs={{0,1},{1,0},{2,3},{3,2},{4,5},{5,4},{6,7},{7,6},{8,9},{9,8},{10,11... | collective-permute-start | bytes 3145736 | tf_op jit(solution)/shard_map/sum_over_col/ppermute | solution.py:39
  28.5 2.4 %collective-permute-done.7 = bf16[16,128,256]{2,1,0:T(8,128)(2,1)S(1)} collective-permute-done((bf16[16,128,256]{2,1,0:T(8,128)(2,1)}, bf16[16,128,256]{2,1,0:T(8,128)(2,1)S(1)}, u32[]{:S(2)}, u32[]{:S(2)}) %collective-permute-start.7) | collective-permute-done | bytes 1048608 | tf_op jit(solution)/shard_map/sum_over_col/ppermute | solution.py:39
  30.9 1.5 add_convert_fusion.7
  32.4 2.4 %collective-permute-start.10 = (bf16[4,128,256]{2,1,0:T(8,128)(2,1)S(1)}, bf16[4,128,256]{2,1,0:T(8,128)(2,1)S(1)}, u32[]{:S(2)}, u32[]{:S(2)}) collective-permute-start(bf16[4,128,256]{2,1,0:T(8,128)(2,1)S(1)} %get-tuple-element.46), channel_id=1, source_target_pairs={{0,6},{1,7},{2,0},{3,1},{4,2},{5,3},{6,4},{7,5},{8,14},{9,15},{10,... | collective-permute-start | bytes 786440 | tf_op jit(solution)/shard_map/sum_over_col/ppermute | solution.py:39
  35.1 5.0 %collective-permute-start.8 = (bf16[4,128,256]{2,1,0:T(8,128)(2,1)S(1)}, bf16[4,128,256]{2,1,0:T(8,128)(2,1)S(1)}, u32[]{:S(2)}, u32[]{:S(2)}) collective-permute-start(bf16[4,128,256]{2,1,0:T(8,128)(2,1)S(1)} %get-tuple-element.48), channel_id=1, source_target_pairs={{0,4},{1,5},{2,6},{3,7},{4,0},{5,1},{6,2},{7,3},{8,12},{9,13},{10,... | collective-permute-start | bytes 786440 | tf_op jit(solution)/shard_map/sum_over_col/ppermute | solution.py:39
  40.0 1.5 add_convert_fusion
  41.6 1.3 collective-permute-start.14
  42.9 1.5 collective-permute-start.15
  44.9 6.5 %collective-permute-done.8 = bf16[4,128,256]{2,1,0:T(8,128)(2,1)S(1)} collective-permute-done((bf16[4,128,256]{2,1,0:T(8,128)(2,1)S(1)}, bf16[4,128,256]{2,1,0:T(8,128)(2,1)S(1)}, u32[]{:S(2)}, u32[]{:S(2)}) %collective-permute-start.8) | collective-permute-done | bytes 262176 | tf_op jit(solution)/shard_map/sum_over_col/ppermute | solution.py:39
  51.6 2.1 %collective-permute-start.16 = (bf16[2,128,256]{2,1,0:T(8,128)(2,1)S(1)}, bf16[2,128,256]{2,1,0:T(8,128)(2,1)S(1)}, u32[]{:S(2)}, u32[]{:S(2)}) collective-permute-start(bf16[2,128,256]{2,1,0:T(8,128)(2,1)S(1)} %get-tuple-element.51), channel_id=1, source_target_pairs={{0,8},{1,9},{2,10},{3,11},{4,12},{5,13},{6,14},{7,15},{8,16},{9,17... | collective-permute-start | bytes 393224 | tf_op jit(solution)/shard_map/sum_over_col/ppermute | solution.py:39
  53.7 9.5 %collective-permute-start.11 = (bf16[2,128,256]{2,1,0:T(8,128)(2,1)S(1)}, bf16[2,128,256]{2,1,0:T(8,128)(2,1)S(1)}, u32[]{:S(2)}, u32[]{:S(2)}) collective-permute-start(bf16[2,128,256]{2,1,0:T(8,128)(2,1)S(1)} %get-tuple-element.52), channel_id=1, source_target_pairs={{0,16},{1,17},{2,18},{3,19},{4,20},{5,21},{6,22},{7,23},{8,24},{9,... | collective-permute-start | bytes 393224 | tf_op jit(solution)/shard_map/sum_over_col/ppermute | solution.py:39
  63.5 0.8 add_convert_fusion.8
  64.3 2.7 %collective-permute-start.17 = (bf16[2,128,256]{2,1,0:T(8,128)(2,1)S(1)}, bf16[2,128,256]{2,1,0:T(8,128)(2,1)S(1)}, u32[]{:S(2)}, u32[]{:S(2)}) collective-permute-start(bf16[2,128,256]{2,1,0:T(8,128)(2,1)S(1)} %get-tuple-element.50), channel_id=1, source_target_pairs={{0,24},{1,25},{2,26},{3,27},{4,28},{5,29},{6,30},{7,31},{8,0},{9,1... | collective-permute-start | bytes 393224 | tf_op jit(solution)/shard_map/sum_over_col/ppermute | solution.py:39
  67.2 7.2 %collective-permute-done.17 = bf16[2,128,256]{2,1,0:T(8,128)(2,1)S(1)} collective-permute-done((bf16[2,128,256]{2,1,0:T(8,128)(2,1)S(1)}, bf16[2,128,256]{2,1,0:T(8,128)(2,1)S(1)}, u32[]{:S(2)}, u32[]{:S(2)}) %collective-permute-start.17) | collective-permute-done | bytes 131104 | tf_op jit(solution)/shard_map/sum_over_col/ppermute | solution.py:39
  75.0 2.5 %pointwise.1 = (bf16[256,256]{1,0:T(8,128)(2,1)}, bf16[256,256]{1,0:T(8,128)(2,1)}, f32[256,256]{1,0:T(8,128)}, f32[256,256]{1,0:T(8,128)}) custom-call(bf16[256,256]{1,0:T(8,128)(2,1)} %bitcast.44, bf16[256,256]{1,0:T(8,128)(2,1)} %bitcast.43, bf16[256,256]{1,0:T(8,128)(2,1)} %bitcast.45, bf16[256,256]{1,0:T(8,128)(2,1)} %bitcast.41, ...), custom_call_target="tpu_custom_call" | custom-call | tf_op jit(solution)/shard_map/pointwise/pallas_call | solution.py:182
  77.7 4.1 %collective-permute-start.19 = (bf16[256,256]{1,0:T(8,128)(2,1)}, bf16[256,256]{1,0:T(8,128)(2,1)S(1)}, u32[]{:S(2)}, u32[]{:S(2)}) collective-permute-start(bf16[256,256]{1,0:T(8,128)(2,1)} %get-tuple-element.31), channel_id=1, source_target_pairs={{0,16},{1,17},{2,18},{3,19},{4,20},{5,21},{6,22},{7,23},{8,24},{9,... | collective-permute-start | bytes 393224 | tf_op jit(solution)/shard_map/gather_gradients/ppermute | solution.py:39
  81.8 1.5 collective-permute-start.20
  83.2 2.0 %gather_gradients.1 = bf16[256,384]{1,0:T(8,128)(2,1)} custom-call(f32[256,256]{1,0:T(8,128)} %get-tuple-element.32.total, f32[256,256]{1,0:T(8,128)} %get-tuple-element.33.pre_grad), custom_call_target="tpu_custom_call" | custom-call | tf_op jit(solution)/shard_map/gather_gradients/pallas_call | solution.py:204
  85.8 1.2 collective-permute-done.20
  87.0 18.6 %all-to-all-start.1 = ((bf16[32,8,384]{2,1,0:T(8,128)(2,1)}), bf16[32,8,384]{2,1,0:T(8,128)(2,1)S(1)}, u32[]{:S(2)}, u32[]{:S(2)}) async-start(bf16[32,8,384]{2,1,0:T(8,128)(2,1)} %bitcast.33), calls=%async_computation.1 | async-start | bytes 393216 | tf_op jit(solution)/shard_map/sum_weight_grad/all_to_all | solution.py:295
  105.6 0.9 constant_dynamic-update-slice_fusion.3
  106.6 1.5 collective-permute-start.21
  108.0 2.4 %collective-permute-start.22 = (bf16[1024,256]{1,0:T(8,128)(2,1)S(1)}, bf16[1024,256]{1,0:T(8,128)(2,1)S(1)}, u32[]{:S(2)}, u32[]{:S(2)}) collective-permute-start(bf16[1024,256]{1,0:T(8,128)(2,1)S(1)} %constant_dynamic-update-slice_fusion), channel_id=1, source_target_pairs={{0,4},{1,5},{2,6},{3,7},{4,0},{5,1},{6,2},{7,3},{8,12},{9,13},{10,... | collective-permute-start | bytes 1572872 | tf_op jit(solution)/shard_map/gather_gradients/ppermute | solution.py:39
  110.4 1.2 collective-permute-start.23
  111.6 6.8 %all-to-all-done.1 = bf16[32,8,384]{2,1,0:T(8,128)(2,1)S(1)} async-done(((bf16[32,8,384]{2,1,0:T(8,128)(2,1)}), bf16[32,8,384]{2,1,0:T(8,128)(2,1)S(1)}, u32[]{:S(2)}, u32[]{:S(2)}) %all-to-all-start.1) | async-done | bytes 196640 | tf_op jit(solution)/shard_map/sum_weight_grad/all_to_all | solution.py:295
  118.4 10.1 %all_to_all.20 = f32[8,8,384]{2,1,0:T(8,128)S(1)} all-to-all(f32[8,8,384]{2,1,0:T(8,128)S(1)} %broadcast_in_dim.6), channel_id=1, replica_groups=mesh['row'=8,'col'=32] {'row'}, dimensions={0} | all-to-all | bytes 196608 | tf_op jit(solution)/shard_map/sum_weight_grad/all_to_all | solution.py:298
  128.6 0.8 broadcast_in_dim.7
  129.3 4.9 %all-to-all-start.3 = ((f32[32,8,384]{2,1,0:T(8,128)}), f32[32,8,384]{2,1,0:T(8,128)S(1)}, u32[]{:S(2)}, u32[]{:S(2)}) async-start(f32[32,8,384]{2,1,0:T(8,128)} %broadcast_in_dim.7), calls=%async_computation.3 | async-start | bytes 786432 | tf_op jit(solution)/shard_map/sum_weight_grad/all_to_all | solution.py:312
  135.3 0.9 collective-permute-start.26
  137.0 0.7 collective-permute-done.26
  137.7 0.7 collective-permute-done.27
  138.5 0.8 copy-done.8
  139.3 6.6 %tiles_backward.1 = bf16[16,128,256]{2,1,0:T(8,128)(2,1)} custom-call(s32[1]{0:T(128)} %bitcast.28.live, s32[192]{0:T(256)} %get-tuple-element.38.take, s32[192]{0:T(256)} %bitcast.47, bf16[1,192,128,128]{3,2,1,0:T(8,128)(2,1)} %tiles.3, bf16[8,128,256]{2,1,0:T(8,128)(2,1)} %bitcast.32, bf16[8,128,256]{2,1,0:T(8,128)(2,1)} %bitcast.34, ...), custom_call_target="tpu_custom_call" | custom-call | flops 1610612736 | bytes 6291456 | tf_op jit(solution)/shard_map/tiles_backward/pallas_call | solution.py:127
  146.0 4.1 %all-to-all-done.3 = f32[32,8,384]{2,1,0:T(8,128)S(1)} async-done(((f32[32,8,384]{2,1,0:T(8,128)}), f32[32,8,384]{2,1,0:T(8,128)S(1)}, u32[]{:S(2)}, u32[]{:S(2)}) %all-to-all-start.3) | async-done | bytes 393248 | tf_op jit(solution)/shard_map/sum_weight_grad/all_to_all | solution.py:312
  150.0 3.6 %all-to-all-start = ((bf16[8,256,256]{2,1,0:T(8,128)(2,1)}), bf16[8,256,256]{2,1,0:T(8,128)(2,1)S(1)}, u32[]{:S(2)}, u32[]{:S(2)}) async-start(bf16[8,256,256]{2,1,0:T(8,128)(2,1)} %bitcast.29), calls=%async_computation | async-start | bytes 2097152 | tf_op jit(solution)/shard_map/sum_over_row/all_to_all | solution.py:308
  155.0 12.6 %all-to-all-done.pieces = bf16[8,256,256]{2,1,0:T(8,128)(2,1)S(1)} async-done(((bf16[8,256,256]{2,1,0:T(8,128)(2,1)}), bf16[8,256,256]{2,1,0:T(8,128)(2,1)S(1)}, u32[]{:S(2)}, u32[]{:S(2)}) %all-to-all-start) | async-done | bytes 1048608 | tf_op jit(solution)/shard_map/sum_over_row/all_to_all | solution.py:308
  167.6 1.0 copy-done
  168.6 2.2 %sum_over_row.1 = bf16[256,256]{1,0:T(8,128)(2,1)} custom-call(bf16[8,256,256]{2,1,0:T(8,128)(2,1)} %copy-done, bf16[256,256]{1,0:T(8,128)(2,1)} %weight.1), custom_call_target="tpu_custom_call" | custom-call | tf_op jit(solution)/shard_map/sum_over_row/pallas_call | solution.py:228
  (61 shorter events, 6.5 us)
Async XLA Ops:
  0.6 10.8 %collective-permute-start = (bf16[256,256]{1,0:T(8,128)(2,1)}, bf16[256,256]{1,0:T(8,128)(2,1)}, u32[]{:S(2)}, u32[]{:S(2)}) collective-permute-start(bf16[256,256]{1,0:T(8,128)(2,1)} %param.8), channel_id=1, source_target_pairs={{0,32},{32,0},{64,96},{96,64},{128,160},{160,128},{192,224},{224,1... | collective-permute-start | bytes 393224 | tf_op jit(solution)/shard_map/gather_features/ppermute | solution.py:29
  3.2 9.7 %collective-permute-start.1 = (bf16[256,256]{1,0:T(8,128)(2,1)}, bf16[256,256]{1,0:T(8,128)(2,1)}, u32[]{:S(2)}, u32[]{:S(2)}) collective-permute-start(bf16[256,256]{1,0:T(8,128)(2,1)} %param.8), channel_id=1, source_target_pairs={{0,64},{32,96},{64,128},{96,160},{128,192},{160,224},{192,0},{224,... | collective-permute-start | bytes 393224 | tf_op jit(solution)/shard_map/gather_features/ppermute | solution.py:29
  4.4 9.9 %collective-permute-start.2 = (bf16[256,256]{1,0:T(8,128)(2,1)}, bf16[256,256]{1,0:T(8,128)(2,1)}, u32[]{:S(2)}, u32[]{:S(2)}) collective-permute-start(bf16[256,256]{1,0:T(8,128)(2,1)} %param.8), channel_id=1, source_target_pairs={{0,96},{32,64},{64,160},{96,128},{128,224},{160,192},{192,32},{224... | collective-permute-start | bytes 393224 | tf_op jit(solution)/shard_map/gather_features/ppermute | solution.py:29
  5.4 12.9 %collective-permute-start.3 = (bf16[256,256]{1,0:T(8,128)(2,1)}, bf16[256,256]{1,0:T(8,128)(2,1)}, u32[]{:S(2)}, u32[]{:S(2)}) collective-permute-start(bf16[256,256]{1,0:T(8,128)(2,1)} %param.8), channel_id=1, source_target_pairs={{0,128},{32,160},{64,192},{96,224},{128,0},{160,32},{192,64},{224,... | collective-permute-start | bytes 393224 | tf_op jit(solution)/shard_map/gather_features/ppermute | solution.py:29
  6.9 11.5 %collective-permute-start.4 = (bf16[256,256]{1,0:T(8,128)(2,1)}, bf16[256,256]{1,0:T(8,128)(2,1)}, u32[]{:S(2)}, u32[]{:S(2)}) collective-permute-start(bf16[256,256]{1,0:T(8,128)(2,1)} %param.8), channel_id=1, source_target_pairs={{0,160},{32,128},{64,224},{96,192},{128,32},{160,0},{192,96},{224,... | collective-permute-start | bytes 393224 | tf_op jit(solution)/shard_map/gather_features/ppermute | solution.py:29
  11.4 6.9 %collective-permute-start.5 = (bf16[256,256]{1,0:T(8,128)(2,1)}, bf16[256,256]{1,0:T(8,128)(2,1)}, u32[]{:S(2)}, u32[]{:S(2)}) collective-permute-start(bf16[256,256]{1,0:T(8,128)(2,1)} %param.8), channel_id=1, source_target_pairs={{0,192},{32,224},{64,0},{96,32},{128,64},{160,96},{192,128},{224,1... | collective-permute-start | bytes 393224 | tf_op jit(solution)/shard_map/gather_features/ppermute | solution.py:29
  12.9 5.4 %collective-permute-start.6 = (bf16[256,256]{1,0:T(8,128)(2,1)}, bf16[256,256]{1,0:T(8,128)(2,1)}, u32[]{:S(2)}, u32[]{:S(2)}) collective-permute-start(bf16[256,256]{1,0:T(8,128)(2,1)} %param.8), channel_id=1, source_target_pairs={{0,224},{32,192},{64,32},{96,0},{128,96},{160,64},{192,160},{224,1... | collective-permute-start | bytes 393224 | tf_op jit(solution)/shard_map/gather_features/ppermute | solution.py:29
  25.0 5.9 %collective-permute-start.7 = (bf16[16,128,256]{2,1,0:T(8,128)(2,1)}, bf16[16,128,256]{2,1,0:T(8,128)(2,1)S(1)}, u32[]{:S(2)}, u32[]{:S(2)}) collective-permute-start(bf16[16,128,256]{2,1,0:T(8,128)(2,1)} %get-tuple-element.22), channel_id=1, source_target_pairs={{0,1},{1,0},{2,3},{3,2},{4,5},{5,4},{6,7},{7,6},{8,9},{9,8},{10,11... | collective-permute-start | bytes 3145736 | tf_op jit(solution)/shard_map/sum_over_col/ppermute | solution.py:39
  28.4 11.6 %collective-permute-start.12 = (bf16[16,128,256]{2,1,0:T(8,128)(2,1)}, bf16[16,128,256]{2,1,0:T(8,128)(2,1)S(1)}, u32[]{:S(2)}, u32[]{:S(2)}) collective-permute-start(bf16[16,128,256]{2,1,0:T(8,128)(2,1)} %get-tuple-element.24), channel_id=1, source_target_pairs={{0,1},{1,0},{2,3},{3,2},{4,5},{5,4},{6,7},{7,6},{8,9},{9,8},{10,11... | collective-permute-start | bytes 3145736 | tf_op jit(solution)/shard_map/sum_over_col/ppermute | solution.py:39
  32.4 10.5 %collective-permute-start.10 = (bf16[4,128,256]{2,1,0:T(8,128)(2,1)S(1)}, bf16[4,128,256]{2,1,0:T(8,128)(2,1)S(1)}, u32[]{:S(2)}, u32[]{:S(2)}) collective-permute-start(bf16[4,128,256]{2,1,0:T(8,128)(2,1)S(1)} %get-tuple-element.46), channel_id=1, source_target_pairs={{0,6},{1,7},{2,0},{3,1},{4,2},{5,3},{6,4},{7,5},{8,14},{9,15},{10,... | collective-permute-start | bytes 786440 | tf_op jit(solution)/shard_map/sum_over_col/ppermute | solution.py:39
  34.8 10.1 %collective-permute-start.9 = (bf16[4,128,256]{2,1,0:T(8,128)(2,1)S(1)}, bf16[4,128,256]{2,1,0:T(8,128)(2,1)S(1)}, u32[]{:S(2)}, u32[]{:S(2)}) collective-permute-start(bf16[4,128,256]{2,1,0:T(8,128)(2,1)S(1)} %get-tuple-element.47), channel_id=1, source_target_pairs={{0,2},{1,3},{2,4},{3,5},{4,6},{5,7},{6,0},{7,1},{8,10},{9,11},{10,... | collective-permute-start | bytes 786440 | tf_op jit(solution)/shard_map/sum_over_col/ppermute | solution.py:39
  35.1 16.4 %collective-permute-start.8 = (bf16[4,128,256]{2,1,0:T(8,128)(2,1)S(1)}, bf16[4,128,256]{2,1,0:T(8,128)(2,1)S(1)}, u32[]{:S(2)}, u32[]{:S(2)}) collective-permute-start(bf16[4,128,256]{2,1,0:T(8,128)(2,1)S(1)} %get-tuple-element.48), channel_id=1, source_target_pairs={{0,4},{1,5},{2,6},{3,7},{4,0},{5,1},{6,2},{7,3},{8,12},{9,13},{10,... | collective-permute-start | bytes 786440 | tf_op jit(solution)/shard_map/sum_over_col/ppermute | solution.py:39
  41.5 21.7 %collective-permute-start.13 = (bf16[4,128,256]{2,1,0:T(8,128)(2,1)S(1)}, bf16[4,128,256]{2,1,0:T(8,128)(2,1)S(1)}, u32[]{:S(2)}, u32[]{:S(2)}) collective-permute-start(bf16[4,128,256]{2,1,0:T(8,128)(2,1)S(1)} %get-tuple-element.43), channel_id=1, source_target_pairs={{0,4},{1,5},{2,6},{3,7},{4,0},{5,1},{6,2},{7,3},{8,12},{9,13},{10,... | collective-permute-start | bytes 786440 | tf_op jit(solution)/shard_map/sum_over_col/ppermute | solution.py:39
  41.6 21.6 %collective-permute-start.14 = (bf16[4,128,256]{2,1,0:T(8,128)(2,1)S(1)}, bf16[4,128,256]{2,1,0:T(8,128)(2,1)S(1)}, u32[]{:S(2)}, u32[]{:S(2)}) collective-permute-start(bf16[4,128,256]{2,1,0:T(8,128)(2,1)S(1)} %get-tuple-element.42), channel_id=1, source_target_pairs={{0,2},{1,3},{2,4},{3,5},{4,6},{5,7},{6,0},{7,1},{8,10},{9,11},{10,... | collective-permute-start | bytes 786440 | tf_op jit(solution)/shard_map/sum_over_col/ppermute | solution.py:39
  42.9 20.3 %collective-permute-start.15 = (bf16[4,128,256]{2,1,0:T(8,128)(2,1)S(1)}, bf16[4,128,256]{2,1,0:T(8,128)(2,1)S(1)}, u32[]{:S(2)}, u32[]{:S(2)}) collective-permute-start(bf16[4,128,256]{2,1,0:T(8,128)(2,1)S(1)} %get-tuple-element.41), channel_id=1, source_target_pairs={{0,6},{1,7},{2,0},{3,1},{4,2},{5,3},{6,4},{7,5},{8,14},{9,15},{10,... | collective-permute-start | bytes 786440 | tf_op jit(solution)/shard_map/sum_over_col/ppermute | solution.py:39
  51.6 11.9 %collective-permute-start.16 = (bf16[2,128,256]{2,1,0:T(8,128)(2,1)S(1)}, bf16[2,128,256]{2,1,0:T(8,128)(2,1)S(1)}, u32[]{:S(2)}, u32[]{:S(2)}) collective-permute-start(bf16[2,128,256]{2,1,0:T(8,128)(2,1)S(1)} %get-tuple-element.51), channel_id=1, source_target_pairs={{0,8},{1,9},{2,10},{3,11},{4,12},{5,13},{6,14},{7,15},{8,16},{9,17... | collective-permute-start | bytes 393224 | tf_op jit(solution)/shard_map/sum_over_col/ppermute | solution.py:39
  53.7 13.5 %collective-permute-start.11 = (bf16[2,128,256]{2,1,0:T(8,128)(2,1)S(1)}, bf16[2,128,256]{2,1,0:T(8,128)(2,1)S(1)}, u32[]{:S(2)}, u32[]{:S(2)}) collective-permute-start(bf16[2,128,256]{2,1,0:T(8,128)(2,1)S(1)} %get-tuple-element.52), channel_id=1, source_target_pairs={{0,16},{1,17},{2,18},{3,19},{4,20},{5,21},{6,22},{7,23},{8,24},{9,... | collective-permute-start | bytes 393224 | tf_op jit(solution)/shard_map/sum_over_col/ppermute | solution.py:39
  63.5 10.9 %copy-start.9 = (bf16[2,128,256]{2,1,0:T(8,128)(2,1)}, bf16[2,128,256]{2,1,0:T(8,128)(2,1)S(1)}, u32[]{:S(2)}) copy-start(bf16[2,128,256]{2,1,0:T(8,128)(2,1)S(1)} %collective-permute-done.16) | copy-start | bytes 393220
  64.3 10.1 %collective-permute-start.17 = (bf16[2,128,256]{2,1,0:T(8,128)(2,1)S(1)}, bf16[2,128,256]{2,1,0:T(8,128)(2,1)S(1)}, u32[]{:S(2)}, u32[]{:S(2)}) collective-permute-start(bf16[2,128,256]{2,1,0:T(8,128)(2,1)S(1)} %get-tuple-element.50), channel_id=1, source_target_pairs={{0,24},{1,25},{2,26},{3,27},{4,28},{5,29},{6,30},{7,31},{8,0},{9,1... | collective-permute-start | bytes 393224 | tf_op jit(solution)/shard_map/sum_over_col/ppermute | solution.py:39
  67.2 7.2 %copy-start.10 = (bf16[2,128,256]{2,1,0:T(8,128)(2,1)}, bf16[2,128,256]{2,1,0:T(8,128)(2,1)S(1)}, u32[]{:S(2)}) copy-start(bf16[2,128,256]{2,1,0:T(8,128)(2,1)S(1)} %collective-permute-done.11) | copy-start | bytes 393220
  74.3 0.6 copy-start.11
  77.5 7.8 %collective-permute-start.18 = (bf16[256,256]{1,0:T(8,128)(2,1)}, bf16[256,256]{1,0:T(8,128)(2,1)S(1)}, u32[]{:S(2)}, u32[]{:S(2)}) collective-permute-start(bf16[256,256]{1,0:T(8,128)(2,1)} %get-tuple-element.31), channel_id=1, source_target_pairs={{0,8},{1,9},{2,10},{3,11},{4,12},{5,13},{6,14},{7,15},{8,16},{9,17... | collective-permute-start | bytes 393224 | tf_op jit(solution)/shard_map/gather_gradients/ppermute | solution.py:39
  77.7 8.1 %collective-permute-start.19 = (bf16[256,256]{1,0:T(8,128)(2,1)}, bf16[256,256]{1,0:T(8,128)(2,1)S(1)}, u32[]{:S(2)}, u32[]{:S(2)}) collective-permute-start(bf16[256,256]{1,0:T(8,128)(2,1)} %get-tuple-element.31), channel_id=1, source_target_pairs={{0,16},{1,17},{2,18},{3,19},{4,20},{5,21},{6,22},{7,23},{8,24},{9,... | collective-permute-start | bytes 393224 | tf_op jit(solution)/shard_map/gather_gradients/ppermute | solution.py:39
  81.8 5.2 %collective-permute-start.20 = (bf16[256,256]{1,0:T(8,128)(2,1)}, bf16[256,256]{1,0:T(8,128)(2,1)S(1)}, u32[]{:S(2)}, u32[]{:S(2)}) collective-permute-start(bf16[256,256]{1,0:T(8,128)(2,1)} %get-tuple-element.31), channel_id=1, source_target_pairs={{0,24},{1,25},{2,26},{3,27},{4,28},{5,29},{6,30},{7,31},{8,0},{9,1... | collective-permute-start | bytes 393224 | tf_op jit(solution)/shard_map/gather_gradients/ppermute | solution.py:39
  87.0 31.4 %all-to-all-start.1 = ((bf16[32,8,384]{2,1,0:T(8,128)(2,1)}), bf16[32,8,384]{2,1,0:T(8,128)(2,1)S(1)}, u32[]{:S(2)}, u32[]{:S(2)}) async-start(bf16[32,8,384]{2,1,0:T(8,128)(2,1)} %bitcast.33), calls=%async_computation.1 | async-start | bytes 393216 | tf_op jit(solution)/shard_map/sum_weight_grad/all_to_all | solution.py:295
  106.6 32.7 %copy-start.1 = (bf16[1024,256]{1,0:T(8,128)(2,1)}, bf16[1024,256]{1,0:T(8,128)(2,1)S(1)}, u32[]{:S(2)}) copy-start(bf16[1024,256]{1,0:T(8,128)(2,1)S(1)} %constant_dynamic-update-slice_fusion) | copy-start | bytes 1572868
  106.6 28.1 %collective-permute-start.21 = (bf16[1024,256]{1,0:T(8,128)(2,1)S(1)}, bf16[1024,256]{1,0:T(8,128)(2,1)S(1)}, u32[]{:S(2)}, u32[]{:S(2)}) collective-permute-start(bf16[1024,256]{1,0:T(8,128)(2,1)S(1)} %constant_dynamic-update-slice_fusion), channel_id=1, source_target_pairs={{0,2},{1,3},{2,4},{3,5},{4,6},{5,7},{6,0},{7,1},{8,10},{9,11},{10,... | collective-permute-start | bytes 1572872 | tf_op jit(solution)/shard_map/gather_gradients/ppermute | solution.py:39
  108.0 27.2 %collective-permute-start.22 = (bf16[1024,256]{1,0:T(8,128)(2,1)S(1)}, bf16[1024,256]{1,0:T(8,128)(2,1)S(1)}, u32[]{:S(2)}, u32[]{:S(2)}) collective-permute-start(bf16[1024,256]{1,0:T(8,128)(2,1)S(1)} %constant_dynamic-update-slice_fusion), channel_id=1, source_target_pairs={{0,4},{1,5},{2,6},{3,7},{4,0},{5,1},{6,2},{7,3},{8,12},{9,13},{10,... | collective-permute-start | bytes 1572872 | tf_op jit(solution)/shard_map/gather_gradients/ppermute | solution.py:39
  110.4 25.7 %collective-permute-start.23 = (bf16[1024,256]{1,0:T(8,128)(2,1)S(1)}, bf16[1024,256]{1,0:T(8,128)(2,1)S(1)}, u32[]{:S(2)}, u32[]{:S(2)}) collective-permute-start(bf16[1024,256]{1,0:T(8,128)(2,1)S(1)} %constant_dynamic-update-slice_fusion), channel_id=1, source_target_pairs={{0,6},{1,7},{2,0},{3,1},{4,2},{5,3},{6,4},{7,5},{8,14},{9,15},{10,... | collective-permute-start | bytes 1572872 | tf_op jit(solution)/shard_map/gather_gradients/ppermute | solution.py:39
  129.3 20.7 %all-to-all-start.3 = ((f32[32,8,384]{2,1,0:T(8,128)}), f32[32,8,384]{2,1,0:T(8,128)S(1)}, u32[]{:S(2)}, u32[]{:S(2)}) async-start(f32[32,8,384]{2,1,0:T(8,128)} %broadcast_in_dim.7), calls=%async_computation.3 | async-start | bytes 786432 | tf_op jit(solution)/shard_map/sum_weight_grad/all_to_all | solution.py:312
  134.2 2.0 %collective-permute-start.24 = (bf16[1024,256]{1,0:T(8,128)(2,1)S(1)}, bf16[1024,256]{1,0:T(8,128)(2,1)S(1)}, u32[]{:S(2)}, u32[]{:S(2)}) collective-permute-start(bf16[1024,256]{1,0:T(8,128)(2,1)S(1)} %constant_dynamic-update-slice_fusion), channel_id=1, source_target_pairs={{0,1},{1,0},{2,3},{3,2},{4,5},{5,4},{6,7},{7,6},{8,9},{9,8},{10,11... | collective-permute-start | bytes 1572872 | tf_op jit(solution)/shard_map/gather_gradients/ppermute | solution.py:39
  134.6 4.7 %copy-start.2 = (bf16[1024,256]{1,0:T(8,128)(2,1)}, bf16[1024,256]{1,0:T(8,128)(2,1)S(1)}, u32[]{:S(2)}) copy-start(bf16[1024,256]{1,0:T(8,128)(2,1)S(1)} %collective-permute-done.21) | copy-start | bytes 1572868
  134.6 2.3 %collective-permute-start.25 = (bf16[1024,256]{1,0:T(8,128)(2,1)S(1)}, bf16[1024,256]{1,0:T(8,128)(2,1)S(1)}, u32[]{:S(2)}, u32[]{:S(2)}) collective-permute-start(bf16[1024,256]{1,0:T(8,128)(2,1)S(1)} %collective-permute-done.21), channel_id=1, source_target_pairs={{0,1},{1,0},{2,3},{3,2},{4,5},{5,4},{6,7},{7,6},{8,9},{9,8},{10,11... | collective-permute-start | bytes 1572872 | tf_op jit(solution)/shard_map/gather_gradients/ppermute | solution.py:39
  135.3 4.0 %copy-start.3 = (bf16[1024,256]{1,0:T(8,128)(2,1)}, bf16[1024,256]{1,0:T(8,128)(2,1)S(1)}, u32[]{:S(2)}) copy-start(bf16[1024,256]{1,0:T(8,128)(2,1)S(1)} %collective-permute-done.22) | copy-start | bytes 1572868
  135.3 2.4 %collective-permute-start.26 = (bf16[1024,256]{1,0:T(8,128)(2,1)S(1)}, bf16[1024,256]{1,0:T(8,128)(2,1)S(1)}, u32[]{:S(2)}, u32[]{:S(2)}) collective-permute-start(bf16[1024,256]{1,0:T(8,128)(2,1)S(1)} %collective-permute-done.22), channel_id=1, source_target_pairs={{0,1},{1,0},{2,3},{3,2},{4,5},{5,4},{6,7},{7,6},{8,9},{9,8},{10,11... | collective-permute-start | bytes 1572872 | tf_op jit(solution)/shard_map/gather_gradients/ppermute | solution.py:39
  136.1 3.2 %copy-start.4 = (bf16[1024,256]{1,0:T(8,128)(2,1)}, bf16[1024,256]{1,0:T(8,128)(2,1)S(1)}, u32[]{:S(2)}) copy-start(bf16[1024,256]{1,0:T(8,128)(2,1)S(1)} %collective-permute-done.23) | copy-start | bytes 1572868
  136.1 2.3 %collective-permute-start.27 = (bf16[1024,256]{1,0:T(8,128)(2,1)S(1)}, bf16[1024,256]{1,0:T(8,128)(2,1)S(1)}, u32[]{:S(2)}, u32[]{:S(2)}) collective-permute-start(bf16[1024,256]{1,0:T(8,128)(2,1)S(1)} %collective-permute-done.23), channel_id=1, source_target_pairs={{0,1},{1,0},{2,3},{3,2},{4,5},{5,4},{6,7},{7,6},{8,9},{9,8},{10,11... | collective-permute-start | bytes 1572872 | tf_op jit(solution)/shard_map/gather_gradients/ppermute | solution.py:39
  136.2 3.1 %copy-start.5 = (bf16[1024,256]{1,0:T(8,128)(2,1)}, bf16[1024,256]{1,0:T(8,128)(2,1)S(1)}, u32[]{:S(2)}) copy-start(bf16[1024,256]{1,0:T(8,128)(2,1)S(1)} %collective-permute-done.24) | copy-start | bytes 1572868
  137.0 2.4 %copy-start.6 = (bf16[1024,256]{1,0:T(8,128)(2,1)}, bf16[1024,256]{1,0:T(8,128)(2,1)S(1)}, u32[]{:S(2)}) copy-start(bf16[1024,256]{1,0:T(8,128)(2,1)S(1)} %collective-permute-done.25) | copy-start | bytes 1572868
  137.7 1.6 copy-start.7
  138.5 0.8 copy-start.8
  150.0 17.6 %all-to-all-start = ((bf16[8,256,256]{2,1,0:T(8,128)(2,1)}), bf16[8,256,256]{2,1,0:T(8,128)(2,1)S(1)}, u32[]{:S(2)}, u32[]{:S(2)}) async-start(bf16[8,256,256]{2,1,0:T(8,128)(2,1)} %bitcast.29), calls=%async_computation | async-start | bytes 2097152 | tf_op jit(solution)/shard_map/sum_over_row/all_to_all | solution.py:308
  167.6 1.0 copy-start
